TPU v7x, 32 devices: a whole 2x2x4 slice. The times are simulated.
32 devices in a mesh: seq: 8 (over z, y), mp: 4 (over x, core).
Axes of the slice: x: 2, y: 2, z: 4, core: 2. Of those that a mesh axis runs over, the one named last changes fastest.
Arguments:
- byte_hidden: bfloat16 [8192, 1024], P('seq', 'mp'), may hold values from -6 to 6
- patch_start: int32 [8192], P('seq'), may hold values from 0 to 1, as said below
- pool_query: bfloat16 [1024], P('mp'), may hold values from -4 to 4
- in_weight: bfloat16 [1024, 4096], P('seq', 'mp'), may hold values from -0.1875 to 0.1875
- latent_grad: bfloat16 [4096, 4096], P('seq', 'mp'), may hold values from -6 to 6
Outputs:
- latent: bfloat16 [4096, 4096], P('seq', 'mp')
- grad_weight: float32 [1024, 4096], P('seq', 'mp')
- grad_bytes: bfloat16 [8192, 1024], P('seq', 'mp')
Inputs may be any that keep to these rules, and one draw needn't show every extreme that they name: `patch_start`: byte 0 begins a patch, and so does every byte whose position is 16 // 2 modulo 16; of the bytes 2k and 2k+1 at most one begins a patch. So no patch is longer than 16 bytes, and some patch is exactly 16 long. Each aligned block of 1024 bytes holds at most 512 patch starts, and one block holds exactly 512.
All inputs are finite; a program needn't handle non-finite values.
Results may differ from a plain program's by a relative error of at most 0.0049.
Values may be sent and summed in bfloat16 or wider, within the bound.
No kernel may reach another device: no remote copies, remote signals or barrier semaphores. Data moves between devices by JAX's collectives and lax.ppermute only.
A program may use at most 64 MiB of HBM per device.

v0:
```python
import math

import jax
import jax.numpy as jnp
from jax import lax
from jax.sharding import PartitionSpec as P

HEAD_DIM = 64
MAXLEN = 16


soft_cap = 20.0


def from_behind(value, axis, steps):
    count = lax.axis_size(axis)
    leading, last = (max(0, -steps), min(count, count - steps))
    return lax.ppermute(value, axis, [(source, source + steps) for source in range(leading, last)])


def shards(byte_hidden, patch_start, pool_query, in_weight, latent_grad):
    rows_local, feats = byte_hidden.shape
    slots = latent_grad.shape[0]
    head_dim = HEAD_DIM
    local_heads = feats // head_dim
    inv_root = 1.0 / math.sqrt(head_dim)
    query = pool_query.astype(jnp.float32)

    def capped_scores(block):
        raw = (block.astype(jnp.float32) * query).reshape(-1, local_heads, head_dim).sum(
            -1
        ) * inv_root
        return soft_cap * jnp.tanh(raw / soft_cap)

    capped = capped_scores(byte_hidden)
    weight_exp = jnp.exp(capped)
    hidden_f = byte_hidden.astype(jnp.float32)
    patch_total = jnp.sum(patch_start)
    segment = jnp.cumsum(patch_start) - 1
    leading = segment < 0
    inside = jnp.maximum(segment, 0)
    keep_own = jnp.where(leading, 0.0, 1.0).astype(jnp.float32)[:, None]
    weighted = jnp.repeat(weight_exp, head_dim, axis=1) * hidden_f
    numer = jax.ops.segment_sum(weighted * keep_own, inside, num_segments=slots)
    denom = jax.ops.segment_sum(weight_exp * keep_own, inside, num_segments=slots)
    lead_mask = leading[:MAXLEN].astype(jnp.bfloat16)
    next_rows, next_mask = from_behind((byte_hidden[:MAXLEN], lead_mask), "seq", -1)
    next_exp = jnp.exp(capped_scores(next_rows)) * next_mask.astype(jnp.float32)[:, None]
    recv_num = jnp.sum(
        jnp.repeat(next_exp, head_dim, axis=1) * next_rows.astype(jnp.float32), axis=0
    )
    recv_den = jnp.sum(next_exp, axis=0)
    slot_index = jnp.arange(slots)
    last_row = (slot_index == patch_total - 1).astype(jnp.float32)[:, None]
    numer = numer + last_row * recv_num
    denom = denom + last_row * recv_den
    live = (slot_index < patch_total)[:, None]
    safe = jnp.where(live, denom, jnp.float32(1.0))
    pooled = jnp.where(live, numer / jnp.repeat(safe, head_dim, axis=1), jnp.float32(0.0))
    pooled_low = pooled.astype(jnp.bfloat16)
    pooled_full = lax.all_gather(pooled_low, "mp", axis=1, tiled=True)
    weight_full = lax.all_gather(in_weight, "seq", axis=0, tiled=True)
    latent = jnp.dot(pooled_full, weight_full, preferred_element_type=jnp.float32)
    partial_value = lax.dot_general(
        latent_grad, weight_full, (((1,), (1,)), ((), ())), preferred_element_type=jnp.float32
    )
    latent_out = latent.astype(jnp.bfloat16)
    received = lax.all_to_all(
        partial_value.astype(jnp.bfloat16), "mp", split_axis=1, concat_axis=0, tiled=True
    )
    grad_pooled = received.reshape(-1, slots, feats).astype(jnp.float32).sum(0)
    grad_scale = 1.0 / math.sqrt(lax.axis_size("seq") * slots)
    grad_weight = lax.psum_scatter(
        lax.dot_general(
            pooled_full, latent_grad, (((0,), (0,)), ((), ())), preferred_element_type=jnp.float32
        )
        * grad_scale,
        "seq",
        scatter_dimension=0,
        tiled=True,
    )
    last_grad = jnp.sum(last_row * grad_pooled, axis=0)
    last_pooled = jnp.sum(last_row * pooled, axis=0)
    last_den = jnp.sum(last_row * safe, axis=0)
    prev_grad, prev_pooled, prev_den = from_behind((last_grad, last_pooled, last_den), "seq", 1)
    lead_col = leading[:, None]
    grad_rows = jnp.where(lead_col, prev_grad[None, :], jnp.take(grad_pooled, inside, axis=0))
    pooled_rows = jnp.where(lead_col, prev_pooled[None, :], jnp.take(pooled, inside, axis=0))
    den_rows = jnp.where(lead_col, prev_den[None, :], jnp.take(safe, inside, axis=0))
    share = weight_exp / den_rows
    inner = (
        (grad_rows * (hidden_f - pooled_rows)).reshape(rows_local, local_heads, head_dim).sum(-1)
    )
    coeff = share * inner * (1.0 - (capped / soft_cap) ** 2) * inv_root
    grad_bytes = (
        jnp.repeat(share, head_dim, axis=1) * grad_rows
        + jnp.repeat(coeff, head_dim, axis=1) * query
    )
    return (latent_out, grad_weight, grad_bytes.astype(jnp.bfloat16))


def solution(mesh):
    in_specs = (P("seq", "mp"), P("seq"), P("mp"), P("seq", "mp"), P("seq", "mp"))
    out_specs = (P("seq", "mp"), P("seq", "mp"), P("seq", "mp"))
    return jax.shard_map(shards, mesh=mesh, in_specs=in_specs, out_specs=out_specs, check_vma=False)
```

profile of v0, /device:TPU:0, one launch (start us, length us, event | category | flops | bytes accessed | tf_op | source)
XLA Modules:
  0.0 208.5 jit_solution(16157713605653174010)
XLA Ops:
  9.2 1.3 collective-permute-start.1
  11.2 1.3 collective-permute-start
  12.5 1.3 reduce_sum.90
  19.4 42.8 %all-gather.5.cloned.1.call-done = bf16[1024,1024]{1,0:T(8,128)(2,1)} async-done(((bf16[128,1024]{1,0:T(8,128)(2,1)}), bf16[1024,1024]{1,0:T(8,128)(2,1)}) %all-gather.5.cloned.1.call-update) | async-done | bytes 2097168 | tf_op jit(solution)/shard_map/all_gather | solution.py:62
  62.2 2.9 %convolution_convert_fusion = bf16[512,1024]{1,0:T(8,128)(2,1)S(1)} fusion(bf16[512,1024]{1,0:T(8,128)(2,1)S(1)} %copy-done, bf16[1024,1024]{1,0:T(8,128)(2,1)} %all-gather.5.cloned.1.call-done), kind=kOutput, calls=%fused_computation.10 | convolution fusion | flops 1074266112 | bytes 4194304 | tf_op jit(solution)/shard_map/dot_general | solution.py:64
  66.1 4.2 %all-to-all-start = ((bf16[512,4,256]{2,0,1:T(8,128)(2,1)}), bf16[512,4,256]{2,0,1:T(8,128)(2,1)}, u32[]{:S(2)}, u32[]{:S(2)}) async-start(bf16[512,4,256]{2,0,1:T(8,128)(2,1)} %bitcast.24), calls=%async_computation.1 | async-start | bytes 2097152 | tf_op jit(solution)/shard_map/all_to_all | solution.py:68
  70.5 6.7 %scatter_fusion = f32[512,4]{1,0:T(8,128)S(1)} fusion(f32[512,4]{1,0:T(8,128)S(1)} %broadcast_multiply_fusion.1, s32[1024]{0:T(1024)S(1)} %get-tuple-element.9, f32[1024,4]{1,0:T(8,128)S(1)} %copy-done.3), kind=kCustom, calls=%fused_computation.4 | custom fusion | flops 4096 | bytes 53248 | tf_op jit(solution)/shard_map/scatter-add | solution.py:45
  80.6 8.9 %scatter_custom_fusion = f32[512,256]{1,0:T(8,128)} fusion(f32[512,256]{1,0:T(8,128)} %broadcast_multiply_fusion, s32[1024]{0:T(1024)S(1)} %get-tuple-element.9, f32[1024,256]{1,0:T(8,128)S(1)} %copy.42, bf16[1024,256]{1,0:T(8,128)(2,1)S(1)} %copy-done.1, f32[1024]{0:T(1024)S(1)} %get-tuple-element.15), kind=kCustom, calls=%fused_computation.13 | custom fusion | flops 1048576 | bytes 2101248 | tf_op jit(solution)/shard_map/scatter-add | solution.py:44
  89.5 1.4 convert_reduce_fusion
  93.0 16.4 %all-gather.3.cloned.1.call-done = bf16[512,1024]{1,0:T(8,128)(2,1)} async-done(((bf16[512,256]{1,0:T(8,128)(2,1)}), bf16[512,1024]{1,0:T(8,128)(2,1)}) %all-gather.3.cloned.1.call-update) | async-done | bytes 1048592 | tf_op jit(solution)/shard_map/all_gather | solution.py:61
  109.4 4.4 %convolution_multiply_fusion = f32[1024,1024]{1,0:T(8,128)} fusion(bf16[512,1024]{1,0:T(8,128)(2,1)} %all-gather.3.cloned.1.call-done, bf16[512,1024]{1,0:T(8,128)(2,1)S(1)} %copy-done), kind=kOutput, calls=%fused_computation.5 | convolution fusion | flops 1074790400 | bytes 6291456 | tf_op jit(solution)/shard_map/dot_general | solution.py:74
  113.9 3.4 %collective-permute-start.3 = (f32[256]{0:T(256)S(1)}, f32[256]{0:T(256)S(1)}, u32[]{:S(2)}, u32[]{:S(2)}) collective-permute-start(f32[256]{0:T(256)S(1)} %get-tuple-element.4), channel_id=1, source_target_pairs={{0,4},{4,8},{8,12},{12,16},{16,20},{20,24},{24,28},{1,5},{5,9},{9,... | collective-permute-start | bytes 3080 | tf_op jit(solution)/shard_map/ppermute | solution.py:18
  117.3 3.4 %collective-permute-start.4 = (f32[256]{0:T(256)S(1)}, f32[256]{0:T(256)S(1)}, u32[]{:S(2)}, u32[]{:S(2)}) collective-permute-start(f32[256]{0:T(256)S(1)} %get-tuple-element.5), channel_id=1, source_target_pairs={{0,4},{4,8},{8,12},{12,16},{16,20},{20,24},{24,28},{1,5},{5,9},{9,... | collective-permute-start | bytes 3080 | tf_op jit(solution)/shard_map/ppermute | solution.py:18
  120.7 3.6 %collective-permute-start.2 = (f32[4]{0:T(128)S(1)}, f32[4]{0:T(128)S(1)}, u32[]{:S(2)}, u32[]{:S(2)}) collective-permute-start(f32[4]{0:T(128)S(1)} %get-tuple-element.11), channel_id=1, source_target_pairs={{0,4},{4,8},{8,12},{12,16},{16,20},{20,24},{24,28},{1,5},{5,9},{9,... | collective-permute-start | bytes 56 | tf_op jit(solution)/shard_map/ppermute | solution.py:18
  124.2 2.8 %gather_fusion = f32[1024,4]{1,0:T(8,128)S(1)} fusion(f32[512,4]{1,0:T(8,128)S(1)} %get-tuple-element.12, s32[1024]{0:T(1024)S(1)} %get-tuple-element.19), kind=kCustom, calls=%fused_computation.2 | custom fusion | bytes 36864 | tf_op jit(solution)/shard_map/jit(_take)/gather | solution.py:89
  127.2 3.5 %gather_fusion.1 = f32[1024,256]{1,0:T(8,128)S(1)} fusion(f32[512,256]{1,0:T(8,128)S(1)} %convert_reduce_fusion, s32[1024]{0:T(1024)S(1)} %get-tuple-element.20), kind=kCustom, calls=%fused_computation.clone | custom fusion | bytes 2101248 | tf_op jit(solution)/shard_map/jit(_take)/gather | solution.py:87
  130.7 4.7 %gather_fusion.2 = f32[1024,256]{1,0:T(8,128)} fusion(f32[512,256]{1,0:T(8,128)S(1)} %get-tuple-element.10, s32[1024]{0:T(1024)S(1)} %get-tuple-element.20), kind=kCustom, calls=%fused_computation.1.clone | custom fusion | bytes 2101248 | tf_op jit(solution)/shard_map/jit(_take)/gather | solution.py:88
  135.4 2.8 %fusion.3 = f32[1024,256]{1,0:T(8,128)} fusion(bf16[1024,256]{1,0:T(8,128)(2,1)S(1)} %copy-done.2, f32[1024,256]{1,0:T(8,128)} %gather_fusion.2, f32[1024,256]{1,0:T(8,128)S(1)} %gather_fusion.1, f32[256]{0:T(256)S(1)} %collective-permute-done.4, f32[256]{0:T(256)S(1)} %collective-permute-done.3, pred[1024]{0:T(1024)(128)(4,1)S(1)} %get-tuple-element.8, ...), kind=kLoop, calls=%fused_computation.14 | loop fusion | flops 1835008 | bytes 3674112 | tf_op jit(solution)/shard_map/mul | solution.py:92
  138.2 1.6 copy.49
  140.1 1.3 copy.50
  141.5 1.3 copy.48
  142.8 2.9 %add_convert_fusion = bf16[1024,256]{1,0:T(8,128)(2,1)} fusion(f32[1024,256]{1,0:T(8,128)} %copy.50, f32[1024,256]{1,0:T(8,128)} %copy.48, f32[1024,256]{1,0:T(8,128)S(1)} %gather_fusion.1, f32[256]{0:T(256)S(1)} %collective-permute-done.3, f32[256]{0:T(256)S(1)} %convert_element_type.42, pred[1024]{0:T(1024)(128)(4,1)S(1)} %get-tuple-element.8, ...), kind=kLoop, calls=%fused_computation.20 | loop fusion | flops 1572864 | bytes 3674112 | tf_op jit(solution)/shard_map/convert_element_type | solution.py:99
  145.7 2.2 %convolution_convert_fusion.1 = bf16[512,1024]{1,0:T(8,128)(2,1)} fusion(bf16[512,1024]{1,0:T(8,128)(2,1)S(1)} %copy-done.4, bf16[1024,1024]{1,0:T(8,128)(2,1)S(1)} %copy-done.5), kind=kOutput, calls=%fused_computation.11 | convolution fusion | flops 1074266112 | bytes 4194304 | tf_op jit(solution)/shard_map/dot_general | solution.py:63
  147.9 54.0 %reduce-scatter.2.cloned.1.call-done = f32[128,1024]{1,0:T(8,128)} async-done(((f32[1024,1024]{1,0:T(8,128)}), f32[128,1024]{1,0:T(8,128)}) %reduce-scatter.2.cloned.1.call-update) | async-done | bytes 524304 | tf_op jit(solution)/shard_map/reduce_scatter | solution.py:73
  (66 shorter events, 14.8 us)
Async XLA Ops:
  7.2 55.0 %copy-start = (bf16[512,1024]{1,0:T(8,128)(2,1)S(1)}, bf16[512,1024]{1,0:T(8,128)(2,1)}, u32[]{:S(2)}) copy-start(bf16[512,1024]{1,0:T(8,128)(2,1)} %param.11) | copy-start | bytes 3145732
  7.2 55.0 %all-gather.5.cloned.1.call-start = ((), (), s32[]{:S(2)}) async-start(), calls=%async_computation.3 | async-start | bytes 2359296 | tf_op jit(solution)/shard_map/all_gather | solution.py:62
  9.2 9.7 %collective-permute-start.1 = (bf16[16]{0:T(256)(128)(2,1)S(1)}, bf16[16]{0:T(256)(128)(2,1)S(1)}, u32[]{:S(2)}, u32[]{:S(2)}) collective-permute-start(bf16[16]{0:T(256)(128)(2,1)S(1)} %slice_convert_fusion), channel_id=1, source_target_pairs={{4,0},{8,4},{12,8},{16,12},{20,16},{24,20},{28,24},{5,1},{9,5},{13... | collective-permute-start | bytes 104 | tf_op jit(solution)/shard_map/ppermute | solution.py:18
  11.2 7.8 %collective-permute-start = (bf16[16,256]{1,0:T(8,128)(2,1)S(1)}, bf16[16,256]{1,0:T(8,128)(2,1)S(1)}, u32[]{:S(2)}, u32[]{:S(2)}) collective-permute-start(bf16[16,256]{1,0:T(8,128)(2,1)S(1)} %slice.13), channel_id=1, source_target_pairs={{4,0},{8,4},{12,8},{16,12},{20,16},{24,20},{28,24},{5,1},{9,5},{13... | collective-permute-start | bytes 24584 | tf_op jit(solution)/shard_map/ppermute | solution.py:18
  65.0 5.5 %copy-start.3 = (f32[1024,4]{1,0:T(8,128)S(1)}, f32[1024,4]{1,0:T(8,128)}, u32[]{:S(2)}) copy-start(f32[1024,4]{1,0:T(8,128)} %copy.43) | copy-start | bytes 49156
  66.1 23.4 %all-to-all-start = ((bf16[512,4,256]{2,0,1:T(8,128)(2,1)}), bf16[512,4,256]{2,0,1:T(8,128)(2,1)}, u32[]{:S(2)}, u32[]{:S(2)}) async-start(bf16[512,4,256]{2,0,1:T(8,128)(2,1)} %bitcast.24), calls=%async_computation.1 | async-start | bytes 2097152 | tf_op jit(solution)/shard_map/all_to_all | solution.py:68
  70.3 39.1 %all-gather.3.cloned.1.call-start = ((), (), s32[]{:S(2)}) async-start(), calls=%async_computation.2 | async-start | bytes 1310720 | tf_op jit(solution)/shard_map/all_gather | solution.py:61
  77.2 3.4 %copy-start.1 = (bf16[1024,256]{1,0:T(8,128)(2,1)S(1)}, bf16[1024,256]{1,0:T(8,128)(2,1)}, u32[]{:S(2)}) copy-start(bf16[1024,256]{1,0:T(8,128)(2,1)} %param.7) | copy-start | bytes 1572868
  93.0 109.0 %reduce-scatter.2.cloned.1.call-start = ((), (), s32[]{:S(2)}) async-start(), calls=%async_computation.4 | async-start | bytes 4718592 | tf_op jit(solution)/shard_map/reduce_scatter | solution.py:73
  113.9 21.5 %collective-permute-start.3 = (f32[256]{0:T(256)S(1)}, f32[256]{0:T(256)S(1)}, u32[]{:S(2)}, u32[]{:S(2)}) collective-permute-start(f32[256]{0:T(256)S(1)} %get-tuple-element.4), channel_id=1, source_target_pairs={{0,4},{4,8},{8,12},{12,16},{16,20},{20,24},{24,28},{1,5},{5,9},{9,... | collective-permute-start | bytes 3080 | tf_op jit(solution)/shard_map/ppermute | solution.py:18
  117.3 18.2 %collective-permute-start.4 = (f32[256]{0:T(256)S(1)}, f32[256]{0:T(256)S(1)}, u32[]{:S(2)}, u32[]{:S(2)}) collective-permute-start(f32[256]{0:T(256)S(1)} %get-tuple-element.5), channel_id=1, source_target_pairs={{0,4},{4,8},{8,12},{12,16},{16,20},{20,24},{24,28},{1,5},{5,9},{9,... | collective-permute-start | bytes 3080 | tf_op jit(solution)/shard_map/ppermute | solution.py:18
  120.7 19.2 %collective-permute-start.2 = (f32[4]{0:T(128)S(1)}, f32[4]{0:T(128)S(1)}, u32[]{:S(2)}, u32[]{:S(2)}) collective-permute-start(f32[4]{0:T(128)S(1)} %get-tuple-element.11), channel_id=1, source_target_pairs={{0,4},{4,8},{8,12},{12,16},{16,20},{20,24},{24,28},{1,5},{5,9},{9,... | collective-permute-start | bytes 56 | tf_op jit(solution)/shard_map/ppermute | solution.py:18
  130.7 4.7 %copy-start.2 = (bf16[1024,256]{1,0:T(8,128)(2,1)S(1)}, bf16[1024,256]{1,0:T(8,128)(2,1)}, u32[]{:S(2)}) copy-start(bf16[1024,256]{1,0:T(8,128)(2,1)} %param.7) | copy-start | bytes 1572868
  142.8 2.9 %copy-start.4 = (bf16[512,1024]{1,0:T(8,128)(2,1)S(1)}, bf16[512,1024]{1,0:T(8,128)(2,1)}, u32[]{:S(2)}) copy-start(bf16[512,1024]{1,0:T(8,128)(2,1)} %all-gather.3.cloned.1.call-done) | copy-start | bytes 3145732
  142.8 2.9 %copy-start.5 = (bf16[1024,1024]{1,0:T(8,128)(2,1)S(1)}, bf16[1024,1024]{1,0:T(8,128)(2,1)}, u32[]{:S(2)}) copy-start(bf16[1024,1024]{1,0:T(8,128)(2,1)} %all-gather.5.cloned.1.call-done) | copy-start | bytes 6291460
Sparse Core Ops, SparseCore 0:
  10.1 51.9 all-gather.4
  93.1 16.2 all-gather.2
  114.0 87.9 reduce-scatter.1
where the time goes:
time: 209 us; the launch traced here: 208 us
  waiting for transfers between devices  114 us (55%)
  other arithmetic  31.3 us (15%)
  local copies, waits for them, and re-layouts  21.8 us (10%)
  starting transfers between devices  17.2 us (8%)
  between operations  14.7 us (7%)
  matrix products  9.55 us (5%)
    reduce_scatter x1, waiting for transfers between devices, shards(): lax.psum_scatter(lax.dot_general(pooled_full, latent_grad, (((0,), (0,)),...  54 us
    all_gather x1, waiting for transfers between devices, shards(): weight_full = lax.all_gather(in_weight, 'seq', axis=0, tiled=True)  42.8 us
    all_gather x1, waiting for transfers between devices, shards(): pooled_full = lax.all_gather(pooled_low, 'mp', axis=1, tiled=True)  16.4 us
    ppermute x5, starting transfers between devices, from_behind(): lax.ppermute(value, axis, [(source, source + steps) for source in range(l...  12.9 us
    scatter-add x1, other arithmetic, shards(): numer = jax.ops.segment_sum(weighted * keep_own, inside, num_segments=slots)  8.88 us
    scatter-add x1, other arithmetic, shards(): jax.ops.segment_sum(weight_exp * keep_own, inside, num_segments=slots)  6.68 us
    gather x1, local copies, waits for them, and re-layouts, shards(): jnp.take(pooled, inside, axis=0)  4.68 us
    dot_general x1, matrix products, shards(): lax.dot_general(pooled_full, latent_grad, (((0,), (0,)), ((), ())), prefe...  4.44 us
  transfers between devices with their start and end apart: 9, of which 3 were waited for; matrix products, arithmetic and copies ran while one was open for 24% of the time, Pallas kernels for 0%

commit v1 on v0

v1 whole, which is shorter than its diff:
```python
import functools
import math

import jax
import jax.numpy as jnp
from jax import lax
from jax.experimental import pallas as pl
from jax.experimental.pallas import tpu as pltpu
from jax.sharding import PartitionSpec as P

HEAD_DIM = 64
EDGE = 16
LANES = 128

soft_cap = 20.0
inv_root = 1.0 / math.sqrt(HEAD_DIM)
F32 = jnp.float32
BF16 = jnp.bfloat16
VMEM_LIMIT = 48 * 1024 * 1024
VMEM_MOST = 53 * 1024 * 1024


def iota(shape, dim):
    return lax.broadcasted_iota(jnp.int32, shape, dim)


def split(value):
    high = value.astype(BF16)
    return high, (value - high.astype(F32)).astype(BF16)


def dot(left, right, dims=((1,), (0,))):
    return lax.dot_general(left, right, (dims, ((), ())), preferred_element_type=F32)


def dot_split(left, value):
    high, low = split(value)
    return dot(left, high) + dot(left, low)


def head_sum(value):
    feats = value.shape[1]
    same = (iota((feats, feats), 0) // HEAD_DIM) == (iota((feats, feats), 1) // HEAD_DIM)
    block = jnp.where(same, 1.0, 0.0).astype(BF16)
    high, low = split(value)
    return dot(high, block) + dot(low, block)


def row_of(ref):
    value = ref[...].astype(F32)
    return jnp.concatenate([value[at : at + 1] for at in range(value.shape[0])], axis=1)


def scores(hidden, query):
    raw = head_sum(hidden * query) * inv_root
    bent = jnp.tanh(raw / soft_cap)
    return bent, jnp.exp(soft_cap * bent)


def segment_rows(start):
    upper = jnp.where(iota((LANES, LANES), 0) <= iota((LANES, LANES), 1), 1.0, 0.0).astype(BF16)
    count = dot(start.astype(F32).astype(BF16), upper)
    rows, total = [], jnp.full((1, 1), -1.0, F32)
    for index in range(start.shape[0]):
        row = count[index : index + 1]
        rows.append(row + total)
        total = total + row[:, LANES - 1 :]
    return rows, total


def lead_mask(start):
    first = jnp.broadcast_to(start[0:1].astype(F32), (EDGE, LANES))
    before = jnp.where(iota((EDGE, LANES), 1) <= iota((EDGE, LANES), 0), first, 0.0)
    return jnp.where(jnp.sum(before, axis=1, keepdims=True) > 0.0, 0.0, 1.0)


def tail_mask(start):
    rows = start.shape[0]
    last = jnp.broadcast_to(start[rows - 1 : rows].astype(F32), (EDGE, LANES))
    after = jnp.where(iota((EDGE, LANES), 1) > iota((EDGE, LANES), 0) + (LANES - EDGE), last, 0.0)
    return jnp.where(jnp.sum(after, axis=1, keepdims=True) > 0.0, 0.0, 1.0)


def load_kernel(hidden_hbm, start_hbm, grad_hbm,
                back_ref, ahead_ref, hidden_ref, start_ref, rows_v, sem):
    pairs = [(start_hbm, start_ref), (hidden_hbm, hidden_ref)]
    copies = [pltpu.make_async_copy(*pair, sem.at[at]) for at, pair in enumerate(pairs)]
    for copy in copies:
        copy.start()
    bytes_, feats = hidden_ref.shape
    width = grad_hbm.shape[1]
    copies[0].wait()
    start = start_ref[...]
    last = jnp.sum(start) - 1
    group = pl.multiple_of((last // EDGE) * EDGE, EDGE)
    rows = pltpu.make_async_copy(grad_hbm.at[pl.ds(group, EDGE), :], rows_v, sem.at[2])
    rows.start()
    back_ref[:, feats:] = jnp.broadcast_to(lead_mask(start), (EDGE, LANES)).astype(BF16)
    ahead_ref[:, width + feats :] = jnp.broadcast_to(tail_mask(start), (EDGE, LANES)).astype(BF16)
    copies[1].wait()
    back_ref[:, :feats] = hidden_ref[:EDGE]
    ahead_ref[:, width : width + feats] = hidden_ref[bytes_ - EDGE :]
    rows.wait()
    chosen = iota((EDGE, width), 0) == last - group
    ahead_ref[:, :width] = jnp.where(chosen, rows_v[...].astype(F32), 0.0).astype(BF16)


def pool_kernel(hidden_ref, next_ref, start_ref, query_ref, low_ref, pooled_ref, denom_ref):
    bytes_, feats = hidden_ref.shape
    slots = low_ref.shape[0]
    query = row_of(query_ref)
    rows, last = segment_rows(start_ref[...])
    segment = jnp.concatenate(rows, axis=1).astype(jnp.int32)
    onehot = jnp.where(iota((slots, bytes_), 0) == segment, 1.0, 0.0).astype(BF16)
    hidden = hidden_ref[...].astype(F32)
    _, weight = scores(hidden, query)
    numer = dot_split(onehot, weight * hidden)
    denom = dot_split(onehot, weight)
    following = next_ref[:, :feats].astype(F32)
    mask = next_ref[:, feats : feats + 1].astype(F32)
    extra = scores(following, query)[1] * mask
    is_last = iota((slots, feats), 0) == last.astype(jnp.int32)
    denom = denom + jnp.where(is_last, jnp.sum(extra, axis=0, keepdims=True), 0.0)
    numer = numer + jnp.where(is_last, jnp.sum(extra * following, axis=0, keepdims=True), 0.0)
    live = denom > 0.0
    pooled = jnp.where(live, numer / jnp.where(live, denom, 1.0), 0.0)
    low_ref[...] = pooled.astype(BF16)
    pooled_ref[...] = pooled
    denom_ref[...] = denom


def spread_kernel(hidden_ref, prev_ref, start_ref, query_ref, pooled_ref, denom_ref,
                  onehot_ref, share_ref, delta_ref, slope_ref):
    bytes_, feats = hidden_ref.shape
    slots = pooled_ref.shape[0]
    query = row_of(query_ref)
    rows, _ = segment_rows(start_ref[...])
    columns = [jnp.transpose(jnp.broadcast_to(row, (LANES, LANES))) for row in rows]
    segment = jnp.concatenate(columns, axis=0).astype(jnp.int32)
    onehot = jnp.concatenate(
        [
            jnp.where(segment == iota((bytes_, LANES), 1) + offset, 1.0, 0.0).astype(BF16)
            for offset in range(0, slots, LANES)
        ],
        axis=1,
    )
    onehot_ref[...] = onehot
    hidden = hidden_ref[...].astype(F32)
    bent, weight = scores(hidden, query)
    width = prev_ref.shape[1] - feats - LANES
    before = prev_ref[:, width : width + feats].astype(F32)
    part = scores(before, query)[1] * prev_ref[:, width + feats : width + feats + 1].astype(F32)
    lead = lead_mask(start_ref[...])
    own = weight[:EDGE] * lead
    first_denom = jnp.sum(part + own, axis=0, keepdims=True)
    first_numer = jnp.sum(part * before + own * hidden[:EDGE], axis=0, keepdims=True)
    full = first_denom > 0.0
    first_pooled = jnp.where(full, first_numer / jnp.where(full, first_denom, 1.0), 0.0)
    denom = dot_split(onehot, denom_ref[...])
    pooled = dot_split(onehot, pooled_ref[...])
    denom = jnp.concatenate([denom[:EDGE] + lead * first_denom, denom[EDGE:]], axis=0)
    pooled = jnp.concatenate([pooled[:EDGE] + lead * first_pooled, pooled[EDGE:]], axis=0)
    share = weight / denom
    share_ref[...] = share
    delta_ref[...] = hidden - pooled
    slope_ref[...] = share * (1.0 - bent * bent) * (inv_root * query)


def bytes_kernel(parts, *refs):
    recv_refs, (start_ref, onehot_ref, share_ref, delta_ref, slope_ref, out_ref) = (
        refs[:parts],
        refs[parts:],
    )
    slots = onehot_ref.shape[1]
    grad = recv_refs[0][...].astype(F32)
    for ref in recv_refs[1:]:
        grad = grad + ref[...].astype(F32)
    rows = dot_split(onehot_ref[...], grad[:slots])
    first = jnp.sum(grad[slots:], axis=0, keepdims=True)
    rows = jnp.concatenate([rows[:EDGE] + lead_mask(start_ref[...]) * first, rows[EDGE:]], axis=0)
    inner = head_sum(rows * delta_ref[...])
    out_ref[...] = (share_ref[...] * rows + slope_ref[...] * inner).astype(BF16)


def gather_parts(part_refs, full_ref):
    feats = part_refs[0].shape[1]
    place = lax.axis_index("mp")
    for index, ref in enumerate(part_refs):
        owner = pl.multiple_of((place ^ index) * feats, feats)
        full_ref[:, pl.ds(owner, feats)] = ref[...]


def outer_kernel(parts, scale, *refs):
    part_refs, grad_ref, out_refs = refs[:parts], refs[parts], refs[parts + 1 : -2]
    full_ref, terms_ref = refs[-2:]
    gather_parts(part_refs, full_ref)
    terms_ref[...] = dot(full_ref[...], grad_ref[...], ((0,), (0,))) * scale
    if len(out_refs) == 1:
        out_refs[0][...] = terms_ref[...].astype(out_refs[0].dtype)
        return
    place = lax.axis_index("seq")
    rows = out_refs[0].shape[0]
    for index, ref in enumerate(out_refs):
        owner = pl.multiple_of((place ^ index) * rows, rows)
        ref[...] = terms_ref[pl.ds(owner, rows), :].astype(ref.dtype)


def latent_kernel(parts, *refs):
    part_refs, (weight_ref, out_ref, full_ref) = refs[:parts], refs[parts:]
    gather_parts(part_refs, full_ref)
    out_ref[...] = dot(full_ref[...], weight_ref[...]).astype(BF16)


def partial_kernel(parts, grad_ref, prev_ref, *refs):
    piece_refs, out_refs, full_ref = refs[: -parts - 1], refs[-parts - 1 : -1], refs[-1]
    slots, width = grad_ref.shape
    feats = out_refs[0].shape[1]
    if len(piece_refs) == 1:
        full_ref[...] = piece_refs[0][...]
    else:
        rows = piece_refs[0].shape[0]
        spot = lax.axis_index("seq")
        for index, ref in enumerate(piece_refs):
            owner = pl.multiple_of((spot ^ index) * rows, rows)
            full_ref[pl.ds(owner, rows), :] = ref[...]
    place = lax.axis_index("mp")
    for index, ref in enumerate(out_refs):
        owner = pl.multiple_of((place ^ index) * feats, feats)
        block = full_ref[pl.ds(owner, feats), :]
        ref[:slots] = dot(grad_ref[...], block, ((1,), (1,))).astype(BF16)
        ref[slots:] = dot(prev_ref[:, :width], block, ((1,), (1,))).astype(BF16)


def call(kernel, out_shape, *args, flops=0, scratch=(), in_specs=None, limit=VMEM_LIMIT):
    if in_specs is None:
        in_specs = [pl.BlockSpec(memory_space=pltpu.VMEM)] * len(args)
    return pl.pallas_call(
        kernel,
        out_shape=out_shape,
        in_specs=in_specs,
        out_specs=jax.tree.map(lambda _: pl.BlockSpec(memory_space=pltpu.VMEM), out_shape),
        scratch_shapes=list(scratch),
        cost_estimate=pl.CostEstimate(flops=0, bytes_accessed=0, transcendentals=0),
        compiler_params=pltpu.CompilerParams(vmem_limit_bytes=limit),
    )(*args)


def shape(dims, dtype):
    return jax.ShapeDtypeStruct(dims, dtype)


VMEM = pl.BlockSpec(memory_space=pltpu.VMEM)
after = lax.optimization_barrier
HBM = pl.BlockSpec(memory_space=pltpu.HBM)


def shards(byte_hidden, patch_start, pool_query, in_weight, latent_grad):
    bytes_, feats = byte_hidden.shape
    slots, width = latent_grad.shape
    n_seq, n_mp = lax.axis_size("seq"), lax.axis_size("mp")
    latent_dim = feats * n_mp
    rows = latent_dim // n_seq
    staged = n_seq <= 8

    def swap(value, step):
        return lax.ppermute(value, "mp", [(i, i ^ step) for i in range(n_mp)])

    def trade(value, step):
        return lax.ppermute(value, "seq", [(i, i ^ step) for i in range(n_seq)])

    arguments = (
        byte_hidden,
        patch_start.reshape(bytes_ // LANES, LANES),
        latent_grad,
    )
    query = pool_query.reshape(feats // LANES, LANES)
    back, ahead, byte_hidden, start = call(
        load_kernel,
        (
            shape((EDGE, feats + LANES), BF16),
            shape((EDGE, width + feats + LANES), BF16),
            shape(byte_hidden.shape, BF16),
            shape(arguments[1].shape, jnp.int32),
        ),
        *arguments,
        in_specs=[HBM] * len(arguments),
        limit=VMEM_MOST,
        scratch=(
            pltpu.VMEM((EDGE, width), BF16),
            pltpu.SemaphoreType.DMA((len(arguments),)),
        ),
    )
    following = lax.ppermute(back, "seq", [(i, i - 1) for i in range(1, n_seq)])
    previous = lax.ppermute(ahead, "seq", [(i, i + 1) for i in range(n_seq - 1)])

    if staged:
        in_weight, _ = after((in_weight, back))
        pieces = [in_weight] + [None] * (n_seq - 1)
        pieces[1] = trade(in_weight, 1)
        for step in range(2, n_seq, 2):
            source = after((in_weight, pieces[2]))[0] if step == 4 else in_weight
            pieces[step] = trade(source, step)
    else:
        pieces = [lax.all_gather(in_weight, "seq", axis=0, tiled=True)]

    low, pooled, denom = call(
        pool_kernel,
        (shape((slots, feats), BF16), shape((slots, feats), F32), shape((slots, feats), F32)),
        byte_hidden,
        following,
        start,
        query,
        flops=8 * bytes_ * slots * feats,
    )

    if staged:
        low, previous, *pieces[1:3] = after((low, previous, *pieces[1:3]))
    parts = [low] + [swap(low, step) for step in range(1, n_mp)]
    if staged:
        latest = low
        for at, step in enumerate((2, *range(n_seq - 2, 2, -2))):
            wait = (latest, parts[at + 1]) if at else latest
            pieces[step], _ = after((pieces[step], wait))
            latest = pieces[step + 1] = trade(pieces[step], 1)
    onehot, share, delta, slope = call(
        spread_kernel,
        (shape((bytes_, slots), BF16),) + (shape((bytes_, feats), F32),) * 3,
        byte_hidden,
        previous,
        start,
        query,
        pooled,
        denom,
        flops=8 * bytes_ * slots * feats,
    )
    work = 2 * slots * width * latent_dim
    scale = 1.0 / math.sqrt(n_seq * slots)
    if staged:
        blocks = [shape((rows, width), BF16 if index % 2 else F32) for index in range(n_seq)]
    else:
        blocks = [shape((latent_dim, width), BF16)]
    if staged:
        parts, pieces[-1], share = after((parts, pieces[-1], share))
    terms = call(
        functools.partial(outer_kernel, n_mp, scale),
        tuple(blocks),
        *parts,
        latent_grad,
        flops=work,
        scratch=(pltpu.VMEM((slots, latent_dim), BF16), pltpu.VMEM((latent_dim, width), F32)),
    )
    if staged:
        fetched, pairs, sums = [], [], []
        for at, step in enumerate(reversed(range(0, n_seq, 2))):
            away = terms[step + 1]
            if at >= 2:
                away, _ = after((away, pairs[0] if at == 2 else fetched[1]))
            if at == 1:
                away, _ = after((away, latest))
            fetched.append(trade(away, 1))
            if at == 0:
                previous, _ = after((previous, fetched[0]))
            pairs.append(terms[step] + fetched[-1].astype(F32))
            if step:
                fetched.append(trade(pairs[-1].astype(BF16), step))
            sums.append(fetched[-1].astype(F32) if step else pairs[-1])
        grad_weight = sum(sums[1:], sums[0])
    else:
        received = lax.all_to_all(terms[0], "seq", split_axis=0, concat_axis=0, tiled=True)
        grad_weight = received.reshape(n_seq, rows, width).astype(F32).sum(0)

    *partials, weight_full = call(
        functools.partial(partial_kernel, n_mp),
        (shape((slots + EDGE, feats), BF16),) * n_mp + (shape((latent_dim, width), BF16),),
        latent_grad,
        previous,
        *pieces,
        flops=work,
    )
    grads = [partials[0]] + [swap(partials[step], step) for step in range(1, n_mp)]
    latent = call(
        functools.partial(latent_kernel, n_mp),
        shape((slots, width), BF16),
        *parts,
        weight_full,
        flops=work,
        scratch=(pltpu.VMEM((slots, latent_dim), BF16),),
    )
    grad_bytes = call(
        functools.partial(bytes_kernel, n_mp),
        shape((bytes_, feats), BF16),
        *grads,
        start,
        onehot,
        share,
        delta,
        slope,
        flops=4 * bytes_ * slots * feats,
    )
    return latent, grad_weight, grad_bytes


def solution(mesh):
    in_specs = (P("seq", "mp"), P("seq"), P("mp"), P("seq", "mp"), P("seq", "mp"))
    out_specs = (P("seq", "mp"), P("seq", "mp"), P("seq", "mp"))
    return jax.shard_map(shards, mesh=mesh, in_specs=in_specs, out_specs=out_specs, check_vma=False)
```

time: 209 us -> 78.7 us (0.38)
  waiting for transfers between devices: 114 us -> 30.8 us
  other arithmetic: 31.3 us -> 1.13 us
  local copies, waits for them, and re-layouts: 21.8 us -> 1.45 us
  between operations: 14.7 us -> 0.78 us
  starting transfers between devices: 17.2 us -> 31 us
  Pallas kernels: 0 us -> 13.4 us
  matrix products: 9.55 us -> 0 us
    all_gather x2 -> x0, waiting for transfers between devices: 59.2 us -> none  [the longest x1 42.8 us: shards(): weight_full = lax.all_gather(in_weight, 'seq', axis=0, tiled=True)]
    reduce_scatter x1 -> x0, waiting for transfers between devices: 54 us -> none  [shards(): lax.psum_scatter(lax.dot_general(pooled_full, latent_grad, (((0,), (0,)),...]
    ppermute x5 -> x22, waiting for transfers between devices: 0.01 us -> 30.8 us  [the longest x14 24.8 us: trade(): return lax.ppermute(value, 'seq', [(i, i ^ step) for i in range(n_seq)])]
    ppermute x5 -> x22, starting transfers between devices: 12.9 us -> 31 us  [the longest x14 24 us: trade(): return lax.ppermute(value, 'seq', [(i, i ^ step) for i in range(n_seq)])]
    scatter-add x2 -> x0, other arithmetic: 15.6 us -> none  [the longest x1 8.88 us: shards(): numer = jax.ops.segment_sum(weighted * keep_own, inside, num_segments=slots)]
    pallas_call x0 -> x7, Pallas kernels: none -> 13.4 us  [call(): pl.pallas_call(kernel, out_shape=out_shape, in_specs=in_specs, out_specs=...]
    gather x4 -> x0, local copies, waits for them, and re-layouts: 11.2 us -> none  [the longest x1 4.68 us: shards(): jnp.take(pooled, inside, axis=0)]
    dot_general x3 -> x0, matrix products: 9.55 us -> none  [the longest x1 4.44 us: shards(): lax.dot_general(pooled_full, latent_grad, (((0,), (0,)), ((), ())), prefe...]
  transfers between devices with their start and end apart: 9 -> 22, of which waited for: 3 -> 8; matrix products, arithmetic and copies ran while one was open for 24% -> 0% of each run, Pallas kernels for 0% -> 16%
where the time goes in v1:
time: 78.7 us; the launch traced here: 78.5 us
  starting transfers between devices  31 us (39%)
  waiting for transfers between devices  30.8 us (39%)
  Pallas kernels  13.4 us (17%)
  local copies, waits for them, and re-layouts  1.45 us (2%)
  other arithmetic  1.13 us (1%)
    ppermute x14, waiting for transfers between devices, trade(): return lax.ppermute(value, 'seq', [(i, i ^ step) for i in range(n_seq)])  24.8 us
    ppermute x14, starting transfers between devices, trade(): return lax.ppermute(value, 'seq', [(i, i ^ step) for i in range(n_seq)])  24 us
    pallas_call x7, Pallas kernels, call(): pl.pallas_call(kernel, out_shape=out_shape, in_specs=in_specs, out_specs=...  13.4 us
    ppermute x6, waiting for transfers between devices, swap(): return lax.ppermute(value, 'mp', [(i, i ^ step) for i in range(n_mp)])  5.91 us
    ppermute x6, starting transfers between devices, swap(): return lax.ppermute(value, 'mp', [(i, i ^ step) for i in range(n_mp)])  3.36 us
    ppermute x1, starting transfers between devices, shards(): lax.ppermute(ahead, 'seq', [(i, i + 1) for i in range(n_seq - 1)])  2.4 us
  transfers between devices with their start and end apart: 22, of which 8 were waited for; matrix products, arithmetic and copies ran while one was open for 0% of the time, Pallas kernels for 16%

profile of v1, /device:TPU:0, one launch (start us, length us, event | category | flops | bytes accessed | tf_op | source)
XLA Modules:
  0.0 78.5 jit_solution(14833160223715793649)
XLA Ops:
  2.5 3.1 %collective-permute-start.3 = (bf16[128,1024]{1,0:T(8,128)(2,1)}, bf16[128,1024]{1,0:T(8,128)(2,1)S(1)}, u32[]{:S(2)}, u32[]{:S(2)}) collective-permute-start(bf16[128,1024]{1,0:T(8,128)(2,1)} %refs_0_), channel_id=1, source_target_pairs={{0,8},{4,12},{8,0},{12,4},{16,24},{20,28},{24,16},{28,20},{1,9},{5... | collective-permute-start | bytes 786440 | tf_op jit(solution)/shard_map/ppermute | solution.py:269
  5.6 1.5 %collective-permute-start.2 = (bf16[128,1024]{1,0:T(8,128)(2,1)}, bf16[128,1024]{1,0:T(8,128)(2,1)S(1)}, u32[]{:S(2)}, u32[]{:S(2)}) collective-permute-start(bf16[128,1024]{1,0:T(8,128)(2,1)} %refs_0_), channel_id=1, source_target_pairs={{0,4},{4,0},{8,12},{12,8},{16,20},{20,16},{24,28},{28,24},{1,5},{5... | collective-permute-start | bytes 786440 | tf_op jit(solution)/shard_map/ppermute | solution.py:269
  7.1 2.4 %collective-permute-start.1 = (bf16[16,1408]{1,0:T(8,128)(2,1)S(1)}, bf16[16,1408]{1,0:T(8,128)(2,1)S(1)}, u32[]{:S(2)}, u32[]{:S(2)}) collective-permute-start(bf16[16,1408]{1,0:T(8,128)(2,1)S(1)} %get-tuple-element.50), channel_id=1, source_target_pairs={{0,4},{4,8},{8,12},{12,16},{16,20},{20,24},{24,28},{1,5},{5,9},{9,... | collective-permute-start | bytes 135176 | tf_op jit(solution)/shard_map/ppermute | solution.py:294
  10.8 5.6 %collective-permute-start.7 = (bf16[128,1024]{1,0:T(8,128)(2,1)}, bf16[128,1024]{1,0:T(8,128)(2,1)S(1)}, u32[]{:S(2)}, u32[]{:S(2)}) collective-permute-start(bf16[128,1024]{1,0:T(8,128)(2,1)} %refs_0_), channel_id=1, source_target_pairs={{0,24},{4,28},{8,16},{12,20},{16,8},{20,12},{24,0},{28,4},{1,25},{... | collective-permute-start | bytes 786440 | tf_op jit(solution)/shard_map/ppermute | solution.py:269
  17.1 2.1 %shard_map.77 = (bf16[512,256]{1,0:T(8,128)(2,1)S(1)}, f32[512,256]{1,0:T(8,128)S(1)}, f32[512,256]{1,0:T(8,128)S(1)}) custom-call(bf16[1024,256]{1,0:T(8,128)(2,1)S(1)} %get-tuple-element.46.hidden_ref, bf16[16,384]{1,0:T(8,128)(2,1)S(1)} %collective-permute-done.next_ref, s32[8,128]{1,0:T(8,128)S(1)} %get-tuple-element.48.start_ref.refs_4_, ...), custom_call_target="tpu_custom_call" | custom-call | tf_op jit(solution)/shard_map/pallas_call | solution.py:237
  20.3 1.5 %collective-permute-start.5 = (bf16[512,256]{1,0:T(8,128)(2,1)S(1)}, bf16[512,256]{1,0:T(8,128)(2,1)S(1)}, u32[]{:S(2)}, u32[]{:S(2)}) collective-permute-start(bf16[512,256]{1,0:T(8,128)(2,1)S(1)} %get-tuple-element.60.refs_0_), channel_id=1, source_target_pairs={{0,2},{1,3},{2,0},{3,1},{4,6},{5,7},{6,4},{7,5},{8,10},{9,11},{10,... | collective-permute-start | bytes 786440 | tf_op jit(solution)/shard_map/ppermute | solution.py:266
  21.8 2.8 %collective-permute-start.11 = (bf16[128,1024]{1,0:T(8,128)(2,1)S(1)}, bf16[128,1024]{1,0:T(8,128)(2,1)S(1)}, u32[]{:S(2)}, u32[]{:S(2)}) collective-permute-start(bf16[128,1024]{1,0:T(8,128)(2,1)S(1)} %copy-done.2), channel_id=1, source_target_pairs={{0,16},{4,20},{8,24},{12,28},{16,0},{20,4},{24,8},{28,12},{1,17},{... | collective-permute-start | bytes 786440 | tf_op jit(solution)/shard_map/ppermute | solution.py:269
  24.6 1.3 %collective-permute-done.8.refs_3_ = bf16[128,1024]{1,0:T(8,128)(2,1)S(1)} collective-permute-done((bf16[128,1024]{1,0:T(8,128)(2,1)S(1)}, bf16[128,1024]{1,0:T(8,128)(2,1)S(1)}, u32[]{:S(2)}, u32[]{:S(2)}) %collective-permute-start.8) | collective-permute-done | bytes 262176 | tf_op jit(solution)/shard_map/ppermute | solution.py:269
  25.9 2.6 %collective-permute-done.5.refs_2_ = bf16[512,256]{1,0:T(8,128)(2,1)S(1)} collective-permute-done((bf16[512,256]{1,0:T(8,128)(2,1)S(1)}, bf16[512,256]{1,0:T(8,128)(2,1)S(1)}, u32[]{:S(2)}, u32[]{:S(2)}) %collective-permute-start.5) | collective-permute-done | bytes 262176 | tf_op jit(solution)/shard_map/ppermute | solution.py:266
  29.6 1.8 %shard_map.78 = (bf16[1024,512]{1,0:T(8,128)(2,1)S(1)}, f32[1024,256]{1,0:T(8,128)S(1)}, f32[1024,256]{1,0:T(8,128)S(1)}, f32[1024,256]{1,0:T(8,128)S(1)}) custom-call(bf16[1024,256]{1,0:T(8,128)(2,1)S(1)} %get-tuple-element.46.hidden_ref, bf16[16,1408]{1,0:T(8,128)(2,1)S(1)} %collective-permute-done.1.prev_ref, ...), custom_call_target="tpu_custom_call" | custom-call | tf_op jit(solution)/shard_map/pallas_call | solution.py:237
  31.3 7.5 %collective-permute-done.11.refs_4_ = bf16[128,1024]{1,0:T(8,128)(2,1)S(1)} collective-permute-done((bf16[128,1024]{1,0:T(8,128)(2,1)S(1)}, bf16[128,1024]{1,0:T(8,128)(2,1)S(1)}, u32[]{:S(2)}, u32[]{:S(2)}) %collective-permute-start.11) | collective-permute-done | bytes 262176 | tf_op jit(solution)/shard_map/ppermute | solution.py:269
  39.4 1.7 %shard_map.79 = (f32[128,1024]{1,0:T(8,128)S(1)}, bf16[128,1024]{1,0:T(8,128)(2,1)S(1)}, f32[128,1024]{1,0:T(8,128)S(1)}, bf16[128,1024]{1,0:T(8,128)(2,1)S(1)},...) custom-call(bf16[512,256]{1,0:T(8,128)(2,1)S(1)} %get-tuple-element., ...), custom_call_target="tpu_custom_call" | custom-call | tf_op jit(solution)/shard_map/pallas_call | solution.py:237
  41.1 1.6 %collective-permute-start.10 = (bf16[128,1024]{1,0:T(8,128)(2,1)S(1)}, bf16[128,1024]{1,0:T(8,128)(2,1)S(1)}, u32[]{:S(2)}, u32[]{:S(2)}) collective-permute-start(bf16[128,1024]{1,0:T(8,128)(2,1)S(1)} %get-tuple-element.64), channel_id=1, source_target_pairs={{0,4},{4,0},{8,12},{12,8},{16,20},{20,16},{24,28},{28,24},{1,5},{5... | collective-permute-start | bytes 786440 | tf_op jit(solution)/shard_map/ppermute | solution.py:269
  42.6 5.4 %collective-permute-done.12.refs_5_ = bf16[128,1024]{1,0:T(8,128)(2,1)S(1)} collective-permute-done((bf16[128,1024]{1,0:T(8,128)(2,1)S(1)}, bf16[128,1024]{1,0:T(8,128)(2,1)S(1)}, u32[]{:S(2)}, u32[]{:S(2)}) %collective-permute-start.12) | collective-permute-done | bytes 262176 | tf_op jit(solution)/shard_map/ppermute | solution.py:269
  48.5 5.1 %collective-permute-done.10 = bf16[128,1024]{1,0:T(8,128)(2,1)S(1)} collective-permute-done((bf16[128,1024]{1,0:T(8,128)(2,1)S(1)}, bf16[128,1024]{1,0:T(8,128)(2,1)S(1)}, u32[]{:S(2)}, u32[]{:S(2)}) %collective-permute-start.10) | collective-permute-done | bytes 262176 | tf_op jit(solution)/shard_map/ppermute | solution.py:269
  54.3 2.2 %collective-permute-start.13 = (bf16[128,1024]{1,0:T(8,128)(2,1)S(1)}, bf16[128,1024]{1,0:T(8,128)(2,1)S(1)}, u32[]{:S(2)}, u32[]{:S(2)}) collective-permute-start(bf16[128,1024]{1,0:T(8,128)(2,1)S(1)} %convert_add_fusion), channel_id=1, source_target_pairs={{0,24},{4,28},{8,16},{12,20},{16,8},{20,12},{24,0},{28,4},{1,25},{... | collective-permute-start | bytes 786440 | tf_op jit(solution)/shard_map/ppermute | solution.py:269
  56.5 2.2 %shard_map.80 = (bf16[528,256]{1,0:T(8,128)(2,1)S(1)}, bf16[528,256]{1,0:T(8,128)(2,1)S(1)}, bf16[528,256]{1,0:T(8,128)(2,1)S(1)}, bf16[528,256]{1,0:T(8,128)(2,1)S(1)}, bf16[1024,1024]{1,0:T(8,128)(2,1)}) custom-call(bf16[512,1024]{1,0:T(8,128)(2,1)S(1)} %copy-done, bf16[16,1408]{1,0:T(8,128)(2,1)S(1)} %collective-permute-done.1.prev_ref, ...), custom_call_target="tpu_custom_call" | custom-call | tf_op jit(solution)/shard_map/pallas_call | solution.py:237
  58.7 1.5 %collective-permute-start.20 = (bf16[528,256]{1,0:T(8,128)(2,1)S(1)}, bf16[528,256]{1,0:T(8,128)(2,1)S(1)}, u32[]{:S(2)}, u32[]{:S(2)}) collective-permute-start(bf16[528,256]{1,0:T(8,128)(2,1)S(1)} %get-tuple-element.83), channel_id=1, source_target_pairs={{0,2},{1,3},{2,0},{3,1},{4,6},{5,7},{6,4},{7,5},{8,10},{9,11},{10,... | collective-permute-start | bytes 811016 | tf_op jit(solution)/shard_map/ppermute | solution.py:266
  60.6 3.2 %collective-permute-done.16 = bf16[128,1024]{1,0:T(8,128)(2,1)S(1)} collective-permute-done((bf16[128,1024]{1,0:T(8,128)(2,1)S(1)}, bf16[128,1024]{1,0:T(8,128)(2,1)S(1)}, u32[]{:S(2)}, u32[]{:S(2)}) %collective-permute-start.16) | collective-permute-done | bytes 262176 | tf_op jit(solution)/shard_map/ppermute | solution.py:269
  64.2 2.7 %collective-permute-start.17 = (bf16[128,1024]{1,0:T(8,128)(2,1)S(1)}, bf16[128,1024]{1,0:T(8,128)(2,1)S(1)}, u32[]{:S(2)}, u32[]{:S(2)}) collective-permute-start(bf16[128,1024]{1,0:T(8,128)(2,1)S(1)} %add_convert_fusion), channel_id=1, source_target_pairs={{0,8},{4,12},{8,0},{12,4},{16,24},{20,28},{24,16},{28,20},{1,9},{5... | collective-permute-start | bytes 786440 | tf_op jit(solution)/shard_map/ppermute | solution.py:269
  67.3 2.4 %shard_map.81 = bf16[512,1024]{1,0:T(8,128)(2,1)} custom-call(bf16[512,256]{1,0:T(8,128)(2,1)S(1)} %get-tuple-element.60.refs_0_, bf16[512,256]{1,0:T(8,128)(2,1)S(1)} %collective-permute-done.4.refs_1_, bf16[512,256]{1,0:T(8,128)(2,1)S(1)} %collective-permute-done.5.refs_2_, bf16[512,256]{1,0:T(8,128)(2,1)S(1)} %collective-permute-done.6.refs_3_, ...), custom_call_target="tpu_custom_call" | custom-call | tf_op jit(solution)/shard_map/pallas_call | solution.py:237
  69.7 3.3 %collective-permute-done.21.refs_3_ = bf16[528,256]{1,0:T(8,128)(2,1)S(1)} collective-permute-done((bf16[528,256]{1,0:T(8,128)(2,1)S(1)}, bf16[528,256]{1,0:T(8,128)(2,1)S(1)}, u32[]{:S(2)}, u32[]{:S(2)}) %collective-permute-start.21) | collective-permute-done | bytes 270368 | tf_op jit(solution)/shard_map/ppermute | solution.py:266
  73.0 2.2 %shard_map.82 = bf16[1024,256]{1,0:T(8,128)(2,1)} custom-call(bf16[528,256]{1,0:T(8,128)(2,1)S(1)} %get-tuple-element.81.refs_0_, bf16[528,256]{1,0:T(8,128)(2,1)S(1)} %collective-permute-done.19.refs_1_, bf16[528,256]{1,0:T(8,128)(2,1)S(1)} %collective-permute-done.20.refs_2_, bf16[528,256]{1,0:T(8,128)(2,1)S(1)} %collective-permute-done.21.refs_3_, ...), custom_call_target="tpu_custom_call" | custom-call | tf_op jit(solution)/shard_map/pallas_call | solution.py:237
  75.2 2.3 %collective-permute-done.15 = bf16[128,1024]{1,0:T(8,128)(2,1)S(1)} collective-permute-done((bf16[128,1024]{1,0:T(8,128)(2,1)S(1)}, bf16[128,1024]{1,0:T(8,128)(2,1)S(1)}, u32[]{:S(2)}, u32[]{:S(2)}) %collective-permute-start.15) | collective-permute-done | bytes 262176 | tf_op jit(solution)/shard_map/ppermute | solution.py:269
  (41 shorter events, 9.9 us)
Async XLA Ops:
  0.6 38.7 %copy-start = (bf16[512,1024]{1,0:T(8,128)(2,1)S(1)}, bf16[512,1024]{1,0:T(8,128)(2,1)}, u32[]{:S(2)}) copy-start(bf16[512,1024]{1,0:T(8,128)(2,1)} %grad_ref.1) | copy-start | bytes 3145732
  0.6 21.1 %copy-start.2 = (bf16[128,1024]{1,0:T(8,128)(2,1)S(1)}, bf16[128,1024]{1,0:T(8,128)(2,1)}, u32[]{:S(2)}) copy-start(bf16[128,1024]{1,0:T(8,128)(2,1)} %refs_0_) | copy-start | bytes 786436
  2.5 16.7 %collective-permute-start.3 = (bf16[128,1024]{1,0:T(8,128)(2,1)}, bf16[128,1024]{1,0:T(8,128)(2,1)S(1)}, u32[]{:S(2)}, u32[]{:S(2)}) collective-permute-start(bf16[128,1024]{1,0:T(8,128)(2,1)} %refs_0_), channel_id=1, source_target_pairs={{0,8},{4,12},{8,0},{12,4},{16,24},{20,28},{24,16},{28,20},{1,9},{5... | collective-permute-start | bytes 786440 | tf_op jit(solution)/shard_map/ppermute | solution.py:269
  5.6 13.6 %collective-permute-start.2 = (bf16[128,1024]{1,0:T(8,128)(2,1)}, bf16[128,1024]{1,0:T(8,128)(2,1)S(1)}, u32[]{:S(2)}, u32[]{:S(2)}) collective-permute-start(bf16[128,1024]{1,0:T(8,128)(2,1)} %refs_0_), channel_id=1, source_target_pairs={{0,4},{4,0},{8,12},{12,8},{16,20},{20,16},{24,28},{28,24},{1,5},{5... | collective-permute-start | bytes 786440 | tf_op jit(solution)/shard_map/ppermute | solution.py:269
  7.1 12.0 %collective-permute-start.1 = (bf16[16,1408]{1,0:T(8,128)(2,1)S(1)}, bf16[16,1408]{1,0:T(8,128)(2,1)S(1)}, u32[]{:S(2)}, u32[]{:S(2)}) collective-permute-start(bf16[16,1408]{1,0:T(8,128)(2,1)S(1)} %get-tuple-element.50), channel_id=1, source_target_pairs={{0,4},{4,8},{8,12},{12,16},{16,20},{20,24},{24,28},{1,5},{5,9},{9,... | collective-permute-start | bytes 135176 | tf_op jit(solution)/shard_map/ppermute | solution.py:294
  9.5 6.9 %collective-permute-start = (bf16[16,384]{1,0:T(8,128)(2,1)S(1)}, bf16[16,384]{1,0:T(8,128)(2,1)S(1)}, u32[]{:S(2)}, u32[]{:S(2)}) collective-permute-start(bf16[16,384]{1,0:T(8,128)(2,1)S(1)} %get-tuple-element.47), channel_id=1, source_target_pairs={{4,0},{8,4},{12,8},{16,12},{20,16},{24,20},{28,24},{5,1},{9,5},{13... | collective-permute-start | bytes 36872 | tf_op jit(solution)/shard_map/ppermute | solution.py:293
  10.8 13.7 %collective-permute-start.7 = (bf16[128,1024]{1,0:T(8,128)(2,1)}, bf16[128,1024]{1,0:T(8,128)(2,1)S(1)}, u32[]{:S(2)}, u32[]{:S(2)}) collective-permute-start(bf16[128,1024]{1,0:T(8,128)(2,1)} %refs_0_), channel_id=1, source_target_pairs={{0,24},{4,28},{8,16},{12,20},{16,8},{20,12},{24,0},{28,4},{1,25},{... | collective-permute-start | bytes 786440 | tf_op jit(solution)/shard_map/ppermute | solution.py:269
  19.2 6.7 %collective-permute-start.8 = (bf16[128,1024]{1,0:T(8,128)(2,1)S(1)}, bf16[128,1024]{1,0:T(8,128)(2,1)S(1)}, u32[]{:S(2)}, u32[]{:S(2)}) collective-permute-start(bf16[128,1024]{1,0:T(8,128)(2,1)S(1)} %collective-permute-done.3.refs_2_), channel_id=1, source_target_pairs={{0,4},{4,0},{8,12},{12,8},{16,20},{20,16},{24,28},{28,24},{1,5},{5... | collective-permute-start | bytes 786440 | tf_op jit(solution)/shard_map/ppermute | solution.py:269
  20.3 8.3 %collective-permute-start.5 = (bf16[512,256]{1,0:T(8,128)(2,1)S(1)}, bf16[512,256]{1,0:T(8,128)(2,1)S(1)}, u32[]{:S(2)}, u32[]{:S(2)}) collective-permute-start(bf16[512,256]{1,0:T(8,128)(2,1)S(1)} %get-tuple-element.60.refs_0_), channel_id=1, source_target_pairs={{0,2},{1,3},{2,0},{3,1},{4,6},{5,7},{6,4},{7,5},{8,10},{9,11},{10,... | collective-permute-start | bytes 786440 | tf_op jit(solution)/shard_map/ppermute | solution.py:266
  21.8 17.0 %collective-permute-start.6 = (bf16[512,256]{1,0:T(8,128)(2,1)S(1)}, bf16[512,256]{1,0:T(8,128)(2,1)S(1)}, u32[]{:S(2)}, u32[]{:S(2)}) collective-permute-start(bf16[512,256]{1,0:T(8,128)(2,1)S(1)} %get-tuple-element.60.refs_0_), channel_id=1, source_target_pairs={{0,3},{1,2},{2,1},{3,0},{4,7},{5,6},{6,5},{7,4},{8,11},{9,10},{10,... | collective-permute-start | bytes 786440 | tf_op jit(solution)/shard_map/ppermute | solution.py:266
  21.8 17.0 %collective-permute-start.11 = (bf16[128,1024]{1,0:T(8,128)(2,1)S(1)}, bf16[128,1024]{1,0:T(8,128)(2,1)S(1)}, u32[]{:S(2)}, u32[]{:S(2)}) collective-permute-start(bf16[128,1024]{1,0:T(8,128)(2,1)S(1)} %copy-done.2), channel_id=1, source_target_pairs={{0,16},{4,20},{8,24},{12,28},{16,0},{20,4},{24,8},{28,12},{1,17},{... | collective-permute-start | bytes 786440 | tf_op jit(solution)/shard_map/ppermute | solution.py:269
  28.5 10.3 %collective-permute-start.9 = (bf16[128,1024]{1,0:T(8,128)(2,1)S(1)}, bf16[128,1024]{1,0:T(8,128)(2,1)S(1)}, u32[]{:S(2)}, u32[]{:S(2)}) collective-permute-start(bf16[128,1024]{1,0:T(8,128)(2,1)S(1)} %collective-permute-done.7.refs_6_), channel_id=1, source_target_pairs={{0,4},{4,0},{8,12},{12,8},{16,20},{20,16},{24,28},{28,24},{1,5},{5... | collective-permute-start | bytes 786440 | tf_op jit(solution)/shard_map/ppermute | solution.py:269
  29.6 9.8 %collective-permute-start.4 = (bf16[512,256]{1,0:T(8,128)(2,1)S(1)}, bf16[512,256]{1,0:T(8,128)(2,1)S(1)}, u32[]{:S(2)}, u32[]{:S(2)}) collective-permute-start(bf16[512,256]{1,0:T(8,128)(2,1)S(1)} %get-tuple-element.60.refs_0_), channel_id=1, source_target_pairs={{0,1},{1,0},{2,3},{3,2},{4,5},{5,4},{6,7},{7,6},{8,9},{9,8},{10,11... | collective-permute-start | bytes 786440 | tf_op jit(solution)/shard_map/ppermute | solution.py:266
  38.8 9.2 %collective-permute-start.12 = (bf16[128,1024]{1,0:T(8,128)(2,1)S(1)}, bf16[128,1024]{1,0:T(8,128)(2,1)S(1)}, u32[]{:S(2)}, u32[]{:S(2)}) collective-permute-start(bf16[128,1024]{1,0:T(8,128)(2,1)S(1)} %collective-permute-done.11.refs_4_), channel_id=1, source_target_pairs={{0,4},{4,0},{8,12},{12,8},{16,20},{20,16},{24,28},{28,24},{1,5},{5... | collective-permute-start | bytes 786440 | tf_op jit(solution)/shard_map/ppermute | solution.py:269
  41.1 12.6 %collective-permute-start.10 = (bf16[128,1024]{1,0:T(8,128)(2,1)S(1)}, bf16[128,1024]{1,0:T(8,128)(2,1)S(1)}, u32[]{:S(2)}, u32[]{:S(2)}) collective-permute-start(bf16[128,1024]{1,0:T(8,128)(2,1)S(1)} %get-tuple-element.64), channel_id=1, source_target_pairs={{0,4},{4,0},{8,12},{12,8},{16,20},{20,16},{24,28},{28,24},{1,5},{5... | collective-permute-start | bytes 786440 | tf_op jit(solution)/shard_map/ppermute | solution.py:269
  48.0 12.2 %collective-permute-start.14 = (bf16[128,1024]{1,0:T(8,128)(2,1)S(1)}, bf16[128,1024]{1,0:T(8,128)(2,1)S(1)}, u32[]{:S(2)}, u32[]{:S(2)}) collective-permute-start(bf16[128,1024]{1,0:T(8,128)(2,1)S(1)} %get-tuple-element.74), channel_id=1, source_target_pairs={{0,4},{4,0},{8,12},{12,8},{16,20},{20,16},{24,28},{28,24},{1,5},{5... | collective-permute-start | bytes 786440 | tf_op jit(solution)/shard_map/ppermute | solution.py:269
  53.7 10.1 %collective-permute-start.16 = (bf16[128,1024]{1,0:T(8,128)(2,1)S(1)}, bf16[128,1024]{1,0:T(8,128)(2,1)S(1)}, u32[]{:S(2)}, u32[]{:S(2)}) collective-permute-start(bf16[128,1024]{1,0:T(8,128)(2,1)S(1)} %get-tuple-element.77), channel_id=1, source_target_pairs={{0,4},{4,0},{8,12},{12,8},{16,20},{20,16},{24,28},{28,24},{1,5},{5... | collective-permute-start | bytes 786440 | tf_op jit(solution)/shard_map/ppermute | solution.py:269
  54.3 10.0 %collective-permute-start.13 = (bf16[128,1024]{1,0:T(8,128)(2,1)S(1)}, bf16[128,1024]{1,0:T(8,128)(2,1)S(1)}, u32[]{:S(2)}, u32[]{:S(2)}) collective-permute-start(bf16[128,1024]{1,0:T(8,128)(2,1)S(1)} %convert_add_fusion), channel_id=1, source_target_pairs={{0,24},{4,28},{8,16},{12,20},{16,8},{20,12},{24,0},{28,4},{1,25},{... | collective-permute-start | bytes 786440 | tf_op jit(solution)/shard_map/ppermute | solution.py:269
  58.6 8.2 %collective-permute-start.19 = (bf16[528,256]{1,0:T(8,128)(2,1)S(1)}, bf16[528,256]{1,0:T(8,128)(2,1)S(1)}, u32[]{:S(2)}, u32[]{:S(2)}) collective-permute-start(bf16[528,256]{1,0:T(8,128)(2,1)S(1)} %get-tuple-element.82), channel_id=1, source_target_pairs={{0,1},{1,0},{2,3},{3,2},{4,5},{5,4},{6,7},{7,6},{8,9},{9,8},{10,11... | collective-permute-start | bytes 811016 | tf_op jit(solution)/shard_map/ppermute | solution.py:266
  58.7 11.0 %collective-permute-start.20 = (bf16[528,256]{1,0:T(8,128)(2,1)S(1)}, bf16[528,256]{1,0:T(8,128)(2,1)S(1)}, u32[]{:S(2)}, u32[]{:S(2)}) collective-permute-start(bf16[528,256]{1,0:T(8,128)(2,1)S(1)} %get-tuple-element.83), channel_id=1, source_target_pairs={{0,2},{1,3},{2,0},{3,1},{4,6},{5,7},{6,4},{7,5},{8,10},{9,11},{10,... | collective-permute-start | bytes 811016 | tf_op jit(solution)/shard_map/ppermute | solution.py:266
  60.2 12.8 %collective-permute-start.21 = (bf16[528,256]{1,0:T(8,128)(2,1)S(1)}, bf16[528,256]{1,0:T(8,128)(2,1)S(1)}, u32[]{:S(2)}, u32[]{:S(2)}) collective-permute-start(bf16[528,256]{1,0:T(8,128)(2,1)S(1)} %get-tuple-element.84), channel_id=1, source_target_pairs={{0,3},{1,2},{2,1},{3,0},{4,7},{5,6},{6,5},{7,4},{8,11},{9,10},{10,... | collective-permute-start | bytes 811016 | tf_op jit(solution)/shard_map/ppermute | solution.py:266
  63.8 13.7 %collective-permute-start.15 = (bf16[128,1024]{1,0:T(8,128)(2,1)S(1)}, bf16[128,1024]{1,0:T(8,128)(2,1)S(1)}, u32[]{:S(2)}, u32[]{:S(2)}) collective-permute-start(bf16[128,1024]{1,0:T(8,128)(2,1)S(1)} %add_convert_fusion.1), channel_id=1, source_target_pairs={{0,16},{4,20},{8,24},{12,28},{16,0},{20,4},{24,8},{28,12},{1,17},{... | collective-permute-start | bytes 786440 | tf_op jit(solution)/shard_map/ppermute | solution.py:269
  64.2 13.3 %collective-permute-start.17 = (bf16[128,1024]{1,0:T(8,128)(2,1)S(1)}, bf16[128,1024]{1,0:T(8,128)(2,1)S(1)}, u32[]{:S(2)}, u32[]{:S(2)}) collective-permute-start(bf16[128,1024]{1,0:T(8,128)(2,1)S(1)} %add_convert_fusion), channel_id=1, source_target_pairs={{0,8},{4,12},{8,0},{12,4},{16,24},{20,28},{24,16},{28,20},{1,9},{5... | collective-permute-start | bytes 786440 | tf_op jit(solution)/shard_map/ppermute | solution.py:269
  66.9 10.6 %collective-permute-start.18 = (bf16[128,1024]{1,0:T(8,128)(2,1)S(1)}, bf16[128,1024]{1,0:T(8,128)(2,1)S(1)}, u32[]{:S(2)}, u32[]{:S(2)}) collective-permute-start(bf16[128,1024]{1,0:T(8,128)(2,1)S(1)} %get-tuple-element.80), channel_id=1, source_target_pairs={{0,4},{4,0},{8,12},{12,8},{16,20},{20,16},{24,28},{28,24},{1,5},{5... | collective-permute-start | bytes 786440 | tf_op jit(solution)/shard_map/ppermute | solution.py:269
  (3 other events, 10.1 us)

commit v2 on v1

--- a/solution.py
+++ b/solution.py
@@ -96,13 +96,19 @@
     rows = pltpu.make_async_copy(grad_hbm.at[pl.ds(group, EDGE), :], rows_v, sem.at[2])
     rows.start()
     back_ref[:, feats:] = jnp.broadcast_to(lead_mask(start), (EDGE, LANES)).astype(BF16)
-    ahead_ref[:, width + feats :] = jnp.broadcast_to(tail_mask(start), (EDGE, LANES)).astype(BF16)
+    ahead_ref[:EDGE, feats:] = jnp.broadcast_to(tail_mask(start), (EDGE, LANES)).astype(BF16)
     copies[1].wait()
     back_ref[:, :feats] = hidden_ref[:EDGE]
-    ahead_ref[:, width : width + feats] = hidden_ref[bytes_ - EDGE :]
+    ahead_ref[:EDGE, :feats] = hidden_ref[bytes_ - EDGE :]
     rows.wait()
     chosen = iota((EDGE, width), 0) == last - group
-    ahead_ref[:, :width] = jnp.where(chosen, rows_v[...].astype(F32), 0.0).astype(BF16)
+    row = jnp.sum(jnp.where(chosen, rows_v[...].astype(F32), 0.0), axis=0, keepdims=True)
+    ahead_ref[EDGE:] = jnp.zeros((EDGE, feats + LANES), BF16)
+    for at in range(width // feats):
+        piece = row[:, at * feats : (at + 1) * feats]
+        spread = jnp.where(iota((EDGE, feats), 0) == at, piece, 0.0)
+        old = ahead_ref[EDGE:, :feats].astype(F32)
+        ahead_ref[EDGE:, :feats] = (old + spread).astype(BF16)
 
 
 def pool_kernel(hidden_ref, next_ref, start_ref, query_ref, low_ref, pooled_ref, denom_ref):
@@ -147,9 +153,8 @@
     onehot_ref[...] = onehot
     hidden = hidden_ref[...].astype(F32)
     bent, weight = scores(hidden, query)
-    width = prev_ref.shape[1] - feats - LANES
-    before = prev_ref[:, width : width + feats].astype(F32)
-    part = scores(before, query)[1] * prev_ref[:, width + feats : width + feats + 1].astype(F32)
+    before = prev_ref[:EDGE, :feats].astype(F32)
+    part = scores(before, query)[1] * prev_ref[:EDGE, feats : feats + 1].astype(F32)
     lead = lead_mask(start_ref[...])
     own = weight[:EDGE] * lead
     first_denom = jnp.sum(part + own, axis=0, keepdims=True)
@@ -223,12 +228,15 @@
         for index, ref in enumerate(piece_refs):
             owner = pl.multiple_of((spot ^ index) * rows, rows)
             full_ref[pl.ds(owner, rows), :] = ref[...]
+    last = prev_ref[EDGE:, :feats].astype(F32)
+    row = jnp.concatenate([last[at : at + 1] for at in range(width // feats)], axis=1)
+    row = jnp.where(iota((EDGE, width), 0) == 0, row, 0.0).astype(BF16)
     place = lax.axis_index("mp")
     for index, ref in enumerate(out_refs):
         owner = pl.multiple_of((place ^ index) * feats, feats)
         block = full_ref[pl.ds(owner, feats), :]
         ref[:slots] = dot(grad_ref[...], block, ((1,), (1,))).astype(BF16)
-        ref[slots:] = dot(prev_ref[:, :width], block, ((1,), (1,))).astype(BF16)
+        ref[slots:] = dot(row, block, ((1,), (1,))).astype(BF16)
 
 
 def call(kernel, out_shape, *args, flops=0, scratch=(), in_specs=None, limit=VMEM_LIMIT):
@@ -260,7 +268,7 @@
     n_seq, n_mp = lax.axis_size("seq"), lax.axis_size("mp")
     latent_dim = feats * n_mp
     rows = latent_dim // n_seq
-    staged = n_seq <= 8
+    staged = n_seq == 8
 
     def swap(value, step):
         return lax.ppermute(value, "mp", [(i, i ^ step) for i in range(n_mp)])
@@ -278,7 +286,7 @@
         load_kernel,
         (
             shape((EDGE, feats + LANES), BF16),
-            shape((EDGE, width + feats + LANES), BF16),
+            shape((2 * EDGE, feats + LANES), BF16),
             shape(byte_hidden.shape, BF16),
             shape(arguments[1].shape, jnp.int32),
         ),
@@ -298,8 +306,7 @@
         pieces = [in_weight] + [None] * (n_seq - 1)
         pieces[1] = trade(in_weight, 1)
         for step in range(2, n_seq, 2):
-            source = after((in_weight, pieces[2]))[0] if step == 4 else in_weight
-            pieces[step] = trade(source, step)
+            pieces[step] = trade(in_weight, step)
     else:
         pieces = [lax.all_gather(in_weight, "seq", axis=0, tiled=True)]
 
@@ -314,14 +321,13 @@
     )
 
     if staged:
-        low, previous, *pieces[1:3] = after((low, previous, *pieces[1:3]))
-    parts = [low] + [swap(low, step) for step in range(1, n_mp)]
-    if staged:
-        latest = low
-        for at, step in enumerate((2, *range(n_seq - 2, 2, -2))):
-            wait = (latest, parts[at + 1]) if at else latest
-            pieces[step], _ = after((pieces[step], wait))
-            latest = pieces[step + 1] = trade(pieces[step], 1)
+        low, *pieces[1:3] = after((low, *pieces[1:3]))
+        pieces[3] = trade(after((pieces[2], low))[0], 1)
+    parts = [low]
+    for step in reversed([1 << bit for bit in range(n_mp.bit_length() - 1)]):
+        if staged and step == 1:
+            parts[0], pieces[6], pieces[3] = after((parts[0], pieces[6], pieces[3]))
+        parts = [part for held in parts for part in (held, swap(held, step))]
     onehot, share, delta, slope = call(
         spread_kernel,
         (shape((bytes_, slots), BF16),) + (shape((bytes_, feats), F32),) * 3,
@@ -339,8 +345,6 @@
         blocks = [shape((rows, width), BF16 if index % 2 else F32) for index in range(n_seq)]
     else:
         blocks = [shape((latent_dim, width), BF16)]
-    if staged:
-        parts, pieces[-1], share = after((parts, pieces[-1], share))
     terms = call(
         functools.partial(outer_kernel, n_mp, scale),
         tuple(blocks),
@@ -350,24 +354,11 @@
         scratch=(pltpu.VMEM((slots, latent_dim), BF16), pltpu.VMEM((latent_dim, width), F32)),
     )
     if staged:
-        fetched, pairs, sums = [], [], []
-        for at, step in enumerate(reversed(range(0, n_seq, 2))):
-            away = terms[step + 1]
-            if at >= 2:
-                away, _ = after((away, pairs[0] if at == 2 else fetched[1]))
-            if at == 1:
-                away, _ = after((away, latest))
-            fetched.append(trade(away, 1))
-            if at == 0:
-                previous, _ = after((previous, fetched[0]))
-            pairs.append(terms[step] + fetched[-1].astype(F32))
-            if step:
-                fetched.append(trade(pairs[-1].astype(BF16), step))
-            sums.append(fetched[-1].astype(F32) if step else pairs[-1])
-        grad_weight = sum(sums[1:], sums[0])
-    else:
-        received = lax.all_to_all(terms[0], "seq", split_axis=0, concat_axis=0, tiled=True)
-        grad_weight = received.reshape(n_seq, rows, width).astype(F32).sum(0)
+        fetched = {}
+        fetched[7] = trade(terms[7], 1)
+        pieces[7] = trade(after((pieces[6], terms[0]))[0], 1)
+        pieces[5] = trade(after((pieces[4], fetched[7]))[0], 1)
+        fetched[5] = trade(after((terms[5], pieces[7], previous))[0], 1)
 
     *partials, weight_full = call(
         functools.partial(partial_kernel, n_mp),
@@ -378,6 +369,20 @@
         flops=work,
     )
     grads = [partials[0]] + [swap(partials[step], step) for step in range(1, n_mp)]
+
+    if staged:
+        fetched[6] = trade((terms[6] + fetched[7].astype(F32)).astype(BF16), 6)
+        fetched[3] = trade(after((terms[3], weight_full, share, fetched[6]))[0], 1)
+        fetched[4] = trade((terms[4] + fetched[5].astype(F32)).astype(BF16), 4)
+        fetched[1] = trade(after((terms[1], fetched[5], grads[2]))[0], 1)
+        fetched[2] = trade((terms[2] + fetched[3].astype(F32)).astype(BF16), 2)
+        grad_weight = terms[0] + fetched[1].astype(F32)
+        for step in (6, 4, 2):
+            grad_weight = grad_weight + fetched[step].astype(F32)
+    else:
+        received = lax.all_to_all(terms[0], "seq", split_axis=0, concat_axis=0, tiled=True)
+        grad_weight = received.reshape(n_seq, rows, width).astype(F32).sum(0)
+
     latent = call(
         functools.partial(latent_kernel, n_mp),
         shape((slots, width), BF16),

time: 78.7 us -> 73.1 us (0.929)
  waiting for transfers between devices: 30.8 us -> 16.6 us
  starting transfers between devices: 31 us -> 38.5 us
    ppermute x14, waiting for transfers between devices: 24.8 us -> 15.7 us  [trade(): return lax.ppermute(value, 'seq', [(i, i ^ step) for i in range(n_seq)])]
    ppermute x14, starting transfers between devices: 24 us -> 30.2 us  [trade(): return lax.ppermute(value, 'seq', [(i, i ^ step) for i in range(n_seq)])]
    ppermute x6, waiting for transfers between devices: 5.91 us -> 0.09 us  [swap(): return lax.ppermute(value, 'mp', [(i, i ^ step) for i in range(n_mp)])]
  transfers between devices with their start and end apart: 22 -> 22, of which waited for: 8 -> 10; matrix products, arithmetic and copies ran while one was open for 0% -> 0% of each run, Pallas kernels for 16% -> 18%
where the time goes in v2:
time: 73.1 us; the launch traced here: 72.3 us
  starting transfers between devices  38.5 us (53%)
  waiting for transfers between devices  16.6 us (23%)
  Pallas kernels  13.8 us (19%)
  local copies, waits for them, and re-layouts  1.45 us (2%)
  other arithmetic  1.16 us (2%)
  between operations  0.77 us (1%)
    ppermute x14, starting transfers between devices, trade(): return lax.ppermute(value, 'seq', [(i, i ^ step) for i in range(n_seq)])  30.2 us
    ppermute x14, waiting for transfers between devices, trade(): return lax.ppermute(value, 'seq', [(i, i ^ step) for i in range(n_seq)])  15.7 us
    pallas_call x7, Pallas kernels, call(): pl.pallas_call(kernel, out_shape=out_shape, in_specs=in_specs, out_specs=...  13.8 us
    ppermute x6, starting transfers between devices, swap(): return lax.ppermute(value, 'mp', [(i, i ^ step) for i in range(n_mp)])  4.06 us
    ppermute x1, starting transfers between devices, shards(): lax.ppermute(ahead, 'seq', [(i, i + 1) for i in range(n_seq - 1)])  3 us
  transfers between devices with their start and end apart: 22, of which 10 were waited for; matrix products, arithmetic and copies ran while one was open for 0% of the time, Pallas kernels for 18%

profile of v2, /device:TPU:0, one launch (start us, length us, event | category | flops | bytes accessed | tf_op | source)
XLA Modules:
  0.0 72.3 jit_solution(8962124550054593645)
XLA Ops:
  2.5 3.1 %collective-permute-start.2 = (bf16[128,1024]{1,0:T(8,128)(2,1)}, bf16[128,1024]{1,0:T(8,128)(2,1)S(1)}, u32[]{:S(2)}, u32[]{:S(2)}) collective-permute-start(bf16[128,1024]{1,0:T(8,128)(2,1)} %refs_0_), channel_id=1, source_target_pairs={{0,8},{4,12},{8,0},{12,4},{16,24},{20,28},{24,16},{28,20},{1,9},{5... | collective-permute-start | bytes 786440 | tf_op jit(solution)/shard_map/ppermute | solution.py:277
  5.6 1.5 %collective-permute-start.1 = (bf16[128,1024]{1,0:T(8,128)(2,1)}, bf16[128,1024]{1,0:T(8,128)(2,1)S(1)}, u32[]{:S(2)}, u32[]{:S(2)}) collective-permute-start(bf16[128,1024]{1,0:T(8,128)(2,1)} %refs_0_), channel_id=1, source_target_pairs={{0,4},{4,0},{8,12},{12,8},{16,20},{20,16},{24,28},{28,24},{1,5},{5... | collective-permute-start | bytes 786440 | tf_op jit(solution)/shard_map/ppermute | solution.py:277
  8.4 4.7 %collective-permute-start.3 = (bf16[128,1024]{1,0:T(8,128)(2,1)}, bf16[128,1024]{1,0:T(8,128)(2,1)S(1)}, u32[]{:S(2)}, u32[]{:S(2)}) collective-permute-start(bf16[128,1024]{1,0:T(8,128)(2,1)} %refs_0_), channel_id=1, source_target_pairs={{0,24},{4,28},{8,16},{12,20},{16,8},{20,12},{24,0},{28,4},{1,25},{... | collective-permute-start | bytes 786440 | tf_op jit(solution)/shard_map/ppermute | solution.py:277
  14.5 2.1 %shard_map.77 = (bf16[512,256]{1,0:T(8,128)(2,1)S(1)}, f32[512,256]{1,0:T(8,128)S(1)}, f32[512,256]{1,0:T(8,128)S(1)}) custom-call(bf16[1024,256]{1,0:T(8,128)(2,1)S(1)} %get-tuple-element.40.hidden_ref, bf16[16,384]{1,0:T(8,128)(2,1)S(1)} %collective-permute-done.next_ref, s32[8,128]{1,0:T(8,128)S(1)} %get-tuple-element.42.start_ref.refs_4_, ...), custom_call_target="tpu_custom_call" | custom-call | tf_op jit(solution)/shard_map/pallas_call | solution.py:245
  17.1 1.5 %collective-permute-start.6 = (bf16[512,256]{1,0:T(8,128)(2,1)S(1)}, bf16[512,256]{1,0:T(8,128)(2,1)S(1)}, u32[]{:S(2)}, u32[]{:S(2)}) collective-permute-start(bf16[512,256]{1,0:T(8,128)(2,1)S(1)} %get-tuple-element.48.refs_0_), channel_id=1, source_target_pairs={{0,2},{1,3},{2,0},{3,1},{4,6},{5,7},{6,4},{7,5},{8,10},{9,11},{10,... | collective-permute-start | bytes 786440 | tf_op jit(solution)/shard_map/ppermute | solution.py:274
  18.6 1.8 %collective-permute-done.3.refs_6_ = bf16[128,1024]{1,0:T(8,128)(2,1)S(1)} collective-permute-done((bf16[128,1024]{1,0:T(8,128)(2,1)}, bf16[128,1024]{1,0:T(8,128)(2,1)S(1)}, u32[]{:S(2)}, u32[]{:S(2)}) %collective-permute-start.3) | collective-permute-done | bytes 262176 | tf_op jit(solution)/shard_map/ppermute | solution.py:277
  20.3 3.2 %collective-permute-done.4.refs_3_ = bf16[128,1024]{1,0:T(8,128)(2,1)S(1)} collective-permute-done((bf16[128,1024]{1,0:T(8,128)(2,1)S(1)}, bf16[128,1024]{1,0:T(8,128)(2,1)S(1)}, u32[]{:S(2)}, u32[]{:S(2)}) %collective-permute-start.4) | collective-permute-done | bytes 262176 | tf_op jit(solution)/shard_map/ppermute | solution.py:277
  24.1 2.9 %collective-permute-start.9 = (bf16[128,1024]{1,0:T(8,128)(2,1)S(1)}, bf16[128,1024]{1,0:T(8,128)(2,1)S(1)}, u32[]{:S(2)}, u32[]{:S(2)}) collective-permute-start(bf16[128,1024]{1,0:T(8,128)(2,1)S(1)} %copy-done.2), channel_id=1, source_target_pairs={{0,16},{4,20},{8,24},{12,28},{16,0},{20,4},{24,8},{28,12},{1,17},{... | collective-permute-start | bytes 786440 | tf_op jit(solution)/shard_map/ppermute | solution.py:277
  27.0 1.7 %shard_map.78 = (f32[128,1024]{1,0:T(8,128)S(1)}, bf16[128,1024]{1,0:T(8,128)(2,1)S(1)}, f32[128,1024]{1,0:T(8,128)S(1)}, bf16[128,1024]{1,0:T(8,128)(2,1)S(1)},...) custom-call(bf16[512,256]{1,0:T(8,128)(2,1)S(1)} %get-tuple-element., ...), custom_call_target="tpu_custom_call" | custom-call | tf_op jit(solution)/shard_map/pallas_call | solution.py:245
  29.7 3.0 %collective-permute-start.8 = (bf16[32,384]{1,0:T(8,128)(2,1)S(1)}, bf16[32,384]{1,0:T(8,128)(2,1)S(1)}, u32[]{:S(2)}, u32[]{:S(2)}) collective-permute-start(bf16[32,384]{1,0:T(8,128)(2,1)S(1)} %get-tuple-element.49), channel_id=1, source_target_pairs={{0,4},{4,8},{8,12},{12,16},{16,20},{20,24},{24,28},{1,5},{5,9},{9,... | collective-permute-start | bytes 73736 | tf_op jit(solution)/shard_map/ppermute | solution.py:302
  32.7 3.0 %collective-permute-start.12 = (bf16[128,1024]{1,0:T(8,128)(2,1)S(1)}, bf16[128,1024]{1,0:T(8,128)(2,1)S(1)}, u32[]{:S(2)}, u32[]{:S(2)}) collective-permute-start(bf16[128,1024]{1,0:T(8,128)(2,1)S(1)} %collective-permute-done.3.refs_6_), channel_id=1, source_target_pairs={{0,4},{4,0},{8,12},{12,8},{16,20},{20,16},{24,28},{28,24},{1,5},{5... | collective-permute-start | bytes 786440 | tf_op jit(solution)/shard_map/ppermute | solution.py:277
  35.7 3.8 %collective-permute-done.9.refs_4_ = bf16[128,1024]{1,0:T(8,128)(2,1)S(1)} collective-permute-done((bf16[128,1024]{1,0:T(8,128)(2,1)S(1)}, bf16[128,1024]{1,0:T(8,128)(2,1)S(1)}, u32[]{:S(2)}, u32[]{:S(2)}) %collective-permute-start.9) | collective-permute-done | bytes 262176 | tf_op jit(solution)/shard_map/ppermute | solution.py:277
  40.6 3.7 %collective-permute-start.16 = (bf16[128,1024]{1,0:T(8,128)(2,1)S(1)}, bf16[128,1024]{1,0:T(8,128)(2,1)S(1)}, u32[]{:S(2)}, u32[]{:S(2)}) collective-permute-start(bf16[128,1024]{1,0:T(8,128)(2,1)S(1)} %add_convert_fusion.2), channel_id=1, source_target_pairs={{0,24},{4,28},{8,16},{12,20},{16,8},{20,12},{24,0},{28,4},{1,25},{... | collective-permute-start | bytes 786440 | tf_op jit(solution)/shard_map/ppermute | solution.py:277
  45.3 1.8 %shard_map.81 = (bf16[1024,512]{1,0:T(8,128)(2,1)S(1)}, f32[1024,256]{1,0:T(8,128)S(1)}, f32[1024,256]{1,0:T(8,128)S(1)}, f32[1024,256]{1,0:T(8,128)S(1)}) custom-call(bf16[1024,256]{1,0:T(8,128)(2,1)S(1)} %get-tuple-element.40.hidden_ref, bf16[32,384]{1,0:T(8,128)(2,1)S(1)} %collective-permute-done.8.prev_ref, ...), custom_call_target="tpu_custom_call" | custom-call | tf_op jit(solution)/shard_map/pallas_call | solution.py:245
  47.0 2.1 %collective-permute-done.11.refs_5_ = bf16[128,1024]{1,0:T(8,128)(2,1)S(1)} collective-permute-done((bf16[128,1024]{1,0:T(8,128)(2,1)S(1)}, bf16[128,1024]{1,0:T(8,128)(2,1)S(1)}, u32[]{:S(2)}, u32[]{:S(2)}) %collective-permute-start.11) | collective-permute-done | bytes 262176 | tf_op jit(solution)/shard_map/ppermute | solution.py:277
  49.2 2.5 %shard_map.79 = (bf16[528,256]{1,0:T(8,128)(2,1)S(1)}, bf16[528,256]{1,0:T(8,128)(2,1)S(1)}, bf16[528,256]{1,0:T(8,128)(2,1)S(1)}, bf16[528,256]{1,0:T(8,128)(2,1)S(1)}, bf16[1024,1024]{1,0:T(8,128)(2,1)}) custom-call(bf16[512,1024]{1,0:T(8,128)(2,1)S(1)} %copy-done, bf16[32,384]{1,0:T(8,128)(2,1)S(1)} %collective-permute-done.8.prev_ref, ...), custom_call_target="tpu_custom_call" | custom-call | tf_op jit(solution)/shard_map/pallas_call | solution.py:245
  51.7 1.4 %collective-permute-start.18 = (bf16[128,1024]{1,0:T(8,128)(2,1)S(1)}, bf16[128,1024]{1,0:T(8,128)(2,1)S(1)}, u32[]{:S(2)}, u32[]{:S(2)}) collective-permute-start(bf16[128,1024]{1,0:T(8,128)(2,1)S(1)} %get-tuple-element.70), channel_id=1, source_target_pairs={{0,4},{4,0},{8,12},{12,8},{16,20},{20,16},{24,28},{28,24},{1,5},{5... | collective-permute-start | bytes 786440 | tf_op jit(solution)/shard_map/ppermute | solution.py:277
  53.1 1.5 %collective-permute-start.14 = (bf16[528,256]{1,0:T(8,128)(2,1)S(1)}, bf16[528,256]{1,0:T(8,128)(2,1)S(1)}, u32[]{:S(2)}, u32[]{:S(2)}) collective-permute-start(bf16[528,256]{1,0:T(8,128)(2,1)S(1)} %get-tuple-element.61), channel_id=1, source_target_pairs={{0,2},{1,3},{2,0},{3,1},{4,6},{5,7},{6,4},{7,5},{8,10},{9,11},{10,... | collective-permute-start | bytes 811016 | tf_op jit(solution)/shard_map/ppermute | solution.py:274
  54.8 2.6 %collective-permute-start.17 = (bf16[128,1024]{1,0:T(8,128)(2,1)S(1)}, bf16[128,1024]{1,0:T(8,128)(2,1)S(1)}, u32[]{:S(2)}, u32[]{:S(2)}) collective-permute-start(bf16[128,1024]{1,0:T(8,128)(2,1)S(1)} %add_convert_fusion.1), channel_id=1, source_target_pairs={{0,16},{4,20},{8,24},{12,28},{16,0},{20,4},{24,8},{28,12},{1,17},{... | collective-permute-start | bytes 786440 | tf_op jit(solution)/shard_map/ppermute | solution.py:277
  58.1 1.6 %collective-permute-done.18 = bf16[128,1024]{1,0:T(8,128)(2,1)S(1)} collective-permute-done((bf16[128,1024]{1,0:T(8,128)(2,1)S(1)}, bf16[128,1024]{1,0:T(8,128)(2,1)S(1)}, u32[]{:S(2)}, u32[]{:S(2)}) %collective-permute-start.18) | collective-permute-done | bytes 262176 | tf_op jit(solution)/shard_map/ppermute | solution.py:277
  59.8 3.6 %collective-permute-start.19 = (bf16[128,1024]{1,0:T(8,128)(2,1)S(1)}, bf16[128,1024]{1,0:T(8,128)(2,1)S(1)}, u32[]{:S(2)}, u32[]{:S(2)}) collective-permute-start(bf16[128,1024]{1,0:T(8,128)(2,1)S(1)} %add_convert_fusion), channel_id=1, source_target_pairs={{0,8},{4,12},{8,0},{12,4},{16,24},{20,28},{24,16},{28,20},{1,9},{5... | collective-permute-start | bytes 786440 | tf_op jit(solution)/shard_map/ppermute | solution.py:277
  63.7 2.4 %shard_map.80 = bf16[512,1024]{1,0:T(8,128)(2,1)} custom-call(bf16[512,256]{1,0:T(8,128)(2,1)S(1)} %get-tuple-element.48.refs_0_, bf16[512,256]{1,0:T(8,128)(2,1)S(1)} %collective-permute-done.5.refs_1_, bf16[512,256]{1,0:T(8,128)(2,1)S(1)} %collective-permute-done.6.refs_2_, bf16[512,256]{1,0:T(8,128)(2,1)S(1)} %collective-permute-done.7.refs_3_, ...), custom_call_target="tpu_custom_call" | custom-call | tf_op jit(solution)/shard_map/pallas_call | solution.py:245
  66.0 2.3 %shard_map.82 = bf16[1024,256]{1,0:T(8,128)(2,1)} custom-call(bf16[528,256]{1,0:T(8,128)(2,1)S(1)} %get-tuple-element.71.refs_0_, bf16[528,256]{1,0:T(8,128)(2,1)S(1)} %collective-permute-done.20.refs_1_, bf16[528,256]{1,0:T(8,128)(2,1)S(1)} %collective-permute-done.14.refs_2_, bf16[528,256]{1,0:T(8,128)(2,1)S(1)} %collective-permute-done.21.refs_3_, ...), custom_call_target="tpu_custom_call" | custom-call | tf_op jit(solution)/shard_map/pallas_call | solution.py:245
  68.4 2.8 %collective-permute-done.19 = bf16[128,1024]{1,0:T(8,128)(2,1)S(1)} collective-permute-done((bf16[128,1024]{1,0:T(8,128)(2,1)S(1)}, bf16[128,1024]{1,0:T(8,128)(2,1)S(1)}, u32[]{:S(2)}, u32[]{:S(2)}) %collective-permute-start.19) | collective-permute-done | bytes 262176 | tf_op jit(solution)/shard_map/ppermute | solution.py:277
  (41 shorter events, 10.9 us)
Async XLA Ops:
  0.6 26.4 %copy-start = (bf16[512,1024]{1,0:T(8,128)(2,1)S(1)}, bf16[512,1024]{1,0:T(8,128)(2,1)}, u32[]{:S(2)}) copy-start(bf16[512,1024]{1,0:T(8,128)(2,1)} %grad_ref.1) | copy-start | bytes 3145732
  0.6 23.4 %copy-start.2 = (bf16[128,1024]{1,0:T(8,128)(2,1)S(1)}, bf16[128,1024]{1,0:T(8,128)(2,1)}, u32[]{:S(2)}) copy-start(bf16[128,1024]{1,0:T(8,128)(2,1)} %refs_0_) | copy-start | bytes 786436
  2.5 14.1 %collective-permute-start.2 = (bf16[128,1024]{1,0:T(8,128)(2,1)}, bf16[128,1024]{1,0:T(8,128)(2,1)S(1)}, u32[]{:S(2)}, u32[]{:S(2)}) collective-permute-start(bf16[128,1024]{1,0:T(8,128)(2,1)} %refs_0_), channel_id=1, source_target_pairs={{0,8},{4,12},{8,0},{12,4},{16,24},{20,28},{24,16},{28,20},{1,9},{5... | collective-permute-start | bytes 786440 | tf_op jit(solution)/shard_map/ppermute | solution.py:277
  5.6 11.0 %collective-permute-start.1 = (bf16[128,1024]{1,0:T(8,128)(2,1)}, bf16[128,1024]{1,0:T(8,128)(2,1)S(1)}, u32[]{:S(2)}, u32[]{:S(2)}) collective-permute-start(bf16[128,1024]{1,0:T(8,128)(2,1)} %refs_0_), channel_id=1, source_target_pairs={{0,4},{4,0},{8,12},{12,8},{16,20},{20,16},{24,28},{28,24},{1,5},{5... | collective-permute-start | bytes 786440 | tf_op jit(solution)/shard_map/ppermute | solution.py:277
  7.2 6.7 %collective-permute-start = (bf16[16,384]{1,0:T(8,128)(2,1)S(1)}, bf16[16,384]{1,0:T(8,128)(2,1)S(1)}, u32[]{:S(2)}, u32[]{:S(2)}) collective-permute-start(bf16[16,384]{1,0:T(8,128)(2,1)S(1)} %get-tuple-element.41), channel_id=1, source_target_pairs={{4,0},{8,4},{12,8},{16,12},{20,16},{24,20},{28,24},{5,1},{9,5},{13... | collective-permute-start | bytes 36872 | tf_op jit(solution)/shard_map/ppermute | solution.py:301
  8.4 11.9 %collective-permute-start.3 = (bf16[128,1024]{1,0:T(8,128)(2,1)}, bf16[128,1024]{1,0:T(8,128)(2,1)S(1)}, u32[]{:S(2)}, u32[]{:S(2)}) collective-permute-start(bf16[128,1024]{1,0:T(8,128)(2,1)} %refs_0_), channel_id=1, source_target_pairs={{0,24},{4,28},{8,16},{12,20},{16,8},{20,12},{24,0},{28,4},{1,25},{... | collective-permute-start | bytes 786440 | tf_op jit(solution)/shard_map/ppermute | solution.py:277
  16.6 6.9 %collective-permute-start.4 = (bf16[128,1024]{1,0:T(8,128)(2,1)S(1)}, bf16[128,1024]{1,0:T(8,128)(2,1)S(1)}, u32[]{:S(2)}, u32[]{:S(2)}) collective-permute-start(bf16[128,1024]{1,0:T(8,128)(2,1)S(1)} %collective-permute-done.2.refs_2_), channel_id=1, source_target_pairs={{0,4},{4,0},{8,12},{12,8},{16,20},{20,16},{24,28},{28,24},{1,5},{5... | collective-permute-start | bytes 786440 | tf_op jit(solution)/shard_map/ppermute | solution.py:277
  17.1 6.6 %collective-permute-start.6 = (bf16[512,256]{1,0:T(8,128)(2,1)S(1)}, bf16[512,256]{1,0:T(8,128)(2,1)S(1)}, u32[]{:S(2)}, u32[]{:S(2)}) collective-permute-start(bf16[512,256]{1,0:T(8,128)(2,1)S(1)} %get-tuple-element.48.refs_0_), channel_id=1, source_target_pairs={{0,2},{1,3},{2,0},{3,1},{4,6},{5,7},{6,4},{7,5},{8,10},{9,11},{10,... | collective-permute-start | bytes 786440 | tf_op jit(solution)/shard_map/ppermute | solution.py:274
  23.6 3.4 %collective-permute-start.5 = (bf16[512,256]{1,0:T(8,128)(2,1)S(1)}, bf16[512,256]{1,0:T(8,128)(2,1)S(1)}, u32[]{:S(2)}, u32[]{:S(2)}) collective-permute-start(bf16[512,256]{1,0:T(8,128)(2,1)S(1)} %get-tuple-element.48.refs_0_), channel_id=1, source_target_pairs={{0,1},{1,0},{2,3},{3,2},{4,5},{5,4},{6,7},{7,6},{8,9},{9,8},{10,11... | collective-permute-start | bytes 786440 | tf_op jit(solution)/shard_map/ppermute | solution.py:274
  23.6 3.4 %collective-permute-start.7 = (bf16[512,256]{1,0:T(8,128)(2,1)S(1)}, bf16[512,256]{1,0:T(8,128)(2,1)S(1)}, u32[]{:S(2)}, u32[]{:S(2)}) collective-permute-start(bf16[512,256]{1,0:T(8,128)(2,1)S(1)} %collective-permute-done.6.refs_2_), channel_id=1, source_target_pairs={{0,1},{1,0},{2,3},{3,2},{4,5},{5,4},{6,7},{7,6},{8,9},{9,8},{10,11... | collective-permute-start | bytes 786440 | tf_op jit(solution)/shard_map/ppermute | solution.py:274
  24.1 15.5 %collective-permute-start.9 = (bf16[128,1024]{1,0:T(8,128)(2,1)S(1)}, bf16[128,1024]{1,0:T(8,128)(2,1)S(1)}, u32[]{:S(2)}, u32[]{:S(2)}) collective-permute-start(bf16[128,1024]{1,0:T(8,128)(2,1)S(1)} %copy-done.2), channel_id=1, source_target_pairs={{0,16},{4,20},{8,24},{12,28},{16,0},{20,4},{24,8},{28,12},{1,17},{... | collective-permute-start | bytes 786440 | tf_op jit(solution)/shard_map/ppermute | solution.py:277
  28.7 10.9 %collective-permute-start.10 = (bf16[128,1024]{1,0:T(8,128)(2,1)S(1)}, bf16[128,1024]{1,0:T(8,128)(2,1)S(1)}, u32[]{:S(2)}, u32[]{:S(2)}) collective-permute-start(bf16[128,1024]{1,0:T(8,128)(2,1)S(1)} %get-tuple-element.52), channel_id=1, source_target_pairs={{0,4},{4,0},{8,12},{12,8},{16,20},{20,16},{24,28},{28,24},{1,5},{5... | collective-permute-start | bytes 786440 | tf_op jit(solution)/shard_map/ppermute | solution.py:277
  29.7 14.6 %collective-permute-start.8 = (bf16[32,384]{1,0:T(8,128)(2,1)S(1)}, bf16[32,384]{1,0:T(8,128)(2,1)S(1)}, u32[]{:S(2)}, u32[]{:S(2)}) collective-permute-start(bf16[32,384]{1,0:T(8,128)(2,1)S(1)} %get-tuple-element.49), channel_id=1, source_target_pairs={{0,4},{4,8},{8,12},{12,16},{16,20},{20,24},{24,28},{1,5},{5,9},{9,... | collective-permute-start | bytes 73736 | tf_op jit(solution)/shard_map/ppermute | solution.py:302
  32.7 11.6 %collective-permute-start.12 = (bf16[128,1024]{1,0:T(8,128)(2,1)S(1)}, bf16[128,1024]{1,0:T(8,128)(2,1)S(1)}, u32[]{:S(2)}, u32[]{:S(2)}) collective-permute-start(bf16[128,1024]{1,0:T(8,128)(2,1)S(1)} %collective-permute-done.3.refs_6_), channel_id=1, source_target_pairs={{0,4},{4,0},{8,12},{12,8},{16,20},{20,16},{24,28},{28,24},{1,5},{5... | collective-permute-start | bytes 786440 | tf_op jit(solution)/shard_map/ppermute | solution.py:277
  39.6 9.6 %collective-permute-start.11 = (bf16[128,1024]{1,0:T(8,128)(2,1)S(1)}, bf16[128,1024]{1,0:T(8,128)(2,1)S(1)}, u32[]{:S(2)}, u32[]{:S(2)}) collective-permute-start(bf16[128,1024]{1,0:T(8,128)(2,1)S(1)} %collective-permute-done.9.refs_4_), channel_id=1, source_target_pairs={{0,4},{4,0},{8,12},{12,8},{16,20},{20,16},{24,28},{28,24},{1,5},{5... | collective-permute-start | bytes 786440 | tf_op jit(solution)/shard_map/ppermute | solution.py:277
  40.6 11.1 %collective-permute-start.16 = (bf16[128,1024]{1,0:T(8,128)(2,1)S(1)}, bf16[128,1024]{1,0:T(8,128)(2,1)S(1)}, u32[]{:S(2)}, u32[]{:S(2)}) collective-permute-start(bf16[128,1024]{1,0:T(8,128)(2,1)S(1)} %add_convert_fusion.2), channel_id=1, source_target_pairs={{0,24},{4,28},{8,16},{12,20},{16,8},{20,12},{24,0},{28,4},{1,25},{... | collective-permute-start | bytes 786440 | tf_op jit(solution)/shard_map/ppermute | solution.py:277
  44.3 10.5 %collective-permute-start.13 = (bf16[128,1024]{1,0:T(8,128)(2,1)S(1)}, bf16[128,1024]{1,0:T(8,128)(2,1)S(1)}, u32[]{:S(2)}, u32[]{:S(2)}) collective-permute-start(bf16[128,1024]{1,0:T(8,128)(2,1)S(1)} %get-tuple-element.60), channel_id=1, source_target_pairs={{0,4},{4,0},{8,12},{12,8},{16,20},{20,16},{24,28},{28,24},{1,5},{5... | collective-permute-start | bytes 786440 | tf_op jit(solution)/shard_map/ppermute | solution.py:277
  51.7 8.0 %collective-permute-start.18 = (bf16[128,1024]{1,0:T(8,128)(2,1)S(1)}, bf16[128,1024]{1,0:T(8,128)(2,1)S(1)}, u32[]{:S(2)}, u32[]{:S(2)}) collective-permute-start(bf16[128,1024]{1,0:T(8,128)(2,1)S(1)} %get-tuple-element.70), channel_id=1, source_target_pairs={{0,4},{4,0},{8,12},{12,8},{16,20},{20,16},{24,28},{28,24},{1,5},{5... | collective-permute-start | bytes 786440 | tf_op jit(solution)/shard_map/ppermute | solution.py:277
  53.1 10.2 %collective-permute-start.14 = (bf16[528,256]{1,0:T(8,128)(2,1)S(1)}, bf16[528,256]{1,0:T(8,128)(2,1)S(1)}, u32[]{:S(2)}, u32[]{:S(2)}) collective-permute-start(bf16[528,256]{1,0:T(8,128)(2,1)S(1)} %get-tuple-element.61), channel_id=1, source_target_pairs={{0,2},{1,3},{2,0},{3,1},{4,6},{5,7},{6,4},{7,5},{8,10},{9,11},{10,... | collective-permute-start | bytes 811016 | tf_op jit(solution)/shard_map/ppermute | solution.py:274
  54.8 13.6 %collective-permute-start.17 = (bf16[128,1024]{1,0:T(8,128)(2,1)S(1)}, bf16[128,1024]{1,0:T(8,128)(2,1)S(1)}, u32[]{:S(2)}, u32[]{:S(2)}) collective-permute-start(bf16[128,1024]{1,0:T(8,128)(2,1)S(1)} %add_convert_fusion.1), channel_id=1, source_target_pairs={{0,16},{4,20},{8,24},{12,28},{16,0},{20,4},{24,8},{28,12},{1,17},{... | collective-permute-start | bytes 786440 | tf_op jit(solution)/shard_map/ppermute | solution.py:277
  57.4 8.6 %collective-permute-start.20 = (bf16[528,256]{1,0:T(8,128)(2,1)S(1)}, bf16[528,256]{1,0:T(8,128)(2,1)S(1)}, u32[]{:S(2)}, u32[]{:S(2)}) collective-permute-start(bf16[528,256]{1,0:T(8,128)(2,1)S(1)} %get-tuple-element.72), channel_id=1, source_target_pairs={{0,1},{1,0},{2,3},{3,2},{4,5},{5,4},{6,7},{7,6},{8,9},{9,8},{10,11... | collective-permute-start | bytes 811016 | tf_op jit(solution)/shard_map/ppermute | solution.py:274
  57.4 8.6 %collective-permute-start.21 = (bf16[528,256]{1,0:T(8,128)(2,1)S(1)}, bf16[528,256]{1,0:T(8,128)(2,1)S(1)}, u32[]{:S(2)}, u32[]{:S(2)}) collective-permute-start(bf16[528,256]{1,0:T(8,128)(2,1)S(1)} %get-tuple-element.73), channel_id=1, source_target_pairs={{0,3},{1,2},{2,1},{3,0},{4,7},{5,6},{6,5},{7,4},{8,11},{9,10},{10,... | collective-permute-start | bytes 811016 | tf_op jit(solution)/shard_map/ppermute | solution.py:274
  59.8 11.5 %collective-permute-start.19 = (bf16[128,1024]{1,0:T(8,128)(2,1)S(1)}, bf16[128,1024]{1,0:T(8,128)(2,1)S(1)}, u32[]{:S(2)}, u32[]{:S(2)}) collective-permute-start(bf16[128,1024]{1,0:T(8,128)(2,1)S(1)} %add_convert_fusion), channel_id=1, source_target_pairs={{0,8},{4,12},{8,0},{12,4},{16,24},{20,28},{24,16},{28,20},{1,9},{5... | collective-permute-start | bytes 786440 | tf_op jit(solution)/shard_map/ppermute | solution.py:277
  63.4 7.9 %collective-permute-start.15 = (bf16[128,1024]{1,0:T(8,128)(2,1)S(1)}, bf16[128,1024]{1,0:T(8,128)(2,1)S(1)}, u32[]{:S(2)}, u32[]{:S(2)}) collective-permute-start(bf16[128,1024]{1,0:T(8,128)(2,1)S(1)} %get-tuple-element.62), channel_id=1, source_target_pairs={{0,4},{4,0},{8,12},{12,8},{16,20},{20,16},{24,28},{28,24},{1,5},{5... | collective-permute-start | bytes 786440 | tf_op jit(solution)/shard_map/ppermute | solution.py:277
  (3 other events, 13.4 us)

commit v3 on v2

--- a/solution.py
+++ b/solution.py
@@ -82,36 +82,48 @@
 
 
 def load_kernel(hidden_hbm, start_hbm, grad_hbm,
-                back_ref, ahead_ref, hidden_ref, start_ref, rows_v, sem):
+                even_ref, odd_ref, hidden_ref, start_ref, rows_v, sem):
     pairs = [(start_hbm, start_ref), (hidden_hbm, hidden_ref)]
     copies = [pltpu.make_async_copy(*pair, sem.at[at]) for at, pair in enumerate(pairs)]
     for copy in copies:
         copy.start()
     bytes_, feats = hidden_ref.shape
     width = grad_hbm.shape[1]
+    is_odd = lax.rem(lax.axis_index("seq"), 2) == 1
     copies[0].wait()
     start = start_ref[...]
     last = jnp.sum(start) - 1
     group = pl.multiple_of((last // EDGE) * EDGE, EDGE)
     rows = pltpu.make_async_copy(grad_hbm.at[pl.ds(group, EDGE), :], rows_v, sem.at[2])
     rows.start()
-    back_ref[:, feats:] = jnp.broadcast_to(lead_mask(start), (EDGE, LANES)).astype(BF16)
-    ahead_ref[:EDGE, feats:] = jnp.broadcast_to(tail_mask(start), (EDGE, LANES)).astype(BF16)
+    lead = jnp.broadcast_to(lead_mask(start), (EDGE, LANES))
+    tail = jnp.broadcast_to(tail_mask(start), (EDGE, LANES))
+    even_ref[:EDGE, feats:] = jnp.where(is_odd, lead, tail).astype(BF16)
+    odd_ref[:EDGE, feats:] = jnp.where(is_odd, tail, lead).astype(BF16)
     copies[1].wait()
-    back_ref[:, :feats] = hidden_ref[:EDGE]
-    ahead_ref[:EDGE, :feats] = hidden_ref[bytes_ - EDGE :]
+    head = hidden_ref[:EDGE].astype(F32)
+    foot = hidden_ref[bytes_ - EDGE :].astype(F32)
+    even_ref[:EDGE, :feats] = jnp.where(is_odd, head, foot).astype(BF16)
+    odd_ref[:EDGE, :feats] = jnp.where(is_odd, foot, head).astype(BF16)
     rows.wait()
     chosen = iota((EDGE, width), 0) == last - group
     row = jnp.sum(jnp.where(chosen, rows_v[...].astype(F32), 0.0), axis=0, keepdims=True)
-    ahead_ref[EDGE:] = jnp.zeros((EDGE, feats + LANES), BF16)
+    spread = jnp.zeros((EDGE, feats), F32)
     for at in range(width // feats):
         piece = row[:, at * feats : (at + 1) * feats]
-        spread = jnp.where(iota((EDGE, feats), 0) == at, piece, 0.0)
-        old = ahead_ref[EDGE:, :feats].astype(F32)
-        ahead_ref[EDGE:, :feats] = (old + spread).astype(BF16)
-
-
-def pool_kernel(hidden_ref, next_ref, start_ref, query_ref, low_ref, pooled_ref, denom_ref):
+        spread = spread + jnp.where(iota((EDGE, feats), 0) == at, piece, 0.0)
+    for ref in (even_ref, odd_ref):
+        ref[EDGE:, :feats] = spread.astype(BF16)
+        ref[EDGE:, feats:] = jnp.zeros((EDGE, LANES), BF16)
+
+
+def halos(even_ref, odd_ref):
+    is_odd = lax.rem(lax.axis_index("seq"), 2) == 1
+    even, odd = even_ref[...].astype(F32), odd_ref[...].astype(F32)
+    return jnp.where(is_odd, odd, even), jnp.where(is_odd, even, odd)
+
+
+def pool_kernel(hidden_ref, even_ref, odd_ref, start_ref, query_ref, low_ref, pooled_ref, denom_ref):
     bytes_, feats = hidden_ref.shape
     slots = low_ref.shape[0]
     query = row_of(query_ref)
@@ -122,8 +134,8 @@
     _, weight = scores(hidden, query)
     numer = dot_split(onehot, weight * hidden)
     denom = dot_split(onehot, weight)
-    following = next_ref[:, :feats].astype(F32)
-    mask = next_ref[:, feats : feats + 1].astype(F32)
+    halo, _ = halos(even_ref, odd_ref)
+    following, mask = halo[:EDGE, :feats], halo[:EDGE, feats : feats + 1]
     extra = scores(following, query)[1] * mask
     is_last = iota((slots, feats), 0) == last.astype(jnp.int32)
     denom = denom + jnp.where(is_last, jnp.sum(extra, axis=0, keepdims=True), 0.0)
@@ -135,7 +147,7 @@
     denom_ref[...] = denom
 
 
-def spread_kernel(hidden_ref, prev_ref, start_ref, query_ref, pooled_ref, denom_ref,
+def spread_kernel(hidden_ref, even_ref, odd_ref, start_ref, query_ref, pooled_ref, denom_ref,
                   onehot_ref, share_ref, delta_ref, slope_ref):
     bytes_, feats = hidden_ref.shape
     slots = pooled_ref.shape[0]
@@ -153,8 +165,9 @@
     onehot_ref[...] = onehot
     hidden = hidden_ref[...].astype(F32)
     bent, weight = scores(hidden, query)
-    before = prev_ref[:EDGE, :feats].astype(F32)
-    part = scores(before, query)[1] * prev_ref[:EDGE, feats : feats + 1].astype(F32)
+    _, halo = halos(even_ref, odd_ref)
+    before = halo[:EDGE, :feats]
+    part = scores(before, query)[1] * halo[:EDGE, feats : feats + 1]
     lead = lead_mask(start_ref[...])
     own = weight[:EDGE] * lead
     first_denom = jnp.sum(part + own, axis=0, keepdims=True)
@@ -216,7 +229,7 @@
     out_ref[...] = dot(full_ref[...], weight_ref[...]).astype(BF16)
 
 
-def partial_kernel(parts, grad_ref, prev_ref, *refs):
+def partial_kernel(parts, grad_ref, even_ref, odd_ref, *refs):
     piece_refs, out_refs, full_ref = refs[: -parts - 1], refs[-parts - 1 : -1], refs[-1]
     slots, width = grad_ref.shape
     feats = out_refs[0].shape[1]
@@ -228,7 +241,7 @@
         for index, ref in enumerate(piece_refs):
             owner = pl.multiple_of((spot ^ index) * rows, rows)
             full_ref[pl.ds(owner, rows), :] = ref[...]
-    last = prev_ref[EDGE:, :feats].astype(F32)
+    last = halos(even_ref, odd_ref)[1][EDGE:, :feats]
     row = jnp.concatenate([last[at : at + 1] for at in range(width // feats)], axis=1)
     row = jnp.where(iota((EDGE, width), 0) == 0, row, 0.0).astype(BF16)
     place = lax.axis_index("mp")
@@ -282,10 +295,10 @@
         latent_grad,
     )
     query = pool_query.reshape(feats // LANES, LANES)
-    back, ahead, byte_hidden, start = call(
+    even, odd, byte_hidden, start = call(
         load_kernel,
         (
-            shape((EDGE, feats + LANES), BF16),
+            shape((2 * EDGE, feats + LANES), BF16),
             shape((2 * EDGE, feats + LANES), BF16),
             shape(byte_hidden.shape, BF16),
             shape(arguments[1].shape, jnp.int32),
@@ -298,15 +311,17 @@
             pltpu.SemaphoreType.DMA((len(arguments),)),
         ),
     )
-    following = lax.ppermute(back, "seq", [(i, i - 1) for i in range(1, n_seq)])
-    previous = lax.ppermute(ahead, "seq", [(i, i + 1) for i in range(n_seq - 1)])
+    in_weight, _ = after((in_weight, even))
+    even = trade(even, 1)
+    inner = [(i, i + 1) for i in range(1, n_seq - 1, 2)]
+    odd = lax.ppermute(odd, "seq", inner + [(j, i) for i, j in inner])
 
     if staged:
-        in_weight, _ = after((in_weight, back))
         pieces = [in_weight] + [None] * (n_seq - 1)
-        pieces[1] = trade(in_weight, 1)
+        pieces[1] = trade(after((in_weight, even))[0], 1)
         for step in range(2, n_seq, 2):
-            pieces[step] = trade(in_weight, step)
+            source = in_weight if step == 4 else after((in_weight, odd))[0]
+            pieces[step] = trade(source, step)
     else:
         pieces = [lax.all_gather(in_weight, "seq", axis=0, tiled=True)]
 
@@ -314,15 +329,16 @@
         pool_kernel,
         (shape((slots, feats), BF16), shape((slots, feats), F32), shape((slots, feats), F32)),
         byte_hidden,
-        following,
+        even,
+        odd,
         start,
         query,
         flops=8 * bytes_ * slots * feats,
     )
 
     if staged:
-        low, *pieces[1:3] = after((low, *pieces[1:3]))
-        pieces[3] = trade(after((pieces[2], low))[0], 1)
+        low, pieces[2] = after((low, pieces[2]))
+        pieces[3] = trade(after((pieces[2], pieces[1]))[0], 1)
     parts = [low]
     for step in reversed([1 << bit for bit in range(n_mp.bit_length() - 1)]):
         if staged and step == 1:
@@ -332,7 +348,8 @@
         spread_kernel,
         (shape((bytes_, slots), BF16),) + (shape((bytes_, feats), F32),) * 3,
         byte_hidden,
-        previous,
+        even,
+        odd,
         start,
         query,
         pooled,
@@ -358,13 +375,14 @@
         fetched[7] = trade(terms[7], 1)
         pieces[7] = trade(after((pieces[6], terms[0]))[0], 1)
         pieces[5] = trade(after((pieces[4], fetched[7]))[0], 1)
-        fetched[5] = trade(after((terms[5], pieces[7], previous))[0], 1)
+        fetched[5] = trade(after((terms[5], pieces[7]))[0], 1)
 
     *partials, weight_full = call(
         functools.partial(partial_kernel, n_mp),
         (shape((slots + EDGE, feats), BF16),) * n_mp + (shape((latent_dim, width), BF16),),
         latent_grad,
-        previous,
+        even,
+        odd,
         *pieces,
         flops=work,
     )

time: 73.1 us -> 76.8 us (1.051)
  waiting for transfers between devices: 16.6 us -> 20 us
    ppermute x14 -> x15, starting transfers between devices: 30.2 us -> 34.3 us  [trade(): return lax.ppermute(value, 'seq', [(i, i ^ step) for i in range(n_seq)])]
    ppermute x2 -> x1, starting transfers between devices: 4.28 us -> 0.66 us  [shards(): odd = lax.ppermute(odd, 'seq', inner + [(j, i) for i, j in inner])]
    ppermute x14 -> x15, waiting for transfers between devices: 15.7 us -> 18.3 us  [trade(): return lax.ppermute(value, 'seq', [(i, i ^ step) for i in range(n_seq)])]
    ppermute x6, waiting for transfers between devices: 0.09 us -> 1.7 us  [swap(): return lax.ppermute(value, 'mp', [(i, i ^ step) for i in range(n_mp)])]
  transfers between devices with their start and end apart: 22 -> 22, of which waited for: 10 -> 8; matrix products, arithmetic and copies ran while one was open for 0% -> 0% of each run, Pallas kernels for 18% -> 17%
where the time goes in v3:
time: 76.8 us; the launch traced here: 75.7 us
  starting transfers between devices  38.6 us (50%)
  waiting for transfers between devices  20 us (26%)
  Pallas kernels  13.7 us (18%)
  local copies, waits for them, and re-layouts  1.45 us (2%)
  other arithmetic  1.16 us (2%)
    ppermute x15, starting transfers between devices, trade(): return lax.ppermute(value, 'seq', [(i, i ^ step) for i in range(n_seq)])  34.3 us
    ppermute x15, waiting for transfers between devices, trade(): return lax.ppermute(value, 'seq', [(i, i ^ step) for i in range(n_seq)])  18.3 us
    pallas_call x7, Pallas kernels, call(): pl.pallas_call(kernel, out_shape=out_shape, in_specs=in_specs, out_specs=...  13.7 us
    ppermute x6, starting transfers between devices, swap(): return lax.ppermute(value, 'mp', [(i, i ^ step) for i in range(n_mp)])  3.63 us
    ppermute x6, waiting for transfers between devices, swap(): return lax.ppermute(value, 'mp', [(i, i ^ step) for i in range(n_mp)])  1.7 us
  transfers between devices with their start and end apart: 22, of which 8 were waited for; matrix products, arithmetic and copies ran while one was open for 0% of the time, Pallas kernels for 17%

profile of v3, /device:TPU:0, one launch (start us, length us, event | category | flops | bytes accessed | tf_op | source)
XLA Modules:
  0.0 75.7 jit_solution(2376042572604427460)
XLA Ops:
  3.2 5.8 %collective-permute-start = (bf16[32,384]{1,0:T(8,128)(2,1)S(1)}, bf16[32,384]{1,0:T(8,128)(2,1)S(1)}, u32[]{:S(2)}, u32[]{:S(2)}) collective-permute-start(bf16[32,384]{1,0:T(8,128)(2,1)S(1)} %get-tuple-element.42), channel_id=1, source_target_pairs={{0,4},{4,0},{8,12},{12,8},{16,20},{20,16},{24,28},{28,24},{1,5},{5... | collective-permute-start | bytes 73736 | tf_op jit(solution)/shard_map/ppermute | solution.py:290
  9.0 3.2 %collective-permute-start.2 = (bf16[128,1024]{1,0:T(8,128)(2,1)}, bf16[128,1024]{1,0:T(8,128)(2,1)S(1)}, u32[]{:S(2)}, u32[]{:S(2)}) collective-permute-start(bf16[128,1024]{1,0:T(8,128)(2,1)} %refs_0_), channel_id=1, source_target_pairs={{0,8},{4,12},{8,0},{12,4},{16,24},{20,28},{24,16},{28,20},{1,9},{5... | collective-permute-start | bytes 786440 | tf_op jit(solution)/shard_map/ppermute | solution.py:290
  12.2 1.5 %collective-permute-start.4 = (bf16[128,1024]{1,0:T(8,128)(2,1)}, bf16[128,1024]{1,0:T(8,128)(2,1)S(1)}, u32[]{:S(2)}, u32[]{:S(2)}) collective-permute-start(bf16[128,1024]{1,0:T(8,128)(2,1)} %refs_0_), channel_id=1, source_target_pairs={{0,4},{4,0},{8,12},{12,8},{16,20},{20,16},{24,28},{28,24},{1,5},{5... | collective-permute-start | bytes 786440 | tf_op jit(solution)/shard_map/ppermute | solution.py:290
  13.7 2.5 %collective-permute-start.3 = (bf16[128,1024]{1,0:T(8,128)(2,1)}, bf16[128,1024]{1,0:T(8,128)(2,1)S(1)}, u32[]{:S(2)}, u32[]{:S(2)}) collective-permute-start(bf16[128,1024]{1,0:T(8,128)(2,1)} %refs_0_), channel_id=1, source_target_pairs={{0,24},{4,28},{8,16},{12,20},{16,8},{20,12},{24,0},{28,4},{1,25},{... | collective-permute-start | bytes 786440 | tf_op jit(solution)/shard_map/ppermute | solution.py:290
  16.8 2.1 %shard_map.77 = (bf16[512,256]{1,0:T(8,128)(2,1)S(1)}, f32[512,256]{1,0:T(8,128)S(1)}, f32[512,256]{1,0:T(8,128)S(1)}) custom-call(bf16[1024,256]{1,0:T(8,128)(2,1)S(1)} %get-tuple-element.41.hidden_ref, bf16[32,384]{1,0:T(8,128)(2,1)S(1)} %collective-permute-done.even_ref, bf16[32,384]{1,0:T(8,128)(2,1)S(1)} %collective-permute-done.1.odd_ref, ...), custom_call_target="tpu_custom_call" | custom-call | tf_op jit(solution)/shard_map/pallas_call | solution.py:258
  19.1 1.7 %collective-permute-start.5 = (bf16[128,1024]{1,0:T(8,128)(2,1)S(1)}, bf16[128,1024]{1,0:T(8,128)(2,1)S(1)}, u32[]{:S(2)}, u32[]{:S(2)}) collective-permute-start(bf16[128,1024]{1,0:T(8,128)(2,1)S(1)} %collective-permute-done.2.refs_2_), channel_id=1, source_target_pairs={{0,4},{4,0},{8,12},{12,8},{16,20},{20,16},{24,28},{28,24},{1,5},{5... | collective-permute-start | bytes 786440 | tf_op jit(solution)/shard_map/ppermute | solution.py:290
  20.8 1.5 %collective-permute-start.7 = (bf16[512,256]{1,0:T(8,128)(2,1)S(1)}, bf16[512,256]{1,0:T(8,128)(2,1)S(1)}, u32[]{:S(2)}, u32[]{:S(2)}) collective-permute-start(bf16[512,256]{1,0:T(8,128)(2,1)S(1)} %get-tuple-element.52.refs_0_), channel_id=1, source_target_pairs={{0,2},{1,3},{2,0},{3,1},{4,6},{5,7},{6,4},{7,5},{8,10},{9,11},{10,... | collective-permute-start | bytes 786440 | tf_op jit(solution)/shard_map/ppermute | solution.py:287
  22.3 3.2 %collective-permute-done.3.refs_6_ = bf16[128,1024]{1,0:T(8,128)(2,1)S(1)} collective-permute-done((bf16[128,1024]{1,0:T(8,128)(2,1)}, bf16[128,1024]{1,0:T(8,128)(2,1)S(1)}, u32[]{:S(2)}, u32[]{:S(2)}) %collective-permute-start.3) | collective-permute-done | bytes 262176 | tf_op jit(solution)/shard_map/ppermute | solution.py:290
  25.5 1.7 %collective-permute-done.7.refs_2_ = bf16[512,256]{1,0:T(8,128)(2,1)S(1)} collective-permute-done((bf16[512,256]{1,0:T(8,128)(2,1)S(1)}, bf16[512,256]{1,0:T(8,128)(2,1)S(1)}, u32[]{:S(2)}, u32[]{:S(2)}) %collective-permute-start.7) | collective-permute-done | bytes 262176 | tf_op jit(solution)/shard_map/ppermute | solution.py:287
  27.2 3.4 %collective-permute-start.9 = (bf16[128,1024]{1,0:T(8,128)(2,1)S(1)}, bf16[128,1024]{1,0:T(8,128)(2,1)S(1)}, u32[]{:S(2)}, u32[]{:S(2)}) collective-permute-start(bf16[128,1024]{1,0:T(8,128)(2,1)S(1)} %copy-done.2), channel_id=1, source_target_pairs={{0,16},{4,20},{8,24},{12,28},{16,0},{20,4},{24,8},{28,12},{1,17},{... | collective-permute-start | bytes 786440 | tf_op jit(solution)/shard_map/ppermute | solution.py:290
  30.6 1.7 %shard_map.78 = (f32[128,1024]{1,0:T(8,128)S(1)}, bf16[128,1024]{1,0:T(8,128)(2,1)S(1)}, f32[128,1024]{1,0:T(8,128)S(1)}, bf16[128,1024]{1,0:T(8,128)(2,1)S(1)},...) custom-call(bf16[512,256]{1,0:T(8,128)(2,1)S(1)} %get-tuple-element., ...), custom_call_target="tpu_custom_call" | custom-call | tf_op jit(solution)/shard_map/pallas_call | solution.py:258
  32.9 1.5 %collective-permute-start.12 = (bf16[128,1024]{1,0:T(8,128)(2,1)S(1)}, bf16[128,1024]{1,0:T(8,128)(2,1)S(1)}, u32[]{:S(2)}, u32[]{:S(2)}) collective-permute-start(bf16[128,1024]{1,0:T(8,128)(2,1)S(1)} %collective-permute-done.3.refs_6_), channel_id=1, source_target_pairs={{0,4},{4,0},{8,12},{12,8},{16,20},{20,16},{24,28},{28,24},{1,5},{5... | collective-permute-start | bytes 786440 | tf_op jit(solution)/shard_map/ppermute | solution.py:290
  34.4 8.8 %collective-permute-done.9.refs_4_ = bf16[128,1024]{1,0:T(8,128)(2,1)S(1)} collective-permute-done((bf16[128,1024]{1,0:T(8,128)(2,1)S(1)}, bf16[128,1024]{1,0:T(8,128)(2,1)S(1)}, u32[]{:S(2)}, u32[]{:S(2)}) %collective-permute-start.9) | collective-permute-done | bytes 262176 | tf_op jit(solution)/shard_map/ppermute | solution.py:290
  43.7 4.2 %collective-permute-start.16 = (bf16[128,1024]{1,0:T(8,128)(2,1)S(1)}, bf16[128,1024]{1,0:T(8,128)(2,1)S(1)}, u32[]{:S(2)}, u32[]{:S(2)}) collective-permute-start(bf16[128,1024]{1,0:T(8,128)(2,1)S(1)} %add_convert_fusion.2), channel_id=1, source_target_pairs={{0,24},{4,28},{8,16},{12,20},{16,8},{20,12},{24,0},{28,4},{1,25},{... | collective-permute-start | bytes 786440 | tf_op jit(solution)/shard_map/ppermute | solution.py:290
  48.8 1.7 %shard_map.81 = (bf16[1024,512]{1,0:T(8,128)(2,1)S(1)}, f32[1024,256]{1,0:T(8,128)S(1)}, f32[1024,256]{1,0:T(8,128)S(1)}, f32[1024,256]{1,0:T(8,128)S(1)}) custom-call(bf16[1024,256]{1,0:T(8,128)(2,1)S(1)} %get-tuple-element.41.hidden_ref, bf16[32,384]{1,0:T(8,128)(2,1)S(1)} %collective-permute-done.even_ref, ...), custom_call_target="tpu_custom_call" | custom-call | tf_op jit(solution)/shard_map/pallas_call | solution.py:258
  50.6 2.1 %collective-permute-done.11.refs_5_ = bf16[128,1024]{1,0:T(8,128)(2,1)S(1)} collective-permute-done((bf16[128,1024]{1,0:T(8,128)(2,1)S(1)}, bf16[128,1024]{1,0:T(8,128)(2,1)S(1)}, u32[]{:S(2)}, u32[]{:S(2)}) %collective-permute-start.11) | collective-permute-done | bytes 262176 | tf_op jit(solution)/shard_map/ppermute | solution.py:290
  52.7 2.5 %shard_map.79 = (bf16[528,256]{1,0:T(8,128)(2,1)S(1)}, bf16[528,256]{1,0:T(8,128)(2,1)S(1)}, bf16[528,256]{1,0:T(8,128)(2,1)S(1)}, bf16[528,256]{1,0:T(8,128)(2,1)S(1)}, bf16[1024,1024]{1,0:T(8,128)(2,1)}) custom-call(bf16[512,1024]{1,0:T(8,128)(2,1)S(1)} %copy-done, bf16[32,384]{1,0:T(8,128)(2,1)S(1)} %collective-permute-done.even_ref, ...), custom_call_target="tpu_custom_call" | custom-call | tf_op jit(solution)/shard_map/pallas_call | solution.py:258
  55.8 1.5 %collective-permute-start.14 = (bf16[528,256]{1,0:T(8,128)(2,1)S(1)}, bf16[528,256]{1,0:T(8,128)(2,1)S(1)}, u32[]{:S(2)}, u32[]{:S(2)}) collective-permute-start(bf16[528,256]{1,0:T(8,128)(2,1)S(1)} %get-tuple-element.63), channel_id=1, source_target_pairs={{0,2},{1,3},{2,0},{3,1},{4,6},{5,7},{6,4},{7,5},{8,10},{9,11},{10,... | collective-permute-start | bytes 811016 | tf_op jit(solution)/shard_map/ppermute | solution.py:287
  58.4 2.5 %collective-permute-start.17 = (bf16[128,1024]{1,0:T(8,128)(2,1)S(1)}, bf16[128,1024]{1,0:T(8,128)(2,1)S(1)}, u32[]{:S(2)}, u32[]{:S(2)}) collective-permute-start(bf16[128,1024]{1,0:T(8,128)(2,1)S(1)} %add_convert_fusion.1), channel_id=1, source_target_pairs={{0,16},{4,20},{8,24},{12,28},{16,0},{20,4},{24,8},{28,12},{1,17},{... | collective-permute-start | bytes 786440 | tf_op jit(solution)/shard_map/ppermute | solution.py:290
  61.6 1.6 %collective-permute-done.18 = bf16[128,1024]{1,0:T(8,128)(2,1)S(1)} collective-permute-done((bf16[128,1024]{1,0:T(8,128)(2,1)S(1)}, bf16[128,1024]{1,0:T(8,128)(2,1)S(1)}, u32[]{:S(2)}, u32[]{:S(2)}) %collective-permute-start.18) | collective-permute-done | bytes 262176 | tf_op jit(solution)/shard_map/ppermute | solution.py:290
  63.3 3.7 %collective-permute-start.19 = (bf16[128,1024]{1,0:T(8,128)(2,1)S(1)}, bf16[128,1024]{1,0:T(8,128)(2,1)S(1)}, u32[]{:S(2)}, u32[]{:S(2)}) collective-permute-start(bf16[128,1024]{1,0:T(8,128)(2,1)S(1)} %add_convert_fusion), channel_id=1, source_target_pairs={{0,8},{4,12},{8,0},{12,4},{16,24},{20,28},{24,16},{28,20},{1,9},{5... | collective-permute-start | bytes 786440 | tf_op jit(solution)/shard_map/ppermute | solution.py:290
  67.0 1.7 %collective-permute-start.15 = (bf16[128,1024]{1,0:T(8,128)(2,1)S(1)}, bf16[128,1024]{1,0:T(8,128)(2,1)S(1)}, u32[]{:S(2)}, u32[]{:S(2)}) collective-permute-start(bf16[128,1024]{1,0:T(8,128)(2,1)S(1)} %get-tuple-element.64), channel_id=1, source_target_pairs={{0,4},{4,0},{8,12},{12,8},{16,20},{20,16},{24,28},{28,24},{1,5},{5... | collective-permute-start | bytes 786440 | tf_op jit(solution)/shard_map/ppermute | solution.py:290
  68.7 2.4 %shard_map.80 = bf16[512,1024]{1,0:T(8,128)(2,1)} custom-call(bf16[512,256]{1,0:T(8,128)(2,1)S(1)} %get-tuple-element.52.refs_0_, bf16[512,256]{1,0:T(8,128)(2,1)S(1)} %collective-permute-done.6.refs_1_, bf16[512,256]{1,0:T(8,128)(2,1)S(1)} %collective-permute-done.7.refs_2_, bf16[512,256]{1,0:T(8,128)(2,1)S(1)} %collective-permute-done.8.refs_3_, ...), custom_call_target="tpu_custom_call" | custom-call | tf_op jit(solution)/shard_map/pallas_call | solution.py:258
  71.1 2.3 %shard_map.82 = bf16[1024,256]{1,0:T(8,128)(2,1)} custom-call(bf16[528,256]{1,0:T(8,128)(2,1)S(1)} %get-tuple-element.73.refs_0_, bf16[528,256]{1,0:T(8,128)(2,1)S(1)} %collective-permute-done.20.refs_1_, bf16[528,256]{1,0:T(8,128)(2,1)S(1)} %collective-permute-done.14.refs_2_, bf16[528,256]{1,0:T(8,128)(2,1)S(1)} %collective-permute-done.21.refs_3_, ...), custom_call_target="tpu_custom_call" | custom-call | tf_op jit(solution)/shard_map/pallas_call | solution.py:258
  (41 shorter events, 10.2 us)
Async XLA Ops:
  0.6 29.9 %copy-start = (bf16[512,1024]{1,0:T(8,128)(2,1)S(1)}, bf16[512,1024]{1,0:T(8,128)(2,1)}, u32[]{:S(2)}) copy-start(bf16[512,1024]{1,0:T(8,128)(2,1)} %grad_ref.1) | copy-start | bytes 3145732
  0.6 26.5 %copy-start.2 = (bf16[128,1024]{1,0:T(8,128)(2,1)S(1)}, bf16[128,1024]{1,0:T(8,128)(2,1)}, u32[]{:S(2)}) copy-start(bf16[128,1024]{1,0:T(8,128)(2,1)} %refs_0_) | copy-start | bytes 786436
  2.5 6.5 %collective-permute-start.1 = (bf16[32,384]{1,0:T(8,128)(2,1)S(1)}, bf16[32,384]{1,0:T(8,128)(2,1)S(1)}, u32[]{:S(2)}, u32[]{:S(2)}) collective-permute-start(bf16[32,384]{1,0:T(8,128)(2,1)S(1)} %get-tuple-element.43), channel_id=1, source_target_pairs={{4,8},{12,16},{20,24},{8,4},{16,12},{24,20},{5,9},{13,17},{21,25},... | collective-permute-start | bytes 73736 | tf_op jit(solution)/shard_map/ppermute | solution.py:317
  3.2 9.0 %collective-permute-start = (bf16[32,384]{1,0:T(8,128)(2,1)S(1)}, bf16[32,384]{1,0:T(8,128)(2,1)S(1)}, u32[]{:S(2)}, u32[]{:S(2)}) collective-permute-start(bf16[32,384]{1,0:T(8,128)(2,1)S(1)} %get-tuple-element.42), channel_id=1, source_target_pairs={{0,4},{4,0},{8,12},{12,8},{16,20},{20,16},{24,28},{28,24},{1,5},{5... | collective-permute-start | bytes 73736 | tf_op jit(solution)/shard_map/ppermute | solution.py:290
  9.0 10.1 %collective-permute-start.2 = (bf16[128,1024]{1,0:T(8,128)(2,1)}, bf16[128,1024]{1,0:T(8,128)(2,1)S(1)}, u32[]{:S(2)}, u32[]{:S(2)}) collective-permute-start(bf16[128,1024]{1,0:T(8,128)(2,1)} %refs_0_), channel_id=1, source_target_pairs={{0,8},{4,12},{8,0},{12,4},{16,24},{20,28},{24,16},{28,20},{1,9},{5... | collective-permute-start | bytes 786440 | tf_op jit(solution)/shard_map/ppermute | solution.py:290
  12.2 6.9 %collective-permute-start.4 = (bf16[128,1024]{1,0:T(8,128)(2,1)}, bf16[128,1024]{1,0:T(8,128)(2,1)S(1)}, u32[]{:S(2)}, u32[]{:S(2)}) collective-permute-start(bf16[128,1024]{1,0:T(8,128)(2,1)} %refs_0_), channel_id=1, source_target_pairs={{0,4},{4,0},{8,12},{12,8},{16,20},{20,16},{24,28},{28,24},{1,5},{5... | collective-permute-start | bytes 786440 | tf_op jit(solution)/shard_map/ppermute | solution.py:290
  13.7 11.8 %collective-permute-start.3 = (bf16[128,1024]{1,0:T(8,128)(2,1)}, bf16[128,1024]{1,0:T(8,128)(2,1)S(1)}, u32[]{:S(2)}, u32[]{:S(2)}) collective-permute-start(bf16[128,1024]{1,0:T(8,128)(2,1)} %refs_0_), channel_id=1, source_target_pairs={{0,24},{4,28},{8,16},{12,20},{16,8},{20,12},{24,0},{28,4},{1,25},{... | collective-permute-start | bytes 786440 | tf_op jit(solution)/shard_map/ppermute | solution.py:290
  19.1 6.4 %collective-permute-start.5 = (bf16[128,1024]{1,0:T(8,128)(2,1)S(1)}, bf16[128,1024]{1,0:T(8,128)(2,1)S(1)}, u32[]{:S(2)}, u32[]{:S(2)}) collective-permute-start(bf16[128,1024]{1,0:T(8,128)(2,1)S(1)} %collective-permute-done.2.refs_2_), channel_id=1, source_target_pairs={{0,4},{4,0},{8,12},{12,8},{16,20},{20,16},{24,28},{28,24},{1,5},{5... | collective-permute-start | bytes 786440 | tf_op jit(solution)/shard_map/ppermute | solution.py:290
  20.8 6.4 %collective-permute-start.7 = (bf16[512,256]{1,0:T(8,128)(2,1)S(1)}, bf16[512,256]{1,0:T(8,128)(2,1)S(1)}, u32[]{:S(2)}, u32[]{:S(2)}) collective-permute-start(bf16[512,256]{1,0:T(8,128)(2,1)S(1)} %get-tuple-element.52.refs_0_), channel_id=1, source_target_pairs={{0,2},{1,3},{2,0},{3,1},{4,6},{5,7},{6,4},{7,5},{8,10},{9,11},{10,... | collective-permute-start | bytes 786440 | tf_op jit(solution)/shard_map/ppermute | solution.py:287
  25.5 5.1 %collective-permute-start.6 = (bf16[512,256]{1,0:T(8,128)(2,1)S(1)}, bf16[512,256]{1,0:T(8,128)(2,1)S(1)}, u32[]{:S(2)}, u32[]{:S(2)}) collective-permute-start(bf16[512,256]{1,0:T(8,128)(2,1)S(1)} %get-tuple-element.52.refs_0_), channel_id=1, source_target_pairs={{0,1},{1,0},{2,3},{3,2},{4,5},{5,4},{6,7},{7,6},{8,9},{9,8},{10,11... | collective-permute-start | bytes 786440 | tf_op jit(solution)/shard_map/ppermute | solution.py:287
  27.2 3.4 %collective-permute-start.8 = (bf16[512,256]{1,0:T(8,128)(2,1)S(1)}, bf16[512,256]{1,0:T(8,128)(2,1)S(1)}, u32[]{:S(2)}, u32[]{:S(2)}) collective-permute-start(bf16[512,256]{1,0:T(8,128)(2,1)S(1)} %collective-permute-done.7.refs_2_), channel_id=1, source_target_pairs={{0,1},{1,0},{2,3},{3,2},{4,5},{5,4},{6,7},{7,6},{8,9},{9,8},{10,11... | collective-permute-start | bytes 786440 | tf_op jit(solution)/shard_map/ppermute | solution.py:287
  27.2 16.0 %collective-permute-start.9 = (bf16[128,1024]{1,0:T(8,128)(2,1)S(1)}, bf16[128,1024]{1,0:T(8,128)(2,1)S(1)}, u32[]{:S(2)}, u32[]{:S(2)}) collective-permute-start(bf16[128,1024]{1,0:T(8,128)(2,1)S(1)} %copy-done.2), channel_id=1, source_target_pairs={{0,16},{4,20},{8,24},{12,28},{16,0},{20,4},{24,8},{28,12},{1,17},{... | collective-permute-start | bytes 786440 | tf_op jit(solution)/shard_map/ppermute | solution.py:290
  32.3 10.9 %collective-permute-start.10 = (bf16[128,1024]{1,0:T(8,128)(2,1)S(1)}, bf16[128,1024]{1,0:T(8,128)(2,1)S(1)}, u32[]{:S(2)}, u32[]{:S(2)}) collective-permute-start(bf16[128,1024]{1,0:T(8,128)(2,1)S(1)} %get-tuple-element.54), channel_id=1, source_target_pairs={{0,4},{4,0},{8,12},{12,8},{16,20},{20,16},{24,28},{28,24},{1,5},{5... | collective-permute-start | bytes 786440 | tf_op jit(solution)/shard_map/ppermute | solution.py:290
  32.9 15.1 %collective-permute-start.12 = (bf16[128,1024]{1,0:T(8,128)(2,1)S(1)}, bf16[128,1024]{1,0:T(8,128)(2,1)S(1)}, u32[]{:S(2)}, u32[]{:S(2)}) collective-permute-start(bf16[128,1024]{1,0:T(8,128)(2,1)S(1)} %collective-permute-done.3.refs_6_), channel_id=1, source_target_pairs={{0,4},{4,0},{8,12},{12,8},{16,20},{20,16},{24,28},{28,24},{1,5},{5... | collective-permute-start | bytes 786440 | tf_op jit(solution)/shard_map/ppermute | solution.py:290
  43.2 9.6 %collective-permute-start.11 = (bf16[128,1024]{1,0:T(8,128)(2,1)S(1)}, bf16[128,1024]{1,0:T(8,128)(2,1)S(1)}, u32[]{:S(2)}, u32[]{:S(2)}) collective-permute-start(bf16[128,1024]{1,0:T(8,128)(2,1)S(1)} %collective-permute-done.9.refs_4_), channel_id=1, source_target_pairs={{0,4},{4,0},{8,12},{12,8},{16,20},{20,16},{24,28},{28,24},{1,5},{5... | collective-permute-start | bytes 786440 | tf_op jit(solution)/shard_map/ppermute | solution.py:290
  43.7 11.5 %collective-permute-start.16 = (bf16[128,1024]{1,0:T(8,128)(2,1)S(1)}, bf16[128,1024]{1,0:T(8,128)(2,1)S(1)}, u32[]{:S(2)}, u32[]{:S(2)}) collective-permute-start(bf16[128,1024]{1,0:T(8,128)(2,1)S(1)} %add_convert_fusion.2), channel_id=1, source_target_pairs={{0,24},{4,28},{8,16},{12,20},{16,8},{20,12},{24,0},{28,4},{1,25},{... | collective-permute-start | bytes 786440 | tf_op jit(solution)/shard_map/ppermute | solution.py:290
  47.9 10.4 %collective-permute-start.13 = (bf16[128,1024]{1,0:T(8,128)(2,1)S(1)}, bf16[128,1024]{1,0:T(8,128)(2,1)S(1)}, u32[]{:S(2)}, u32[]{:S(2)}) collective-permute-start(bf16[128,1024]{1,0:T(8,128)(2,1)S(1)} %get-tuple-element.62), channel_id=1, source_target_pairs={{0,4},{4,0},{8,12},{12,8},{16,20},{20,16},{24,28},{28,24},{1,5},{5... | collective-permute-start | bytes 786440 | tf_op jit(solution)/shard_map/ppermute | solution.py:290
  55.2 8.0 %collective-permute-start.18 = (bf16[128,1024]{1,0:T(8,128)(2,1)S(1)}, bf16[128,1024]{1,0:T(8,128)(2,1)S(1)}, u32[]{:S(2)}, u32[]{:S(2)}) collective-permute-start(bf16[128,1024]{1,0:T(8,128)(2,1)S(1)} %get-tuple-element.72), channel_id=1, source_target_pairs={{0,4},{4,0},{8,12},{12,8},{16,20},{20,16},{24,28},{28,24},{1,5},{5... | collective-permute-start | bytes 786440 | tf_op jit(solution)/shard_map/ppermute | solution.py:290
  55.8 11.2 %collective-permute-start.14 = (bf16[528,256]{1,0:T(8,128)(2,1)S(1)}, bf16[528,256]{1,0:T(8,128)(2,1)S(1)}, u32[]{:S(2)}, u32[]{:S(2)}) collective-permute-start(bf16[528,256]{1,0:T(8,128)(2,1)S(1)} %get-tuple-element.63), channel_id=1, source_target_pairs={{0,2},{1,3},{2,0},{3,1},{4,6},{5,7},{6,4},{7,5},{8,10},{9,11},{10,... | collective-permute-start | bytes 811016 | tf_op jit(solution)/shard_map/ppermute | solution.py:287
  58.4 14.9 %collective-permute-start.17 = (bf16[128,1024]{1,0:T(8,128)(2,1)S(1)}, bf16[128,1024]{1,0:T(8,128)(2,1)S(1)}, u32[]{:S(2)}, u32[]{:S(2)}) collective-permute-start(bf16[128,1024]{1,0:T(8,128)(2,1)S(1)} %add_convert_fusion.1), channel_id=1, source_target_pairs={{0,16},{4,20},{8,24},{12,28},{16,0},{20,4},{24,8},{28,12},{1,17},{... | collective-permute-start | bytes 786440 | tf_op jit(solution)/shard_map/ppermute | solution.py:290
  61.0 10.1 %collective-permute-start.20 = (bf16[528,256]{1,0:T(8,128)(2,1)S(1)}, bf16[528,256]{1,0:T(8,128)(2,1)S(1)}, u32[]{:S(2)}, u32[]{:S(2)}) collective-permute-start(bf16[528,256]{1,0:T(8,128)(2,1)S(1)} %get-tuple-element.74), channel_id=1, source_target_pairs={{0,1},{1,0},{2,3},{3,2},{4,5},{5,4},{6,7},{7,6},{8,9},{9,8},{10,11... | collective-permute-start | bytes 811016 | tf_op jit(solution)/shard_map/ppermute | solution.py:287
  61.0 10.1 %collective-permute-start.21 = (bf16[528,256]{1,0:T(8,128)(2,1)S(1)}, bf16[528,256]{1,0:T(8,128)(2,1)S(1)}, u32[]{:S(2)}, u32[]{:S(2)}) collective-permute-start(bf16[528,256]{1,0:T(8,128)(2,1)S(1)} %get-tuple-element.75), channel_id=1, source_target_pairs={{0,3},{1,2},{2,1},{3,0},{4,7},{5,6},{6,5},{7,4},{8,11},{9,10},{10,... | collective-permute-start | bytes 811016 | tf_op jit(solution)/shard_map/ppermute | solution.py:287
  63.3 11.4 %collective-permute-start.19 = (bf16[128,1024]{1,0:T(8,128)(2,1)S(1)}, bf16[128,1024]{1,0:T(8,128)(2,1)S(1)}, u32[]{:S(2)}, u32[]{:S(2)}) collective-permute-start(bf16[128,1024]{1,0:T(8,128)(2,1)S(1)} %add_convert_fusion), channel_id=1, source_target_pairs={{0,8},{4,12},{8,0},{12,4},{16,24},{20,28},{24,16},{28,20},{1,9},{5... | collective-permute-start | bytes 786440 | tf_op jit(solution)/shard_map/ppermute | solution.py:290
  67.0 7.7 %collective-permute-start.15 = (bf16[128,1024]{1,0:T(8,128)(2,1)S(1)}, bf16[128,1024]{1,0:T(8,128)(2,1)S(1)}, u32[]{:S(2)}, u32[]{:S(2)}) collective-permute-start(bf16[128,1024]{1,0:T(8,128)(2,1)S(1)} %get-tuple-element.64), channel_id=1, source_target_pairs={{0,4},{4,0},{8,12},{12,8},{16,20},{20,16},{24,28},{28,24},{1,5},{5... | collective-permute-start | bytes 786440 | tf_op jit(solution)/shard_map/ppermute | solution.py:290
  (3 other events, 14.9 us)

commit v4 on v3

--- a/solution.py
+++ b/solution.py
@@ -318,10 +318,9 @@
 
     if staged:
         pieces = [in_weight] + [None] * (n_seq - 1)
-        pieces[1] = trade(after((in_weight, even))[0], 1)
+        pieces[1] = trade(in_weight, 1)
         for step in range(2, n_seq, 2):
-            source = in_weight if step == 4 else after((in_weight, odd))[0]
-            pieces[step] = trade(source, step)
+            pieces[step] = trade(in_weight, step)
     else:
         pieces = [lax.all_gather(in_weight, "seq", axis=0, tiled=True)]
 
@@ -337,12 +336,12 @@
     )
 
     if staged:
-        low, pieces[2] = after((low, pieces[2]))
-        pieces[3] = trade(after((pieces[2], pieces[1]))[0], 1)
+        low, pieces[1] = after((low, pieces[1]))
+        pieces[3] = trade(after((pieces[2], low))[0], 1)
     parts = [low]
     for step in reversed([1 << bit for bit in range(n_mp.bit_length() - 1)]):
         if staged and step == 1:
-            parts[0], pieces[6], pieces[3] = after((parts[0], pieces[6], pieces[3]))
+            parts[0], pieces[6] = after((parts[0], pieces[6]))
         parts = [part for held in parts for part in (held, swap(held, step))]
     onehot, share, delta, slope = call(
         spread_kernel,
@@ -372,7 +371,7 @@
     )
     if staged:
         fetched = {}
-        fetched[7] = trade(terms[7], 1)
+        fetched[7] = trade(after((terms[7], pieces[3]))[0], 1)
         pieces[7] = trade(after((pieces[6], terms[0]))[0], 1)
         pieces[5] = trade(after((pieces[4], fetched[7]))[0], 1)
         fetched[5] = trade(after((terms[5], pieces[7]))[0], 1)

time: 76.8 us -> 76.9 us (level); the launches traced: 75.7 us -> 76.7 us
  waiting for transfers between devices: 20 us -> 33.6 us
  starting transfers between devices: 38.6 us -> 26 us
    ppermute x15, waiting for transfers between devices: 18.3 us -> 32.5 us  [trade(): return lax.ppermute(value, 'seq', [(i, i ^ step) for i in range(n_seq)])]
    ppermute x15, starting transfers between devices: 34.3 us -> 20.2 us  [trade(): return lax.ppermute(value, 'seq', [(i, i ^ step) for i in range(n_seq)])]
    ppermute x6, starting transfers between devices: 3.63 us -> 5.16 us  [swap(): return lax.ppermute(value, 'mp', [(i, i ^ step) for i in range(n_mp)])]
  transfers between devices with their start and end apart: 22 -> 22, of which waited for: 8 -> 12; matrix products, arithmetic and copies ran while one was open for 0% -> 0% of each run, Pallas kernels for 17% -> 16%
where the time goes in v4:
time: 76.9 us; the launch traced here: 76.7 us
  waiting for transfers between devices  33.6 us (44%)
  starting transfers between devices  26 us (34%)
  Pallas kernels  13.7 us (18%)
  local copies, waits for them, and re-layouts  1.45 us (2%)
  other arithmetic  1.14 us (1%)
    ppermute x15, waiting for transfers between devices, trade(): return lax.ppermute(value, 'seq', [(i, i ^ step) for i in range(n_seq)])  32.5 us
    ppermute x15, starting transfers between devices, trade(): return lax.ppermute(value, 'seq', [(i, i ^ step) for i in range(n_seq)])  20.2 us
    pallas_call x7, Pallas kernels, call(): pl.pallas_call(kernel, out_shape=out_shape, in_specs=in_specs, out_specs=...  13.7 us
    ppermute x6, starting transfers between devices, swap(): return lax.ppermute(value, 'mp', [(i, i ^ step) for i in range(n_mp)])  5.16 us
  transfers between devices with their start and end apart: 22, of which 12 were waited for; matrix products, arithmetic and copies ran while one was open for 0% of the time, Pallas kernels for 16%

profile of v4, /device:TPU:0, one launch (start us, length us, event | category | flops | bytes accessed | tf_op | source)
XLA Modules:
  0.0 76.7 jit_solution(7096131948332113907)
XLA Ops:
  2.5 3.0 %collective-permute-start.2 = (bf16[128,1024]{1,0:T(8,128)(2,1)}, bf16[128,1024]{1,0:T(8,128)(2,1)S(1)}, u32[]{:S(2)}, u32[]{:S(2)}) collective-permute-start(bf16[128,1024]{1,0:T(8,128)(2,1)} %refs_0_), channel_id=1, source_target_pairs={{0,4},{4,0},{8,12},{12,8},{16,20},{20,16},{24,28},{28,24},{1,5},{5... | collective-permute-start | bytes 786440 | tf_op jit(solution)/shard_map/ppermute | solution.py:290
  6.2 4.3 %collective-permute-start = (bf16[32,384]{1,0:T(8,128)(2,1)S(1)}, bf16[32,384]{1,0:T(8,128)(2,1)S(1)}, u32[]{:S(2)}, u32[]{:S(2)}) collective-permute-start(bf16[32,384]{1,0:T(8,128)(2,1)S(1)} %get-tuple-element.40), channel_id=1, source_target_pairs={{0,4},{4,0},{8,12},{12,8},{16,20},{20,16},{24,28},{28,24},{1,5},{5... | collective-permute-start | bytes 73736 | tf_op jit(solution)/shard_map/ppermute | solution.py:290
  10.6 1.6 %collective-permute-start.7 = (bf16[128,1024]{1,0:T(8,128)(2,1)}, bf16[128,1024]{1,0:T(8,128)(2,1)S(1)}, u32[]{:S(2)}, u32[]{:S(2)}) collective-permute-start(bf16[128,1024]{1,0:T(8,128)(2,1)} %refs_0_), channel_id=1, source_target_pairs={{0,8},{4,12},{8,0},{12,4},{16,24},{20,28},{24,16},{28,20},{1,9},{5... | collective-permute-start | bytes 786440 | tf_op jit(solution)/shard_map/ppermute | solution.py:290
  12.2 2.5 %collective-permute-start.3 = (bf16[128,1024]{1,0:T(8,128)(2,1)}, bf16[128,1024]{1,0:T(8,128)(2,1)S(1)}, u32[]{:S(2)}, u32[]{:S(2)}) collective-permute-start(bf16[128,1024]{1,0:T(8,128)(2,1)} %refs_0_), channel_id=1, source_target_pairs={{0,24},{4,28},{8,16},{12,20},{16,8},{20,12},{24,0},{28,4},{1,25},{... | collective-permute-start | bytes 786440 | tf_op jit(solution)/shard_map/ppermute | solution.py:290
  15.3 2.1 %shard_map.77 = (bf16[512,256]{1,0:T(8,128)(2,1)S(1)}, f32[512,256]{1,0:T(8,128)S(1)}, f32[512,256]{1,0:T(8,128)S(1)}) custom-call(bf16[1024,256]{1,0:T(8,128)(2,1)S(1)} %get-tuple-element.39.hidden_ref, bf16[32,384]{1,0:T(8,128)(2,1)S(1)} %collective-permute-done.even_ref, bf16[32,384]{1,0:T(8,128)(2,1)S(1)} %collective-permute-done.1.odd_ref, ...), custom_call_target="tpu_custom_call" | custom-call | tf_op jit(solution)/shard_map/pallas_call | solution.py:258
  17.4 1.6 %collective-permute-start.5 = (bf16[512,256]{1,0:T(8,128)(2,1)S(1)}, bf16[512,256]{1,0:T(8,128)(2,1)S(1)}, u32[]{:S(2)}, u32[]{:S(2)}) collective-permute-start(bf16[512,256]{1,0:T(8,128)(2,1)S(1)} %get-tuple-element.46.refs_0_), channel_id=1, source_target_pairs={{0,2},{1,3},{2,0},{3,1},{4,6},{5,7},{6,4},{7,5},{8,10},{9,11},{10,... | collective-permute-start | bytes 786440 | tf_op jit(solution)/shard_map/ppermute | solution.py:287
  19.2 6.4 %collective-permute-done.3.refs_6_ = bf16[128,1024]{1,0:T(8,128)(2,1)S(1)} collective-permute-done((bf16[128,1024]{1,0:T(8,128)(2,1)}, bf16[128,1024]{1,0:T(8,128)(2,1)S(1)}, u32[]{:S(2)}, u32[]{:S(2)}) %collective-permute-start.3) | collective-permute-done | bytes 262176 | tf_op jit(solution)/shard_map/ppermute | solution.py:290
  27.6 1.7 %shard_map.78 = (f32[128,1024]{1,0:T(8,128)S(1)}, bf16[128,1024]{1,0:T(8,128)(2,1)S(1)}, f32[128,1024]{1,0:T(8,128)S(1)}, bf16[128,1024]{1,0:T(8,128)(2,1)S(1)},...) custom-call(bf16[512,256]{1,0:T(8,128)(2,1)S(1)} %get-tuple-element., ...), custom_call_target="tpu_custom_call" | custom-call | tf_op jit(solution)/shard_map/pallas_call | solution.py:258
  29.3 5.1 %collective-permute-done.8.refs_3_ = bf16[128,1024]{1,0:T(8,128)(2,1)S(1)} collective-permute-done((bf16[128,1024]{1,0:T(8,128)(2,1)S(1)}, bf16[128,1024]{1,0:T(8,128)(2,1)S(1)}, u32[]{:S(2)}, u32[]{:S(2)}) %collective-permute-start.8) | collective-permute-done | bytes 262176 | tf_op jit(solution)/shard_map/ppermute | solution.py:290
  34.7 1.7 %collective-permute-start.12 = (bf16[128,1024]{1,0:T(8,128)(2,1)S(1)}, bf16[128,1024]{1,0:T(8,128)(2,1)S(1)}, u32[]{:S(2)}, u32[]{:S(2)}) collective-permute-start(bf16[128,1024]{1,0:T(8,128)(2,1)S(1)} %collective-permute-done.3.refs_6_), channel_id=1, source_target_pairs={{0,4},{4,0},{8,12},{12,8},{16,20},{20,16},{24,28},{28,24},{1,5},{5... | collective-permute-start | bytes 786440 | tf_op jit(solution)/shard_map/ppermute | solution.py:290
  36.4 4.4 %collective-permute-done.9.refs_4_ = bf16[128,1024]{1,0:T(8,128)(2,1)S(1)} collective-permute-done((bf16[128,1024]{1,0:T(8,128)(2,1)S(1)}, bf16[128,1024]{1,0:T(8,128)(2,1)S(1)}, u32[]{:S(2)}, u32[]{:S(2)}) %collective-permute-start.9) | collective-permute-done | bytes 262176 | tf_op jit(solution)/shard_map/ppermute | solution.py:290
  40.8 2.8 %collective-permute-done.10 = bf16[128,1024]{1,0:T(8,128)(2,1)S(1)} collective-permute-done((bf16[128,1024]{1,0:T(8,128)(2,1)S(1)}, bf16[128,1024]{1,0:T(8,128)(2,1)S(1)}, u32[]{:S(2)}, u32[]{:S(2)}) %collective-permute-start.10) | collective-permute-done | bytes 262176 | tf_op jit(solution)/shard_map/ppermute | solution.py:290
  44.0 2.0 %collective-permute-start.16 = (bf16[128,1024]{1,0:T(8,128)(2,1)S(1)}, bf16[128,1024]{1,0:T(8,128)(2,1)S(1)}, u32[]{:S(2)}, u32[]{:S(2)}) collective-permute-start(bf16[128,1024]{1,0:T(8,128)(2,1)S(1)} %add_convert_fusion.2), channel_id=1, source_target_pairs={{0,24},{4,28},{8,16},{12,20},{16,8},{20,12},{24,0},{28,4},{1,25},{... | collective-permute-start | bytes 786440 | tf_op jit(solution)/shard_map/ppermute | solution.py:290
  46.0 3.2 %collective-permute-done.12.refs_7_ = bf16[128,1024]{1,0:T(8,128)(2,1)S(1)} collective-permute-done((bf16[128,1024]{1,0:T(8,128)(2,1)S(1)}, bf16[128,1024]{1,0:T(8,128)(2,1)S(1)}, u32[]{:S(2)}, u32[]{:S(2)}) %collective-permute-start.12) | collective-permute-done | bytes 262176 | tf_op jit(solution)/shard_map/ppermute | solution.py:290
  49.6 1.7 %shard_map.81 = (bf16[1024,512]{1,0:T(8,128)(2,1)S(1)}, f32[1024,256]{1,0:T(8,128)S(1)}, f32[1024,256]{1,0:T(8,128)S(1)}, f32[1024,256]{1,0:T(8,128)S(1)}) custom-call(bf16[1024,256]{1,0:T(8,128)(2,1)S(1)} %get-tuple-element.39.hidden_ref, bf16[32,384]{1,0:T(8,128)(2,1)S(1)} %collective-permute-done.even_ref, ...), custom_call_target="tpu_custom_call" | custom-call | tf_op jit(solution)/shard_map/pallas_call | solution.py:258
  51.3 3.5 %collective-permute-done.11.refs_5_ = bf16[128,1024]{1,0:T(8,128)(2,1)S(1)} collective-permute-done((bf16[128,1024]{1,0:T(8,128)(2,1)S(1)}, bf16[128,1024]{1,0:T(8,128)(2,1)S(1)}, u32[]{:S(2)}, u32[]{:S(2)}) %collective-permute-start.11) | collective-permute-done | bytes 262176 | tf_op jit(solution)/shard_map/ppermute | solution.py:290
  54.9 2.5 %shard_map.79 = (bf16[528,256]{1,0:T(8,128)(2,1)S(1)}, bf16[528,256]{1,0:T(8,128)(2,1)S(1)}, bf16[528,256]{1,0:T(8,128)(2,1)S(1)}, bf16[528,256]{1,0:T(8,128)(2,1)S(1)}, bf16[1024,1024]{1,0:T(8,128)(2,1)}) custom-call(bf16[512,1024]{1,0:T(8,128)(2,1)S(1)} %copy-done, bf16[32,384]{1,0:T(8,128)(2,1)S(1)} %collective-permute-done.even_ref, ...), custom_call_target="tpu_custom_call" | custom-call | tf_op jit(solution)/shard_map/pallas_call | solution.py:258
  57.7 1.5 %collective-permute-start.14 = (bf16[528,256]{1,0:T(8,128)(2,1)S(1)}, bf16[528,256]{1,0:T(8,128)(2,1)S(1)}, u32[]{:S(2)}, u32[]{:S(2)}) collective-permute-start(bf16[528,256]{1,0:T(8,128)(2,1)S(1)} %get-tuple-element.59), channel_id=1, source_target_pairs={{0,2},{1,3},{2,0},{3,1},{4,6},{5,7},{6,4},{7,5},{8,10},{9,11},{10,... | collective-permute-start | bytes 811016 | tf_op jit(solution)/shard_map/ppermute | solution.py:287
  60.9 1.6 %collective-permute-start.21 = (bf16[528,256]{1,0:T(8,128)(2,1)S(1)}, bf16[528,256]{1,0:T(8,128)(2,1)S(1)}, u32[]{:S(2)}, u32[]{:S(2)}) collective-permute-start(bf16[528,256]{1,0:T(8,128)(2,1)S(1)} %get-tuple-element.71), channel_id=1, source_target_pairs={{0,3},{1,2},{2,1},{3,0},{4,7},{5,6},{6,5},{7,4},{8,11},{9,10},{10,... | collective-permute-start | bytes 811016 | tf_op jit(solution)/shard_map/ppermute | solution.py:287
  62.5 1.7 %collective-permute-done.18 = bf16[128,1024]{1,0:T(8,128)(2,1)S(1)} collective-permute-done((bf16[128,1024]{1,0:T(8,128)(2,1)S(1)}, bf16[128,1024]{1,0:T(8,128)(2,1)S(1)}, u32[]{:S(2)}, u32[]{:S(2)}) %collective-permute-start.18) | collective-permute-done | bytes 262176 | tf_op jit(solution)/shard_map/ppermute | solution.py:290
  64.4 1.9 %collective-permute-start.15 = (bf16[128,1024]{1,0:T(8,128)(2,1)S(1)}, bf16[128,1024]{1,0:T(8,128)(2,1)S(1)}, u32[]{:S(2)}, u32[]{:S(2)}) collective-permute-start(bf16[128,1024]{1,0:T(8,128)(2,1)S(1)} %get-tuple-element.60), channel_id=1, source_target_pairs={{0,4},{4,0},{8,12},{12,8},{16,20},{20,16},{24,28},{28,24},{1,5},{5... | collective-permute-start | bytes 786440 | tf_op jit(solution)/shard_map/ppermute | solution.py:290
  66.3 2.4 %shard_map.80 = bf16[512,1024]{1,0:T(8,128)(2,1)} custom-call(bf16[512,256]{1,0:T(8,128)(2,1)S(1)} %get-tuple-element.46.refs_0_, bf16[512,256]{1,0:T(8,128)(2,1)S(1)} %collective-permute-done.4.refs_1_, bf16[512,256]{1,0:T(8,128)(2,1)S(1)} %collective-permute-done.5.refs_2_, bf16[512,256]{1,0:T(8,128)(2,1)S(1)} %collective-permute-done.6.refs_3_, ...), custom_call_target="tpu_custom_call" | custom-call | tf_op jit(solution)/shard_map/pallas_call | solution.py:258
  69.6 2.3 %shard_map.82 = bf16[1024,256]{1,0:T(8,128)(2,1)} custom-call(bf16[528,256]{1,0:T(8,128)(2,1)S(1)} %get-tuple-element.69.refs_0_, bf16[528,256]{1,0:T(8,128)(2,1)S(1)} %collective-permute-done.20.refs_1_, bf16[528,256]{1,0:T(8,128)(2,1)S(1)} %collective-permute-done.14.refs_2_, bf16[528,256]{1,0:T(8,128)(2,1)S(1)} %collective-permute-done.21.refs_3_, ...), custom_call_target="tpu_custom_call" | custom-call | tf_op jit(solution)/shard_map/pallas_call | solution.py:258
  71.9 3.9 %collective-permute-done.19 = bf16[128,1024]{1,0:T(8,128)(2,1)S(1)} collective-permute-done((bf16[128,1024]{1,0:T(8,128)(2,1)S(1)}, bf16[128,1024]{1,0:T(8,128)(2,1)S(1)}, u32[]{:S(2)}, u32[]{:S(2)}) %collective-permute-start.19) | collective-permute-done | bytes 262176 | tf_op jit(solution)/shard_map/ppermute | solution.py:290
  (41 shorter events, 10.7 us)
Async XLA Ops:
  0.6 26.9 %copy-start = (bf16[512,1024]{1,0:T(8,128)(2,1)S(1)}, bf16[512,1024]{1,0:T(8,128)(2,1)}, u32[]{:S(2)}) copy-start(bf16[512,1024]{1,0:T(8,128)(2,1)} %grad_ref.1) | copy-start | bytes 3145732
  0.6 25.9 %copy-start.2 = (bf16[128,1024]{1,0:T(8,128)(2,1)S(1)}, bf16[128,1024]{1,0:T(8,128)(2,1)}, u32[]{:S(2)}) copy-start(bf16[128,1024]{1,0:T(8,128)(2,1)} %refs_0_) | copy-start | bytes 786436
  2.5 14.8 %collective-permute-start.2 = (bf16[128,1024]{1,0:T(8,128)(2,1)}, bf16[128,1024]{1,0:T(8,128)(2,1)S(1)}, u32[]{:S(2)}, u32[]{:S(2)}) collective-permute-start(bf16[128,1024]{1,0:T(8,128)(2,1)} %refs_0_), channel_id=1, source_target_pairs={{0,4},{4,0},{8,12},{12,8},{16,20},{20,16},{24,28},{28,24},{1,5},{5... | collective-permute-start | bytes 786440 | tf_op jit(solution)/shard_map/ppermute | solution.py:290
  5.6 9.1 %collective-permute-start.1 = (bf16[32,384]{1,0:T(8,128)(2,1)S(1)}, bf16[32,384]{1,0:T(8,128)(2,1)S(1)}, u32[]{:S(2)}, u32[]{:S(2)}) collective-permute-start(bf16[32,384]{1,0:T(8,128)(2,1)S(1)} %get-tuple-element.41), channel_id=1, source_target_pairs={{4,8},{12,16},{20,24},{8,4},{16,12},{24,20},{5,9},{13,17},{21,25},... | collective-permute-start | bytes 73736 | tf_op jit(solution)/shard_map/ppermute | solution.py:317
  6.2 8.4 %collective-permute-start = (bf16[32,384]{1,0:T(8,128)(2,1)S(1)}, bf16[32,384]{1,0:T(8,128)(2,1)S(1)}, u32[]{:S(2)}, u32[]{:S(2)}) collective-permute-start(bf16[32,384]{1,0:T(8,128)(2,1)S(1)} %get-tuple-element.40), channel_id=1, source_target_pairs={{0,4},{4,0},{8,12},{12,8},{16,20},{20,16},{24,28},{28,24},{1,5},{5... | collective-permute-start | bytes 73736 | tf_op jit(solution)/shard_map/ppermute | solution.py:290
  10.6 8.7 %collective-permute-start.7 = (bf16[128,1024]{1,0:T(8,128)(2,1)}, bf16[128,1024]{1,0:T(8,128)(2,1)S(1)}, u32[]{:S(2)}, u32[]{:S(2)}) collective-permute-start(bf16[128,1024]{1,0:T(8,128)(2,1)} %refs_0_), channel_id=1, source_target_pairs={{0,8},{4,12},{8,0},{12,4},{16,24},{20,28},{24,16},{28,20},{1,9},{5... | collective-permute-start | bytes 786440 | tf_op jit(solution)/shard_map/ppermute | solution.py:290
  12.2 13.5 %collective-permute-start.3 = (bf16[128,1024]{1,0:T(8,128)(2,1)}, bf16[128,1024]{1,0:T(8,128)(2,1)S(1)}, u32[]{:S(2)}, u32[]{:S(2)}) collective-permute-start(bf16[128,1024]{1,0:T(8,128)(2,1)} %refs_0_), channel_id=1, source_target_pairs={{0,24},{4,28},{8,16},{12,20},{16,8},{20,12},{24,0},{28,4},{1,25},{... | collective-permute-start | bytes 786440 | tf_op jit(solution)/shard_map/ppermute | solution.py:290
  17.4 8.3 %collective-permute-start.5 = (bf16[512,256]{1,0:T(8,128)(2,1)S(1)}, bf16[512,256]{1,0:T(8,128)(2,1)S(1)}, u32[]{:S(2)}, u32[]{:S(2)}) collective-permute-start(bf16[512,256]{1,0:T(8,128)(2,1)S(1)} %get-tuple-element.46.refs_0_), channel_id=1, source_target_pairs={{0,2},{1,3},{2,0},{3,1},{4,6},{5,7},{6,4},{7,5},{8,10},{9,11},{10,... | collective-permute-start | bytes 786440 | tf_op jit(solution)/shard_map/ppermute | solution.py:287
  25.6 1.8 %collective-permute-start.4 = (bf16[512,256]{1,0:T(8,128)(2,1)S(1)}, bf16[512,256]{1,0:T(8,128)(2,1)S(1)}, u32[]{:S(2)}, u32[]{:S(2)}) collective-permute-start(bf16[512,256]{1,0:T(8,128)(2,1)S(1)} %get-tuple-element.46.refs_0_), channel_id=1, source_target_pairs={{0,1},{1,0},{2,3},{3,2},{4,5},{5,4},{6,7},{7,6},{8,9},{9,8},{10,11... | collective-permute-start | bytes 786440 | tf_op jit(solution)/shard_map/ppermute | solution.py:287
  25.6 1.9 %collective-permute-start.6 = (bf16[512,256]{1,0:T(8,128)(2,1)S(1)}, bf16[512,256]{1,0:T(8,128)(2,1)S(1)}, u32[]{:S(2)}, u32[]{:S(2)}) collective-permute-start(bf16[512,256]{1,0:T(8,128)(2,1)S(1)} %collective-permute-done.5.refs_2_), channel_id=1, source_target_pairs={{0,1},{1,0},{2,3},{3,2},{4,5},{5,4},{6,7},{7,6},{8,9},{9,8},{10,11... | collective-permute-start | bytes 786440 | tf_op jit(solution)/shard_map/ppermute | solution.py:287
  26.2 8.2 %collective-permute-start.8 = (bf16[128,1024]{1,0:T(8,128)(2,1)S(1)}, bf16[128,1024]{1,0:T(8,128)(2,1)S(1)}, u32[]{:S(2)}, u32[]{:S(2)}) collective-permute-start(bf16[128,1024]{1,0:T(8,128)(2,1)S(1)} %collective-permute-done.7.refs_2_), channel_id=1, source_target_pairs={{0,4},{4,0},{8,12},{12,8},{16,20},{20,16},{24,28},{28,24},{1,5},{5... | collective-permute-start | bytes 786440 | tf_op jit(solution)/shard_map/ppermute | solution.py:290
  26.5 14.3 %collective-permute-start.9 = (bf16[128,1024]{1,0:T(8,128)(2,1)S(1)}, bf16[128,1024]{1,0:T(8,128)(2,1)S(1)}, u32[]{:S(2)}, u32[]{:S(2)}) collective-permute-start(bf16[128,1024]{1,0:T(8,128)(2,1)S(1)} %copy-done.2), channel_id=1, source_target_pairs={{0,16},{4,20},{8,24},{12,28},{16,0},{20,4},{24,8},{28,12},{1,17},{... | collective-permute-start | bytes 786440 | tf_op jit(solution)/shard_map/ppermute | solution.py:290
  34.4 9.2 %collective-permute-start.10 = (bf16[128,1024]{1,0:T(8,128)(2,1)S(1)}, bf16[128,1024]{1,0:T(8,128)(2,1)S(1)}, u32[]{:S(2)}, u32[]{:S(2)}) collective-permute-start(bf16[128,1024]{1,0:T(8,128)(2,1)S(1)} %get-tuple-element.50), channel_id=1, source_target_pairs={{0,4},{4,0},{8,12},{12,8},{16,20},{20,16},{24,28},{28,24},{1,5},{5... | collective-permute-start | bytes 786440 | tf_op jit(solution)/shard_map/ppermute | solution.py:290
  34.7 14.5 %collective-permute-start.12 = (bf16[128,1024]{1,0:T(8,128)(2,1)S(1)}, bf16[128,1024]{1,0:T(8,128)(2,1)S(1)}, u32[]{:S(2)}, u32[]{:S(2)}) collective-permute-start(bf16[128,1024]{1,0:T(8,128)(2,1)S(1)} %collective-permute-done.3.refs_6_), channel_id=1, source_target_pairs={{0,4},{4,0},{8,12},{12,8},{16,20},{20,16},{24,28},{28,24},{1,5},{5... | collective-permute-start | bytes 786440 | tf_op jit(solution)/shard_map/ppermute | solution.py:290
  43.6 11.2 %collective-permute-start.11 = (bf16[128,1024]{1,0:T(8,128)(2,1)S(1)}, bf16[128,1024]{1,0:T(8,128)(2,1)S(1)}, u32[]{:S(2)}, u32[]{:S(2)}) collective-permute-start(bf16[128,1024]{1,0:T(8,128)(2,1)S(1)} %collective-permute-done.9.refs_4_), channel_id=1, source_target_pairs={{0,4},{4,0},{8,12},{12,8},{16,20},{20,16},{24,28},{28,24},{1,5},{5... | collective-permute-start | bytes 786440 | tf_op jit(solution)/shard_map/ppermute | solution.py:290
  44.0 13.3 %collective-permute-start.16 = (bf16[128,1024]{1,0:T(8,128)(2,1)S(1)}, bf16[128,1024]{1,0:T(8,128)(2,1)S(1)}, u32[]{:S(2)}, u32[]{:S(2)}) collective-permute-start(bf16[128,1024]{1,0:T(8,128)(2,1)S(1)} %add_convert_fusion.2), channel_id=1, source_target_pairs={{0,24},{4,28},{8,16},{12,20},{16,8},{20,12},{24,0},{28,4},{1,25},{... | collective-permute-start | bytes 786440 | tf_op jit(solution)/shard_map/ppermute | solution.py:290
  49.2 11.2 %collective-permute-start.13 = (bf16[128,1024]{1,0:T(8,128)(2,1)S(1)}, bf16[128,1024]{1,0:T(8,128)(2,1)S(1)}, u32[]{:S(2)}, u32[]{:S(2)}) collective-permute-start(bf16[128,1024]{1,0:T(8,128)(2,1)S(1)} %get-tuple-element.58), channel_id=1, source_target_pairs={{0,4},{4,0},{8,12},{12,8},{16,20},{20,16},{24,28},{28,24},{1,5},{5... | collective-permute-start | bytes 786440 | tf_op jit(solution)/shard_map/ppermute | solution.py:290
  57.4 6.8 %collective-permute-start.18 = (bf16[128,1024]{1,0:T(8,128)(2,1)S(1)}, bf16[128,1024]{1,0:T(8,128)(2,1)S(1)}, u32[]{:S(2)}, u32[]{:S(2)}) collective-permute-start(bf16[128,1024]{1,0:T(8,128)(2,1)S(1)} %get-tuple-element.68), channel_id=1, source_target_pairs={{0,4},{4,0},{8,12},{12,8},{16,20},{20,16},{24,28},{28,24},{1,5},{5... | collective-permute-start | bytes 786440 | tf_op jit(solution)/shard_map/ppermute | solution.py:290
  57.7 6.6 %collective-permute-start.14 = (bf16[528,256]{1,0:T(8,128)(2,1)S(1)}, bf16[528,256]{1,0:T(8,128)(2,1)S(1)}, u32[]{:S(2)}, u32[]{:S(2)}) collective-permute-start(bf16[528,256]{1,0:T(8,128)(2,1)S(1)} %get-tuple-element.59), channel_id=1, source_target_pairs={{0,2},{1,3},{2,0},{3,1},{4,6},{5,7},{6,4},{7,5},{8,10},{9,11},{10,... | collective-permute-start | bytes 811016 | tf_op jit(solution)/shard_map/ppermute | solution.py:287
  60.5 11.3 %collective-permute-start.17 = (bf16[128,1024]{1,0:T(8,128)(2,1)S(1)}, bf16[128,1024]{1,0:T(8,128)(2,1)S(1)}, u32[]{:S(2)}, u32[]{:S(2)}) collective-permute-start(bf16[128,1024]{1,0:T(8,128)(2,1)S(1)} %add_convert_fusion.1), channel_id=1, source_target_pairs={{0,16},{4,20},{8,24},{12,28},{16,0},{20,4},{24,8},{28,12},{1,17},{... | collective-permute-start | bytes 786440 | tf_op jit(solution)/shard_map/ppermute | solution.py:290
  60.9 7.7 %collective-permute-start.20 = (bf16[528,256]{1,0:T(8,128)(2,1)S(1)}, bf16[528,256]{1,0:T(8,128)(2,1)S(1)}, u32[]{:S(2)}, u32[]{:S(2)}) collective-permute-start(bf16[528,256]{1,0:T(8,128)(2,1)S(1)} %get-tuple-element.70), channel_id=1, source_target_pairs={{0,1},{1,0},{2,3},{3,2},{4,5},{5,4},{6,7},{7,6},{8,9},{9,8},{10,11... | collective-permute-start | bytes 811016 | tf_op jit(solution)/shard_map/ppermute | solution.py:287
  60.9 8.6 %collective-permute-start.21 = (bf16[528,256]{1,0:T(8,128)(2,1)S(1)}, bf16[528,256]{1,0:T(8,128)(2,1)S(1)}, u32[]{:S(2)}, u32[]{:S(2)}) collective-permute-start(bf16[528,256]{1,0:T(8,128)(2,1)S(1)} %get-tuple-element.71), channel_id=1, source_target_pairs={{0,3},{1,2},{2,1},{3,0},{4,7},{5,6},{6,5},{7,4},{8,11},{9,10},{10,... | collective-permute-start | bytes 811016 | tf_op jit(solution)/shard_map/ppermute | solution.py:287
  64.3 11.5 %collective-permute-start.19 = (bf16[128,1024]{1,0:T(8,128)(2,1)S(1)}, bf16[128,1024]{1,0:T(8,128)(2,1)S(1)}, u32[]{:S(2)}, u32[]{:S(2)}) collective-permute-start(bf16[128,1024]{1,0:T(8,128)(2,1)S(1)} %add_convert_fusion), channel_id=1, source_target_pairs={{0,8},{4,12},{8,0},{12,4},{16,24},{20,28},{24,16},{28,20},{1,9},{5... | collective-permute-start | bytes 786440 | tf_op jit(solution)/shard_map/ppermute | solution.py:290
  64.4 11.3 %collective-permute-start.15 = (bf16[128,1024]{1,0:T(8,128)(2,1)S(1)}, bf16[128,1024]{1,0:T(8,128)(2,1)S(1)}, u32[]{:S(2)}, u32[]{:S(2)}) collective-permute-start(bf16[128,1024]{1,0:T(8,128)(2,1)S(1)} %get-tuple-element.60), channel_id=1, source_target_pairs={{0,4},{4,0},{8,12},{12,8},{16,20},{20,16},{24,28},{28,24},{1,5},{5... | collective-permute-start | bytes 786440 | tf_op jit(solution)/shard_map/ppermute | solution.py:290
  (3 other events, 10.4 us)

commit v5 on v4

--- a/solution.py
+++ b/solution.py
@@ -252,7 +252,7 @@
         ref[slots:] = dot(row, block, ((1,), (1,))).astype(BF16)
 
 
-def call(kernel, out_shape, *args, flops=0, scratch=(), in_specs=None, limit=VMEM_LIMIT):
+def call(kernel, out_shape, *args, weight=0, scratch=(), in_specs=None, limit=VMEM_LIMIT):
     if in_specs is None:
         in_specs = [pl.BlockSpec(memory_space=pltpu.VMEM)] * len(args)
     return pl.pallas_call(
@@ -261,7 +261,7 @@
         in_specs=in_specs,
         out_specs=jax.tree.map(lambda _: pl.BlockSpec(memory_space=pltpu.VMEM), out_shape),
         scratch_shapes=list(scratch),
-        cost_estimate=pl.CostEstimate(flops=0, bytes_accessed=0, transcendentals=0),
+        cost_estimate=pl.CostEstimate(flops=0, bytes_accessed=weight, transcendentals=0),
         compiler_params=pltpu.CompilerParams(vmem_limit_bytes=limit),
     )(*args)
 
@@ -332,16 +332,15 @@
         odd,
         start,
         query,
-        flops=8 * bytes_ * slots * feats,
     )
 
     if staged:
-        low, pieces[1] = after((low, pieces[1]))
-        pieces[3] = trade(after((pieces[2], low))[0], 1)
+        low = after((low, (pieces[1],)))[0]
+        pieces[3] = trade(after((pieces[2], (low,)))[0], 1)
     parts = [low]
     for step in reversed([1 << bit for bit in range(n_mp.bit_length() - 1)]):
         if staged and step == 1:
-            parts[0], pieces[6] = after((parts[0], pieces[6]))
+            parts[0] = after((parts[0], (pieces[6], pieces[3],)))[0]
         parts = [part for held in parts for part in (held, swap(held, step))]
     onehot, share, delta, slope = call(
         spread_kernel,
@@ -353,9 +352,7 @@
         query,
         pooled,
         denom,
-        flops=8 * bytes_ * slots * feats,
-    )
-    work = 2 * slots * width * latent_dim
+    )
     scale = 1.0 / math.sqrt(n_seq * slots)
     if staged:
         blocks = [shape((rows, width), BF16 if index % 2 else F32) for index in range(n_seq)]
@@ -366,15 +363,14 @@
         tuple(blocks),
         *parts,
         latent_grad,
-        flops=work,
         scratch=(pltpu.VMEM((slots, latent_dim), BF16), pltpu.VMEM((latent_dim, width), F32)),
     )
     if staged:
         fetched = {}
-        fetched[7] = trade(after((terms[7], pieces[3]))[0], 1)
-        pieces[7] = trade(after((pieces[6], terms[0]))[0], 1)
-        pieces[5] = trade(after((pieces[4], fetched[7]))[0], 1)
-        fetched[5] = trade(after((terms[5], pieces[7]))[0], 1)
+        pieces[7] = trade(after((pieces[6], (pieces[3],)))[0], 1)
+        fetched[7] = trade(terms[7], 1)
+        fetched[5] = trade(terms[5], 1)
+        pieces[5] = trade(after((pieces[4], (fetched[7], pieces[7],)))[0], 1)
 
     *partials, weight_full = call(
         functools.partial(partial_kernel, n_mp),
@@ -383,15 +379,14 @@
         even,
         odd,
         *pieces,
-        flops=work,
     )
     grads = [partials[0]] + [swap(partials[step], step) for step in range(1, n_mp)]
 
     if staged:
         fetched[6] = trade((terms[6] + fetched[7].astype(F32)).astype(BF16), 6)
-        fetched[3] = trade(after((terms[3], weight_full, share, fetched[6]))[0], 1)
+        fetched[3] = trade(after((terms[3], (fetched[6], weight_full, share,)))[0], 1)
         fetched[4] = trade((terms[4] + fetched[5].astype(F32)).astype(BF16), 4)
-        fetched[1] = trade(after((terms[1], fetched[5], grads[2]))[0], 1)
+        fetched[1] = trade(after((terms[1], (grads[2], fetched[5],)))[0], 1)
         fetched[2] = trade((terms[2] + fetched[3].astype(F32)).astype(BF16), 2)
         grad_weight = terms[0] + fetched[1].astype(F32)
         for step in (6, 4, 2):
@@ -405,7 +400,6 @@
         shape((slots, width), BF16),
         *parts,
         weight_full,
-        flops=work,
         scratch=(pltpu.VMEM((slots, latent_dim), BF16),),
     )
     grad_bytes = call(
@@ -417,7 +411,6 @@
         share,
         delta,
         slope,
-        flops=4 * bytes_ * slots * feats,
     )
     return latent, grad_weight, grad_bytes
 

time: 76.9 us -> 76.1 us (0.990)
  waiting for transfers between devices: 33.6 us -> 23.8 us
  starting transfers between devices: 26 us -> 35 us
    ppermute x15, starting transfers between devices: 20.2 us -> 30.7 us  [trade(): return lax.ppermute(value, 'seq', [(i, i ^ step) for i in range(n_seq)])]
    ppermute x15, waiting for transfers between devices: 32.5 us -> 22.2 us  [trade(): return lax.ppermute(value, 'seq', [(i, i ^ step) for i in range(n_seq)])]
    ppermute x6, starting transfers between devices: 5.16 us -> 3.64 us  [swap(): return lax.ppermute(value, 'mp', [(i, i ^ step) for i in range(n_mp)])]
  transfers between devices with their start and end apart: 22 -> 22, of which waited for: 12 -> 9; matrix products, arithmetic and copies ran while one was open for 0% -> 0% of each run, Pallas kernels for 16% -> 17%
where the time goes in v5:
time: 76.1 us; the launch traced here: 75.9 us
  starting transfers between devices  35 us (46%)
  waiting for transfers between devices  23.8 us (31%)
  Pallas kernels  13.7 us (18%)
  local copies, waits for them, and re-layouts  1.45 us (2%)
  other arithmetic  1.14 us (1%)
    ppermute x15, starting transfers between devices, trade(): return lax.ppermute(value, 'seq', [(i, i ^ step) for i in range(n_seq)])  30.7 us
    ppermute x15, waiting for transfers between devices, trade(): return lax.ppermute(value, 'seq', [(i, i ^ step) for i in range(n_seq)])  22.2 us
    pallas_call x7, Pallas kernels, call(): pl.pallas_call(kernel, out_shape=out_shape, in_specs=in_specs, out_specs=...  13.7 us
    ppermute x6, starting transfers between devices, swap(): return lax.ppermute(value, 'mp', [(i, i ^ step) for i in range(n_mp)])  3.64 us
    ppermute x6, waiting for transfers between devices, swap(): return lax.ppermute(value, 'mp', [(i, i ^ step) for i in range(n_mp)])  1.56 us
  transfers between devices with their start and end apart: 22, of which 9 were waited for; matrix products, arithmetic and copies ran while one was open for 0% of the time, Pallas kernels for 17%

profile of v5, /device:TPU:0, one launch (start us, length us, event | category | flops | bytes accessed | tf_op | source)
XLA Modules:
  0.0 75.9 jit_solution(249053965907994008)
XLA Ops:
  2.5 3.0 %collective-permute-start.2 = (bf16[128,1024]{1,0:T(8,128)(2,1)}, bf16[128,1024]{1,0:T(8,128)(2,1)S(1)}, u32[]{:S(2)}, u32[]{:S(2)}) collective-permute-start(bf16[128,1024]{1,0:T(8,128)(2,1)} %refs_0_), channel_id=1, source_target_pairs={{0,4},{4,0},{8,12},{12,8},{16,20},{20,16},{24,28},{28,24},{1,5},{5... | collective-permute-start | bytes 786440 | tf_op jit(solution)/shard_map/ppermute | solution.py:290
  5.6 1.6 %collective-permute-start.4 = (bf16[128,1024]{1,0:T(8,128)(2,1)}, bf16[128,1024]{1,0:T(8,128)(2,1)S(1)}, u32[]{:S(2)}, u32[]{:S(2)}) collective-permute-start(bf16[128,1024]{1,0:T(8,128)(2,1)} %refs_0_), channel_id=1, source_target_pairs={{0,8},{4,12},{8,0},{12,4},{16,24},{20,28},{24,16},{28,20},{1,9},{5... | collective-permute-start | bytes 786440 | tf_op jit(solution)/shard_map/ppermute | solution.py:290
  7.8 3.2 %collective-permute-start = (bf16[32,384]{1,0:T(8,128)(2,1)S(1)}, bf16[32,384]{1,0:T(8,128)(2,1)S(1)}, u32[]{:S(2)}, u32[]{:S(2)}) collective-permute-start(bf16[32,384]{1,0:T(8,128)(2,1)S(1)} %get-tuple-element.36), channel_id=1, source_target_pairs={{0,4},{4,0},{8,12},{12,8},{16,20},{20,16},{24,28},{28,24},{1,5},{5... | collective-permute-start | bytes 73736 | tf_op jit(solution)/shard_map/ppermute | solution.py:290
  11.0 2.2 %collective-permute-start.3 = (bf16[128,1024]{1,0:T(8,128)(2,1)}, bf16[128,1024]{1,0:T(8,128)(2,1)S(1)}, u32[]{:S(2)}, u32[]{:S(2)}) collective-permute-start(bf16[128,1024]{1,0:T(8,128)(2,1)} %refs_0_), channel_id=1, source_target_pairs={{0,24},{4,28},{8,16},{12,20},{16,8},{20,12},{24,0},{28,4},{1,25},{... | collective-permute-start | bytes 786440 | tf_op jit(solution)/shard_map/ppermute | solution.py:290
  13.9 2.1 %shard_map.77 = (bf16[512,256]{1,0:T(8,128)(2,1)S(1)}, f32[512,256]{1,0:T(8,128)S(1)}, f32[512,256]{1,0:T(8,128)S(1)}) custom-call(bf16[1024,256]{1,0:T(8,128)(2,1)S(1)} %get-tuple-element.35.hidden_ref, bf16[32,384]{1,0:T(8,128)(2,1)S(1)} %collective-permute-done.even_ref, bf16[32,384]{1,0:T(8,128)(2,1)S(1)} %collective-permute-done.1.odd_ref, ...), custom_call_target="tpu_custom_call" | custom-call | tf_op jit(solution)/shard_map/pallas_call | solution.py:258
  16.0 2.4 %collective-permute-start.5 = (bf16[128,1024]{1,0:T(8,128)(2,1)S(1)}, bf16[128,1024]{1,0:T(8,128)(2,1)S(1)}, u32[]{:S(2)}, u32[]{:S(2)}) collective-permute-start(bf16[128,1024]{1,0:T(8,128)(2,1)S(1)} %collective-permute-done.4.refs_2_), channel_id=1, source_target_pairs={{0,4},{4,0},{8,12},{12,8},{16,20},{20,16},{24,28},{28,24},{1,5},{5... | collective-permute-start | bytes 786440 | tf_op jit(solution)/shard_map/ppermute | solution.py:290
  18.4 1.5 %collective-permute-start.7 = (bf16[512,256]{1,0:T(8,128)(2,1)S(1)}, bf16[512,256]{1,0:T(8,128)(2,1)S(1)}, u32[]{:S(2)}, u32[]{:S(2)}) collective-permute-start(bf16[512,256]{1,0:T(8,128)(2,1)S(1)} %get-tuple-element.43.refs_0_), channel_id=1, source_target_pairs={{0,2},{1,3},{2,0},{3,1},{4,6},{5,7},{6,4},{7,5},{8,10},{9,11},{10,... | collective-permute-start | bytes 786440 | tf_op jit(solution)/shard_map/ppermute | solution.py:287
  19.9 2.0 %collective-permute-done.3.refs_6_ = bf16[128,1024]{1,0:T(8,128)(2,1)S(1)} collective-permute-done((bf16[128,1024]{1,0:T(8,128)(2,1)}, bf16[128,1024]{1,0:T(8,128)(2,1)S(1)}, u32[]{:S(2)}, u32[]{:S(2)}) %collective-permute-start.3) | collective-permute-done | bytes 262176 | tf_op jit(solution)/shard_map/ppermute | solution.py:290
  23.2 1.5 %collective-permute-done.7.refs_2_ = bf16[512,256]{1,0:T(8,128)(2,1)S(1)} collective-permute-done((bf16[512,256]{1,0:T(8,128)(2,1)S(1)}, bf16[512,256]{1,0:T(8,128)(2,1)S(1)}, u32[]{:S(2)}, u32[]{:S(2)}) %collective-permute-start.7) | collective-permute-done | bytes 262176 | tf_op jit(solution)/shard_map/ppermute | solution.py:287
  24.7 4.1 %collective-permute-start.9 = (bf16[128,1024]{1,0:T(8,128)(2,1)S(1)}, bf16[128,1024]{1,0:T(8,128)(2,1)S(1)}, u32[]{:S(2)}, u32[]{:S(2)}) collective-permute-start(bf16[128,1024]{1,0:T(8,128)(2,1)S(1)} %copy-done.2), channel_id=1, source_target_pairs={{0,16},{4,20},{8,24},{12,28},{16,0},{20,4},{24,8},{28,12},{1,17},{... | collective-permute-start | bytes 786440 | tf_op jit(solution)/shard_map/ppermute | solution.py:290
  29.3 1.7 %shard_map.78 = (f32[128,1024]{1,0:T(8,128)S(1)}, bf16[128,1024]{1,0:T(8,128)(2,1)S(1)}, f32[128,1024]{1,0:T(8,128)S(1)}, bf16[128,1024]{1,0:T(8,128)(2,1)S(1)},...) custom-call(bf16[512,256]{1,0:T(8,128)(2,1)S(1)} %get-tuple-element., ...), custom_call_target="tpu_custom_call" | custom-call | tf_op jit(solution)/shard_map/pallas_call | solution.py:258
  31.0 1.6 %collective-permute-start.10 = (bf16[128,1024]{1,0:T(8,128)(2,1)S(1)}, bf16[128,1024]{1,0:T(8,128)(2,1)S(1)}, u32[]{:S(2)}, u32[]{:S(2)}) collective-permute-start(bf16[128,1024]{1,0:T(8,128)(2,1)S(1)} %get-tuple-element.44), channel_id=1, source_target_pairs={{0,4},{4,0},{8,12},{12,8},{16,20},{20,16},{24,28},{28,24},{1,5},{5... | collective-permute-start | bytes 786440 | tf_op jit(solution)/shard_map/ppermute | solution.py:290
  32.6 8.8 %collective-permute-done.9.refs_4_ = bf16[128,1024]{1,0:T(8,128)(2,1)S(1)} collective-permute-done((bf16[128,1024]{1,0:T(8,128)(2,1)S(1)}, bf16[128,1024]{1,0:T(8,128)(2,1)S(1)}, u32[]{:S(2)}, u32[]{:S(2)}) %collective-permute-start.9) | collective-permute-done | bytes 262176 | tf_op jit(solution)/shard_map/ppermute | solution.py:290
  41.4 1.5 %collective-permute-done.10 = bf16[128,1024]{1,0:T(8,128)(2,1)S(1)} collective-permute-done((bf16[128,1024]{1,0:T(8,128)(2,1)S(1)}, bf16[128,1024]{1,0:T(8,128)(2,1)S(1)}, u32[]{:S(2)}, u32[]{:S(2)}) %collective-permute-start.10) | collective-permute-done | bytes 262176 | tf_op jit(solution)/shard_map/ppermute | solution.py:290
  43.2 2.4 %collective-permute-start.16 = (bf16[128,1024]{1,0:T(8,128)(2,1)S(1)}, bf16[128,1024]{1,0:T(8,128)(2,1)S(1)}, u32[]{:S(2)}, u32[]{:S(2)}) collective-permute-start(bf16[128,1024]{1,0:T(8,128)(2,1)S(1)} %add_convert_fusion.2), channel_id=1, source_target_pairs={{0,24},{4,28},{8,16},{12,20},{16,8},{20,12},{24,0},{28,4},{1,25},{... | collective-permute-start | bytes 786440 | tf_op jit(solution)/shard_map/ppermute | solution.py:290
  46.6 1.7 %shard_map.81 = (bf16[1024,512]{1,0:T(8,128)(2,1)S(1)}, f32[1024,256]{1,0:T(8,128)S(1)}, f32[1024,256]{1,0:T(8,128)S(1)}, f32[1024,256]{1,0:T(8,128)S(1)}) custom-call(bf16[1024,256]{1,0:T(8,128)(2,1)S(1)} %get-tuple-element.35.hidden_ref, bf16[32,384]{1,0:T(8,128)(2,1)S(1)} %collective-permute-done.even_ref, ...), custom_call_target="tpu_custom_call" | custom-call | tf_op jit(solution)/shard_map/pallas_call | solution.py:258
  48.4 3.7 %collective-permute-done.12.refs_5_ = bf16[128,1024]{1,0:T(8,128)(2,1)S(1)} collective-permute-done((bf16[128,1024]{1,0:T(8,128)(2,1)S(1)}, bf16[128,1024]{1,0:T(8,128)(2,1)S(1)}, u32[]{:S(2)}, u32[]{:S(2)}) %collective-permute-start.12) | collective-permute-done | bytes 262176 | tf_op jit(solution)/shard_map/ppermute | solution.py:290
  52.1 2.5 %shard_map.79 = (bf16[528,256]{1,0:T(8,128)(2,1)S(1)}, bf16[528,256]{1,0:T(8,128)(2,1)S(1)}, bf16[528,256]{1,0:T(8,128)(2,1)S(1)}, bf16[528,256]{1,0:T(8,128)(2,1)S(1)}, bf16[1024,1024]{1,0:T(8,128)(2,1)}) custom-call(bf16[512,1024]{1,0:T(8,128)(2,1)S(1)} %copy-done, bf16[32,384]{1,0:T(8,128)(2,1)S(1)} %collective-permute-done.even_ref, ...), custom_call_target="tpu_custom_call" | custom-call | tf_op jit(solution)/shard_map/pallas_call | solution.py:258
  54.9 1.5 %collective-permute-start.13 = (bf16[528,256]{1,0:T(8,128)(2,1)S(1)}, bf16[528,256]{1,0:T(8,128)(2,1)S(1)}, u32[]{:S(2)}, u32[]{:S(2)}) collective-permute-start(bf16[528,256]{1,0:T(8,128)(2,1)S(1)} %get-tuple-element.50), channel_id=1, source_target_pairs={{0,2},{1,3},{2,0},{3,1},{4,6},{5,7},{6,4},{7,5},{8,10},{9,11},{10,... | collective-permute-start | bytes 811016 | tf_op jit(solution)/shard_map/ppermute | solution.py:287
  57.8 2.7 %collective-permute-start.17 = (bf16[128,1024]{1,0:T(8,128)(2,1)S(1)}, bf16[128,1024]{1,0:T(8,128)(2,1)S(1)}, u32[]{:S(2)}, u32[]{:S(2)}) collective-permute-start(bf16[128,1024]{1,0:T(8,128)(2,1)S(1)} %add_convert_fusion.1), channel_id=1, source_target_pairs={{0,16},{4,20},{8,24},{12,28},{16,0},{20,4},{24,8},{28,12},{1,17},{... | collective-permute-start | bytes 786440 | tf_op jit(solution)/shard_map/ppermute | solution.py:290
  61.8 5.2 %collective-permute-start.19 = (bf16[128,1024]{1,0:T(8,128)(2,1)S(1)}, bf16[128,1024]{1,0:T(8,128)(2,1)S(1)}, u32[]{:S(2)}, u32[]{:S(2)}) collective-permute-start(bf16[128,1024]{1,0:T(8,128)(2,1)S(1)} %add_convert_fusion), channel_id=1, source_target_pairs={{0,8},{4,12},{8,0},{12,4},{16,24},{20,28},{24,16},{28,20},{1,9},{5... | collective-permute-start | bytes 786440 | tf_op jit(solution)/shard_map/ppermute | solution.py:290
  67.2 2.4 %shard_map.80 = bf16[512,1024]{1,0:T(8,128)(2,1)} custom-call(bf16[512,256]{1,0:T(8,128)(2,1)S(1)} %get-tuple-element.43.refs_0_, bf16[512,256]{1,0:T(8,128)(2,1)S(1)} %collective-permute-done.6.refs_1_, bf16[512,256]{1,0:T(8,128)(2,1)S(1)} %collective-permute-done.7.refs_2_, bf16[512,256]{1,0:T(8,128)(2,1)S(1)} %collective-permute-done.8.refs_3_, ...), custom_call_target="tpu_custom_call" | custom-call | tf_op jit(solution)/shard_map/pallas_call | solution.py:258
  69.6 2.3 %shard_map.82 = bf16[1024,256]{1,0:T(8,128)(2,1)} custom-call(bf16[528,256]{1,0:T(8,128)(2,1)S(1)} %get-tuple-element.61.refs_0_, bf16[528,256]{1,0:T(8,128)(2,1)S(1)} %collective-permute-done.20.refs_1_, bf16[528,256]{1,0:T(8,128)(2,1)S(1)} %collective-permute-done.13.refs_2_, bf16[528,256]{1,0:T(8,128)(2,1)S(1)} %collective-permute-done.21.refs_3_, ...), custom_call_target="tpu_custom_call" | custom-call | tf_op jit(solution)/shard_map/pallas_call | solution.py:258
  71.8 3.1 %collective-permute-done.19 = bf16[128,1024]{1,0:T(8,128)(2,1)S(1)} collective-permute-done((bf16[128,1024]{1,0:T(8,128)(2,1)S(1)}, bf16[128,1024]{1,0:T(8,128)(2,1)S(1)}, u32[]{:S(2)}, u32[]{:S(2)}) %collective-permute-start.19) | collective-permute-done | bytes 262176 | tf_op jit(solution)/shard_map/ppermute | solution.py:290
  (41 shorter events, 10.6 us)
Async XLA Ops:
  0.6 28.7 %copy-start = (bf16[512,1024]{1,0:T(8,128)(2,1)S(1)}, bf16[512,1024]{1,0:T(8,128)(2,1)}, u32[]{:S(2)}) copy-start(bf16[512,1024]{1,0:T(8,128)(2,1)} %grad_ref.1) | copy-start | bytes 3145732
  0.6 24.1 %copy-start.2 = (bf16[128,1024]{1,0:T(8,128)(2,1)S(1)}, bf16[128,1024]{1,0:T(8,128)(2,1)}, u32[]{:S(2)}) copy-start(bf16[128,1024]{1,0:T(8,128)(2,1)} %refs_0_) | copy-start | bytes 786436
  2.5 13.4 %collective-permute-start.2 = (bf16[128,1024]{1,0:T(8,128)(2,1)}, bf16[128,1024]{1,0:T(8,128)(2,1)S(1)}, u32[]{:S(2)}, u32[]{:S(2)}) collective-permute-start(bf16[128,1024]{1,0:T(8,128)(2,1)} %refs_0_), channel_id=1, source_target_pairs={{0,4},{4,0},{8,12},{12,8},{16,20},{20,16},{24,28},{28,24},{1,5},{5... | collective-permute-start | bytes 786440 | tf_op jit(solution)/shard_map/ppermute | solution.py:290
  5.6 10.4 %collective-permute-start.4 = (bf16[128,1024]{1,0:T(8,128)(2,1)}, bf16[128,1024]{1,0:T(8,128)(2,1)S(1)}, u32[]{:S(2)}, u32[]{:S(2)}) collective-permute-start(bf16[128,1024]{1,0:T(8,128)(2,1)} %refs_0_), channel_id=1, source_target_pairs={{0,8},{4,12},{8,0},{12,4},{16,24},{20,28},{24,16},{28,20},{1,9},{5... | collective-permute-start | bytes 786440 | tf_op jit(solution)/shard_map/ppermute | solution.py:290
  7.2 6.0 %collective-permute-start.1 = (bf16[32,384]{1,0:T(8,128)(2,1)S(1)}, bf16[32,384]{1,0:T(8,128)(2,1)S(1)}, u32[]{:S(2)}, u32[]{:S(2)}) collective-permute-start(bf16[32,384]{1,0:T(8,128)(2,1)S(1)} %get-tuple-element.37), channel_id=1, source_target_pairs={{4,8},{12,16},{20,24},{8,4},{16,12},{24,20},{5,9},{13,17},{21,25},... | collective-permute-start | bytes 73736 | tf_op jit(solution)/shard_map/ppermute | solution.py:317
  7.8 5.4 %collective-permute-start = (bf16[32,384]{1,0:T(8,128)(2,1)S(1)}, bf16[32,384]{1,0:T(8,128)(2,1)S(1)}, u32[]{:S(2)}, u32[]{:S(2)}) collective-permute-start(bf16[32,384]{1,0:T(8,128)(2,1)S(1)} %get-tuple-element.36), channel_id=1, source_target_pairs={{0,4},{4,0},{8,12},{12,8},{16,20},{20,16},{24,28},{28,24},{1,5},{5... | collective-permute-start | bytes 73736 | tf_op jit(solution)/shard_map/ppermute | solution.py:290
  11.0 10.8 %collective-permute-start.3 = (bf16[128,1024]{1,0:T(8,128)(2,1)}, bf16[128,1024]{1,0:T(8,128)(2,1)S(1)}, u32[]{:S(2)}, u32[]{:S(2)}) collective-permute-start(bf16[128,1024]{1,0:T(8,128)(2,1)} %refs_0_), channel_id=1, source_target_pairs={{0,24},{4,28},{8,16},{12,20},{16,8},{20,12},{24,0},{28,4},{1,25},{... | collective-permute-start | bytes 786440 | tf_op jit(solution)/shard_map/ppermute | solution.py:290
  16.0 7.2 %collective-permute-start.5 = (bf16[128,1024]{1,0:T(8,128)(2,1)S(1)}, bf16[128,1024]{1,0:T(8,128)(2,1)S(1)}, u32[]{:S(2)}, u32[]{:S(2)}) collective-permute-start(bf16[128,1024]{1,0:T(8,128)(2,1)S(1)} %collective-permute-done.4.refs_2_), channel_id=1, source_target_pairs={{0,4},{4,0},{8,12},{12,8},{16,20},{20,16},{24,28},{28,24},{1,5},{5... | collective-permute-start | bytes 786440 | tf_op jit(solution)/shard_map/ppermute | solution.py:290
  18.4 6.4 %collective-permute-start.7 = (bf16[512,256]{1,0:T(8,128)(2,1)S(1)}, bf16[512,256]{1,0:T(8,128)(2,1)S(1)}, u32[]{:S(2)}, u32[]{:S(2)}) collective-permute-start(bf16[512,256]{1,0:T(8,128)(2,1)S(1)} %get-tuple-element.43.refs_0_), channel_id=1, source_target_pairs={{0,2},{1,3},{2,0},{3,1},{4,6},{5,7},{6,4},{7,5},{8,10},{9,11},{10,... | collective-permute-start | bytes 786440 | tf_op jit(solution)/shard_map/ppermute | solution.py:287
  23.2 6.1 %collective-permute-start.6 = (bf16[512,256]{1,0:T(8,128)(2,1)S(1)}, bf16[512,256]{1,0:T(8,128)(2,1)S(1)}, u32[]{:S(2)}, u32[]{:S(2)}) collective-permute-start(bf16[512,256]{1,0:T(8,128)(2,1)S(1)} %get-tuple-element.43.refs_0_), channel_id=1, source_target_pairs={{0,1},{1,0},{2,3},{3,2},{4,5},{5,4},{6,7},{7,6},{8,9},{9,8},{10,11... | collective-permute-start | bytes 786440 | tf_op jit(solution)/shard_map/ppermute | solution.py:287
  24.7 4.6 %collective-permute-start.8 = (bf16[512,256]{1,0:T(8,128)(2,1)S(1)}, bf16[512,256]{1,0:T(8,128)(2,1)S(1)}, u32[]{:S(2)}, u32[]{:S(2)}) collective-permute-start(bf16[512,256]{1,0:T(8,128)(2,1)S(1)} %collective-permute-done.7.refs_2_), channel_id=1, source_target_pairs={{0,1},{1,0},{2,3},{3,2},{4,5},{5,4},{6,7},{7,6},{8,9},{9,8},{10,11... | collective-permute-start | bytes 786440 | tf_op jit(solution)/shard_map/ppermute | solution.py:287
  24.7 16.6 %collective-permute-start.9 = (bf16[128,1024]{1,0:T(8,128)(2,1)S(1)}, bf16[128,1024]{1,0:T(8,128)(2,1)S(1)}, u32[]{:S(2)}, u32[]{:S(2)}) collective-permute-start(bf16[128,1024]{1,0:T(8,128)(2,1)S(1)} %copy-done.2), channel_id=1, source_target_pairs={{0,16},{4,20},{8,24},{12,28},{16,0},{20,4},{24,8},{28,12},{1,17},{... | collective-permute-start | bytes 786440 | tf_op jit(solution)/shard_map/ppermute | solution.py:290
  28.8 12.6 %collective-permute-start.11 = (bf16[128,1024]{1,0:T(8,128)(2,1)S(1)}, bf16[128,1024]{1,0:T(8,128)(2,1)S(1)}, u32[]{:S(2)}, u32[]{:S(2)}) collective-permute-start(bf16[128,1024]{1,0:T(8,128)(2,1)S(1)} %collective-permute-done.3.refs_6_), channel_id=1, source_target_pairs={{0,4},{4,0},{8,12},{12,8},{16,20},{20,16},{24,28},{28,24},{1,5},{5... | collective-permute-start | bytes 786440 | tf_op jit(solution)/shard_map/ppermute | solution.py:290
  31.0 11.8 %collective-permute-start.10 = (bf16[128,1024]{1,0:T(8,128)(2,1)S(1)}, bf16[128,1024]{1,0:T(8,128)(2,1)S(1)}, u32[]{:S(2)}, u32[]{:S(2)}) collective-permute-start(bf16[128,1024]{1,0:T(8,128)(2,1)S(1)} %get-tuple-element.44), channel_id=1, source_target_pairs={{0,4},{4,0},{8,12},{12,8},{16,20},{20,16},{24,28},{28,24},{1,5},{5... | collective-permute-start | bytes 786440 | tf_op jit(solution)/shard_map/ppermute | solution.py:290
  42.8 9.2 %collective-permute-start.12 = (bf16[128,1024]{1,0:T(8,128)(2,1)S(1)}, bf16[128,1024]{1,0:T(8,128)(2,1)S(1)}, u32[]{:S(2)}, u32[]{:S(2)}) collective-permute-start(bf16[128,1024]{1,0:T(8,128)(2,1)S(1)} %collective-permute-done.9.refs_4_), channel_id=1, source_target_pairs={{0,4},{4,0},{8,12},{12,8},{16,20},{20,16},{24,28},{28,24},{1,5},{5... | collective-permute-start | bytes 786440 | tf_op jit(solution)/shard_map/ppermute | solution.py:290
  43.2 11.4 %collective-permute-start.16 = (bf16[128,1024]{1,0:T(8,128)(2,1)S(1)}, bf16[128,1024]{1,0:T(8,128)(2,1)S(1)}, u32[]{:S(2)}, u32[]{:S(2)}) collective-permute-start(bf16[128,1024]{1,0:T(8,128)(2,1)S(1)} %add_convert_fusion.2), channel_id=1, source_target_pairs={{0,24},{4,28},{8,16},{12,20},{16,8},{20,12},{24,0},{28,4},{1,25},{... | collective-permute-start | bytes 786440 | tf_op jit(solution)/shard_map/ppermute | solution.py:290
  45.6 12.1 %collective-permute-start.14 = (bf16[128,1024]{1,0:T(8,128)(2,1)S(1)}, bf16[128,1024]{1,0:T(8,128)(2,1)S(1)}, u32[]{:S(2)}, u32[]{:S(2)}) collective-permute-start(bf16[128,1024]{1,0:T(8,128)(2,1)S(1)} %get-tuple-element.51), channel_id=1, source_target_pairs={{0,4},{4,0},{8,12},{12,8},{16,20},{20,16},{24,28},{28,24},{1,5},{5... | collective-permute-start | bytes 786440 | tf_op jit(solution)/shard_map/ppermute | solution.py:290
  54.6 7.1 %collective-permute-start.18 = (bf16[128,1024]{1,0:T(8,128)(2,1)S(1)}, bf16[128,1024]{1,0:T(8,128)(2,1)S(1)}, u32[]{:S(2)}, u32[]{:S(2)}) collective-permute-start(bf16[128,1024]{1,0:T(8,128)(2,1)S(1)} %get-tuple-element.60), channel_id=1, source_target_pairs={{0,4},{4,0},{8,12},{12,8},{16,20},{20,16},{24,28},{28,24},{1,5},{5... | collective-permute-start | bytes 786440 | tf_op jit(solution)/shard_map/ppermute | solution.py:290
  54.9 12.0 %collective-permute-start.13 = (bf16[528,256]{1,0:T(8,128)(2,1)S(1)}, bf16[528,256]{1,0:T(8,128)(2,1)S(1)}, u32[]{:S(2)}, u32[]{:S(2)}) collective-permute-start(bf16[528,256]{1,0:T(8,128)(2,1)S(1)} %get-tuple-element.50), channel_id=1, source_target_pairs={{0,2},{1,3},{2,0},{3,1},{4,6},{5,7},{6,4},{7,5},{8,10},{9,11},{10,... | collective-permute-start | bytes 811016 | tf_op jit(solution)/shard_map/ppermute | solution.py:287
  57.8 14.1 %collective-permute-start.17 = (bf16[128,1024]{1,0:T(8,128)(2,1)S(1)}, bf16[128,1024]{1,0:T(8,128)(2,1)S(1)}, u32[]{:S(2)}, u32[]{:S(2)}) collective-permute-start(bf16[128,1024]{1,0:T(8,128)(2,1)S(1)} %add_convert_fusion.1), channel_id=1, source_target_pairs={{0,16},{4,20},{8,24},{12,28},{16,0},{20,4},{24,8},{28,12},{1,17},{... | collective-permute-start | bytes 786440 | tf_op jit(solution)/shard_map/ppermute | solution.py:290
  60.5 9.1 %collective-permute-start.20 = (bf16[528,256]{1,0:T(8,128)(2,1)S(1)}, bf16[528,256]{1,0:T(8,128)(2,1)S(1)}, u32[]{:S(2)}, u32[]{:S(2)}) collective-permute-start(bf16[528,256]{1,0:T(8,128)(2,1)S(1)} %get-tuple-element.62), channel_id=1, source_target_pairs={{0,1},{1,0},{2,3},{3,2},{4,5},{5,4},{6,7},{7,6},{8,9},{9,8},{10,11... | collective-permute-start | bytes 811016 | tf_op jit(solution)/shard_map/ppermute | solution.py:287
  60.5 9.1 %collective-permute-start.21 = (bf16[528,256]{1,0:T(8,128)(2,1)S(1)}, bf16[528,256]{1,0:T(8,128)(2,1)S(1)}, u32[]{:S(2)}, u32[]{:S(2)}) collective-permute-start(bf16[528,256]{1,0:T(8,128)(2,1)S(1)} %get-tuple-element.63), channel_id=1, source_target_pairs={{0,3},{1,2},{2,1},{3,0},{4,7},{5,6},{6,5},{7,4},{8,11},{9,10},{10,... | collective-permute-start | bytes 811016 | tf_op jit(solution)/shard_map/ppermute | solution.py:287
  61.8 13.2 %collective-permute-start.19 = (bf16[128,1024]{1,0:T(8,128)(2,1)S(1)}, bf16[128,1024]{1,0:T(8,128)(2,1)S(1)}, u32[]{:S(2)}, u32[]{:S(2)}) collective-permute-start(bf16[128,1024]{1,0:T(8,128)(2,1)S(1)} %add_convert_fusion), channel_id=1, source_target_pairs={{0,8},{4,12},{8,0},{12,4},{16,24},{20,28},{24,16},{28,20},{1,9},{5... | collective-permute-start | bytes 786440 | tf_op jit(solution)/shard_map/ppermute | solution.py:290
  66.9 8.0 %collective-permute-start.15 = (bf16[128,1024]{1,0:T(8,128)(2,1)S(1)}, bf16[128,1024]{1,0:T(8,128)(2,1)S(1)}, u32[]{:S(2)}, u32[]{:S(2)}) collective-permute-start(bf16[128,1024]{1,0:T(8,128)(2,1)S(1)} %get-tuple-element.52), channel_id=1, source_target_pairs={{0,4},{4,0},{8,12},{12,8},{16,20},{20,16},{24,28},{28,24},{1,5},{5... | collective-permute-start | bytes 786440 | tf_op jit(solution)/shard_map/ppermute | solution.py:290
  (3 other events, 14.1 us)

commit v6 on v5

--- a/solution.py
+++ b/solution.py
@@ -318,9 +318,9 @@
 
     if staged:
         pieces = [in_weight] + [None] * (n_seq - 1)
-        pieces[1] = trade(in_weight, 1)
-        for step in range(2, n_seq, 2):
-            pieces[step] = trade(in_weight, step)
+        for step in (1, 2, 4):
+            first = even if step == 1 else odd
+            pieces[step] = trade(after((in_weight, first))[0], step)
     else:
         pieces = [lax.all_gather(in_weight, "seq", axis=0, tiled=True)]
 
@@ -335,12 +335,11 @@
     )
 
     if staged:
-        low = after((low, (pieces[1],)))[0]
-        pieces[3] = trade(after((pieces[2], (low,)))[0], 1)
+        pieces[3] = trade(after((pieces[2], (low, pieces[1],)))[0], 1)
     parts = [low]
     for step in reversed([1 << bit for bit in range(n_mp.bit_length() - 1)]):
         if staged and step == 1:
-            parts[0] = after((parts[0], (pieces[6], pieces[3],)))[0]
+            parts[0] = after((parts[0], (pieces[4], pieces[3],)))[0]
         parts = [part for held in parts for part in (held, swap(held, step))]
     onehot, share, delta, slope = call(
         spread_kernel,
@@ -368,10 +367,15 @@
     if staged:
         fetched = {}
         pieces[7] = trade(after((pieces[6], (pieces[3],)))[0], 1)
+        pieces[5] = trade(pieces[4], 1)
+        pieces[6] = trade(pieces[4], 2)
+        pieces[7] = trade(after((pieces[6], (pieces[5],)))[0], 1)
         fetched[7] = trade(terms[7], 1)
-        fetched[5] = trade(terms[5], 1)
-        pieces[5] = trade(after((pieces[4], (fetched[7], pieces[7],)))[0], 1)
-
+        fetched[6] = trade((terms[6] + fetched[7].astype(F32)).astype(BF16), 2)
+        fetched[5] = trade(after((terms[5], (pieces[7],)))[0], 1)
+
+    if staged:
+        latent_grad, _ = after((latent_grad, (fetched[7],)))
     *partials, weight_full = call(
         functools.partial(partial_kernel, n_mp),
         (shape((slots + EDGE, feats), BF16),) * n_mp + (shape((latent_dim, width), BF16),),
@@ -383,13 +387,13 @@
     grads = [partials[0]] + [swap(partials[step], step) for step in range(1, n_mp)]
 
     if staged:
-        fetched[6] = trade((terms[6] + fetched[7].astype(F32)).astype(BF16), 6)
-        fetched[3] = trade(after((terms[3], (fetched[6], weight_full, share,)))[0], 1)
-        fetched[4] = trade((terms[4] + fetched[5].astype(F32)).astype(BF16), 4)
-        fetched[1] = trade(after((terms[1], (grads[2], fetched[5],)))[0], 1)
+        fetched[3] = trade(after((terms[3], (fetched[5], fetched[6], weight_full, share,)))[0], 1)
+        pair = terms[4] + fetched[5].astype(F32) + fetched[6].astype(F32)
+        fetched[4] = trade(pair.astype(BF16), 4)
+        fetched[1] = trade(after((terms[1], (grads[2],)))[0], 1)
         fetched[2] = trade((terms[2] + fetched[3].astype(F32)).astype(BF16), 2)
         grad_weight = terms[0] + fetched[1].astype(F32)
-        for step in (6, 4, 2):
+        for step in (4, 2):
             grad_weight = grad_weight + fetched[step].astype(F32)
     else:
         received = lax.all_to_all(terms[0], "seq", split_axis=0, concat_axis=0, tiled=True)

time: 76.1 us -> 76.2 us (level)
  waiting for transfers between devices: 23.8 us -> 33 us
  starting transfers between devices: 35 us -> 25.9 us
    ppermute x15, waiting for transfers between devices: 22.2 us -> 33 us  [trade(): return lax.ppermute(value, 'seq', [(i, i ^ step) for i in range(n_seq)])]
    ppermute x15, starting transfers between devices: 30.7 us -> 20.4 us  [trade(): return lax.ppermute(value, 'seq', [(i, i ^ step) for i in range(n_seq)])]
    ppermute x6, waiting for transfers between devices: 1.56 us -> 0.02 us  [swap(): return lax.ppermute(value, 'mp', [(i, i ^ step) for i in range(n_mp)])]
    ppermute x6, starting transfers between devices: 3.64 us -> 4.65 us  [swap(): return lax.ppermute(value, 'mp', [(i, i ^ step) for i in range(n_mp)])]
  transfers between devices with their start and end apart: 22 -> 22, of which waited for: 9 -> 11; matrix products, arithmetic and copies ran while one was open for 0% -> 0% of each run, Pallas kernels for 17% -> 17%
where the time goes in v6:
time: 76.2 us; the launch traced here: 76 us
  waiting for transfers between devices  33 us (43%)
  starting transfers between devices  25.9 us (34%)
  Pallas kernels  13.8 us (18%)
  local copies, waits for them, and re-layouts  1.44 us (2%)
  other arithmetic  1.17 us (2%)
    ppermute x15, waiting for transfers between devices, trade(): return lax.ppermute(value, 'seq', [(i, i ^ step) for i in range(n_seq)])  33 us
    ppermute x15, starting transfers between devices, trade(): return lax.ppermute(value, 'seq', [(i, i ^ step) for i in range(n_seq)])  20.4 us
    pallas_call x7, Pallas kernels, call(): pl.pallas_call(kernel, out_shape=out_shape, in_specs=in_specs, out_specs=...  13.8 us
    ppermute x6, starting transfers between devices, swap(): return lax.ppermute(value, 'mp', [(i, i ^ step) for i in range(n_mp)])  4.65 us
  transfers between devices with their start and end apart: 22, of which 11 were waited for; matrix products, arithmetic and copies ran while one was open for 0% of the time, Pallas kernels for 17%

profile of v6, /device:TPU:0, one launch (start us, length us, event | category | flops | bytes accessed | tf_op | source)
XLA Modules:
  0.0 76.0 jit_solution(8108467992451949759)
XLA Ops:
  3.3 5.8 %collective-permute-start = (bf16[32,384]{1,0:T(8,128)(2,1)S(1)}, bf16[32,384]{1,0:T(8,128)(2,1)S(1)}, u32[]{:S(2)}, u32[]{:S(2)}) collective-permute-start(bf16[32,384]{1,0:T(8,128)(2,1)S(1)} %get-tuple-element.38), channel_id=1, source_target_pairs={{0,4},{4,0},{8,12},{12,8},{16,20},{20,16},{24,28},{28,24},{1,5},{5... | collective-permute-start | bytes 73736 | tf_op jit(solution)/shard_map/ppermute | solution.py:290
  9.1 1.8 %collective-permute-done.even_ref = bf16[32,384]{1,0:T(8,128)(2,1)S(1)} collective-permute-done((bf16[32,384]{1,0:T(8,128)(2,1)S(1)}, bf16[32,384]{1,0:T(8,128)(2,1)S(1)}, u32[]{:S(2)}, u32[]{:S(2)}) %collective-permute-start) | collective-permute-done | bytes 24608 | tf_op jit(solution)/shard_map/ppermute | solution.py:290
  10.9 2.0 %collective-permute-start.4 = (bf16[128,1024]{1,0:T(8,128)(2,1)}, bf16[128,1024]{1,0:T(8,128)(2,1)S(1)}, u32[]{:S(2)}, u32[]{:S(2)}) collective-permute-start(bf16[128,1024]{1,0:T(8,128)(2,1)} %refs_0_), channel_id=1, source_target_pairs={{0,4},{4,0},{8,12},{12,8},{16,20},{20,16},{24,28},{28,24},{1,5},{5... | collective-permute-start | bytes 786440 | tf_op jit(solution)/shard_map/ppermute | solution.py:290
  13.0 1.6 %collective-permute-start.3 = (bf16[128,1024]{1,0:T(8,128)(2,1)}, bf16[128,1024]{1,0:T(8,128)(2,1)S(1)}, u32[]{:S(2)}, u32[]{:S(2)}) collective-permute-start(bf16[128,1024]{1,0:T(8,128)(2,1)} %refs_0_), channel_id=1, source_target_pairs={{0,8},{4,12},{8,0},{12,4},{16,24},{20,28},{24,16},{28,20},{1,9},{5... | collective-permute-start | bytes 786440 | tf_op jit(solution)/shard_map/ppermute | solution.py:290
  16.2 2.1 %shard_map.77 = (bf16[512,256]{1,0:T(8,128)(2,1)S(1)}, f32[512,256]{1,0:T(8,128)S(1)}, f32[512,256]{1,0:T(8,128)S(1)}) custom-call(bf16[1024,256]{1,0:T(8,128)(2,1)S(1)} %get-tuple-element.37.hidden_ref, bf16[32,384]{1,0:T(8,128)(2,1)S(1)} %collective-permute-done.even_ref, bf16[32,384]{1,0:T(8,128)(2,1)S(1)} %collective-permute-done.1.odd_ref, ...), custom_call_target="tpu_custom_call" | custom-call | tf_op jit(solution)/shard_map/pallas_call | solution.py:258
  18.3 1.6 %collective-permute-start.7 = (bf16[512,256]{1,0:T(8,128)(2,1)S(1)}, bf16[512,256]{1,0:T(8,128)(2,1)S(1)}, u32[]{:S(2)}, u32[]{:S(2)}) collective-permute-start(bf16[512,256]{1,0:T(8,128)(2,1)S(1)} %get-tuple-element.46.refs_0_), channel_id=1, source_target_pairs={{0,2},{1,3},{2,0},{3,1},{4,6},{5,7},{6,4},{7,5},{8,10},{9,11},{10,... | collective-permute-start | bytes 786440 | tf_op jit(solution)/shard_map/ppermute | solution.py:287
  19.9 5.1 %collective-permute-done.3.refs_2_ = bf16[128,1024]{1,0:T(8,128)(2,1)S(1)} collective-permute-done((bf16[128,1024]{1,0:T(8,128)(2,1)}, bf16[128,1024]{1,0:T(8,128)(2,1)S(1)}, u32[]{:S(2)}, u32[]{:S(2)}) %collective-permute-start.3) | collective-permute-done | bytes 262176 | tf_op jit(solution)/shard_map/ppermute | solution.py:290
  25.2 2.3 %collective-permute-done.2.refs_4_ = bf16[128,1024]{1,0:T(8,128)(2,1)S(1)} collective-permute-done((bf16[128,1024]{1,0:T(8,128)(2,1)}, bf16[128,1024]{1,0:T(8,128)(2,1)S(1)}, u32[]{:S(2)}, u32[]{:S(2)}) %collective-permute-start.2) | collective-permute-done | bytes 262176 | tf_op jit(solution)/shard_map/ppermute | solution.py:290
  28.2 4.4 %collective-permute-done.5.refs_3_ = bf16[128,1024]{1,0:T(8,128)(2,1)S(1)} collective-permute-done((bf16[128,1024]{1,0:T(8,128)(2,1)S(1)}, bf16[128,1024]{1,0:T(8,128)(2,1)S(1)}, u32[]{:S(2)}, u32[]{:S(2)}) %collective-permute-start.5) | collective-permute-done | bytes 262176 | tf_op jit(solution)/shard_map/ppermute | solution.py:290
  32.6 1.3 %collective-permute-done.11.refs_6_ = bf16[128,1024]{1,0:T(8,128)(2,1)S(1)} collective-permute-done((bf16[128,1024]{1,0:T(8,128)(2,1)S(1)}, bf16[128,1024]{1,0:T(8,128)(2,1)S(1)}, u32[]{:S(2)}, u32[]{:S(2)}) %collective-permute-start.11) | collective-permute-done | bytes 262176 | tf_op jit(solution)/shard_map/ppermute | solution.py:290
  33.8 1.5 %collective-permute-done.10.refs_5_ = bf16[128,1024]{1,0:T(8,128)(2,1)S(1)} collective-permute-done((bf16[128,1024]{1,0:T(8,128)(2,1)S(1)}, bf16[128,1024]{1,0:T(8,128)(2,1)S(1)}, u32[]{:S(2)}, u32[]{:S(2)}) %collective-permute-start.10) | collective-permute-done | bytes 262176 | tf_op jit(solution)/shard_map/ppermute | solution.py:290
  35.8 1.7 %shard_map.78 = (f32[128,1024]{1,0:T(8,128)S(1)}, bf16[128,1024]{1,0:T(8,128)(2,1)S(1)}, f32[128,1024]{1,0:T(8,128)S(1)}, bf16[128,1024]{1,0:T(8,128)(2,1)S(1)},...) custom-call(bf16[512,256]{1,0:T(8,128)(2,1)S(1)} %get-tuple-element., ...), custom_call_target="tpu_custom_call" | custom-call | tf_op jit(solution)/shard_map/pallas_call | solution.py:258
  37.5 1.7 %collective-permute-start.9 = (bf16[128,1024]{1,0:T(8,128)(2,1)S(1)}, bf16[128,1024]{1,0:T(8,128)(2,1)S(1)}, u32[]{:S(2)}, u32[]{:S(2)}) collective-permute-start(bf16[128,1024]{1,0:T(8,128)(2,1)S(1)} %get-tuple-element.47), channel_id=1, source_target_pairs={{0,4},{4,0},{8,12},{12,8},{16,20},{20,16},{24,28},{28,24},{1,5},{5... | collective-permute-start | bytes 786440 | tf_op jit(solution)/shard_map/ppermute | solution.py:290
  39.2 5.4 %collective-permute-done.12.refs_7_ = bf16[128,1024]{1,0:T(8,128)(2,1)S(1)} collective-permute-done((bf16[128,1024]{1,0:T(8,128)(2,1)S(1)}, bf16[128,1024]{1,0:T(8,128)(2,1)S(1)}, u32[]{:S(2)}, u32[]{:S(2)}) %collective-permute-start.12) | collective-permute-done | bytes 262176 | tf_op jit(solution)/shard_map/ppermute | solution.py:290
  44.9 4.9 %collective-permute-done.9 = bf16[128,1024]{1,0:T(8,128)(2,1)S(1)} collective-permute-done((bf16[128,1024]{1,0:T(8,128)(2,1)S(1)}, bf16[128,1024]{1,0:T(8,128)(2,1)S(1)}, u32[]{:S(2)}, u32[]{:S(2)}) %collective-permute-start.9) | collective-permute-done | bytes 262176 | tf_op jit(solution)/shard_map/ppermute | solution.py:290
  50.3 2.5 %shard_map.79 = (bf16[528,256]{1,0:T(8,128)(2,1)S(1)}, bf16[528,256]{1,0:T(8,128)(2,1)S(1)}, bf16[528,256]{1,0:T(8,128)(2,1)S(1)}, bf16[528,256]{1,0:T(8,128)(2,1)S(1)}, bf16[1024,1024]{1,0:T(8,128)(2,1)}) custom-call(bf16[512,1024]{1,0:T(8,128)(2,1)S(1)} %copy-done, bf16[32,384]{1,0:T(8,128)(2,1)S(1)} %collective-permute-done.even_ref, ...), custom_call_target="tpu_custom_call" | custom-call | tf_op jit(solution)/shard_map/pallas_call | solution.py:258
  52.8 1.5 %collective-permute-start.13 = (bf16[528,256]{1,0:T(8,128)(2,1)S(1)}, bf16[528,256]{1,0:T(8,128)(2,1)S(1)}, u32[]{:S(2)}, u32[]{:S(2)}) collective-permute-start(bf16[528,256]{1,0:T(8,128)(2,1)S(1)} %get-tuple-element.53), channel_id=1, source_target_pairs={{0,2},{1,3},{2,0},{3,1},{4,6},{5,7},{6,4},{7,5},{8,10},{9,11},{10,... | collective-permute-start | bytes 811016 | tf_op jit(solution)/shard_map/ppermute | solution.py:287
  54.3 1.7 %shard_map.81 = (bf16[1024,512]{1,0:T(8,128)(2,1)S(1)}, f32[1024,256]{1,0:T(8,128)S(1)}, f32[1024,256]{1,0:T(8,128)S(1)}, f32[1024,256]{1,0:T(8,128)S(1)}) custom-call(bf16[1024,256]{1,0:T(8,128)(2,1)S(1)} %get-tuple-element.37.hidden_ref, bf16[32,384]{1,0:T(8,128)(2,1)S(1)} %collective-permute-done.even_ref, ...), custom_call_target="tpu_custom_call" | custom-call | tf_op jit(solution)/shard_map/pallas_call | solution.py:258
  57.0 1.6 %collective-permute-start.21 = (bf16[528,256]{1,0:T(8,128)(2,1)S(1)}, bf16[528,256]{1,0:T(8,128)(2,1)S(1)}, u32[]{:S(2)}, u32[]{:S(2)}) collective-permute-start(bf16[528,256]{1,0:T(8,128)(2,1)S(1)} %get-tuple-element.67), channel_id=1, source_target_pairs={{0,3},{1,2},{2,1},{3,0},{4,7},{5,6},{6,5},{7,4},{8,11},{9,10},{10,... | collective-permute-start | bytes 811016 | tf_op jit(solution)/shard_map/ppermute | solution.py:287
  58.7 3.6 %collective-permute-start.17 = (bf16[128,1024]{1,0:T(8,128)(2,1)S(1)}, bf16[128,1024]{1,0:T(8,128)(2,1)S(1)}, u32[]{:S(2)}, u32[]{:S(2)}) collective-permute-start(bf16[128,1024]{1,0:T(8,128)(2,1)S(1)} %add_convert_fusion.1), channel_id=1, source_target_pairs={{0,16},{4,20},{8,24},{12,28},{16,0},{20,4},{24,8},{28,12},{1,17},{... | collective-permute-start | bytes 786440 | tf_op jit(solution)/shard_map/ppermute | solution.py:290
  62.8 1.6 %collective-permute-start.19 = (bf16[128,1024]{1,0:T(8,128)(2,1)S(1)}, bf16[128,1024]{1,0:T(8,128)(2,1)S(1)}, u32[]{:S(2)}, u32[]{:S(2)}) collective-permute-start(bf16[128,1024]{1,0:T(8,128)(2,1)S(1)} %add_convert_fusion), channel_id=1, source_target_pairs={{0,8},{4,12},{8,0},{12,4},{16,24},{20,28},{24,16},{28,20},{1,9},{5... | collective-permute-start | bytes 786440 | tf_op jit(solution)/shard_map/ppermute | solution.py:290
  64.4 2.4 %shard_map.80 = bf16[512,1024]{1,0:T(8,128)(2,1)} custom-call(bf16[512,256]{1,0:T(8,128)(2,1)S(1)} %get-tuple-element.46.refs_0_, bf16[512,256]{1,0:T(8,128)(2,1)S(1)} %collective-permute-done.6.refs_1_, bf16[512,256]{1,0:T(8,128)(2,1)S(1)} %collective-permute-done.7.refs_2_, bf16[512,256]{1,0:T(8,128)(2,1)S(1)} %collective-permute-done.8.refs_3_, ...), custom_call_target="tpu_custom_call" | custom-call | tf_op jit(solution)/shard_map/pallas_call | solution.py:258
  66.7 2.3 %shard_map.82 = bf16[1024,256]{1,0:T(8,128)(2,1)} custom-call(bf16[528,256]{1,0:T(8,128)(2,1)S(1)} %get-tuple-element.65.refs_0_, bf16[528,256]{1,0:T(8,128)(2,1)S(1)} %collective-permute-done.20.refs_1_, bf16[528,256]{1,0:T(8,128)(2,1)S(1)} %collective-permute-done.13.refs_2_, bf16[528,256]{1,0:T(8,128)(2,1)S(1)} %collective-permute-done.21.refs_3_, ...), custom_call_target="tpu_custom_call" | custom-call | tf_op jit(solution)/shard_map/pallas_call | solution.py:258
  69.0 5.5 %collective-permute-done.17 = bf16[128,1024]{1,0:T(8,128)(2,1)S(1)} collective-permute-done((bf16[128,1024]{1,0:T(8,128)(2,1)S(1)}, bf16[128,1024]{1,0:T(8,128)(2,1)S(1)}, u32[]{:S(2)}, u32[]{:S(2)}) %collective-permute-start.17) | collective-permute-done | bytes 262176 | tf_op jit(solution)/shard_map/ppermute | solution.py:290
  (41 shorter events, 9.7 us)
Async XLA Ops:
  0.6 35.1 %copy-start = (bf16[512,1024]{1,0:T(8,128)(2,1)S(1)}, bf16[512,1024]{1,0:T(8,128)(2,1)}, u32[]{:S(2)}) copy-start(bf16[512,1024]{1,0:T(8,128)(2,1)} %grad_ref) | copy-start | bytes 3145732
  2.5 47.8 %copy-start.2 = (bf16[128,1024]{1,0:T(8,128)(2,1)S(1)}, bf16[128,1024]{1,0:T(8,128)(2,1)}, u32[]{:S(2)}) copy-start(bf16[128,1024]{1,0:T(8,128)(2,1)} %refs_0_) | copy-start | bytes 786436
  2.5 6.6 %collective-permute-start.1 = (bf16[32,384]{1,0:T(8,128)(2,1)S(1)}, bf16[32,384]{1,0:T(8,128)(2,1)S(1)}, u32[]{:S(2)}, u32[]{:S(2)}) collective-permute-start(bf16[32,384]{1,0:T(8,128)(2,1)S(1)} %get-tuple-element.39), channel_id=1, source_target_pairs={{4,8},{12,16},{20,24},{8,4},{16,12},{24,20},{5,9},{13,17},{21,25},... | collective-permute-start | bytes 73736 | tf_op jit(solution)/shard_map/ppermute | solution.py:317
  3.3 7.6 %collective-permute-start = (bf16[32,384]{1,0:T(8,128)(2,1)S(1)}, bf16[32,384]{1,0:T(8,128)(2,1)S(1)}, u32[]{:S(2)}, u32[]{:S(2)}) collective-permute-start(bf16[32,384]{1,0:T(8,128)(2,1)S(1)} %get-tuple-element.38), channel_id=1, source_target_pairs={{0,4},{4,0},{8,12},{12,8},{16,20},{20,16},{24,28},{28,24},{1,5},{5... | collective-permute-start | bytes 73736 | tf_op jit(solution)/shard_map/ppermute | solution.py:290
  10.9 8.9 %collective-permute-start.4 = (bf16[128,1024]{1,0:T(8,128)(2,1)}, bf16[128,1024]{1,0:T(8,128)(2,1)S(1)}, u32[]{:S(2)}, u32[]{:S(2)}) collective-permute-start(bf16[128,1024]{1,0:T(8,128)(2,1)} %refs_0_), channel_id=1, source_target_pairs={{0,4},{4,0},{8,12},{12,8},{16,20},{20,16},{24,28},{28,24},{1,5},{5... | collective-permute-start | bytes 786440 | tf_op jit(solution)/shard_map/ppermute | solution.py:290
  13.0 12.0 %collective-permute-start.3 = (bf16[128,1024]{1,0:T(8,128)(2,1)}, bf16[128,1024]{1,0:T(8,128)(2,1)S(1)}, u32[]{:S(2)}, u32[]{:S(2)}) collective-permute-start(bf16[128,1024]{1,0:T(8,128)(2,1)} %refs_0_), channel_id=1, source_target_pairs={{0,8},{4,12},{8,0},{12,4},{16,24},{20,28},{24,16},{28,20},{1,9},{5... | collective-permute-start | bytes 786440 | tf_op jit(solution)/shard_map/ppermute | solution.py:290
  14.5 12.9 %collective-permute-start.2 = (bf16[128,1024]{1,0:T(8,128)(2,1)}, bf16[128,1024]{1,0:T(8,128)(2,1)S(1)}, u32[]{:S(2)}, u32[]{:S(2)}) collective-permute-start(bf16[128,1024]{1,0:T(8,128)(2,1)} %refs_0_), channel_id=1, source_target_pairs={{0,16},{4,20},{8,24},{12,28},{16,0},{20,4},{24,8},{28,12},{1,17},{... | collective-permute-start | bytes 786440 | tf_op jit(solution)/shard_map/ppermute | solution.py:290
  18.3 9.9 %collective-permute-start.7 = (bf16[512,256]{1,0:T(8,128)(2,1)S(1)}, bf16[512,256]{1,0:T(8,128)(2,1)S(1)}, u32[]{:S(2)}, u32[]{:S(2)}) collective-permute-start(bf16[512,256]{1,0:T(8,128)(2,1)S(1)} %get-tuple-element.46.refs_0_), channel_id=1, source_target_pairs={{0,2},{1,3},{2,0},{3,1},{4,6},{5,7},{6,4},{7,5},{8,10},{9,11},{10,... | collective-permute-start | bytes 786440 | tf_op jit(solution)/shard_map/ppermute | solution.py:287
  24.9 7.6 %collective-permute-start.5 = (bf16[128,1024]{1,0:T(8,128)(2,1)S(1)}, bf16[128,1024]{1,0:T(8,128)(2,1)S(1)}, u32[]{:S(2)}, u32[]{:S(2)}) collective-permute-start(bf16[128,1024]{1,0:T(8,128)(2,1)S(1)} %collective-permute-done.3.refs_2_), channel_id=1, source_target_pairs={{0,4},{4,0},{8,12},{12,8},{16,20},{20,16},{24,28},{28,24},{1,5},{5... | collective-permute-start | bytes 786440 | tf_op jit(solution)/shard_map/ppermute | solution.py:290
  27.5 6.4 %collective-permute-start.11 = (bf16[128,1024]{1,0:T(8,128)(2,1)S(1)}, bf16[128,1024]{1,0:T(8,128)(2,1)S(1)}, u32[]{:S(2)}, u32[]{:S(2)}) collective-permute-start(bf16[128,1024]{1,0:T(8,128)(2,1)S(1)} %collective-permute-done.2.refs_4_), channel_id=1, source_target_pairs={{0,8},{4,12},{8,0},{12,4},{16,24},{20,28},{24,16},{28,20},{1,9},{5... | collective-permute-start | bytes 786440 | tf_op jit(solution)/shard_map/ppermute | solution.py:290
  27.7 7.6 %collective-permute-start.10 = (bf16[128,1024]{1,0:T(8,128)(2,1)S(1)}, bf16[128,1024]{1,0:T(8,128)(2,1)S(1)}, u32[]{:S(2)}, u32[]{:S(2)}) collective-permute-start(bf16[128,1024]{1,0:T(8,128)(2,1)S(1)} %collective-permute-done.2.refs_4_), channel_id=1, source_target_pairs={{0,4},{4,0},{8,12},{12,8},{16,20},{20,16},{24,28},{28,24},{1,5},{5... | collective-permute-start | bytes 786440 | tf_op jit(solution)/shard_map/ppermute | solution.py:290
  28.2 7.6 %collective-permute-start.8 = (bf16[512,256]{1,0:T(8,128)(2,1)S(1)}, bf16[512,256]{1,0:T(8,128)(2,1)S(1)}, u32[]{:S(2)}, u32[]{:S(2)}) collective-permute-start(bf16[512,256]{1,0:T(8,128)(2,1)S(1)} %collective-permute-done.7.refs_2_), channel_id=1, source_target_pairs={{0,1},{1,0},{2,3},{3,2},{4,5},{5,4},{6,7},{7,6},{8,9},{9,8},{10,11... | collective-permute-start | bytes 786440 | tf_op jit(solution)/shard_map/ppermute | solution.py:287
  32.6 3.2 %collective-permute-start.6 = (bf16[512,256]{1,0:T(8,128)(2,1)S(1)}, bf16[512,256]{1,0:T(8,128)(2,1)S(1)}, u32[]{:S(2)}, u32[]{:S(2)}) collective-permute-start(bf16[512,256]{1,0:T(8,128)(2,1)S(1)} %get-tuple-element.46.refs_0_), channel_id=1, source_target_pairs={{0,1},{1,0},{2,3},{3,2},{4,5},{5,4},{6,7},{7,6},{8,9},{9,8},{10,11... | collective-permute-start | bytes 786440 | tf_op jit(solution)/shard_map/ppermute | solution.py:287
  35.4 9.2 %collective-permute-start.12 = (bf16[128,1024]{1,0:T(8,128)(2,1)S(1)}, bf16[128,1024]{1,0:T(8,128)(2,1)S(1)}, u32[]{:S(2)}, u32[]{:S(2)}) collective-permute-start(bf16[128,1024]{1,0:T(8,128)(2,1)S(1)} %collective-permute-done.11.refs_6_), channel_id=1, source_target_pairs={{0,4},{4,0},{8,12},{12,8},{16,20},{20,16},{24,28},{28,24},{1,5},{5... | collective-permute-start | bytes 786440 | tf_op jit(solution)/shard_map/ppermute | solution.py:290
  37.5 12.4 %collective-permute-start.9 = (bf16[128,1024]{1,0:T(8,128)(2,1)S(1)}, bf16[128,1024]{1,0:T(8,128)(2,1)S(1)}, u32[]{:S(2)}, u32[]{:S(2)}) collective-permute-start(bf16[128,1024]{1,0:T(8,128)(2,1)S(1)} %get-tuple-element.47), channel_id=1, source_target_pairs={{0,4},{4,0},{8,12},{12,8},{16,20},{20,16},{24,28},{28,24},{1,5},{5... | collective-permute-start | bytes 786440 | tf_op jit(solution)/shard_map/ppermute | solution.py:290
  44.5 11.5 %collective-permute-start.15 = (bf16[128,1024]{1,0:T(8,128)(2,1)S(1)}, bf16[128,1024]{1,0:T(8,128)(2,1)S(1)}, u32[]{:S(2)}, u32[]{:S(2)}) collective-permute-start(bf16[128,1024]{1,0:T(8,128)(2,1)S(1)} %get-tuple-element.57), channel_id=1, source_target_pairs={{0,4},{4,0},{8,12},{12,8},{16,20},{20,16},{24,28},{28,24},{1,5},{5... | collective-permute-start | bytes 786440 | tf_op jit(solution)/shard_map/ppermute | solution.py:290
  49.9 6.4 %collective-permute-start.16 = (bf16[128,1024]{1,0:T(8,128)(2,1)S(1)}, bf16[128,1024]{1,0:T(8,128)(2,1)S(1)}, u32[]{:S(2)}, u32[]{:S(2)}) collective-permute-start(bf16[128,1024]{1,0:T(8,128)(2,1)S(1)} %add_convert_fusion.2), channel_id=1, source_target_pairs={{0,8},{4,12},{8,0},{12,4},{16,24},{20,28},{24,16},{28,20},{1,9},{5... | collective-permute-start | bytes 786440 | tf_op jit(solution)/shard_map/ppermute | solution.py:290
  52.8 9.5 %collective-permute-start.13 = (bf16[528,256]{1,0:T(8,128)(2,1)S(1)}, bf16[528,256]{1,0:T(8,128)(2,1)S(1)}, u32[]{:S(2)}, u32[]{:S(2)}) collective-permute-start(bf16[528,256]{1,0:T(8,128)(2,1)S(1)} %get-tuple-element.53), channel_id=1, source_target_pairs={{0,2},{1,3},{2,0},{3,1},{4,6},{5,7},{6,4},{7,5},{8,10},{9,11},{10,... | collective-permute-start | bytes 811016 | tf_op jit(solution)/shard_map/ppermute | solution.py:287
  56.4 6.4 %collective-permute-start.18 = (bf16[128,1024]{1,0:T(8,128)(2,1)S(1)}, bf16[128,1024]{1,0:T(8,128)(2,1)S(1)}, u32[]{:S(2)}, u32[]{:S(2)}) collective-permute-start(bf16[128,1024]{1,0:T(8,128)(2,1)S(1)} %get-tuple-element.64), channel_id=1, source_target_pairs={{0,4},{4,0},{8,12},{12,8},{16,20},{20,16},{24,28},{28,24},{1,5},{5... | collective-permute-start | bytes 786440 | tf_op jit(solution)/shard_map/ppermute | solution.py:290
  57.0 9.8 %collective-permute-start.20 = (bf16[528,256]{1,0:T(8,128)(2,1)S(1)}, bf16[528,256]{1,0:T(8,128)(2,1)S(1)}, u32[]{:S(2)}, u32[]{:S(2)}) collective-permute-start(bf16[528,256]{1,0:T(8,128)(2,1)S(1)} %get-tuple-element.66), channel_id=1, source_target_pairs={{0,1},{1,0},{2,3},{3,2},{4,5},{5,4},{6,7},{7,6},{8,9},{9,8},{10,11... | collective-permute-start | bytes 811016 | tf_op jit(solution)/shard_map/ppermute | solution.py:287
  57.0 9.8 %collective-permute-start.21 = (bf16[528,256]{1,0:T(8,128)(2,1)S(1)}, bf16[528,256]{1,0:T(8,128)(2,1)S(1)}, u32[]{:S(2)}, u32[]{:S(2)}) collective-permute-start(bf16[528,256]{1,0:T(8,128)(2,1)S(1)} %get-tuple-element.67), channel_id=1, source_target_pairs={{0,3},{1,2},{2,1},{3,0},{4,7},{5,6},{6,5},{7,4},{8,11},{9,10},{10,... | collective-permute-start | bytes 811016 | tf_op jit(solution)/shard_map/ppermute | solution.py:287
  58.7 15.8 %collective-permute-start.17 = (bf16[128,1024]{1,0:T(8,128)(2,1)S(1)}, bf16[128,1024]{1,0:T(8,128)(2,1)S(1)}, u32[]{:S(2)}, u32[]{:S(2)}) collective-permute-start(bf16[128,1024]{1,0:T(8,128)(2,1)S(1)} %add_convert_fusion.1), channel_id=1, source_target_pairs={{0,16},{4,20},{8,24},{12,28},{16,0},{20,4},{24,8},{28,12},{1,17},{... | collective-permute-start | bytes 786440 | tf_op jit(solution)/shard_map/ppermute | solution.py:290
  62.3 12.2 %collective-permute-start.14 = (bf16[128,1024]{1,0:T(8,128)(2,1)S(1)}, bf16[128,1024]{1,0:T(8,128)(2,1)S(1)}, u32[]{:S(2)}, u32[]{:S(2)}) collective-permute-start(bf16[128,1024]{1,0:T(8,128)(2,1)S(1)} %get-tuple-element.54), channel_id=1, source_target_pairs={{0,4},{4,0},{8,12},{12,8},{16,20},{20,16},{24,28},{28,24},{1,5},{5... | collective-permute-start | bytes 786440 | tf_op jit(solution)/shard_map/ppermute | solution.py:290
  62.8 12.3 %collective-permute-start.19 = (bf16[128,1024]{1,0:T(8,128)(2,1)S(1)}, bf16[128,1024]{1,0:T(8,128)(2,1)S(1)}, u32[]{:S(2)}, u32[]{:S(2)}) collective-permute-start(bf16[128,1024]{1,0:T(8,128)(2,1)S(1)} %add_convert_fusion), channel_id=1, source_target_pairs={{0,8},{4,12},{8,0},{12,4},{16,24},{20,28},{24,16},{28,20},{1,9},{5... | collective-permute-start | bytes 786440 | tf_op jit(solution)/shard_map/ppermute | solution.py:290
  (3 other events, 13.0 us)

commit v7 on v6

--- a/solution.py
+++ b/solution.py
@@ -319,8 +319,7 @@
     if staged:
         pieces = [in_weight] + [None] * (n_seq - 1)
         for step in (1, 2, 4):
-            first = even if step == 1 else odd
-            pieces[step] = trade(after((in_weight, first))[0], step)
+            pieces[step] = trade(in_weight, step)
     else:
         pieces = [lax.all_gather(in_weight, "seq", axis=0, tiled=True)]
 
@@ -335,11 +334,12 @@
     )
 
     if staged:
-        pieces[3] = trade(after((pieces[2], (low, pieces[1],)))[0], 1)
+        low = after((low, (pieces[1],)))[0]
+        pieces[3] = trade(after((pieces[2], (low,)))[0], 1)
     parts = [low]
     for step in reversed([1 << bit for bit in range(n_mp.bit_length() - 1)]):
         if staged and step == 1:
-            parts[0] = after((parts[0], (pieces[4], pieces[3],)))[0]
+            parts = [after((parts[0], (pieces[4],)))[0], parts[1]]
         parts = [part for held in parts for part in (held, swap(held, step))]
     onehot, share, delta, slope = call(
         spread_kernel,
@@ -367,10 +367,10 @@
     if staged:
         fetched = {}
         pieces[7] = trade(after((pieces[6], (pieces[3],)))[0], 1)
-        pieces[5] = trade(pieces[4], 1)
+        pieces[5] = trade(after((pieces[4], (terms[0],)))[0], 1)
         pieces[6] = trade(pieces[4], 2)
         pieces[7] = trade(after((pieces[6], (pieces[5],)))[0], 1)
-        fetched[7] = trade(terms[7], 1)
+        fetched[7] = trade(after((terms[7], (pieces[3],)))[0], 1)
         fetched[6] = trade((terms[6] + fetched[7].astype(F32)).astype(BF16), 2)
         fetched[5] = trade(after((terms[5], (pieces[7],)))[0], 1)
 

time: 76.2 us -> 81.9 us (1.075)
  waiting for transfers between devices: 33 us -> 38.8 us
    ppermute x15, waiting for transfers between devices: 33 us -> 38 us  [trade(): return lax.ppermute(value, 'seq', [(i, i ^ step) for i in range(n_seq)])]
    ppermute x6, starting transfers between devices: 4.65 us -> 2.07 us  [swap(): return lax.ppermute(value, 'mp', [(i, i ^ step) for i in range(n_mp)])]
    ppermute x15, starting transfers between devices: 20.4 us -> 23 us  [trade(): return lax.ppermute(value, 'seq', [(i, i ^ step) for i in range(n_seq)])]
    ppermute x6, waiting for transfers between devices: 0.02 us -> 0.87 us  [swap(): return lax.ppermute(value, 'mp', [(i, i ^ step) for i in range(n_mp)])]
  transfers between devices with their start and end apart: 22 -> 22, of which waited for: 11 -> 11; matrix products, arithmetic and copies ran while one was open for 0% -> 0% of each run, Pallas kernels for 17% -> 16%
where the time goes in v7:
time: 81.9 us; the launch traced here: 81.7 us
  waiting for transfers between devices  38.8 us (47%)
  starting transfers between devices  25.7 us (31%)
  Pallas kernels  13.8 us (17%)
  local copies, waits for them, and re-layouts  1.45 us (2%)
  other arithmetic  1.15 us (1%)
    ppermute x15, waiting for transfers between devices, trade(): return lax.ppermute(value, 'seq', [(i, i ^ step) for i in range(n_seq)])  38 us
    ppermute x15, starting transfers between devices, trade(): return lax.ppermute(value, 'seq', [(i, i ^ step) for i in range(n_seq)])  23 us
    pallas_call x7, Pallas kernels, call(): pl.pallas_call(kernel, out_shape=out_shape, in_specs=in_specs, out_specs=...  13.8 us
    ppermute x6, starting transfers between devices, swap(): return lax.ppermute(value, 'mp', [(i, i ^ step) for i in range(n_mp)])  2.07 us
  transfers between devices with their start and end apart: 22, of which 11 were waited for; matrix products, arithmetic and copies ran while one was open for 0% of the time, Pallas kernels for 16%

profile of v7, /device:TPU:0, one launch (start us, length us, event | category | flops | bytes accessed | tf_op | source)
XLA Modules:
  0.0 81.7 jit_solution(14106790022800484630)
XLA Ops:
  2.5 3.0 %collective-permute-start.2 = (bf16[128,1024]{1,0:T(8,128)(2,1)}, bf16[128,1024]{1,0:T(8,128)(2,1)S(1)}, u32[]{:S(2)}, u32[]{:S(2)}) collective-permute-start(bf16[128,1024]{1,0:T(8,128)(2,1)} %refs_0_), channel_id=1, source_target_pairs={{0,4},{4,0},{8,12},{12,8},{16,20},{20,16},{24,28},{28,24},{1,5},{5... | collective-permute-start | bytes 786440 | tf_op jit(solution)/shard_map/ppermute | solution.py:290
  6.2 4.3 %collective-permute-start = (bf16[32,384]{1,0:T(8,128)(2,1)S(1)}, bf16[32,384]{1,0:T(8,128)(2,1)S(1)}, u32[]{:S(2)}, u32[]{:S(2)}) collective-permute-start(bf16[32,384]{1,0:T(8,128)(2,1)S(1)} %get-tuple-element.39), channel_id=1, source_target_pairs={{0,4},{4,0},{8,12},{12,8},{16,20},{20,16},{24,28},{28,24},{1,5},{5... | collective-permute-start | bytes 73736 | tf_op jit(solution)/shard_map/ppermute | solution.py:290
  10.6 2.6 %collective-permute-start.3 = (bf16[128,1024]{1,0:T(8,128)(2,1)}, bf16[128,1024]{1,0:T(8,128)(2,1)S(1)}, u32[]{:S(2)}, u32[]{:S(2)}) collective-permute-start(bf16[128,1024]{1,0:T(8,128)(2,1)} %refs_0_), channel_id=1, source_target_pairs={{0,16},{4,20},{8,24},{12,28},{16,0},{20,4},{24,8},{28,12},{1,17},{... | collective-permute-start | bytes 786440 | tf_op jit(solution)/shard_map/ppermute | solution.py:290
  13.8 2.1 %shard_map.77 = (bf16[512,256]{1,0:T(8,128)(2,1)S(1)}, f32[512,256]{1,0:T(8,128)S(1)}, f32[512,256]{1,0:T(8,128)S(1)}) custom-call(bf16[1024,256]{1,0:T(8,128)(2,1)S(1)} %get-tuple-element.38.hidden_ref, bf16[32,384]{1,0:T(8,128)(2,1)S(1)} %collective-permute-done.even_ref, bf16[32,384]{1,0:T(8,128)(2,1)S(1)} %collective-permute-done.1.odd_ref, ...), custom_call_target="tpu_custom_call" | custom-call | tf_op jit(solution)/shard_map/pallas_call | solution.py:258
  17.5 1.8 %collective-permute-start.7 = (bf16[128,1024]{1,0:T(8,128)(2,1)S(1)}, bf16[128,1024]{1,0:T(8,128)(2,1)S(1)}, u32[]{:S(2)}, u32[]{:S(2)}) collective-permute-start(bf16[128,1024]{1,0:T(8,128)(2,1)S(1)} %copy-done.2), channel_id=1, source_target_pairs={{0,8},{4,12},{8,0},{12,4},{16,24},{20,28},{24,16},{28,20},{1,9},{5... | collective-permute-start | bytes 786440 | tf_op jit(solution)/shard_map/ppermute | solution.py:290
  19.3 5.4 %collective-permute-done.3.refs_4_ = bf16[128,1024]{1,0:T(8,128)(2,1)S(1)} collective-permute-done((bf16[128,1024]{1,0:T(8,128)(2,1)}, bf16[128,1024]{1,0:T(8,128)(2,1)S(1)}, u32[]{:S(2)}, u32[]{:S(2)}) %collective-permute-start.3) | collective-permute-done | bytes 262176 | tf_op jit(solution)/shard_map/ppermute | solution.py:290
  25.1 3.5 %collective-permute-done.7.refs_2_ = bf16[128,1024]{1,0:T(8,128)(2,1)S(1)} collective-permute-done((bf16[128,1024]{1,0:T(8,128)(2,1)S(1)}, bf16[128,1024]{1,0:T(8,128)(2,1)S(1)}, u32[]{:S(2)}, u32[]{:S(2)}) %collective-permute-start.7) | collective-permute-done | bytes 262176 | tf_op jit(solution)/shard_map/ppermute | solution.py:290
  28.7 1.8 %collective-permute-start.8 = (bf16[128,1024]{1,0:T(8,128)(2,1)S(1)}, bf16[128,1024]{1,0:T(8,128)(2,1)S(1)}, u32[]{:S(2)}, u32[]{:S(2)}) collective-permute-start(bf16[128,1024]{1,0:T(8,128)(2,1)S(1)} %collective-permute-done.7.refs_2_), channel_id=1, source_target_pairs={{0,4},{4,0},{8,12},{12,8},{16,20},{20,16},{24,28},{28,24},{1,5},{5... | collective-permute-start | bytes 786440 | tf_op jit(solution)/shard_map/ppermute | solution.py:290
  30.5 1.7 %shard_map.78 = (f32[128,1024]{1,0:T(8,128)S(1)}, bf16[128,1024]{1,0:T(8,128)(2,1)S(1)}, f32[128,1024]{1,0:T(8,128)S(1)}, bf16[128,1024]{1,0:T(8,128)(2,1)S(1)},...) custom-call(bf16[512,256]{1,0:T(8,128)(2,1)S(1)} %get-tuple-element., ...), custom_call_target="tpu_custom_call" | custom-call | tf_op jit(solution)/shard_map/pallas_call | solution.py:258
  32.5 5.3 %collective-permute-done.8.refs_3_ = bf16[128,1024]{1,0:T(8,128)(2,1)S(1)} collective-permute-done((bf16[128,1024]{1,0:T(8,128)(2,1)S(1)}, bf16[128,1024]{1,0:T(8,128)(2,1)S(1)}, u32[]{:S(2)}, u32[]{:S(2)}) %collective-permute-start.8) | collective-permute-done | bytes 262176 | tf_op jit(solution)/shard_map/ppermute | solution.py:290
  37.8 1.8 %collective-permute-start.9 = (bf16[128,1024]{1,0:T(8,128)(2,1)S(1)}, bf16[128,1024]{1,0:T(8,128)(2,1)S(1)}, u32[]{:S(2)}, u32[]{:S(2)}) collective-permute-start(bf16[128,1024]{1,0:T(8,128)(2,1)S(1)} %get-tuple-element.48), channel_id=1, source_target_pairs={{0,4},{4,0},{8,12},{12,8},{16,20},{20,16},{24,28},{28,24},{1,5},{5... | collective-permute-start | bytes 786440 | tf_op jit(solution)/shard_map/ppermute | solution.py:290
  39.7 3.8 %collective-permute-done.10.refs_5_ = bf16[128,1024]{1,0:T(8,128)(2,1)S(1)} collective-permute-done((bf16[128,1024]{1,0:T(8,128)(2,1)S(1)}, bf16[128,1024]{1,0:T(8,128)(2,1)S(1)}, u32[]{:S(2)}, u32[]{:S(2)}) %collective-permute-start.10) | collective-permute-done | bytes 262176 | tf_op jit(solution)/shard_map/ppermute | solution.py:290
  43.4 1.8 %collective-permute-start.12 = (bf16[128,1024]{1,0:T(8,128)(2,1)S(1)}, bf16[128,1024]{1,0:T(8,128)(2,1)S(1)}, u32[]{:S(2)}, u32[]{:S(2)}) collective-permute-start(bf16[128,1024]{1,0:T(8,128)(2,1)S(1)} %collective-permute-done.11.refs_6_), channel_id=1, source_target_pairs={{0,4},{4,0},{8,12},{12,8},{16,20},{20,16},{24,28},{28,24},{1,5},{5... | collective-permute-start | bytes 786440 | tf_op jit(solution)/shard_map/ppermute | solution.py:290
  45.3 3.8 %collective-permute-done.9 = bf16[128,1024]{1,0:T(8,128)(2,1)S(1)} collective-permute-done((bf16[128,1024]{1,0:T(8,128)(2,1)S(1)}, bf16[128,1024]{1,0:T(8,128)(2,1)S(1)}, u32[]{:S(2)}, u32[]{:S(2)}) %collective-permute-start.9) | collective-permute-done | bytes 262176 | tf_op jit(solution)/shard_map/ppermute | solution.py:290
  49.3 4.5 %collective-permute-done.12.refs_7_ = bf16[128,1024]{1,0:T(8,128)(2,1)S(1)} collective-permute-done((bf16[128,1024]{1,0:T(8,128)(2,1)S(1)}, bf16[128,1024]{1,0:T(8,128)(2,1)S(1)}, u32[]{:S(2)}, u32[]{:S(2)}) %collective-permute-start.12) | collective-permute-done | bytes 262176 | tf_op jit(solution)/shard_map/ppermute | solution.py:290
  53.8 1.7 %collective-permute-start.15 = (bf16[128,1024]{1,0:T(8,128)(2,1)S(1)}, bf16[128,1024]{1,0:T(8,128)(2,1)S(1)}, u32[]{:S(2)}, u32[]{:S(2)}) collective-permute-start(bf16[128,1024]{1,0:T(8,128)(2,1)S(1)} %get-tuple-element.59), channel_id=1, source_target_pairs={{0,4},{4,0},{8,12},{12,8},{16,20},{20,16},{24,28},{28,24},{1,5},{5... | collective-permute-start | bytes 786440 | tf_op jit(solution)/shard_map/ppermute | solution.py:290
  55.6 2.5 %shard_map.79 = (bf16[528,256]{1,0:T(8,128)(2,1)S(1)}, bf16[528,256]{1,0:T(8,128)(2,1)S(1)}, bf16[528,256]{1,0:T(8,128)(2,1)S(1)}, bf16[528,256]{1,0:T(8,128)(2,1)S(1)}, bf16[1024,1024]{1,0:T(8,128)(2,1)}) custom-call(bf16[512,1024]{1,0:T(8,128)(2,1)S(1)} %copy-done, bf16[32,384]{1,0:T(8,128)(2,1)S(1)} %collective-permute-done.even_ref, ...), custom_call_target="tpu_custom_call" | custom-call | tf_op jit(solution)/shard_map/pallas_call | solution.py:258
  58.1 1.8 %shard_map.81 = (bf16[1024,512]{1,0:T(8,128)(2,1)S(1)}, f32[1024,256]{1,0:T(8,128)S(1)}, f32[1024,256]{1,0:T(8,128)S(1)}, f32[1024,256]{1,0:T(8,128)S(1)}) custom-call(bf16[1024,256]{1,0:T(8,128)(2,1)S(1)} %get-tuple-element.38.hidden_ref, bf16[32,384]{1,0:T(8,128)(2,1)S(1)} %collective-permute-done.even_ref, ...), custom_call_target="tpu_custom_call" | custom-call | tf_op jit(solution)/shard_map/pallas_call | solution.py:258
  61.3 1.6 %collective-permute-start.18 = (bf16[128,1024]{1,0:T(8,128)(2,1)S(1)}, bf16[128,1024]{1,0:T(8,128)(2,1)S(1)}, u32[]{:S(2)}, u32[]{:S(2)}) collective-permute-start(bf16[128,1024]{1,0:T(8,128)(2,1)S(1)} %get-tuple-element.66), channel_id=1, source_target_pairs={{0,4},{4,0},{8,12},{12,8},{16,20},{20,16},{24,28},{28,24},{1,5},{5... | collective-permute-start | bytes 786440 | tf_op jit(solution)/shard_map/ppermute | solution.py:290
  65.8 3.3 %collective-permute-done.18 = bf16[128,1024]{1,0:T(8,128)(2,1)S(1)} collective-permute-done((bf16[128,1024]{1,0:T(8,128)(2,1)S(1)}, bf16[128,1024]{1,0:T(8,128)(2,1)S(1)}, u32[]{:S(2)}, u32[]{:S(2)}) %collective-permute-start.18) | collective-permute-done | bytes 262176 | tf_op jit(solution)/shard_map/ppermute | solution.py:290
  69.2 2.4 %shard_map.80 = bf16[512,1024]{1,0:T(8,128)(2,1)} custom-call(bf16[512,256]{1,0:T(8,128)(2,1)S(1)} %get-tuple-element.45.refs_0_, bf16[512,256]{1,0:T(8,128)(2,1)S(1)} %collective-permute-done.4.refs_1_, bf16[512,256]{1,0:T(8,128)(2,1)S(1)} %collective-permute-done.5.refs_2_, bf16[512,256]{1,0:T(8,128)(2,1)S(1)} %collective-permute-done.6.refs_3_, ...), custom_call_target="tpu_custom_call" | custom-call | tf_op jit(solution)/shard_map/pallas_call | solution.py:258
  71.6 2.3 %shard_map.82 = bf16[1024,256]{1,0:T(8,128)(2,1)} custom-call(bf16[528,256]{1,0:T(8,128)(2,1)S(1)} %get-tuple-element.67.refs_0_, bf16[528,256]{1,0:T(8,128)(2,1)S(1)} %collective-permute-done.20.refs_1_, bf16[528,256]{1,0:T(8,128)(2,1)S(1)} %collective-permute-done.13.refs_2_, bf16[528,256]{1,0:T(8,128)(2,1)S(1)} %collective-permute-done.21.refs_3_, ...), custom_call_target="tpu_custom_call" | custom-call | tf_op jit(solution)/shard_map/pallas_call | solution.py:258
  73.9 4.6 %collective-permute-done.17 = bf16[128,1024]{1,0:T(8,128)(2,1)S(1)} collective-permute-done((bf16[128,1024]{1,0:T(8,128)(2,1)S(1)}, bf16[128,1024]{1,0:T(8,128)(2,1)S(1)}, u32[]{:S(2)}, u32[]{:S(2)}) %collective-permute-start.17) | collective-permute-done | bytes 262176 | tf_op jit(solution)/shard_map/ppermute | solution.py:290
  78.5 2.3 %collective-permute-done.19 = bf16[128,1024]{1,0:T(8,128)(2,1)S(1)} collective-permute-done((bf16[128,1024]{1,0:T(8,128)(2,1)S(1)}, bf16[128,1024]{1,0:T(8,128)(2,1)S(1)}, u32[]{:S(2)}, u32[]{:S(2)}) %collective-permute-start.19) | collective-permute-done | bytes 262176 | tf_op jit(solution)/shard_map/ppermute | solution.py:290
  (41 shorter events, 11.1 us)
Async XLA Ops:
  0.6 29.9 %copy-start = (bf16[512,1024]{1,0:T(8,128)(2,1)S(1)}, bf16[512,1024]{1,0:T(8,128)(2,1)}, u32[]{:S(2)}) copy-start(bf16[512,1024]{1,0:T(8,128)(2,1)} %grad_ref) | copy-start | bytes 3145732
  0.6 16.9 %copy-start.2 = (bf16[128,1024]{1,0:T(8,128)(2,1)S(1)}, bf16[128,1024]{1,0:T(8,128)(2,1)}, u32[]{:S(2)}) copy-start(bf16[128,1024]{1,0:T(8,128)(2,1)} %refs_0_) | copy-start | bytes 786436
  2.5 13.4 %collective-permute-start.2 = (bf16[128,1024]{1,0:T(8,128)(2,1)}, bf16[128,1024]{1,0:T(8,128)(2,1)S(1)}, u32[]{:S(2)}, u32[]{:S(2)}) collective-permute-start(bf16[128,1024]{1,0:T(8,128)(2,1)} %refs_0_), channel_id=1, source_target_pairs={{0,4},{4,0},{8,12},{12,8},{16,20},{20,16},{24,28},{28,24},{1,5},{5... | collective-permute-start | bytes 786440 | tf_op jit(solution)/shard_map/ppermute | solution.py:290
  5.6 7.6 %collective-permute-start.1 = (bf16[32,384]{1,0:T(8,128)(2,1)S(1)}, bf16[32,384]{1,0:T(8,128)(2,1)S(1)}, u32[]{:S(2)}, u32[]{:S(2)}) collective-permute-start(bf16[32,384]{1,0:T(8,128)(2,1)S(1)} %get-tuple-element.40), channel_id=1, source_target_pairs={{4,8},{12,16},{20,24},{8,4},{16,12},{24,20},{5,9},{13,17},{21,25},... | collective-permute-start | bytes 73736 | tf_op jit(solution)/shard_map/ppermute | solution.py:317
  6.2 6.9 %collective-permute-start = (bf16[32,384]{1,0:T(8,128)(2,1)S(1)}, bf16[32,384]{1,0:T(8,128)(2,1)S(1)}, u32[]{:S(2)}, u32[]{:S(2)}) collective-permute-start(bf16[32,384]{1,0:T(8,128)(2,1)S(1)} %get-tuple-element.39), channel_id=1, source_target_pairs={{0,4},{4,0},{8,12},{12,8},{16,20},{20,16},{24,28},{28,24},{1,5},{5... | collective-permute-start | bytes 73736 | tf_op jit(solution)/shard_map/ppermute | solution.py:290
  10.6 14.0 %collective-permute-start.3 = (bf16[128,1024]{1,0:T(8,128)(2,1)}, bf16[128,1024]{1,0:T(8,128)(2,1)S(1)}, u32[]{:S(2)}, u32[]{:S(2)}) collective-permute-start(bf16[128,1024]{1,0:T(8,128)(2,1)} %refs_0_), channel_id=1, source_target_pairs={{0,16},{4,20},{8,24},{12,28},{16,0},{20,4},{24,8},{28,12},{1,17},{... | collective-permute-start | bytes 786440 | tf_op jit(solution)/shard_map/ppermute | solution.py:290
  15.9 8.7 %collective-permute-start.5 = (bf16[512,256]{1,0:T(8,128)(2,1)S(1)}, bf16[512,256]{1,0:T(8,128)(2,1)S(1)}, u32[]{:S(2)}, u32[]{:S(2)}) collective-permute-start(bf16[512,256]{1,0:T(8,128)(2,1)S(1)} %get-tuple-element.45.refs_0_), channel_id=1, source_target_pairs={{0,2},{1,3},{2,0},{3,1},{4,6},{5,7},{6,4},{7,5},{8,10},{9,11},{10,... | collective-permute-start | bytes 786440 | tf_op jit(solution)/shard_map/ppermute | solution.py:287
  17.5 11.2 %collective-permute-start.7 = (bf16[128,1024]{1,0:T(8,128)(2,1)S(1)}, bf16[128,1024]{1,0:T(8,128)(2,1)S(1)}, u32[]{:S(2)}, u32[]{:S(2)}) collective-permute-start(bf16[128,1024]{1,0:T(8,128)(2,1)S(1)} %copy-done.2), channel_id=1, source_target_pairs={{0,8},{4,12},{8,0},{12,4},{16,24},{20,28},{24,16},{28,20},{1,9},{5... | collective-permute-start | bytes 786440 | tf_op jit(solution)/shard_map/ppermute | solution.py:290
  24.6 5.9 %collective-permute-start.4 = (bf16[512,256]{1,0:T(8,128)(2,1)S(1)}, bf16[512,256]{1,0:T(8,128)(2,1)S(1)}, u32[]{:S(2)}, u32[]{:S(2)}) collective-permute-start(bf16[512,256]{1,0:T(8,128)(2,1)S(1)} %get-tuple-element.45.refs_0_), channel_id=1, source_target_pairs={{0,1},{1,0},{2,3},{3,2},{4,5},{5,4},{6,7},{7,6},{8,9},{9,8},{10,11... | collective-permute-start | bytes 786440 | tf_op jit(solution)/shard_map/ppermute | solution.py:287
  24.6 5.9 %collective-permute-start.6 = (bf16[512,256]{1,0:T(8,128)(2,1)S(1)}, bf16[512,256]{1,0:T(8,128)(2,1)S(1)}, u32[]{:S(2)}, u32[]{:S(2)}) collective-permute-start(bf16[512,256]{1,0:T(8,128)(2,1)S(1)} %collective-permute-done.5.refs_2_), channel_id=1, source_target_pairs={{0,1},{1,0},{2,3},{3,2},{4,5},{5,4},{6,7},{7,6},{8,9},{9,8},{10,11... | collective-permute-start | bytes 786440 | tf_op jit(solution)/shard_map/ppermute | solution.py:287
  28.7 9.2 %collective-permute-start.8 = (bf16[128,1024]{1,0:T(8,128)(2,1)S(1)}, bf16[128,1024]{1,0:T(8,128)(2,1)S(1)}, u32[]{:S(2)}, u32[]{:S(2)}) collective-permute-start(bf16[128,1024]{1,0:T(8,128)(2,1)S(1)} %collective-permute-done.7.refs_2_), channel_id=1, source_target_pairs={{0,4},{4,0},{8,12},{12,8},{16,20},{20,16},{24,28},{28,24},{1,5},{5... | collective-permute-start | bytes 786440 | tf_op jit(solution)/shard_map/ppermute | solution.py:290
  30.5 9.2 %collective-permute-start.11 = (bf16[128,1024]{1,0:T(8,128)(2,1)S(1)}, bf16[128,1024]{1,0:T(8,128)(2,1)S(1)}, u32[]{:S(2)}, u32[]{:S(2)}) collective-permute-start(bf16[128,1024]{1,0:T(8,128)(2,1)S(1)} %collective-permute-done.3.refs_4_), channel_id=1, source_target_pairs={{0,8},{4,12},{8,0},{12,4},{16,24},{20,28},{24,16},{28,20},{1,9},{5... | collective-permute-start | bytes 786440 | tf_op jit(solution)/shard_map/ppermute | solution.py:290
  32.2 11.2 %collective-permute-start.10 = (bf16[128,1024]{1,0:T(8,128)(2,1)S(1)}, bf16[128,1024]{1,0:T(8,128)(2,1)S(1)}, u32[]{:S(2)}, u32[]{:S(2)}) collective-permute-start(bf16[128,1024]{1,0:T(8,128)(2,1)S(1)} %collective-permute-done.3.refs_4_), channel_id=1, source_target_pairs={{0,4},{4,0},{8,12},{12,8},{16,20},{20,16},{24,28},{28,24},{1,5},{5... | collective-permute-start | bytes 786440 | tf_op jit(solution)/shard_map/ppermute | solution.py:290
  37.8 11.2 %collective-permute-start.9 = (bf16[128,1024]{1,0:T(8,128)(2,1)S(1)}, bf16[128,1024]{1,0:T(8,128)(2,1)S(1)}, u32[]{:S(2)}, u32[]{:S(2)}) collective-permute-start(bf16[128,1024]{1,0:T(8,128)(2,1)S(1)} %get-tuple-element.48), channel_id=1, source_target_pairs={{0,4},{4,0},{8,12},{12,8},{16,20},{20,16},{24,28},{28,24},{1,5},{5... | collective-permute-start | bytes 786440 | tf_op jit(solution)/shard_map/ppermute | solution.py:290
  43.4 10.4 %collective-permute-start.12 = (bf16[128,1024]{1,0:T(8,128)(2,1)S(1)}, bf16[128,1024]{1,0:T(8,128)(2,1)S(1)}, u32[]{:S(2)}, u32[]{:S(2)}) collective-permute-start(bf16[128,1024]{1,0:T(8,128)(2,1)S(1)} %collective-permute-done.11.refs_6_), channel_id=1, source_target_pairs={{0,4},{4,0},{8,12},{12,8},{16,20},{20,16},{24,28},{28,24},{1,5},{5... | collective-permute-start | bytes 786440 | tf_op jit(solution)/shard_map/ppermute | solution.py:290
  49.1 10.7 %collective-permute-start.16 = (bf16[128,1024]{1,0:T(8,128)(2,1)S(1)}, bf16[128,1024]{1,0:T(8,128)(2,1)S(1)}, u32[]{:S(2)}, u32[]{:S(2)}) collective-permute-start(bf16[128,1024]{1,0:T(8,128)(2,1)S(1)} %add_convert_fusion.2), channel_id=1, source_target_pairs={{0,8},{4,12},{8,0},{12,4},{16,24},{20,28},{24,16},{28,20},{1,9},{5... | collective-permute-start | bytes 786440 | tf_op jit(solution)/shard_map/ppermute | solution.py:290
  53.8 7.5 %collective-permute-start.15 = (bf16[128,1024]{1,0:T(8,128)(2,1)S(1)}, bf16[128,1024]{1,0:T(8,128)(2,1)S(1)}, u32[]{:S(2)}, u32[]{:S(2)}) collective-permute-start(bf16[128,1024]{1,0:T(8,128)(2,1)S(1)} %get-tuple-element.59), channel_id=1, source_target_pairs={{0,4},{4,0},{8,12},{12,8},{16,20},{20,16},{24,28},{28,24},{1,5},{5... | collective-permute-start | bytes 786440 | tf_op jit(solution)/shard_map/ppermute | solution.py:290
  58.1 7.3 %collective-permute-start.13 = (bf16[528,256]{1,0:T(8,128)(2,1)S(1)}, bf16[528,256]{1,0:T(8,128)(2,1)S(1)}, u32[]{:S(2)}, u32[]{:S(2)}) collective-permute-start(bf16[528,256]{1,0:T(8,128)(2,1)S(1)} %get-tuple-element.55), channel_id=1, source_target_pairs={{0,2},{1,3},{2,0},{3,1},{4,6},{5,7},{6,4},{7,5},{8,10},{9,11},{10,... | collective-permute-start | bytes 811016 | tf_op jit(solution)/shard_map/ppermute | solution.py:287
  61.3 7.8 %collective-permute-start.18 = (bf16[128,1024]{1,0:T(8,128)(2,1)S(1)}, bf16[128,1024]{1,0:T(8,128)(2,1)S(1)}, u32[]{:S(2)}, u32[]{:S(2)}) collective-permute-start(bf16[128,1024]{1,0:T(8,128)(2,1)S(1)} %get-tuple-element.66), channel_id=1, source_target_pairs={{0,4},{4,0},{8,12},{12,8},{16,20},{20,16},{24,28},{28,24},{1,5},{5... | collective-permute-start | bytes 786440 | tf_op jit(solution)/shard_map/ppermute | solution.py:290
  63.0 8.7 %collective-permute-start.20 = (bf16[528,256]{1,0:T(8,128)(2,1)S(1)}, bf16[528,256]{1,0:T(8,128)(2,1)S(1)}, u32[]{:S(2)}, u32[]{:S(2)}) collective-permute-start(bf16[528,256]{1,0:T(8,128)(2,1)S(1)} %get-tuple-element.68), channel_id=1, source_target_pairs={{0,1},{1,0},{2,3},{3,2},{4,5},{5,4},{6,7},{7,6},{8,9},{9,8},{10,11... | collective-permute-start | bytes 811016 | tf_op jit(solution)/shard_map/ppermute | solution.py:287
  63.0 8.7 %collective-permute-start.21 = (bf16[528,256]{1,0:T(8,128)(2,1)S(1)}, bf16[528,256]{1,0:T(8,128)(2,1)S(1)}, u32[]{:S(2)}, u32[]{:S(2)}) collective-permute-start(bf16[528,256]{1,0:T(8,128)(2,1)S(1)} %get-tuple-element.69), channel_id=1, source_target_pairs={{0,3},{1,2},{2,1},{3,0},{4,7},{5,6},{6,5},{7,4},{8,11},{9,10},{10,... | collective-permute-start | bytes 811016 | tf_op jit(solution)/shard_map/ppermute | solution.py:287
  63.1 15.4 %collective-permute-start.17 = (bf16[128,1024]{1,0:T(8,128)(2,1)S(1)}, bf16[128,1024]{1,0:T(8,128)(2,1)S(1)}, u32[]{:S(2)}, u32[]{:S(2)}) collective-permute-start(bf16[128,1024]{1,0:T(8,128)(2,1)S(1)} %add_convert_fusion.1), channel_id=1, source_target_pairs={{0,16},{4,20},{8,24},{12,28},{16,0},{20,4},{24,8},{28,12},{1,17},{... | collective-permute-start | bytes 786440 | tf_op jit(solution)/shard_map/ppermute | solution.py:290
  65.4 13.1 %collective-permute-start.14 = (bf16[128,1024]{1,0:T(8,128)(2,1)S(1)}, bf16[128,1024]{1,0:T(8,128)(2,1)S(1)}, u32[]{:S(2)}, u32[]{:S(2)}) collective-permute-start(bf16[128,1024]{1,0:T(8,128)(2,1)S(1)} %get-tuple-element.56), channel_id=1, source_target_pairs={{0,4},{4,0},{8,12},{12,8},{16,20},{20,16},{24,28},{28,24},{1,5},{5... | collective-permute-start | bytes 786440 | tf_op jit(solution)/shard_map/ppermute | solution.py:290
  69.1 11.6 %collective-permute-start.19 = (bf16[128,1024]{1,0:T(8,128)(2,1)S(1)}, bf16[128,1024]{1,0:T(8,128)(2,1)S(1)}, u32[]{:S(2)}, u32[]{:S(2)}) collective-permute-start(bf16[128,1024]{1,0:T(8,128)(2,1)S(1)} %add_convert_fusion), channel_id=1, source_target_pairs={{0,8},{4,12},{8,0},{12,4},{16,24},{20,28},{24,16},{28,20},{1,9},{5... | collective-permute-start | bytes 786440 | tf_op jit(solution)/shard_map/ppermute | solution.py:290
  (3 other events, 12.6 us)

commit v8 on v2

--- a/solution.py
+++ b/solution.py
@@ -304,9 +304,9 @@
     if staged:
         in_weight, _ = after((in_weight, back))
         pieces = [in_weight] + [None] * (n_seq - 1)
-        pieces[1] = trade(in_weight, 1)
-        for step in range(2, n_seq, 2):
+        for step in (1, 2, 4):
             pieces[step] = trade(in_weight, step)
+        pieces[6] = trade(pieces[4], 2)
     else:
         pieces = [lax.all_gather(in_weight, "seq", axis=0, tiled=True)]
 
@@ -326,7 +326,7 @@
     parts = [low]
     for step in reversed([1 << bit for bit in range(n_mp.bit_length() - 1)]):
         if staged and step == 1:
-            parts[0], pieces[6], pieces[3] = after((parts[0], pieces[6], pieces[3]))
+            parts[0], _ = after((parts[0], (pieces[4], pieces[3])))
         parts = [part for held in parts for part in (held, swap(held, step))]
     onehot, share, delta, slope = call(
         spread_kernel,
@@ -356,9 +356,9 @@
     if staged:
         fetched = {}
         fetched[7] = trade(terms[7], 1)
-        pieces[7] = trade(after((pieces[6], terms[0]))[0], 1)
-        pieces[5] = trade(after((pieces[4], fetched[7]))[0], 1)
-        fetched[5] = trade(after((terms[5], pieces[7], previous))[0], 1)
+        pieces[5] = trade(after((pieces[4], terms[0]))[0], 1)
+        pieces[7] = trade(after((pieces[6], fetched[7]))[0], 1)
+        fetched[5] = trade(after((terms[5], pieces[5], previous))[0], 1)
 
     *partials, weight_full = call(
         functools.partial(partial_kernel, n_mp),
@@ -371,13 +371,14 @@
     grads = [partials[0]] + [swap(partials[step], step) for step in range(1, n_mp)]
 
     if staged:
-        fetched[6] = trade((terms[6] + fetched[7].astype(F32)).astype(BF16), 6)
+        fetched[6] = trade((terms[6] + fetched[7].astype(F32)).astype(BF16), 2)
         fetched[3] = trade(after((terms[3], weight_full, share, fetched[6]))[0], 1)
-        fetched[4] = trade((terms[4] + fetched[5].astype(F32)).astype(BF16), 4)
+        pair = terms[4] + fetched[5].astype(F32) + fetched[6].astype(F32)
+        fetched[4] = trade(pair.astype(BF16), 4)
         fetched[1] = trade(after((terms[1], fetched[5], grads[2]))[0], 1)
         fetched[2] = trade((terms[2] + fetched[3].astype(F32)).astype(BF16), 2)
         grad_weight = terms[0] + fetched[1].astype(F32)
-        for step in (6, 4, 2):
+        for step in (4, 2):
             grad_weight = grad_weight + fetched[step].astype(F32)
     else:
         received = lax.all_to_all(terms[0], "seq", split_axis=0, concat_axis=0, tiled=True)

time: 73.1 us -> 73.3 us (level)
  waiting for transfers between devices: 16.6 us -> 25.1 us
  starting transfers between devices: 38.5 us -> 30.8 us
    ppermute x14, starting transfers between devices: 30.2 us -> 21.7 us  [trade(): return lax.ppermute(value, 'seq', [(i, i ^ step) for i in range(n_seq)])]
    ppermute x6, waiting for transfers between devices: 0.09 us -> 4.13 us  [swap(): return lax.ppermute(value, 'mp', [(i, i ^ step) for i in range(n_mp)])]
    ppermute x1, waiting for transfers between devices: 0.01 us -> 2.86 us  [shards(): lax.ppermute(ahead, 'seq', [(i, i + 1) for i in range(n_seq - 1)])]
    ppermute x1, waiting for transfers between devices: 0.76 us -> 2.15 us  [shards(): following = lax.ppermute(back, 'seq', [(i, i - 1) for i in range(1, n_seq)])]
    ppermute x6, starting transfers between devices: 4.06 us -> 4.92 us  [swap(): return lax.ppermute(value, 'mp', [(i, i ^ step) for i in range(n_mp)])]
  transfers between devices with their start and end apart: 22 -> 22, of which waited for: 10 -> 15; matrix products, arithmetic and copies ran while one was open for 0% -> 0% of each run, Pallas kernels for 18% -> 17%
where the time goes in v8:
time: 73.3 us; the launch traced here: 73.1 us
  starting transfers between devices  30.8 us (42%)
  waiting for transfers between devices  25.1 us (34%)
  Pallas kernels  13.8 us (19%)
  local copies, waits for them, and re-layouts  1.44 us (2%)
  other arithmetic  1.16 us (2%)
  between operations  0.76 us (1%)
    ppermute x14, starting transfers between devices, trade(): return lax.ppermute(value, 'seq', [(i, i ^ step) for i in range(n_seq)])  21.7 us
    ppermute x14, waiting for transfers between devices, trade(): return lax.ppermute(value, 'seq', [(i, i ^ step) for i in range(n_seq)])  16 us
    pallas_call x7, Pallas kernels, call(): pl.pallas_call(kernel, out_shape=out_shape, in_specs=in_specs, out_specs=...  13.8 us
    ppermute x6, starting transfers between devices, swap(): return lax.ppermute(value, 'mp', [(i, i ^ step) for i in range(n_mp)])  4.92 us
    ppermute x6, waiting for transfers between devices, swap(): return lax.ppermute(value, 'mp', [(i, i ^ step) for i in range(n_mp)])  4.13 us
    ppermute x1, starting transfers between devices, shards(): lax.ppermute(ahead, 'seq', [(i, i + 1) for i in range(n_seq - 1)])  2.9 us
    ppermute x1, waiting for transfers between devices, shards(): lax.ppermute(ahead, 'seq', [(i, i + 1) for i in range(n_seq - 1)])  2.86 us
    ppermute x1, waiting for transfers between devices, shards(): following = lax.ppermute(back, 'seq', [(i, i - 1) for i in range(1, n_seq)])  2.15 us
  transfers between devices with their start and end apart: 22, of which 15 were waited for; matrix products, arithmetic and copies ran while one was open for 0% of the time, Pallas kernels for 17%

profile of v8, /device:TPU:0, one launch (start us, length us, event | category | flops | bytes accessed | tf_op | source)
XLA Modules:
  0.0 73.1 jit_solution(18276791886579209995)
XLA Ops:
  2.5 3.1 %collective-permute-start.2 = (bf16[128,1024]{1,0:T(8,128)(2,1)}, bf16[128,1024]{1,0:T(8,128)(2,1)S(1)}, u32[]{:S(2)}, u32[]{:S(2)}) collective-permute-start(bf16[128,1024]{1,0:T(8,128)(2,1)} %refs_0_), channel_id=1, source_target_pairs={{0,8},{4,12},{8,0},{12,4},{16,24},{20,28},{24,16},{28,20},{1,9},{5... | collective-permute-start | bytes 786440 | tf_op jit(solution)/shard_map/ppermute | solution.py:277
  5.6 1.5 %collective-permute-start.1 = (bf16[128,1024]{1,0:T(8,128)(2,1)}, bf16[128,1024]{1,0:T(8,128)(2,1)S(1)}, u32[]{:S(2)}, u32[]{:S(2)}) collective-permute-start(bf16[128,1024]{1,0:T(8,128)(2,1)} %refs_0_), channel_id=1, source_target_pairs={{0,4},{4,0},{8,12},{12,8},{16,20},{20,16},{24,28},{28,24},{1,5},{5... | collective-permute-start | bytes 786440 | tf_op jit(solution)/shard_map/ppermute | solution.py:277
  8.4 3.3 %collective-permute-start.3 = (bf16[128,1024]{1,0:T(8,128)(2,1)}, bf16[128,1024]{1,0:T(8,128)(2,1)S(1)}, u32[]{:S(2)}, u32[]{:S(2)}) collective-permute-start(bf16[128,1024]{1,0:T(8,128)(2,1)} %refs_0_), channel_id=1, source_target_pairs={{0,16},{4,20},{8,24},{12,28},{16,0},{20,4},{24,8},{28,12},{1,17},{... | collective-permute-start | bytes 786440 | tf_op jit(solution)/shard_map/ppermute | solution.py:277
  11.7 2.1 %collective-permute-done.next_ref = bf16[16,384]{1,0:T(8,128)(2,1)S(1)} collective-permute-done((bf16[16,384]{1,0:T(8,128)(2,1)S(1)}, bf16[16,384]{1,0:T(8,128)(2,1)S(1)}, u32[]{:S(2)}, u32[]{:S(2)}) %collective-permute-start) | collective-permute-done | bytes 12320 | tf_op jit(solution)/shard_map/ppermute | solution.py:301
  14.5 2.1 %shard_map.77 = (bf16[512,256]{1,0:T(8,128)(2,1)S(1)}, f32[512,256]{1,0:T(8,128)S(1)}, f32[512,256]{1,0:T(8,128)S(1)}) custom-call(bf16[1024,256]{1,0:T(8,128)(2,1)S(1)} %get-tuple-element.38.hidden_ref, bf16[16,384]{1,0:T(8,128)(2,1)S(1)} %collective-permute-done.next_ref, s32[8,128]{1,0:T(8,128)S(1)} %get-tuple-element.40.start_ref.refs_4_, ...), custom_call_target="tpu_custom_call" | custom-call | tf_op jit(solution)/shard_map/pallas_call | solution.py:245
  16.6 1.4 %collective-permute-start.4 = (bf16[128,1024]{1,0:T(8,128)(2,1)S(1)}, bf16[128,1024]{1,0:T(8,128)(2,1)S(1)}, u32[]{:S(2)}, u32[]{:S(2)}) collective-permute-start(bf16[128,1024]{1,0:T(8,128)(2,1)S(1)} %collective-permute-done.2.refs_2_), channel_id=1, source_target_pairs={{0,4},{4,0},{8,12},{12,8},{16,20},{20,16},{24,28},{28,24},{1,5},{5... | collective-permute-start | bytes 786440 | tf_op jit(solution)/shard_map/ppermute | solution.py:277
  18.1 1.8 %collective-permute-start.6 = (bf16[512,256]{1,0:T(8,128)(2,1)S(1)}, bf16[512,256]{1,0:T(8,128)(2,1)S(1)}, u32[]{:S(2)}, u32[]{:S(2)}) collective-permute-start(bf16[512,256]{1,0:T(8,128)(2,1)S(1)} %get-tuple-element.46.refs_0_), channel_id=1, source_target_pairs={{0,2},{1,3},{2,0},{3,1},{4,6},{5,7},{6,4},{7,5},{8,10},{9,11},{10,... | collective-permute-start | bytes 786440 | tf_op jit(solution)/shard_map/ppermute | solution.py:274
  19.9 3.6 %collective-permute-done.3.refs_4_ = bf16[128,1024]{1,0:T(8,128)(2,1)S(1)} collective-permute-done((bf16[128,1024]{1,0:T(8,128)(2,1)}, bf16[128,1024]{1,0:T(8,128)(2,1)S(1)}, u32[]{:S(2)}, u32[]{:S(2)}) %collective-permute-start.3) | collective-permute-done | bytes 262176 | tf_op jit(solution)/shard_map/ppermute | solution.py:277
  26.0 1.7 %shard_map.78 = (f32[128,1024]{1,0:T(8,128)S(1)}, bf16[128,1024]{1,0:T(8,128)(2,1)S(1)}, f32[128,1024]{1,0:T(8,128)S(1)}, bf16[128,1024]{1,0:T(8,128)(2,1)S(1)},...) custom-call(bf16[512,256]{1,0:T(8,128)(2,1)S(1)} %get-tuple-element., ...), custom_call_target="tpu_custom_call" | custom-call | tf_op jit(solution)/shard_map/pallas_call | solution.py:245
  29.8 2.9 %collective-permute-start.8 = (bf16[32,384]{1,0:T(8,128)(2,1)S(1)}, bf16[32,384]{1,0:T(8,128)(2,1)S(1)}, u32[]{:S(2)}, u32[]{:S(2)}) collective-permute-start(bf16[32,384]{1,0:T(8,128)(2,1)S(1)} %get-tuple-element.47), channel_id=1, source_target_pairs={{0,4},{4,8},{8,12},{12,16},{16,20},{20,24},{24,28},{1,5},{5,9},{9,... | collective-permute-start | bytes 73736 | tf_op jit(solution)/shard_map/ppermute | solution.py:302
  33.2 3.8 %collective-permute-done.11 = bf16[128,1024]{1,0:T(8,128)(2,1)S(1)} collective-permute-done((bf16[128,1024]{1,0:T(8,128)(2,1)S(1)}, bf16[128,1024]{1,0:T(8,128)(2,1)S(1)}, u32[]{:S(2)}, u32[]{:S(2)}) %collective-permute-start.11) | collective-permute-done | bytes 262176 | tf_op jit(solution)/shard_map/ppermute | solution.py:277
  38.7 2.9 %collective-permute-done.8.prev_ref = bf16[32,384]{1,0:T(8,128)(2,1)S(1)} collective-permute-done((bf16[32,384]{1,0:T(8,128)(2,1)S(1)}, bf16[32,384]{1,0:T(8,128)(2,1)S(1)}, u32[]{:S(2)}, u32[]{:S(2)}) %collective-permute-start.8) | collective-permute-done | bytes 24608 | tf_op jit(solution)/shard_map/ppermute | solution.py:302
  42.5 1.5 %collective-permute-start.13 = (bf16[128,1024]{1,0:T(8,128)(2,1)S(1)}, bf16[128,1024]{1,0:T(8,128)(2,1)S(1)}, u32[]{:S(2)}, u32[]{:S(2)}) collective-permute-start(bf16[128,1024]{1,0:T(8,128)(2,1)S(1)} %get-tuple-element.56), channel_id=1, source_target_pairs={{0,4},{4,0},{8,12},{12,8},{16,20},{20,16},{24,28},{28,24},{1,5},{5... | collective-permute-start | bytes 786440 | tf_op jit(solution)/shard_map/ppermute | solution.py:277
  44.1 1.7 %shard_map.81 = (bf16[1024,512]{1,0:T(8,128)(2,1)S(1)}, f32[1024,256]{1,0:T(8,128)S(1)}, f32[1024,256]{1,0:T(8,128)S(1)}, f32[1024,256]{1,0:T(8,128)S(1)}) custom-call(bf16[1024,256]{1,0:T(8,128)(2,1)S(1)} %get-tuple-element.38.hidden_ref, bf16[32,384]{1,0:T(8,128)(2,1)S(1)} %collective-permute-done.8.prev_ref, ...), custom_call_target="tpu_custom_call" | custom-call | tf_op jit(solution)/shard_map/pallas_call | solution.py:245
  45.8 2.3 %collective-permute-done.12.refs_7_ = bf16[128,1024]{1,0:T(8,128)(2,1)S(1)} collective-permute-done((bf16[128,1024]{1,0:T(8,128)(2,1)S(1)}, bf16[128,1024]{1,0:T(8,128)(2,1)S(1)}, u32[]{:S(2)}, u32[]{:S(2)}) %collective-permute-start.12) | collective-permute-done | bytes 262176 | tf_op jit(solution)/shard_map/ppermute | solution.py:277
  48.2 2.5 %shard_map.79 = (bf16[528,256]{1,0:T(8,128)(2,1)S(1)}, bf16[528,256]{1,0:T(8,128)(2,1)S(1)}, bf16[528,256]{1,0:T(8,128)(2,1)S(1)}, bf16[528,256]{1,0:T(8,128)(2,1)S(1)}, bf16[1024,1024]{1,0:T(8,128)(2,1)}) custom-call(bf16[512,1024]{1,0:T(8,128)(2,1)S(1)} %copy-done, bf16[32,384]{1,0:T(8,128)(2,1)S(1)} %collective-permute-done.8.prev_ref, ...), custom_call_target="tpu_custom_call" | custom-call | tf_op jit(solution)/shard_map/pallas_call | solution.py:245
  50.7 1.5 %collective-permute-start.18 = (bf16[128,1024]{1,0:T(8,128)(2,1)S(1)}, bf16[128,1024]{1,0:T(8,128)(2,1)S(1)}, u32[]{:S(2)}, u32[]{:S(2)}) collective-permute-start(bf16[128,1024]{1,0:T(8,128)(2,1)S(1)} %get-tuple-element.66), channel_id=1, source_target_pairs={{0,4},{4,0},{8,12},{12,8},{16,20},{20,16},{24,28},{28,24},{1,5},{5... | collective-permute-start | bytes 786440 | tf_op jit(solution)/shard_map/ppermute | solution.py:277
  52.2 1.5 %collective-permute-start.14 = (bf16[528,256]{1,0:T(8,128)(2,1)S(1)}, bf16[528,256]{1,0:T(8,128)(2,1)S(1)}, u32[]{:S(2)}, u32[]{:S(2)}) collective-permute-start(bf16[528,256]{1,0:T(8,128)(2,1)S(1)} %get-tuple-element.57), channel_id=1, source_target_pairs={{0,2},{1,3},{2,0},{3,1},{4,6},{5,7},{6,4},{7,5},{8,10},{9,11},{10,... | collective-permute-start | bytes 811016 | tf_op jit(solution)/shard_map/ppermute | solution.py:274
  53.9 3.1 %collective-permute-start.17 = (bf16[128,1024]{1,0:T(8,128)(2,1)S(1)}, bf16[128,1024]{1,0:T(8,128)(2,1)S(1)}, u32[]{:S(2)}, u32[]{:S(2)}) collective-permute-start(bf16[128,1024]{1,0:T(8,128)(2,1)S(1)} %add_convert_fusion.1), channel_id=1, source_target_pairs={{0,16},{4,20},{8,24},{12,28},{16,0},{20,4},{24,8},{28,12},{1,17},{... | collective-permute-start | bytes 786440 | tf_op jit(solution)/shard_map/ppermute | solution.py:277
  57.0 1.6 %collective-permute-start.21 = (bf16[528,256]{1,0:T(8,128)(2,1)S(1)}, bf16[528,256]{1,0:T(8,128)(2,1)S(1)}, u32[]{:S(2)}, u32[]{:S(2)}) collective-permute-start(bf16[528,256]{1,0:T(8,128)(2,1)S(1)} %get-tuple-element.69), channel_id=1, source_target_pairs={{0,3},{1,2},{2,1},{3,0},{4,7},{5,6},{6,5},{7,4},{8,11},{9,10},{10,... | collective-permute-start | bytes 811016 | tf_op jit(solution)/shard_map/ppermute | solution.py:274
  60.8 2.4 %shard_map.80 = bf16[512,1024]{1,0:T(8,128)(2,1)} custom-call(bf16[512,256]{1,0:T(8,128)(2,1)S(1)} %get-tuple-element.46.refs_0_, bf16[512,256]{1,0:T(8,128)(2,1)S(1)} %collective-permute-done.5.refs_1_, bf16[512,256]{1,0:T(8,128)(2,1)S(1)} %collective-permute-done.6.refs_2_, bf16[512,256]{1,0:T(8,128)(2,1)S(1)} %collective-permute-done.7.refs_3_, ...), custom_call_target="tpu_custom_call" | custom-call | tf_op jit(solution)/shard_map/pallas_call | solution.py:245
  63.1 2.0 %collective-permute-done.21.refs_3_ = bf16[528,256]{1,0:T(8,128)(2,1)S(1)} collective-permute-done((bf16[528,256]{1,0:T(8,128)(2,1)S(1)}, bf16[528,256]{1,0:T(8,128)(2,1)S(1)}, u32[]{:S(2)}, u32[]{:S(2)}) %collective-permute-start.21) | collective-permute-done | bytes 270368 | tf_op jit(solution)/shard_map/ppermute | solution.py:274
  65.1 2.3 %shard_map.82 = bf16[1024,256]{1,0:T(8,128)(2,1)} custom-call(bf16[528,256]{1,0:T(8,128)(2,1)S(1)} %get-tuple-element.67.refs_0_, bf16[528,256]{1,0:T(8,128)(2,1)S(1)} %collective-permute-done.20.refs_1_, bf16[528,256]{1,0:T(8,128)(2,1)S(1)} %collective-permute-done.14.refs_2_, bf16[528,256]{1,0:T(8,128)(2,1)S(1)} %collective-permute-done.21.refs_3_, ...), custom_call_target="tpu_custom_call" | custom-call | tf_op jit(solution)/shard_map/pallas_call | solution.py:245
  67.7 4.5 %collective-permute-done.19 = bf16[128,1024]{1,0:T(8,128)(2,1)S(1)} collective-permute-done((bf16[128,1024]{1,0:T(8,128)(2,1)S(1)}, bf16[128,1024]{1,0:T(8,128)(2,1)S(1)}, u32[]{:S(2)}, u32[]{:S(2)}) %collective-permute-start.19) | collective-permute-done | bytes 262176 | tf_op jit(solution)/shard_map/ppermute | solution.py:277
  (41 shorter events, 15.2 us)
Async XLA Ops:
  0.6 25.3 %copy-start = (bf16[512,1024]{1,0:T(8,128)(2,1)S(1)}, bf16[512,1024]{1,0:T(8,128)(2,1)}, u32[]{:S(2)}) copy-start(bf16[512,1024]{1,0:T(8,128)(2,1)} %grad_ref.1) | copy-start | bytes 3145732
  2.5 14.1 %collective-permute-start.2 = (bf16[128,1024]{1,0:T(8,128)(2,1)}, bf16[128,1024]{1,0:T(8,128)(2,1)S(1)}, u32[]{:S(2)}, u32[]{:S(2)}) collective-permute-start(bf16[128,1024]{1,0:T(8,128)(2,1)} %refs_0_), channel_id=1, source_target_pairs={{0,8},{4,12},{8,0},{12,4},{16,24},{20,28},{24,16},{28,20},{1,9},{5... | collective-permute-start | bytes 786440 | tf_op jit(solution)/shard_map/ppermute | solution.py:277
  5.6 11.0 %collective-permute-start.1 = (bf16[128,1024]{1,0:T(8,128)(2,1)}, bf16[128,1024]{1,0:T(8,128)(2,1)S(1)}, u32[]{:S(2)}, u32[]{:S(2)}) collective-permute-start(bf16[128,1024]{1,0:T(8,128)(2,1)} %refs_0_), channel_id=1, source_target_pairs={{0,4},{4,0},{8,12},{12,8},{16,20},{20,16},{24,28},{28,24},{1,5},{5... | collective-permute-start | bytes 786440 | tf_op jit(solution)/shard_map/ppermute | solution.py:277
  7.1 6.7 %collective-permute-start = (bf16[16,384]{1,0:T(8,128)(2,1)S(1)}, bf16[16,384]{1,0:T(8,128)(2,1)S(1)}, u32[]{:S(2)}, u32[]{:S(2)}) collective-permute-start(bf16[16,384]{1,0:T(8,128)(2,1)S(1)} %get-tuple-element.39), channel_id=1, source_target_pairs={{4,0},{8,4},{12,8},{16,12},{20,16},{24,20},{28,24},{5,1},{9,5},{13... | collective-permute-start | bytes 36872 | tf_op jit(solution)/shard_map/ppermute | solution.py:301
  8.4 15.0 %collective-permute-start.3 = (bf16[128,1024]{1,0:T(8,128)(2,1)}, bf16[128,1024]{1,0:T(8,128)(2,1)S(1)}, u32[]{:S(2)}, u32[]{:S(2)}) collective-permute-start(bf16[128,1024]{1,0:T(8,128)(2,1)} %refs_0_), channel_id=1, source_target_pairs={{0,16},{4,20},{8,24},{12,28},{16,0},{20,4},{24,8},{28,12},{1,17},{... | collective-permute-start | bytes 786440 | tf_op jit(solution)/shard_map/ppermute | solution.py:277
  16.6 31.6 %copy-start.2 = (bf16[128,1024]{1,0:T(8,128)(2,1)S(1)}, bf16[128,1024]{1,0:T(8,128)(2,1)}, u32[]{:S(2)}) copy-start(bf16[128,1024]{1,0:T(8,128)(2,1)} %refs_0_) | copy-start | bytes 786436
  16.6 6.9 %collective-permute-start.4 = (bf16[128,1024]{1,0:T(8,128)(2,1)S(1)}, bf16[128,1024]{1,0:T(8,128)(2,1)S(1)}, u32[]{:S(2)}, u32[]{:S(2)}) collective-permute-start(bf16[128,1024]{1,0:T(8,128)(2,1)S(1)} %collective-permute-done.2.refs_2_), channel_id=1, source_target_pairs={{0,4},{4,0},{8,12},{12,8},{16,20},{20,16},{24,28},{28,24},{1,5},{5... | collective-permute-start | bytes 786440 | tf_op jit(solution)/shard_map/ppermute | solution.py:277
  18.1 6.4 %collective-permute-start.6 = (bf16[512,256]{1,0:T(8,128)(2,1)S(1)}, bf16[512,256]{1,0:T(8,128)(2,1)S(1)}, u32[]{:S(2)}, u32[]{:S(2)}) collective-permute-start(bf16[512,256]{1,0:T(8,128)(2,1)S(1)} %get-tuple-element.46.refs_0_), channel_id=1, source_target_pairs={{0,2},{1,3},{2,0},{3,1},{4,6},{5,7},{6,4},{7,5},{8,10},{9,11},{10,... | collective-permute-start | bytes 786440 | tf_op jit(solution)/shard_map/ppermute | solution.py:274
  23.5 1.5 %collective-permute-start.5 = (bf16[512,256]{1,0:T(8,128)(2,1)S(1)}, bf16[512,256]{1,0:T(8,128)(2,1)S(1)}, u32[]{:S(2)}, u32[]{:S(2)}) collective-permute-start(bf16[512,256]{1,0:T(8,128)(2,1)S(1)} %get-tuple-element.46.refs_0_), channel_id=1, source_target_pairs={{0,1},{1,0},{2,3},{3,2},{4,5},{5,4},{6,7},{7,6},{8,9},{9,8},{10,11... | collective-permute-start | bytes 786440 | tf_op jit(solution)/shard_map/ppermute | solution.py:274
  24.4 1.5 %collective-permute-start.7 = (bf16[512,256]{1,0:T(8,128)(2,1)S(1)}, bf16[512,256]{1,0:T(8,128)(2,1)S(1)}, u32[]{:S(2)}, u32[]{:S(2)}) collective-permute-start(bf16[512,256]{1,0:T(8,128)(2,1)S(1)} %collective-permute-done.6.refs_2_), channel_id=1, source_target_pairs={{0,1},{1,0},{2,3},{3,2},{4,5},{5,4},{6,7},{7,6},{8,9},{9,8},{10,11... | collective-permute-start | bytes 786440 | tf_op jit(solution)/shard_map/ppermute | solution.py:274
  24.4 8.7 %collective-permute-start.10 = (bf16[128,1024]{1,0:T(8,128)(2,1)S(1)}, bf16[128,1024]{1,0:T(8,128)(2,1)S(1)}, u32[]{:S(2)}, u32[]{:S(2)}) collective-permute-start(bf16[128,1024]{1,0:T(8,128)(2,1)S(1)} %collective-permute-done.3.refs_4_), channel_id=1, source_target_pairs={{0,8},{4,12},{8,0},{12,4},{16,24},{20,28},{24,16},{28,20},{1,9},{5... | collective-permute-start | bytes 786440 | tf_op jit(solution)/shard_map/ppermute | solution.py:277
  27.7 9.2 %collective-permute-start.11 = (bf16[128,1024]{1,0:T(8,128)(2,1)S(1)}, bf16[128,1024]{1,0:T(8,128)(2,1)S(1)}, u32[]{:S(2)}, u32[]{:S(2)}) collective-permute-start(bf16[128,1024]{1,0:T(8,128)(2,1)S(1)} %get-tuple-element.51), channel_id=1, source_target_pairs={{0,4},{4,0},{8,12},{12,8},{16,20},{20,16},{24,28},{28,24},{1,5},{5... | collective-permute-start | bytes 786440 | tf_op jit(solution)/shard_map/ppermute | solution.py:277
  28.8 13.8 %collective-permute-start.9 = (bf16[128,1024]{1,0:T(8,128)(2,1)S(1)}, bf16[128,1024]{1,0:T(8,128)(2,1)S(1)}, u32[]{:S(2)}, u32[]{:S(2)}) collective-permute-start(bf16[128,1024]{1,0:T(8,128)(2,1)S(1)} %collective-permute-done.3.refs_4_), channel_id=1, source_target_pairs={{0,4},{4,0},{8,12},{12,8},{16,20},{20,16},{24,28},{28,24},{1,5},{5... | collective-permute-start | bytes 786440 | tf_op jit(solution)/shard_map/ppermute | solution.py:277
  29.8 11.8 %collective-permute-start.8 = (bf16[32,384]{1,0:T(8,128)(2,1)S(1)}, bf16[32,384]{1,0:T(8,128)(2,1)S(1)}, u32[]{:S(2)}, u32[]{:S(2)}) collective-permute-start(bf16[32,384]{1,0:T(8,128)(2,1)S(1)} %get-tuple-element.47), channel_id=1, source_target_pairs={{0,4},{4,8},{8,12},{12,16},{16,20},{20,24},{24,28},{1,5},{5,9},{9,... | collective-permute-start | bytes 73736 | tf_op jit(solution)/shard_map/ppermute | solution.py:302
  36.9 11.2 %collective-permute-start.12 = (bf16[128,1024]{1,0:T(8,128)(2,1)S(1)}, bf16[128,1024]{1,0:T(8,128)(2,1)S(1)}, u32[]{:S(2)}, u32[]{:S(2)}) collective-permute-start(bf16[128,1024]{1,0:T(8,128)(2,1)S(1)} %collective-permute-done.10.refs_6_), channel_id=1, source_target_pairs={{0,4},{4,0},{8,12},{12,8},{16,20},{20,16},{24,28},{28,24},{1,5},{5... | collective-permute-start | bytes 786440 | tf_op jit(solution)/shard_map/ppermute | solution.py:277
  38.0 12.7 %collective-permute-start.16 = (bf16[128,1024]{1,0:T(8,128)(2,1)S(1)}, bf16[128,1024]{1,0:T(8,128)(2,1)S(1)}, u32[]{:S(2)}, u32[]{:S(2)}) collective-permute-start(bf16[128,1024]{1,0:T(8,128)(2,1)S(1)} %add_convert_fusion.2), channel_id=1, source_target_pairs={{0,8},{4,12},{8,0},{12,4},{16,24},{20,28},{24,16},{28,20},{1,9},{5... | collective-permute-start | bytes 786440 | tf_op jit(solution)/shard_map/ppermute | solution.py:277
  42.5 11.2 %collective-permute-start.13 = (bf16[128,1024]{1,0:T(8,128)(2,1)S(1)}, bf16[128,1024]{1,0:T(8,128)(2,1)S(1)}, u32[]{:S(2)}, u32[]{:S(2)}) collective-permute-start(bf16[128,1024]{1,0:T(8,128)(2,1)S(1)} %get-tuple-element.56), channel_id=1, source_target_pairs={{0,4},{4,0},{8,12},{12,8},{16,20},{20,16},{24,28},{28,24},{1,5},{5... | collective-permute-start | bytes 786440 | tf_op jit(solution)/shard_map/ppermute | solution.py:277
  50.7 7.9 %collective-permute-start.18 = (bf16[128,1024]{1,0:T(8,128)(2,1)S(1)}, bf16[128,1024]{1,0:T(8,128)(2,1)S(1)}, u32[]{:S(2)}, u32[]{:S(2)}) collective-permute-start(bf16[128,1024]{1,0:T(8,128)(2,1)S(1)} %get-tuple-element.66), channel_id=1, source_target_pairs={{0,4},{4,0},{8,12},{12,8},{16,20},{20,16},{24,28},{28,24},{1,5},{5... | collective-permute-start | bytes 786440 | tf_op jit(solution)/shard_map/ppermute | solution.py:277
  52.2 7.6 %collective-permute-start.14 = (bf16[528,256]{1,0:T(8,128)(2,1)S(1)}, bf16[528,256]{1,0:T(8,128)(2,1)S(1)}, u32[]{:S(2)}, u32[]{:S(2)}) collective-permute-start(bf16[528,256]{1,0:T(8,128)(2,1)S(1)} %get-tuple-element.57), channel_id=1, source_target_pairs={{0,2},{1,3},{2,0},{3,1},{4,6},{5,7},{6,4},{7,5},{8,10},{9,11},{10,... | collective-permute-start | bytes 811016 | tf_op jit(solution)/shard_map/ppermute | solution.py:274
  53.9 13.8 %collective-permute-start.17 = (bf16[128,1024]{1,0:T(8,128)(2,1)S(1)}, bf16[128,1024]{1,0:T(8,128)(2,1)S(1)}, u32[]{:S(2)}, u32[]{:S(2)}) collective-permute-start(bf16[128,1024]{1,0:T(8,128)(2,1)S(1)} %add_convert_fusion.1), channel_id=1, source_target_pairs={{0,16},{4,20},{8,24},{12,28},{16,0},{20,4},{24,8},{28,12},{1,17},{... | collective-permute-start | bytes 786440 | tf_op jit(solution)/shard_map/ppermute | solution.py:277
  57.0 6.1 %collective-permute-start.20 = (bf16[528,256]{1,0:T(8,128)(2,1)S(1)}, bf16[528,256]{1,0:T(8,128)(2,1)S(1)}, u32[]{:S(2)}, u32[]{:S(2)}) collective-permute-start(bf16[528,256]{1,0:T(8,128)(2,1)S(1)} %get-tuple-element.68), channel_id=1, source_target_pairs={{0,1},{1,0},{2,3},{3,2},{4,5},{5,4},{6,7},{7,6},{8,9},{9,8},{10,11... | collective-permute-start | bytes 811016 | tf_op jit(solution)/shard_map/ppermute | solution.py:274
  57.0 8.1 %collective-permute-start.21 = (bf16[528,256]{1,0:T(8,128)(2,1)S(1)}, bf16[528,256]{1,0:T(8,128)(2,1)S(1)}, u32[]{:S(2)}, u32[]{:S(2)}) collective-permute-start(bf16[528,256]{1,0:T(8,128)(2,1)S(1)} %get-tuple-element.69), channel_id=1, source_target_pairs={{0,3},{1,2},{2,1},{3,0},{4,7},{5,6},{6,5},{7,4},{8,11},{9,10},{10,... | collective-permute-start | bytes 811016 | tf_op jit(solution)/shard_map/ppermute | solution.py:274
  58.7 13.5 %collective-permute-start.19 = (bf16[128,1024]{1,0:T(8,128)(2,1)S(1)}, bf16[128,1024]{1,0:T(8,128)(2,1)S(1)}, u32[]{:S(2)}, u32[]{:S(2)}) collective-permute-start(bf16[128,1024]{1,0:T(8,128)(2,1)S(1)} %add_convert_fusion), channel_id=1, source_target_pairs={{0,8},{4,12},{8,0},{12,4},{16,24},{20,28},{24,16},{28,20},{1,9},{5... | collective-permute-start | bytes 786440 | tf_op jit(solution)/shard_map/ppermute | solution.py:277
  59.8 12.3 %collective-permute-start.15 = (bf16[128,1024]{1,0:T(8,128)(2,1)S(1)}, bf16[128,1024]{1,0:T(8,128)(2,1)S(1)}, u32[]{:S(2)}, u32[]{:S(2)}) collective-permute-start(bf16[128,1024]{1,0:T(8,128)(2,1)S(1)} %get-tuple-element.58), channel_id=1, source_target_pairs={{0,4},{4,0},{8,12},{12,8},{16,20},{20,16},{24,28},{28,24},{1,5},{5... | collective-permute-start | bytes 786440 | tf_op jit(solution)/shard_map/ppermute | solution.py:277
  (3 other events, 11.5 us)

commit v9 on v8

--- a/solution.py
+++ b/solution.py
@@ -326,7 +326,7 @@
     parts = [low]
     for step in reversed([1 << bit for bit in range(n_mp.bit_length() - 1)]):
         if staged and step == 1:
-            parts[0], _ = after((parts[0], (pieces[4], pieces[3])))
+            parts[0], _ = after((parts[0], (pieces[4], pieces[3], previous)))
         parts = [part for held in parts for part in (held, swap(held, step))]
     onehot, share, delta, slope = call(
         spread_kernel,
@@ -356,9 +356,9 @@
     if staged:
         fetched = {}
         fetched[7] = trade(terms[7], 1)
-        pieces[5] = trade(after((pieces[4], terms[0]))[0], 1)
-        pieces[7] = trade(after((pieces[6], fetched[7]))[0], 1)
-        fetched[5] = trade(after((terms[5], pieces[5], previous))[0], 1)
+        pieces[5] = trade(pieces[4], 1)
+        pieces[7] = trade(after((pieces[6], fetched[7], pieces[5]))[0], 1)
+        fetched[5] = trade(after((terms[5], pieces[5]))[0], 1)
 
     *partials, weight_full = call(
         functools.partial(partial_kernel, n_mp),

time: 73.3 us -> 71.4 us (0.974)
  starting transfers between devices: 30.8 us -> 28.9 us
    ppermute x14, waiting for transfers between devices: 16 us -> 17.9 us  [trade(): return lax.ppermute(value, 'seq', [(i, i ^ step) for i in range(n_seq)])]
    ppermute x6, starting transfers between devices: 4.92 us -> 3.01 us  [swap(): return lax.ppermute(value, 'mp', [(i, i ^ step) for i in range(n_mp)])]
    ppermute x1, waiting for transfers between devices: 2.86 us -> 1.5 us  [shards(): lax.ppermute(ahead, 'seq', [(i, i + 1) for i in range(n_seq - 1)])]
  transfers between devices with their start and end apart: 22 -> 22, of which waited for: 15 -> 11; matrix products, arithmetic and copies ran while one was open for 0% -> 0% of each run, Pallas kernels for 17% -> 18%
where the time goes in v9:
time: 71.4 us; the launch traced here: 71.2 us
  starting transfers between devices  28.9 us (40%)
  waiting for transfers between devices  25.1 us (35%)
  Pallas kernels  13.8 us (19%)
  local copies, waits for them, and re-layouts  1.43 us (2%)
  other arithmetic  1.15 us (2%)
  between operations  0.76 us (1%)
    ppermute x14, starting transfers between devices, trade(): return lax.ppermute(value, 'seq', [(i, i ^ step) for i in range(n_seq)])  22.3 us
    ppermute x14, waiting for transfers between devices, trade(): return lax.ppermute(value, 'seq', [(i, i ^ step) for i in range(n_seq)])  17.9 us
    pallas_call x7, Pallas kernels, call(): pl.pallas_call(kernel, out_shape=out_shape, in_specs=in_specs, out_specs=...  13.8 us
    ppermute x6, waiting for transfers between devices, swap(): return lax.ppermute(value, 'mp', [(i, i ^ step) for i in range(n_mp)])  3.52 us
    ppermute x6, starting transfers between devices, swap(): return lax.ppermute(value, 'mp', [(i, i ^ step) for i in range(n_mp)])  3.01 us
    ppermute x1, starting transfers between devices, shards(): lax.ppermute(ahead, 'seq', [(i, i + 1) for i in range(n_seq - 1)])  2.34 us
    ppermute x1, waiting for transfers between devices, shards(): following = lax.ppermute(back, 'seq', [(i, i - 1) for i in range(1, n_seq)])  2.15 us
    ppermute x1, waiting for transfers between devices, shards(): lax.ppermute(ahead, 'seq', [(i, i + 1) for i in range(n_seq - 1)])  1.5 us
  transfers between devices with their start and end apart: 22, of which 11 were waited for; matrix products, arithmetic and copies ran while one was open for 0% of the time, Pallas kernels for 18%

profile of v9, /device:TPU:0, one launch (start us, length us, event | category | flops | bytes accessed | tf_op | source)
XLA Modules:
  0.0 71.2 jit_solution(15098700239328564998)
XLA Ops:
  2.5 3.1 %collective-permute-start.2 = (bf16[128,1024]{1,0:T(8,128)(2,1)}, bf16[128,1024]{1,0:T(8,128)(2,1)S(1)}, u32[]{:S(2)}, u32[]{:S(2)}) collective-permute-start(bf16[128,1024]{1,0:T(8,128)(2,1)} %refs_0_), channel_id=1, source_target_pairs={{0,8},{4,12},{8,0},{12,4},{16,24},{20,28},{24,16},{28,20},{1,9},{5... | collective-permute-start | bytes 786440 | tf_op jit(solution)/shard_map/ppermute | solution.py:277
  5.6 1.5 %collective-permute-start.1 = (bf16[128,1024]{1,0:T(8,128)(2,1)}, bf16[128,1024]{1,0:T(8,128)(2,1)S(1)}, u32[]{:S(2)}, u32[]{:S(2)}) collective-permute-start(bf16[128,1024]{1,0:T(8,128)(2,1)} %refs_0_), channel_id=1, source_target_pairs={{0,4},{4,0},{8,12},{12,8},{16,20},{20,16},{24,28},{28,24},{1,5},{5... | collective-permute-start | bytes 786440 | tf_op jit(solution)/shard_map/ppermute | solution.py:277
  8.4 3.3 %collective-permute-start.3 = (bf16[128,1024]{1,0:T(8,128)(2,1)}, bf16[128,1024]{1,0:T(8,128)(2,1)S(1)}, u32[]{:S(2)}, u32[]{:S(2)}) collective-permute-start(bf16[128,1024]{1,0:T(8,128)(2,1)} %refs_0_), channel_id=1, source_target_pairs={{0,16},{4,20},{8,24},{12,28},{16,0},{20,4},{24,8},{28,12},{1,17},{... | collective-permute-start | bytes 786440 | tf_op jit(solution)/shard_map/ppermute | solution.py:277
  11.7 2.1 %collective-permute-done.next_ref = bf16[16,384]{1,0:T(8,128)(2,1)S(1)} collective-permute-done((bf16[16,384]{1,0:T(8,128)(2,1)S(1)}, bf16[16,384]{1,0:T(8,128)(2,1)S(1)}, u32[]{:S(2)}, u32[]{:S(2)}) %collective-permute-start) | collective-permute-done | bytes 12320 | tf_op jit(solution)/shard_map/ppermute | solution.py:301
  14.5 2.1 %shard_map.77 = (bf16[512,256]{1,0:T(8,128)(2,1)S(1)}, f32[512,256]{1,0:T(8,128)S(1)}, f32[512,256]{1,0:T(8,128)S(1)}) custom-call(bf16[1024,256]{1,0:T(8,128)(2,1)S(1)} %get-tuple-element.37.hidden_ref, bf16[16,384]{1,0:T(8,128)(2,1)S(1)} %collective-permute-done.next_ref, s32[8,128]{1,0:T(8,128)S(1)} %get-tuple-element.39.start_ref.refs_4_, ...), custom_call_target="tpu_custom_call" | custom-call | tf_op jit(solution)/shard_map/pallas_call | solution.py:245
  16.6 1.4 %collective-permute-start.4 = (bf16[128,1024]{1,0:T(8,128)(2,1)S(1)}, bf16[128,1024]{1,0:T(8,128)(2,1)S(1)}, u32[]{:S(2)}, u32[]{:S(2)}) collective-permute-start(bf16[128,1024]{1,0:T(8,128)(2,1)S(1)} %collective-permute-done.2.refs_2_), channel_id=1, source_target_pairs={{0,4},{4,0},{8,12},{12,8},{16,20},{20,16},{24,28},{28,24},{1,5},{5... | collective-permute-start | bytes 786440 | tf_op jit(solution)/shard_map/ppermute | solution.py:277
  18.1 1.8 %collective-permute-start.7 = (bf16[512,256]{1,0:T(8,128)(2,1)S(1)}, bf16[512,256]{1,0:T(8,128)(2,1)S(1)}, u32[]{:S(2)}, u32[]{:S(2)}) collective-permute-start(bf16[512,256]{1,0:T(8,128)(2,1)S(1)} %get-tuple-element.46.refs_0_), channel_id=1, source_target_pairs={{0,2},{1,3},{2,0},{3,1},{4,6},{5,7},{6,4},{7,5},{8,10},{9,11},{10,... | collective-permute-start | bytes 786440 | tf_op jit(solution)/shard_map/ppermute | solution.py:274
  19.9 2.3 %collective-permute-start.5 = (bf16[32,384]{1,0:T(8,128)(2,1)S(1)}, bf16[32,384]{1,0:T(8,128)(2,1)S(1)}, u32[]{:S(2)}, u32[]{:S(2)}) collective-permute-start(bf16[32,384]{1,0:T(8,128)(2,1)S(1)} %get-tuple-element.45), channel_id=1, source_target_pairs={{0,4},{4,8},{8,12},{12,16},{16,20},{20,24},{24,28},{1,5},{5,9},{9,... | collective-permute-start | bytes 73736 | tf_op jit(solution)/shard_map/ppermute | solution.py:302
  22.2 1.5 %collective-permute-done.5.prev_ref = bf16[32,384]{1,0:T(8,128)(2,1)S(1)} collective-permute-done((bf16[32,384]{1,0:T(8,128)(2,1)S(1)}, bf16[32,384]{1,0:T(8,128)(2,1)S(1)}, u32[]{:S(2)}, u32[]{:S(2)}) %collective-permute-start.5) | collective-permute-done | bytes 24608 | tf_op jit(solution)/shard_map/ppermute | solution.py:302
  24.4 2.6 %collective-permute-start.10 = (bf16[128,1024]{1,0:T(8,128)(2,1)S(1)}, bf16[128,1024]{1,0:T(8,128)(2,1)S(1)}, u32[]{:S(2)}, u32[]{:S(2)}) collective-permute-start(bf16[128,1024]{1,0:T(8,128)(2,1)S(1)} %collective-permute-done.3.refs_4_), channel_id=1, source_target_pairs={{0,8},{4,12},{8,0},{12,4},{16,24},{20,28},{24,16},{28,20},{1,9},{5... | collective-permute-start | bytes 786440 | tf_op jit(solution)/shard_map/ppermute | solution.py:277
  28.2 1.7 %shard_map.78 = (f32[128,1024]{1,0:T(8,128)S(1)}, bf16[128,1024]{1,0:T(8,128)(2,1)S(1)}, f32[128,1024]{1,0:T(8,128)S(1)}, bf16[128,1024]{1,0:T(8,128)(2,1)S(1)},...) custom-call(bf16[512,256]{1,0:T(8,128)(2,1)S(1)} %get-tuple-element., ...), custom_call_target="tpu_custom_call" | custom-call | tf_op jit(solution)/shard_map/pallas_call | solution.py:245
  30.9 2.7 %collective-permute-done.10.refs_6_ = bf16[128,1024]{1,0:T(8,128)(2,1)S(1)} collective-permute-done((bf16[128,1024]{1,0:T(8,128)(2,1)S(1)}, bf16[128,1024]{1,0:T(8,128)(2,1)S(1)}, u32[]{:S(2)}, u32[]{:S(2)}) %collective-permute-start.10) | collective-permute-done | bytes 262176 | tf_op jit(solution)/shard_map/ppermute | solution.py:277
  33.6 2.7 %collective-permute-done.9.refs_5_ = bf16[128,1024]{1,0:T(8,128)(2,1)S(1)} collective-permute-done((bf16[128,1024]{1,0:T(8,128)(2,1)S(1)}, bf16[128,1024]{1,0:T(8,128)(2,1)S(1)}, u32[]{:S(2)}, u32[]{:S(2)}) %collective-permute-start.9) | collective-permute-done | bytes 262176 | tf_op jit(solution)/shard_map/ppermute | solution.py:277
  36.2 4.4 %collective-permute-done.11 = bf16[128,1024]{1,0:T(8,128)(2,1)S(1)} collective-permute-done((bf16[128,1024]{1,0:T(8,128)(2,1)S(1)}, bf16[128,1024]{1,0:T(8,128)(2,1)S(1)}, u32[]{:S(2)}, u32[]{:S(2)}) %collective-permute-start.11) | collective-permute-done | bytes 262176 | tf_op jit(solution)/shard_map/ppermute | solution.py:277
  43.1 1.8 %shard_map.81 = (bf16[1024,512]{1,0:T(8,128)(2,1)S(1)}, f32[1024,256]{1,0:T(8,128)S(1)}, f32[1024,256]{1,0:T(8,128)S(1)}, f32[1024,256]{1,0:T(8,128)S(1)}) custom-call(bf16[1024,256]{1,0:T(8,128)(2,1)S(1)} %get-tuple-element.37.hidden_ref, bf16[32,384]{1,0:T(8,128)(2,1)S(1)} %collective-permute-done.5.prev_ref, ...), custom_call_target="tpu_custom_call" | custom-call | tf_op jit(solution)/shard_map/pallas_call | solution.py:245
  44.9 5.0 %collective-permute-done.12.refs_7_ = bf16[128,1024]{1,0:T(8,128)(2,1)S(1)} collective-permute-done((bf16[128,1024]{1,0:T(8,128)(2,1)S(1)}, bf16[128,1024]{1,0:T(8,128)(2,1)S(1)}, u32[]{:S(2)}, u32[]{:S(2)}) %collective-permute-start.12) | collective-permute-done | bytes 262176 | tf_op jit(solution)/shard_map/ppermute | solution.py:277
  49.9 2.5 %shard_map.79 = (bf16[528,256]{1,0:T(8,128)(2,1)S(1)}, bf16[528,256]{1,0:T(8,128)(2,1)S(1)}, bf16[528,256]{1,0:T(8,128)(2,1)S(1)}, bf16[528,256]{1,0:T(8,128)(2,1)S(1)}, bf16[1024,1024]{1,0:T(8,128)(2,1)}) custom-call(bf16[512,1024]{1,0:T(8,128)(2,1)S(1)} %copy-done, bf16[32,384]{1,0:T(8,128)(2,1)S(1)} %collective-permute-done.5.prev_ref, ...), custom_call_target="tpu_custom_call" | custom-call | tf_op jit(solution)/shard_map/pallas_call | solution.py:245
  54.1 1.4 %collective-permute-done.13 = bf16[128,1024]{1,0:T(8,128)(2,1)S(1)} collective-permute-done((bf16[128,1024]{1,0:T(8,128)(2,1)S(1)}, bf16[128,1024]{1,0:T(8,128)(2,1)S(1)}, u32[]{:S(2)}, u32[]{:S(2)}) %collective-permute-start.13) | collective-permute-done | bytes 262176 | tf_op jit(solution)/shard_map/ppermute | solution.py:277
  55.6 2.7 %collective-permute-start.17 = (bf16[128,1024]{1,0:T(8,128)(2,1)S(1)}, bf16[128,1024]{1,0:T(8,128)(2,1)S(1)}, u32[]{:S(2)}, u32[]{:S(2)}) collective-permute-start(bf16[128,1024]{1,0:T(8,128)(2,1)S(1)} %add_convert_fusion.1), channel_id=1, source_target_pairs={{0,16},{4,20},{8,24},{12,28},{16,0},{20,4},{24,8},{28,12},{1,17},{... | collective-permute-start | bytes 786440 | tf_op jit(solution)/shard_map/ppermute | solution.py:277
  59.1 1.7 %collective-permute-start.19 = (bf16[128,1024]{1,0:T(8,128)(2,1)S(1)}, bf16[128,1024]{1,0:T(8,128)(2,1)S(1)}, u32[]{:S(2)}, u32[]{:S(2)}) collective-permute-start(bf16[128,1024]{1,0:T(8,128)(2,1)S(1)} %add_convert_fusion), channel_id=1, source_target_pairs={{0,8},{4,12},{8,0},{12,4},{16,24},{20,28},{24,16},{28,20},{1,9},{5... | collective-permute-start | bytes 786440 | tf_op jit(solution)/shard_map/ppermute | solution.py:277
  61.2 2.4 %shard_map.80 = bf16[512,1024]{1,0:T(8,128)(2,1)} custom-call(bf16[512,256]{1,0:T(8,128)(2,1)S(1)} %get-tuple-element.46.refs_0_, bf16[512,256]{1,0:T(8,128)(2,1)S(1)} %collective-permute-done.6.refs_1_, bf16[512,256]{1,0:T(8,128)(2,1)S(1)} %collective-permute-done.7.refs_2_, bf16[512,256]{1,0:T(8,128)(2,1)S(1)} %collective-permute-done.8.refs_3_, ...), custom_call_target="tpu_custom_call" | custom-call | tf_op jit(solution)/shard_map/pallas_call | solution.py:245
  63.6 2.8 %collective-permute-done.21.refs_3_ = bf16[528,256]{1,0:T(8,128)(2,1)S(1)} collective-permute-done((bf16[528,256]{1,0:T(8,128)(2,1)S(1)}, bf16[528,256]{1,0:T(8,128)(2,1)S(1)}, u32[]{:S(2)}, u32[]{:S(2)}) %collective-permute-start.21) | collective-permute-done | bytes 270368 | tf_op jit(solution)/shard_map/ppermute | solution.py:274
  66.4 2.3 %shard_map.82 = bf16[1024,256]{1,0:T(8,128)(2,1)} custom-call(bf16[528,256]{1,0:T(8,128)(2,1)S(1)} %get-tuple-element.65.refs_0_, bf16[528,256]{1,0:T(8,128)(2,1)S(1)} %collective-permute-done.20.refs_1_, bf16[528,256]{1,0:T(8,128)(2,1)S(1)} %collective-permute-done.14.refs_2_, bf16[528,256]{1,0:T(8,128)(2,1)S(1)} %collective-permute-done.21.refs_3_, ...), custom_call_target="tpu_custom_call" | custom-call | tf_op jit(solution)/shard_map/pallas_call | solution.py:245
  68.7 1.6 %collective-permute-done.19 = bf16[128,1024]{1,0:T(8,128)(2,1)S(1)} collective-permute-done((bf16[128,1024]{1,0:T(8,128)(2,1)S(1)}, bf16[128,1024]{1,0:T(8,128)(2,1)S(1)}, u32[]{:S(2)}, u32[]{:S(2)}) %collective-permute-start.19) | collective-permute-done | bytes 262176 | tf_op jit(solution)/shard_map/ppermute | solution.py:277
  (41 shorter events, 13.0 us)
Async XLA Ops:
  0.6 27.5 %copy-start = (bf16[512,1024]{1,0:T(8,128)(2,1)S(1)}, bf16[512,1024]{1,0:T(8,128)(2,1)}, u32[]{:S(2)}) copy-start(bf16[512,1024]{1,0:T(8,128)(2,1)} %grad_ref.1) | copy-start | bytes 3145732
  2.5 14.1 %collective-permute-start.2 = (bf16[128,1024]{1,0:T(8,128)(2,1)}, bf16[128,1024]{1,0:T(8,128)(2,1)S(1)}, u32[]{:S(2)}, u32[]{:S(2)}) collective-permute-start(bf16[128,1024]{1,0:T(8,128)(2,1)} %refs_0_), channel_id=1, source_target_pairs={{0,8},{4,12},{8,0},{12,4},{16,24},{20,28},{24,16},{28,20},{1,9},{5... | collective-permute-start | bytes 786440 | tf_op jit(solution)/shard_map/ppermute | solution.py:277
  5.6 11.0 %collective-permute-start.1 = (bf16[128,1024]{1,0:T(8,128)(2,1)}, bf16[128,1024]{1,0:T(8,128)(2,1)S(1)}, u32[]{:S(2)}, u32[]{:S(2)}) collective-permute-start(bf16[128,1024]{1,0:T(8,128)(2,1)} %refs_0_), channel_id=1, source_target_pairs={{0,4},{4,0},{8,12},{12,8},{16,20},{20,16},{24,28},{28,24},{1,5},{5... | collective-permute-start | bytes 786440 | tf_op jit(solution)/shard_map/ppermute | solution.py:277
  7.1 6.7 %collective-permute-start = (bf16[16,384]{1,0:T(8,128)(2,1)S(1)}, bf16[16,384]{1,0:T(8,128)(2,1)S(1)}, u32[]{:S(2)}, u32[]{:S(2)}) collective-permute-start(bf16[16,384]{1,0:T(8,128)(2,1)S(1)} %get-tuple-element.38), channel_id=1, source_target_pairs={{4,0},{8,4},{12,8},{16,12},{20,16},{24,20},{28,24},{5,1},{9,5},{13... | collective-permute-start | bytes 36872 | tf_op jit(solution)/shard_map/ppermute | solution.py:301
  8.4 15.3 %collective-permute-start.3 = (bf16[128,1024]{1,0:T(8,128)(2,1)}, bf16[128,1024]{1,0:T(8,128)(2,1)S(1)}, u32[]{:S(2)}, u32[]{:S(2)}) collective-permute-start(bf16[128,1024]{1,0:T(8,128)(2,1)} %refs_0_), channel_id=1, source_target_pairs={{0,16},{4,20},{8,24},{12,28},{16,0},{20,4},{24,8},{28,12},{1,17},{... | collective-permute-start | bytes 786440 | tf_op jit(solution)/shard_map/ppermute | solution.py:277
  16.6 7.1 %collective-permute-start.4 = (bf16[128,1024]{1,0:T(8,128)(2,1)S(1)}, bf16[128,1024]{1,0:T(8,128)(2,1)S(1)}, u32[]{:S(2)}, u32[]{:S(2)}) collective-permute-start(bf16[128,1024]{1,0:T(8,128)(2,1)S(1)} %collective-permute-done.2.refs_2_), channel_id=1, source_target_pairs={{0,4},{4,0},{8,12},{12,8},{16,20},{20,16},{24,28},{28,24},{1,5},{5... | collective-permute-start | bytes 786440 | tf_op jit(solution)/shard_map/ppermute | solution.py:277
  18.1 6.4 %collective-permute-start.7 = (bf16[512,256]{1,0:T(8,128)(2,1)S(1)}, bf16[512,256]{1,0:T(8,128)(2,1)S(1)}, u32[]{:S(2)}, u32[]{:S(2)}) collective-permute-start(bf16[512,256]{1,0:T(8,128)(2,1)S(1)} %get-tuple-element.46.refs_0_), channel_id=1, source_target_pairs={{0,2},{1,3},{2,0},{3,1},{4,6},{5,7},{6,4},{7,5},{8,10},{9,11},{10,... | collective-permute-start | bytes 786440 | tf_op jit(solution)/shard_map/ppermute | solution.py:274
  19.9 30.0 %copy-start.2 = (bf16[128,1024]{1,0:T(8,128)(2,1)S(1)}, bf16[128,1024]{1,0:T(8,128)(2,1)}, u32[]{:S(2)}) copy-start(bf16[128,1024]{1,0:T(8,128)(2,1)} %refs_0_) | copy-start | bytes 786436
  19.9 3.8 %collective-permute-start.5 = (bf16[32,384]{1,0:T(8,128)(2,1)S(1)}, bf16[32,384]{1,0:T(8,128)(2,1)S(1)}, u32[]{:S(2)}, u32[]{:S(2)}) collective-permute-start(bf16[32,384]{1,0:T(8,128)(2,1)S(1)} %get-tuple-element.45), channel_id=1, source_target_pairs={{0,4},{4,8},{8,12},{12,16},{16,20},{20,24},{24,28},{1,5},{5,9},{9,... | collective-permute-start | bytes 73736 | tf_op jit(solution)/shard_map/ppermute | solution.py:302
  23.7 4.4 %collective-permute-start.6 = (bf16[512,256]{1,0:T(8,128)(2,1)S(1)}, bf16[512,256]{1,0:T(8,128)(2,1)S(1)}, u32[]{:S(2)}, u32[]{:S(2)}) collective-permute-start(bf16[512,256]{1,0:T(8,128)(2,1)S(1)} %get-tuple-element.46.refs_0_), channel_id=1, source_target_pairs={{0,1},{1,0},{2,3},{3,2},{4,5},{5,4},{6,7},{7,6},{8,9},{9,8},{10,11... | collective-permute-start | bytes 786440 | tf_op jit(solution)/shard_map/ppermute | solution.py:274
  24.4 3.7 %collective-permute-start.8 = (bf16[512,256]{1,0:T(8,128)(2,1)S(1)}, bf16[512,256]{1,0:T(8,128)(2,1)S(1)}, u32[]{:S(2)}, u32[]{:S(2)}) collective-permute-start(bf16[512,256]{1,0:T(8,128)(2,1)S(1)} %collective-permute-done.7.refs_2_), channel_id=1, source_target_pairs={{0,1},{1,0},{2,3},{3,2},{4,5},{5,4},{6,7},{7,6},{8,9},{9,8},{10,11... | collective-permute-start | bytes 786440 | tf_op jit(solution)/shard_map/ppermute | solution.py:274
  24.4 9.1 %collective-permute-start.10 = (bf16[128,1024]{1,0:T(8,128)(2,1)S(1)}, bf16[128,1024]{1,0:T(8,128)(2,1)S(1)}, u32[]{:S(2)}, u32[]{:S(2)}) collective-permute-start(bf16[128,1024]{1,0:T(8,128)(2,1)S(1)} %collective-permute-done.3.refs_4_), channel_id=1, source_target_pairs={{0,8},{4,12},{8,0},{12,4},{16,24},{20,28},{24,16},{28,20},{1,9},{5... | collective-permute-start | bytes 786440 | tf_op jit(solution)/shard_map/ppermute | solution.py:277
  27.0 9.2 %collective-permute-start.9 = (bf16[128,1024]{1,0:T(8,128)(2,1)S(1)}, bf16[128,1024]{1,0:T(8,128)(2,1)S(1)}, u32[]{:S(2)}, u32[]{:S(2)}) collective-permute-start(bf16[128,1024]{1,0:T(8,128)(2,1)S(1)} %collective-permute-done.3.refs_4_), channel_id=1, source_target_pairs={{0,4},{4,0},{8,12},{12,8},{16,20},{20,16},{24,28},{28,24},{1,5},{5... | collective-permute-start | bytes 786440 | tf_op jit(solution)/shard_map/ppermute | solution.py:277
  29.9 10.8 %collective-permute-start.11 = (bf16[128,1024]{1,0:T(8,128)(2,1)S(1)}, bf16[128,1024]{1,0:T(8,128)(2,1)S(1)}, u32[]{:S(2)}, u32[]{:S(2)}) collective-permute-start(bf16[128,1024]{1,0:T(8,128)(2,1)S(1)} %get-tuple-element.48), channel_id=1, source_target_pairs={{0,4},{4,0},{8,12},{12,8},{16,20},{20,16},{24,28},{28,24},{1,5},{5... | collective-permute-start | bytes 786440 | tf_op jit(solution)/shard_map/ppermute | solution.py:277
  40.7 9.2 %collective-permute-start.12 = (bf16[128,1024]{1,0:T(8,128)(2,1)S(1)}, bf16[128,1024]{1,0:T(8,128)(2,1)S(1)}, u32[]{:S(2)}, u32[]{:S(2)}) collective-permute-start(bf16[128,1024]{1,0:T(8,128)(2,1)S(1)} %collective-permute-done.10.refs_6_), channel_id=1, source_target_pairs={{0,4},{4,0},{8,12},{12,8},{16,20},{20,16},{24,28},{28,24},{1,5},{5... | collective-permute-start | bytes 786440 | tf_op jit(solution)/shard_map/ppermute | solution.py:277
  41.9 10.6 %collective-permute-start.16 = (bf16[128,1024]{1,0:T(8,128)(2,1)S(1)}, bf16[128,1024]{1,0:T(8,128)(2,1)S(1)}, u32[]{:S(2)}, u32[]{:S(2)}) collective-permute-start(bf16[128,1024]{1,0:T(8,128)(2,1)S(1)} %add_convert_fusion.2), channel_id=1, source_target_pairs={{0,8},{4,12},{8,0},{12,4},{16,24},{20,28},{24,16},{28,20},{1,9},{5... | collective-permute-start | bytes 786440 | tf_op jit(solution)/shard_map/ppermute | solution.py:277
  42.3 13.2 %collective-permute-start.13 = (bf16[128,1024]{1,0:T(8,128)(2,1)S(1)}, bf16[128,1024]{1,0:T(8,128)(2,1)S(1)}, u32[]{:S(2)}, u32[]{:S(2)}) collective-permute-start(bf16[128,1024]{1,0:T(8,128)(2,1)S(1)} %get-tuple-element.54), channel_id=1, source_target_pairs={{0,4},{4,0},{8,12},{12,8},{16,20},{20,16},{24,28},{28,24},{1,5},{5... | collective-permute-start | bytes 786440 | tf_op jit(solution)/shard_map/ppermute | solution.py:277
  52.4 6.6 %collective-permute-start.18 = (bf16[128,1024]{1,0:T(8,128)(2,1)S(1)}, bf16[128,1024]{1,0:T(8,128)(2,1)S(1)}, u32[]{:S(2)}, u32[]{:S(2)}) collective-permute-start(bf16[128,1024]{1,0:T(8,128)(2,1)S(1)} %get-tuple-element.64), channel_id=1, source_target_pairs={{0,4},{4,0},{8,12},{12,8},{16,20},{20,16},{24,28},{28,24},{1,5},{5... | collective-permute-start | bytes 786440 | tf_op jit(solution)/shard_map/ppermute | solution.py:277
  53.6 7.3 %collective-permute-start.14 = (bf16[528,256]{1,0:T(8,128)(2,1)S(1)}, bf16[528,256]{1,0:T(8,128)(2,1)S(1)}, u32[]{:S(2)}, u32[]{:S(2)}) collective-permute-start(bf16[528,256]{1,0:T(8,128)(2,1)S(1)} %get-tuple-element.55), channel_id=1, source_target_pairs={{0,2},{1,3},{2,0},{3,1},{4,6},{5,7},{6,4},{7,5},{8,10},{9,11},{10,... | collective-permute-start | bytes 811016 | tf_op jit(solution)/shard_map/ppermute | solution.py:274
  55.6 13.1 %collective-permute-start.17 = (bf16[128,1024]{1,0:T(8,128)(2,1)S(1)}, bf16[128,1024]{1,0:T(8,128)(2,1)S(1)}, u32[]{:S(2)}, u32[]{:S(2)}) collective-permute-start(bf16[128,1024]{1,0:T(8,128)(2,1)S(1)} %add_convert_fusion.1), channel_id=1, source_target_pairs={{0,16},{4,20},{8,24},{12,28},{16,0},{20,4},{24,8},{28,12},{1,17},{... | collective-permute-start | bytes 786440 | tf_op jit(solution)/shard_map/ppermute | solution.py:277
  58.3 5.3 %collective-permute-start.20 = (bf16[528,256]{1,0:T(8,128)(2,1)S(1)}, bf16[528,256]{1,0:T(8,128)(2,1)S(1)}, u32[]{:S(2)}, u32[]{:S(2)}) collective-permute-start(bf16[528,256]{1,0:T(8,128)(2,1)S(1)} %get-tuple-element.66), channel_id=1, source_target_pairs={{0,1},{1,0},{2,3},{3,2},{4,5},{5,4},{6,7},{7,6},{8,9},{9,8},{10,11... | collective-permute-start | bytes 811016 | tf_op jit(solution)/shard_map/ppermute | solution.py:274
  58.3 8.1 %collective-permute-start.21 = (bf16[528,256]{1,0:T(8,128)(2,1)S(1)}, bf16[528,256]{1,0:T(8,128)(2,1)S(1)}, u32[]{:S(2)}, u32[]{:S(2)}) collective-permute-start(bf16[528,256]{1,0:T(8,128)(2,1)S(1)} %get-tuple-element.67), channel_id=1, source_target_pairs={{0,3},{1,2},{2,1},{3,0},{4,7},{5,6},{6,5},{7,4},{8,11},{9,10},{10,... | collective-permute-start | bytes 811016 | tf_op jit(solution)/shard_map/ppermute | solution.py:274
  59.1 11.2 %collective-permute-start.19 = (bf16[128,1024]{1,0:T(8,128)(2,1)S(1)}, bf16[128,1024]{1,0:T(8,128)(2,1)S(1)}, u32[]{:S(2)}, u32[]{:S(2)}) collective-permute-start(bf16[128,1024]{1,0:T(8,128)(2,1)S(1)} %add_convert_fusion), channel_id=1, source_target_pairs={{0,8},{4,12},{8,0},{12,4},{16,24},{20,28},{24,16},{28,20},{1,9},{5... | collective-permute-start | bytes 786440 | tf_op jit(solution)/shard_map/ppermute | solution.py:277
  60.8 9.5 %collective-permute-start.15 = (bf16[128,1024]{1,0:T(8,128)(2,1)S(1)}, bf16[128,1024]{1,0:T(8,128)(2,1)S(1)}, u32[]{:S(2)}, u32[]{:S(2)}) collective-permute-start(bf16[128,1024]{1,0:T(8,128)(2,1)S(1)} %get-tuple-element.56), channel_id=1, source_target_pairs={{0,4},{4,0},{8,12},{12,8},{16,20},{20,16},{24,28},{28,24},{1,5},{5... | collective-permute-start | bytes 786440 | tf_op jit(solution)/shard_map/ppermute | solution.py:277
  (3 other events, 10.2 us)

commit v10 on v9

--- a/solution.py
+++ b/solution.py
@@ -355,10 +355,10 @@
     )
     if staged:
         fetched = {}
-        fetched[7] = trade(terms[7], 1)
         pieces[5] = trade(pieces[4], 1)
-        pieces[7] = trade(after((pieces[6], fetched[7], pieces[5]))[0], 1)
-        fetched[5] = trade(after((terms[5], pieces[5]))[0], 1)
+        fetched[7] = trade(after((terms[7], pieces[5]))[0], 1)
+        pieces[7] = trade(after((pieces[6], terms[0]))[0], 1)
+        fetched[5] = trade(after((terms[5], fetched[7]))[0], 1)
 
     *partials, weight_full = call(
         functools.partial(partial_kernel, n_mp),
@@ -368,14 +368,19 @@
         *pieces,
         flops=work,
     )
-    grads = [partials[0]] + [swap(partials[step], step) for step in range(1, n_mp)]
+    if n_mp == 4:
+        near = swap(partials[3], 1)
+        pair = partials[2].astype(F32) + near.astype(F32)
+        grads = [partials[0], swap(partials[1], 1), swap(pair.astype(BF16), 2)]
+    else:
+        near, grads = None, [swap(partials[step], step) for step in range(n_mp)]
 
     if staged:
         fetched[6] = trade((terms[6] + fetched[7].astype(F32)).astype(BF16), 2)
         fetched[3] = trade(after((terms[3], weight_full, share, fetched[6]))[0], 1)
         pair = terms[4] + fetched[5].astype(F32) + fetched[6].astype(F32)
         fetched[4] = trade(pair.astype(BF16), 4)
-        fetched[1] = trade(after((terms[1], fetched[5], grads[2]))[0], 1)
+        fetched[1] = trade(after((terms[1], fetched[3], near))[0], 1)
         fetched[2] = trade((terms[2] + fetched[3].astype(F32)).astype(BF16), 2)
         grad_weight = terms[0] + fetched[1].astype(F32)
         for step in (4, 2):
@@ -393,7 +398,7 @@
         scratch=(pltpu.VMEM((slots, latent_dim), BF16),),
     )
     grad_bytes = call(
-        functools.partial(bytes_kernel, n_mp),
+        functools.partial(bytes_kernel, len(grads)),
         shape((bytes_, feats), BF16),
         *grads,
         start,

time: 71.4 us -> 76.1 us (1.066)
  starting transfers between devices: 28.9 us -> 32.7 us
  waiting for transfers between devices: 25.1 us -> 26.1 us
    ppermute x14, starting transfers between devices: 22.3 us -> 26.2 us  [trade(): return lax.ppermute(value, 'seq', [(i, i ^ step) for i in range(n_seq)])]
    ppermute x14, waiting for transfers between devices: 17.9 us -> 21.6 us  [trade(): return lax.ppermute(value, 'seq', [(i, i ^ step) for i in range(n_seq)])]
    ppermute x6, waiting for transfers between devices: 3.52 us -> 0.84 us  [swap(): return lax.ppermute(value, 'mp', [(i, i ^ step) for i in range(n_mp)])]
  transfers between devices with their start and end apart: 22 -> 22, of which waited for: 11 -> 9; matrix products, arithmetic and copies ran while one was open for 0% -> 0% of each run, Pallas kernels for 18% -> 17%
where the time goes in v10:
time: 76.1 us; the launch traced here: 75.9 us
  starting transfers between devices  32.7 us (43%)
  waiting for transfers between devices  26.1 us (34%)
  Pallas kernels  13.7 us (18%)
  local copies, waits for them, and re-layouts  1.44 us (2%)
  other arithmetic  1.2 us (2%)
  between operations  0.78 us (1%)
    ppermute x14, starting transfers between devices, trade(): return lax.ppermute(value, 'seq', [(i, i ^ step) for i in range(n_seq)])  26.2 us
    ppermute x14, waiting for transfers between devices, trade(): return lax.ppermute(value, 'seq', [(i, i ^ step) for i in range(n_seq)])  21.6 us
    pallas_call x7, Pallas kernels, call(): pl.pallas_call(kernel, out_shape=out_shape, in_specs=in_specs, out_specs=...  13.7 us
    ppermute x6, starting transfers between devices, swap(): return lax.ppermute(value, 'mp', [(i, i ^ step) for i in range(n_mp)])  2.99 us
    ppermute x1, starting transfers between devices, shards(): lax.ppermute(ahead, 'seq', [(i, i + 1) for i in range(n_seq - 1)])  2.21 us
    ppermute x1, waiting for transfers between devices, shards(): following = lax.ppermute(back, 'seq', [(i, i - 1) for i in range(1, n_seq)])  2.15 us
  transfers between devices with their start and end apart: 22, of which 9 were waited for; matrix products, arithmetic and copies ran while one was open for 0% of the time, Pallas kernels for 17%

profile of v10, /device:TPU:0, one launch (start us, length us, event | category | flops | bytes accessed | tf_op | source)
XLA Modules:
  0.0 75.9 jit_solution(12170526240066688564)
XLA Ops:
  2.5 3.1 %collective-permute-start.2 = (bf16[128,1024]{1,0:T(8,128)(2,1)}, bf16[128,1024]{1,0:T(8,128)(2,1)S(1)}, u32[]{:S(2)}, u32[]{:S(2)}) collective-permute-start(bf16[128,1024]{1,0:T(8,128)(2,1)} %refs_0_), channel_id=1, source_target_pairs={{0,8},{4,12},{8,0},{12,4},{16,24},{20,28},{24,16},{28,20},{1,9},{5... | collective-permute-start | bytes 786440 | tf_op jit(solution)/shard_map/ppermute | solution.py:277
  8.4 3.3 %collective-permute-start.3 = (bf16[128,1024]{1,0:T(8,128)(2,1)}, bf16[128,1024]{1,0:T(8,128)(2,1)S(1)}, u32[]{:S(2)}, u32[]{:S(2)}) collective-permute-start(bf16[128,1024]{1,0:T(8,128)(2,1)} %refs_0_), channel_id=1, source_target_pairs={{0,16},{4,20},{8,24},{12,28},{16,0},{20,4},{24,8},{28,12},{1,17},{... | collective-permute-start | bytes 786440 | tf_op jit(solution)/shard_map/ppermute | solution.py:277
  11.7 2.1 %collective-permute-done.next_ref = bf16[16,384]{1,0:T(8,128)(2,1)S(1)} collective-permute-done((bf16[16,384]{1,0:T(8,128)(2,1)S(1)}, bf16[16,384]{1,0:T(8,128)(2,1)S(1)}, u32[]{:S(2)}, u32[]{:S(2)}) %collective-permute-start) | collective-permute-done | bytes 12320 | tf_op jit(solution)/shard_map/ppermute | solution.py:301
  14.5 2.1 %shard_map.77 = (bf16[512,256]{1,0:T(8,128)(2,1)S(1)}, f32[512,256]{1,0:T(8,128)S(1)}, f32[512,256]{1,0:T(8,128)S(1)}) custom-call(bf16[1024,256]{1,0:T(8,128)(2,1)S(1)} %get-tuple-element.38.hidden_ref, bf16[16,384]{1,0:T(8,128)(2,1)S(1)} %collective-permute-done.next_ref, s32[8,128]{1,0:T(8,128)S(1)} %get-tuple-element.40.start_ref.refs_3_, ...), custom_call_target="tpu_custom_call" | custom-call | tf_op jit(solution)/shard_map/pallas_call | solution.py:245
  18.1 1.8 %collective-permute-start.7 = (bf16[512,256]{1,0:T(8,128)(2,1)S(1)}, bf16[512,256]{1,0:T(8,128)(2,1)S(1)}, u32[]{:S(2)}, u32[]{:S(2)}) collective-permute-start(bf16[512,256]{1,0:T(8,128)(2,1)S(1)} %get-tuple-element.47.refs_0_), channel_id=1, source_target_pairs={{0,2},{1,3},{2,0},{3,1},{4,6},{5,7},{6,4},{7,5},{8,10},{9,11},{10,... | collective-permute-start | bytes 786440 | tf_op jit(solution)/shard_map/ppermute | solution.py:274
  19.9 2.2 %collective-permute-start.5 = (bf16[32,384]{1,0:T(8,128)(2,1)S(1)}, bf16[32,384]{1,0:T(8,128)(2,1)S(1)}, u32[]{:S(2)}, u32[]{:S(2)}) collective-permute-start(bf16[32,384]{1,0:T(8,128)(2,1)S(1)} %get-tuple-element.46), channel_id=1, source_target_pairs={{0,4},{4,8},{8,12},{12,16},{16,20},{20,24},{24,28},{1,5},{5,9},{9,... | collective-permute-start | bytes 73736 | tf_op jit(solution)/shard_map/ppermute | solution.py:302
  24.4 2.0 %collective-permute-start.9 = (bf16[128,1024]{1,0:T(8,128)(2,1)S(1)}, bf16[128,1024]{1,0:T(8,128)(2,1)S(1)}, u32[]{:S(2)}, u32[]{:S(2)}) collective-permute-start(bf16[128,1024]{1,0:T(8,128)(2,1)S(1)} %collective-permute-done.3.refs_4_), channel_id=1, source_target_pairs={{0,4},{4,0},{8,12},{12,8},{16,20},{20,16},{24,28},{28,24},{1,5},{5... | collective-permute-start | bytes 786440 | tf_op jit(solution)/shard_map/ppermute | solution.py:277
  26.4 1.6 %collective-permute-start.10 = (bf16[128,1024]{1,0:T(8,128)(2,1)S(1)}, bf16[128,1024]{1,0:T(8,128)(2,1)S(1)}, u32[]{:S(2)}, u32[]{:S(2)}) collective-permute-start(bf16[128,1024]{1,0:T(8,128)(2,1)S(1)} %collective-permute-done.3.refs_4_), channel_id=1, source_target_pairs={{0,8},{4,12},{8,0},{12,4},{16,24},{20,28},{24,16},{28,20},{1,9},{5... | collective-permute-start | bytes 786440 | tf_op jit(solution)/shard_map/ppermute | solution.py:277
  28.0 1.7 %shard_map.78 = (f32[128,1024]{1,0:T(8,128)S(1)}, bf16[128,1024]{1,0:T(8,128)(2,1)S(1)}, f32[128,1024]{1,0:T(8,128)S(1)}, bf16[128,1024]{1,0:T(8,128)(2,1)S(1)},...) custom-call(bf16[512,256]{1,0:T(8,128)(2,1)S(1)} %get-tuple-element., ...), custom_call_target="tpu_custom_call" | custom-call | tf_op jit(solution)/shard_map/pallas_call | solution.py:245
  29.8 3.4 %collective-permute-done.9.refs_5_ = bf16[128,1024]{1,0:T(8,128)(2,1)S(1)} collective-permute-done((bf16[128,1024]{1,0:T(8,128)(2,1)S(1)}, bf16[128,1024]{1,0:T(8,128)(2,1)S(1)}, u32[]{:S(2)}, u32[]{:S(2)}) %collective-permute-start.9) | collective-permute-done | bytes 262176 | tf_op jit(solution)/shard_map/ppermute | solution.py:277
  33.2 1.6 %collective-permute-start.12 = (bf16[128,1024]{1,0:T(8,128)(2,1)S(1)}, bf16[128,1024]{1,0:T(8,128)(2,1)S(1)}, u32[]{:S(2)}, u32[]{:S(2)}) collective-permute-start(bf16[128,1024]{1,0:T(8,128)(2,1)S(1)} %get-tuple-element.59), channel_id=1, source_target_pairs={{0,4},{4,0},{8,12},{12,8},{16,20},{20,16},{24,28},{28,24},{1,5},{5... | collective-permute-start | bytes 786440 | tf_op jit(solution)/shard_map/ppermute | solution.py:277
  35.2 7.2 %collective-permute-done.12 = bf16[128,1024]{1,0:T(8,128)(2,1)S(1)} collective-permute-done((bf16[128,1024]{1,0:T(8,128)(2,1)S(1)}, bf16[128,1024]{1,0:T(8,128)(2,1)S(1)}, u32[]{:S(2)}, u32[]{:S(2)}) %collective-permute-start.12) | collective-permute-done | bytes 262176 | tf_op jit(solution)/shard_map/ppermute | solution.py:277
  42.4 2.1 %collective-permute-start.13 = (bf16[128,1024]{1,0:T(8,128)(2,1)S(1)}, bf16[128,1024]{1,0:T(8,128)(2,1)S(1)}, u32[]{:S(2)}, u32[]{:S(2)}) collective-permute-start(bf16[128,1024]{1,0:T(8,128)(2,1)S(1)} %add_convert_fusion.3), channel_id=1, source_target_pairs={{0,8},{4,12},{8,0},{12,4},{16,24},{20,28},{24,16},{28,20},{1,9},{5... | collective-permute-start | bytes 786440 | tf_op jit(solution)/shard_map/ppermute | solution.py:277
  45.7 2.3 %collective-permute-done.11.refs_7_ = bf16[128,1024]{1,0:T(8,128)(2,1)S(1)} collective-permute-done((bf16[128,1024]{1,0:T(8,128)(2,1)S(1)}, bf16[128,1024]{1,0:T(8,128)(2,1)S(1)}, u32[]{:S(2)}, u32[]{:S(2)}) %collective-permute-start.11) | collective-permute-done | bytes 262176 | tf_op jit(solution)/shard_map/ppermute | solution.py:277
  48.0 2.5 %shard_map.79 = (bf16[528,256]{1,0:T(8,128)(2,1)S(1)}, bf16[528,256]{1,0:T(8,128)(2,1)S(1)}, bf16[528,256]{1,0:T(8,128)(2,1)S(1)}, bf16[528,256]{1,0:T(8,128)(2,1)S(1)}, bf16[1024,1024]{1,0:T(8,128)(2,1)}) custom-call(bf16[512,1024]{1,0:T(8,128)(2,1)S(1)} %copy-done, bf16[32,384]{1,0:T(8,128)(2,1)S(1)} %collective-permute-done.5.prev_ref, ...), custom_call_target="tpu_custom_call" | custom-call | tf_op jit(solution)/shard_map/pallas_call | solution.py:245
  50.5 1.7 %shard_map.81 = (bf16[1024,512]{1,0:T(8,128)(2,1)S(1)}, f32[1024,256]{1,0:T(8,128)S(1)}, f32[1024,256]{1,0:T(8,128)S(1)}, f32[1024,256]{1,0:T(8,128)S(1)}) custom-call(bf16[1024,256]{1,0:T(8,128)(2,1)S(1)} %get-tuple-element.38.hidden_ref, bf16[32,384]{1,0:T(8,128)(2,1)S(1)} %collective-permute-done.5.prev_ref, ...), custom_call_target="tpu_custom_call" | custom-call | tf_op jit(solution)/shard_map/pallas_call | solution.py:245
  52.8 1.6 %collective-permute-start.14 = (bf16[128,1024]{1,0:T(8,128)(2,1)S(1)}, bf16[128,1024]{1,0:T(8,128)(2,1)S(1)}, u32[]{:S(2)}, u32[]{:S(2)}) collective-permute-start(bf16[128,1024]{1,0:T(8,128)(2,1)S(1)} %get-tuple-element.60), channel_id=1, source_target_pairs={{0,4},{4,0},{8,12},{12,8},{16,20},{20,16},{24,28},{28,24},{1,5},{5... | collective-permute-start | bytes 786440 | tf_op jit(solution)/shard_map/ppermute | solution.py:277
  54.5 3.1 %collective-permute-start.18 = (bf16[128,1024]{1,0:T(8,128)(2,1)S(1)}, bf16[128,1024]{1,0:T(8,128)(2,1)S(1)}, u32[]{:S(2)}, u32[]{:S(2)}) collective-permute-start(bf16[128,1024]{1,0:T(8,128)(2,1)S(1)} %add_convert_fusion.2), channel_id=1, source_target_pairs={{0,16},{4,20},{8,24},{12,28},{16,0},{20,4},{24,8},{28,12},{1,17},{... | collective-permute-start | bytes 786440 | tf_op jit(solution)/shard_map/ppermute | solution.py:277
  58.3 2.8 %collective-permute-done.14 = bf16[128,1024]{1,0:T(8,128)(2,1)S(1)} collective-permute-done((bf16[128,1024]{1,0:T(8,128)(2,1)S(1)}, bf16[128,1024]{1,0:T(8,128)(2,1)S(1)}, u32[]{:S(2)}, u32[]{:S(2)}) %collective-permute-start.14) | collective-permute-done | bytes 262176 | tf_op jit(solution)/shard_map/ppermute | solution.py:277
  61.1 1.6 %collective-permute-start.16 = (bf16[128,1024]{1,0:T(8,128)(2,1)S(1)}, bf16[128,1024]{1,0:T(8,128)(2,1)S(1)}, u32[]{:S(2)}, u32[]{:S(2)}) collective-permute-start(bf16[128,1024]{1,0:T(8,128)(2,1)S(1)} %get-tuple-element.62), channel_id=1, source_target_pairs={{0,4},{4,0},{8,12},{12,8},{16,20},{20,16},{24,28},{28,24},{1,5},{5... | collective-permute-start | bytes 786440 | tf_op jit(solution)/shard_map/ppermute | solution.py:277
  62.8 1.7 %collective-permute-start.19 = (bf16[128,1024]{1,0:T(8,128)(2,1)S(1)}, bf16[128,1024]{1,0:T(8,128)(2,1)S(1)}, u32[]{:S(2)}, u32[]{:S(2)}) collective-permute-start(bf16[128,1024]{1,0:T(8,128)(2,1)S(1)} %add_convert_fusion.1), channel_id=1, source_target_pairs={{0,8},{4,12},{8,0},{12,4},{16,24},{20,28},{24,16},{28,20},{1,9},{5... | collective-permute-start | bytes 786440 | tf_op jit(solution)/shard_map/ppermute | solution.py:277
  64.5 2.4 %shard_map.80 = bf16[512,1024]{1,0:T(8,128)(2,1)} custom-call(bf16[512,256]{1,0:T(8,128)(2,1)S(1)} %get-tuple-element.47.refs_0_, bf16[512,256]{1,0:T(8,128)(2,1)S(1)} %collective-permute-done.6.refs_1_, bf16[512,256]{1,0:T(8,128)(2,1)S(1)} %collective-permute-done.7.refs_2_, bf16[512,256]{1,0:T(8,128)(2,1)S(1)} %collective-permute-done.8.refs_3_, ...), custom_call_target="tpu_custom_call" | custom-call | tf_op jit(solution)/shard_map/pallas_call | solution.py:245
  66.8 2.2 %shard_map.82 = bf16[1024,256]{1,0:T(8,128)(2,1)} custom-call(bf16[528,256]{1,0:T(8,128)(2,1)S(1)} %get-tuple-element.67.refs_0_, bf16[528,256]{1,0:T(8,128)(2,1)S(1)} %collective-permute-done.20.refs_1_, bf16[528,256]{1,0:T(8,128)(2,1)S(1)} %collective-permute-done.21.refs_2_, s32[8,128]{1,0:T(8,128)S(1)} %get-tuple-element.40.start_ref.refs_3_, ...), custom_call_target="tpu_custom_call" | custom-call | tf_op jit(solution)/shard_map/pallas_call | solution.py:245
  69.7 5.3 %collective-permute-done.19 = bf16[128,1024]{1,0:T(8,128)(2,1)S(1)} collective-permute-done((bf16[128,1024]{1,0:T(8,128)(2,1)S(1)}, bf16[128,1024]{1,0:T(8,128)(2,1)S(1)}, u32[]{:S(2)}, u32[]{:S(2)}) %collective-permute-start.19) | collective-permute-done | bytes 262176 | tf_op jit(solution)/shard_map/ppermute | solution.py:277
  (44 shorter events, 13.8 us)
Async XLA Ops:
  0.6 27.4 %copy-start = (bf16[512,1024]{1,0:T(8,128)(2,1)S(1)}, bf16[512,1024]{1,0:T(8,128)(2,1)}, u32[]{:S(2)}) copy-start(bf16[512,1024]{1,0:T(8,128)(2,1)} %grad_ref.1) | copy-start | bytes 3145732
  2.5 45.5 %copy-start.2 = (bf16[128,1024]{1,0:T(8,128)(2,1)S(1)}, bf16[128,1024]{1,0:T(8,128)(2,1)}, u32[]{:S(2)}) copy-start(bf16[128,1024]{1,0:T(8,128)(2,1)} %refs_0_) | copy-start | bytes 786436
  2.5 14.1 %collective-permute-start.2 = (bf16[128,1024]{1,0:T(8,128)(2,1)}, bf16[128,1024]{1,0:T(8,128)(2,1)S(1)}, u32[]{:S(2)}, u32[]{:S(2)}) collective-permute-start(bf16[128,1024]{1,0:T(8,128)(2,1)} %refs_0_), channel_id=1, source_target_pairs={{0,8},{4,12},{8,0},{12,4},{16,24},{20,28},{24,16},{28,20},{1,9},{5... | collective-permute-start | bytes 786440 | tf_op jit(solution)/shard_map/ppermute | solution.py:277
  5.6 11.0 %collective-permute-start.1 = (bf16[128,1024]{1,0:T(8,128)(2,1)}, bf16[128,1024]{1,0:T(8,128)(2,1)S(1)}, u32[]{:S(2)}, u32[]{:S(2)}) collective-permute-start(bf16[128,1024]{1,0:T(8,128)(2,1)} %refs_0_), channel_id=1, source_target_pairs={{0,4},{4,0},{8,12},{12,8},{16,20},{20,16},{24,28},{28,24},{1,5},{5... | collective-permute-start | bytes 786440 | tf_op jit(solution)/shard_map/ppermute | solution.py:277
  7.1 6.7 %collective-permute-start = (bf16[16,384]{1,0:T(8,128)(2,1)S(1)}, bf16[16,384]{1,0:T(8,128)(2,1)S(1)}, u32[]{:S(2)}, u32[]{:S(2)}) collective-permute-start(bf16[16,384]{1,0:T(8,128)(2,1)S(1)} %get-tuple-element.39), channel_id=1, source_target_pairs={{4,0},{8,4},{12,8},{16,12},{20,16},{24,20},{28,24},{5,1},{9,5},{13... | collective-permute-start | bytes 36872 | tf_op jit(solution)/shard_map/ppermute | solution.py:301
  8.4 15.2 %collective-permute-start.3 = (bf16[128,1024]{1,0:T(8,128)(2,1)}, bf16[128,1024]{1,0:T(8,128)(2,1)S(1)}, u32[]{:S(2)}, u32[]{:S(2)}) collective-permute-start(bf16[128,1024]{1,0:T(8,128)(2,1)} %refs_0_), channel_id=1, source_target_pairs={{0,16},{4,20},{8,24},{12,28},{16,0},{20,4},{24,8},{28,12},{1,17},{... | collective-permute-start | bytes 786440 | tf_op jit(solution)/shard_map/ppermute | solution.py:277
  16.6 7.0 %collective-permute-start.4 = (bf16[128,1024]{1,0:T(8,128)(2,1)S(1)}, bf16[128,1024]{1,0:T(8,128)(2,1)S(1)}, u32[]{:S(2)}, u32[]{:S(2)}) collective-permute-start(bf16[128,1024]{1,0:T(8,128)(2,1)S(1)} %collective-permute-done.2.refs_2_), channel_id=1, source_target_pairs={{0,4},{4,0},{8,12},{12,8},{16,20},{20,16},{24,28},{28,24},{1,5},{5... | collective-permute-start | bytes 786440 | tf_op jit(solution)/shard_map/ppermute | solution.py:277
  18.1 6.4 %collective-permute-start.7 = (bf16[512,256]{1,0:T(8,128)(2,1)S(1)}, bf16[512,256]{1,0:T(8,128)(2,1)S(1)}, u32[]{:S(2)}, u32[]{:S(2)}) collective-permute-start(bf16[512,256]{1,0:T(8,128)(2,1)S(1)} %get-tuple-element.47.refs_0_), channel_id=1, source_target_pairs={{0,2},{1,3},{2,0},{3,1},{4,6},{5,7},{6,4},{7,5},{8,10},{9,11},{10,... | collective-permute-start | bytes 786440 | tf_op jit(solution)/shard_map/ppermute | solution.py:274
  19.9 3.7 %collective-permute-start.5 = (bf16[32,384]{1,0:T(8,128)(2,1)S(1)}, bf16[32,384]{1,0:T(8,128)(2,1)S(1)}, u32[]{:S(2)}, u32[]{:S(2)}) collective-permute-start(bf16[32,384]{1,0:T(8,128)(2,1)S(1)} %get-tuple-element.46), channel_id=1, source_target_pairs={{0,4},{4,8},{8,12},{12,16},{16,20},{20,24},{24,28},{1,5},{5,9},{9,... | collective-permute-start | bytes 73736 | tf_op jit(solution)/shard_map/ppermute | solution.py:302
  23.6 4.4 %collective-permute-start.6 = (bf16[512,256]{1,0:T(8,128)(2,1)S(1)}, bf16[512,256]{1,0:T(8,128)(2,1)S(1)}, u32[]{:S(2)}, u32[]{:S(2)}) collective-permute-start(bf16[512,256]{1,0:T(8,128)(2,1)S(1)} %get-tuple-element.47.refs_0_), channel_id=1, source_target_pairs={{0,1},{1,0},{2,3},{3,2},{4,5},{5,4},{6,7},{7,6},{8,9},{9,8},{10,11... | collective-permute-start | bytes 786440 | tf_op jit(solution)/shard_map/ppermute | solution.py:274
  24.4 3.6 %collective-permute-start.8 = (bf16[512,256]{1,0:T(8,128)(2,1)S(1)}, bf16[512,256]{1,0:T(8,128)(2,1)S(1)}, u32[]{:S(2)}, u32[]{:S(2)}) collective-permute-start(bf16[512,256]{1,0:T(8,128)(2,1)S(1)} %collective-permute-done.7.refs_2_), channel_id=1, source_target_pairs={{0,1},{1,0},{2,3},{3,2},{4,5},{5,4},{6,7},{7,6},{8,9},{9,8},{10,11... | collective-permute-start | bytes 786440 | tf_op jit(solution)/shard_map/ppermute | solution.py:274
  24.4 8.7 %collective-permute-start.9 = (bf16[128,1024]{1,0:T(8,128)(2,1)S(1)}, bf16[128,1024]{1,0:T(8,128)(2,1)S(1)}, u32[]{:S(2)}, u32[]{:S(2)}) collective-permute-start(bf16[128,1024]{1,0:T(8,128)(2,1)S(1)} %collective-permute-done.3.refs_4_), channel_id=1, source_target_pairs={{0,4},{4,0},{8,12},{12,8},{16,20},{20,16},{24,28},{28,24},{1,5},{5... | collective-permute-start | bytes 786440 | tf_op jit(solution)/shard_map/ppermute | solution.py:277
  26.4 8.3 %collective-permute-start.10 = (bf16[128,1024]{1,0:T(8,128)(2,1)S(1)}, bf16[128,1024]{1,0:T(8,128)(2,1)S(1)}, u32[]{:S(2)}, u32[]{:S(2)}) collective-permute-start(bf16[128,1024]{1,0:T(8,128)(2,1)S(1)} %collective-permute-done.3.refs_4_), channel_id=1, source_target_pairs={{0,8},{4,12},{8,0},{12,4},{16,24},{20,28},{24,16},{28,20},{1,9},{5... | collective-permute-start | bytes 786440 | tf_op jit(solution)/shard_map/ppermute | solution.py:277
  33.2 9.2 %collective-permute-start.12 = (bf16[128,1024]{1,0:T(8,128)(2,1)S(1)}, bf16[128,1024]{1,0:T(8,128)(2,1)S(1)}, u32[]{:S(2)}, u32[]{:S(2)}) collective-permute-start(bf16[128,1024]{1,0:T(8,128)(2,1)S(1)} %get-tuple-element.59), channel_id=1, source_target_pairs={{0,4},{4,0},{8,12},{12,8},{16,20},{20,16},{24,28},{28,24},{1,5},{5... | collective-permute-start | bytes 786440 | tf_op jit(solution)/shard_map/ppermute | solution.py:277
  34.7 13.3 %collective-permute-start.11 = (bf16[128,1024]{1,0:T(8,128)(2,1)S(1)}, bf16[128,1024]{1,0:T(8,128)(2,1)S(1)}, u32[]{:S(2)}, u32[]{:S(2)}) collective-permute-start(bf16[128,1024]{1,0:T(8,128)(2,1)S(1)} %collective-permute-done.10.refs_6_), channel_id=1, source_target_pairs={{0,4},{4,0},{8,12},{12,8},{16,20},{20,16},{24,28},{28,24},{1,5},{5... | collective-permute-start | bytes 786440 | tf_op jit(solution)/shard_map/ppermute | solution.py:277
  42.4 10.4 %collective-permute-start.13 = (bf16[128,1024]{1,0:T(8,128)(2,1)S(1)}, bf16[128,1024]{1,0:T(8,128)(2,1)S(1)}, u32[]{:S(2)}, u32[]{:S(2)}) collective-permute-start(bf16[128,1024]{1,0:T(8,128)(2,1)S(1)} %add_convert_fusion.3), channel_id=1, source_target_pairs={{0,8},{4,12},{8,0},{12,4},{16,24},{20,28},{24,16},{28,20},{1,9},{5... | collective-permute-start | bytes 786440 | tf_op jit(solution)/shard_map/ppermute | solution.py:277
  44.6 9.9 %collective-permute-start.17 = (bf16[128,1024]{1,0:T(8,128)(2,1)S(1)}, bf16[128,1024]{1,0:T(8,128)(2,1)S(1)}, u32[]{:S(2)}, u32[]{:S(2)}) collective-permute-start(bf16[128,1024]{1,0:T(8,128)(2,1)S(1)} %get-tuple-element.65), channel_id=1, source_target_pairs={{0,4},{4,0},{8,12},{12,8},{16,20},{20,16},{24,28},{28,24},{1,5},{5... | collective-permute-start | bytes 786440 | tf_op jit(solution)/shard_map/ppermute | solution.py:277
  50.5 7.2 %collective-permute-start.15 = (bf16[528,256]{1,0:T(8,128)(2,1)S(1)}, bf16[528,256]{1,0:T(8,128)(2,1)S(1)}, u32[]{:S(2)}, u32[]{:S(2)}) collective-permute-start(bf16[528,256]{1,0:T(8,128)(2,1)S(1)} %get-tuple-element.61), channel_id=1, source_target_pairs={{0,1},{1,0},{2,3},{3,2},{4,5},{5,4},{6,7},{7,6},{8,9},{9,8},{10,11... | collective-permute-start | bytes 811016 | tf_op jit(solution)/shard_map/ppermute | solution.py:274
  52.3 14.6 %collective-permute-start.20 = (bf16[528,256]{1,0:T(8,128)(2,1)S(1)}, bf16[528,256]{1,0:T(8,128)(2,1)S(1)}, u32[]{:S(2)}, u32[]{:S(2)}) collective-permute-start(bf16[528,256]{1,0:T(8,128)(2,1)S(1)} %get-tuple-element.68), channel_id=1, source_target_pairs={{0,1},{1,0},{2,3},{3,2},{4,5},{5,4},{6,7},{7,6},{8,9},{9,8},{10,11... | collective-permute-start | bytes 811016 | tf_op jit(solution)/shard_map/ppermute | solution.py:274
  52.8 8.3 %collective-permute-start.14 = (bf16[128,1024]{1,0:T(8,128)(2,1)S(1)}, bf16[128,1024]{1,0:T(8,128)(2,1)S(1)}, u32[]{:S(2)}, u32[]{:S(2)}) collective-permute-start(bf16[128,1024]{1,0:T(8,128)(2,1)S(1)} %get-tuple-element.60), channel_id=1, source_target_pairs={{0,4},{4,0},{8,12},{12,8},{16,20},{20,16},{24,28},{28,24},{1,5},{5... | collective-permute-start | bytes 786440 | tf_op jit(solution)/shard_map/ppermute | solution.py:277
  54.5 15.2 %collective-permute-start.18 = (bf16[128,1024]{1,0:T(8,128)(2,1)S(1)}, bf16[128,1024]{1,0:T(8,128)(2,1)S(1)}, u32[]{:S(2)}, u32[]{:S(2)}) collective-permute-start(bf16[128,1024]{1,0:T(8,128)(2,1)S(1)} %add_convert_fusion.2), channel_id=1, source_target_pairs={{0,16},{4,20},{8,24},{12,28},{16,0},{20,4},{24,8},{28,12},{1,17},{... | collective-permute-start | bytes 786440 | tf_op jit(solution)/shard_map/ppermute | solution.py:277
  57.7 9.1 %collective-permute-start.21 = (bf16[528,256]{1,0:T(8,128)(2,1)S(1)}, bf16[528,256]{1,0:T(8,128)(2,1)S(1)}, u32[]{:S(2)}, u32[]{:S(2)}) collective-permute-start(bf16[528,256]{1,0:T(8,128)(2,1)S(1)} %add_convert_fusion), channel_id=1, source_target_pairs={{0,2},{1,3},{2,0},{3,1},{4,6},{5,7},{6,4},{7,5},{8,10},{9,11},{10,... | collective-permute-start | bytes 811016 | tf_op jit(solution)/shard_map/ppermute | solution.py:274
  61.1 8.6 %collective-permute-start.16 = (bf16[128,1024]{1,0:T(8,128)(2,1)S(1)}, bf16[128,1024]{1,0:T(8,128)(2,1)S(1)}, u32[]{:S(2)}, u32[]{:S(2)}) collective-permute-start(bf16[128,1024]{1,0:T(8,128)(2,1)S(1)} %get-tuple-element.62), channel_id=1, source_target_pairs={{0,4},{4,0},{8,12},{12,8},{16,20},{20,16},{24,28},{28,24},{1,5},{5... | collective-permute-start | bytes 786440 | tf_op jit(solution)/shard_map/ppermute | solution.py:277
  62.8 12.2 %collective-permute-start.19 = (bf16[128,1024]{1,0:T(8,128)(2,1)S(1)}, bf16[128,1024]{1,0:T(8,128)(2,1)S(1)}, u32[]{:S(2)}, u32[]{:S(2)}) collective-permute-start(bf16[128,1024]{1,0:T(8,128)(2,1)S(1)} %add_convert_fusion.1), channel_id=1, source_target_pairs={{0,8},{4,12},{8,0},{12,4},{16,24},{20,28},{24,16},{28,20},{1,9},{5... | collective-permute-start | bytes 786440 | tf_op jit(solution)/shard_map/ppermute | solution.py:277
  (4 other events, 23.5 us)

commit v11 on v9

--- a/solution.py
+++ b/solution.py
@@ -357,8 +357,8 @@
         fetched = {}
         fetched[7] = trade(terms[7], 1)
         pieces[5] = trade(pieces[4], 1)
-        pieces[7] = trade(after((pieces[6], fetched[7], pieces[5]))[0], 1)
-        fetched[5] = trade(after((terms[5], pieces[5]))[0], 1)
+        pieces[7] = trade(after((pieces[5], terms[0]))[0], 2)
+        fetched[5] = trade(after((terms[5], fetched[7]))[0], 1)
 
     *partials, weight_full = call(
         functools.partial(partial_kernel, n_mp),

time: 71.4 us -> 70.9 us (level)
  waiting for transfers between devices: 25.1 us -> 19.2 us
  starting transfers between devices: 28.9 us -> 34.4 us
    ppermute x14, starting transfers between devices: 22.3 us -> 27.8 us  [trade(): return lax.ppermute(value, 'seq', [(i, i ^ step) for i in range(n_seq)])]
    ppermute x14, waiting for transfers between devices: 17.9 us -> 14.7 us  [trade(): return lax.ppermute(value, 'seq', [(i, i ^ step) for i in range(n_seq)])]
    ppermute x6, waiting for transfers between devices: 3.52 us -> 0.84 us  [swap(): return lax.ppermute(value, 'mp', [(i, i ^ step) for i in range(n_mp)])]
    unnamed x10 -> x12, local copies, waits for them, and re-layouts: 1.43 us -> 1.44 us
  transfers between devices with their start and end apart: 22 -> 22, of which waited for: 11 -> 8; matrix products, arithmetic and copies ran while one was open for 0% -> 0% of each run, Pallas kernels for 18% -> 18%
where the time goes in v11:
time: 70.9 us; the launch traced here: 70.7 us
  starting transfers between devices  34.4 us (49%)
  waiting for transfers between devices  19.2 us (27%)
  Pallas kernels  13.7 us (19%)
  local copies, waits for them, and re-layouts  1.44 us (2%)
  other arithmetic  1.15 us (2%)
  between operations  0.78 us (1%)
    ppermute x14, starting transfers between devices, trade(): return lax.ppermute(value, 'seq', [(i, i ^ step) for i in range(n_seq)])  27.8 us
    ppermute x14, waiting for transfers between devices, trade(): return lax.ppermute(value, 'seq', [(i, i ^ step) for i in range(n_seq)])  14.7 us
    pallas_call x7, Pallas kernels, call(): pl.pallas_call(kernel, out_shape=out_shape, in_specs=in_specs, out_specs=...  13.7 us
    ppermute x6, starting transfers between devices, swap(): return lax.ppermute(value, 'mp', [(i, i ^ step) for i in range(n_mp)])  3.13 us
    ppermute x1, starting transfers between devices, shards(): lax.ppermute(ahead, 'seq', [(i, i + 1) for i in range(n_seq - 1)])  2.21 us
    ppermute x1, waiting for transfers between devices, shards(): following = lax.ppermute(back, 'seq', [(i, i - 1) for i in range(1, n_seq)])  2.15 us
    ppermute x1, waiting for transfers between devices, shards(): lax.ppermute(ahead, 'seq', [(i, i + 1) for i in range(n_seq - 1)])  1.5 us
    unnamed x12, local copies, waits for them, and re-layouts  1.44 us
  transfers between devices with their start and end apart: 22, of which 8 were waited for; matrix products, arithmetic and copies ran while one was open for 0% of the time, Pallas kernels for 18%

profile of v11, /device:TPU:0, one launch (start us, length us, event | category | flops | bytes accessed | tf_op | source)
XLA Modules:
  0.0 70.7 jit_solution(16436531077346812841)
XLA Ops:
  2.5 3.1 %collective-permute-start.2 = (bf16[128,1024]{1,0:T(8,128)(2,1)}, bf16[128,1024]{1,0:T(8,128)(2,1)S(1)}, u32[]{:S(2)}, u32[]{:S(2)}) collective-permute-start(bf16[128,1024]{1,0:T(8,128)(2,1)} %refs_0_), channel_id=1, source_target_pairs={{0,8},{4,12},{8,0},{12,4},{16,24},{20,28},{24,16},{28,20},{1,9},{5... | collective-permute-start | bytes 786440 | tf_op jit(solution)/shard_map/ppermute | solution.py:277
  5.6 1.5 %collective-permute-start.1 = (bf16[128,1024]{1,0:T(8,128)(2,1)}, bf16[128,1024]{1,0:T(8,128)(2,1)S(1)}, u32[]{:S(2)}, u32[]{:S(2)}) collective-permute-start(bf16[128,1024]{1,0:T(8,128)(2,1)} %refs_0_), channel_id=1, source_target_pairs={{0,4},{4,0},{8,12},{12,8},{16,20},{20,16},{24,28},{28,24},{1,5},{5... | collective-permute-start | bytes 786440 | tf_op jit(solution)/shard_map/ppermute | solution.py:277
  8.4 3.3 %collective-permute-start.3 = (bf16[128,1024]{1,0:T(8,128)(2,1)}, bf16[128,1024]{1,0:T(8,128)(2,1)S(1)}, u32[]{:S(2)}, u32[]{:S(2)}) collective-permute-start(bf16[128,1024]{1,0:T(8,128)(2,1)} %refs_0_), channel_id=1, source_target_pairs={{0,16},{4,20},{8,24},{12,28},{16,0},{20,4},{24,8},{28,12},{1,17},{... | collective-permute-start | bytes 786440 | tf_op jit(solution)/shard_map/ppermute | solution.py:277
  11.7 2.1 %collective-permute-done.next_ref = bf16[16,384]{1,0:T(8,128)(2,1)S(1)} collective-permute-done((bf16[16,384]{1,0:T(8,128)(2,1)S(1)}, bf16[16,384]{1,0:T(8,128)(2,1)S(1)}, u32[]{:S(2)}, u32[]{:S(2)}) %collective-permute-start) | collective-permute-done | bytes 12320 | tf_op jit(solution)/shard_map/ppermute | solution.py:301
  14.5 2.1 %shard_map.77 = (bf16[512,256]{1,0:T(8,128)(2,1)S(1)}, f32[512,256]{1,0:T(8,128)S(1)}, f32[512,256]{1,0:T(8,128)S(1)}) custom-call(bf16[1024,256]{1,0:T(8,128)(2,1)S(1)} %get-tuple-element.37.hidden_ref, bf16[16,384]{1,0:T(8,128)(2,1)S(1)} %collective-permute-done.next_ref, s32[8,128]{1,0:T(8,128)S(1)} %get-tuple-element.39.start_ref.refs_4_, ...), custom_call_target="tpu_custom_call" | custom-call | tf_op jit(solution)/shard_map/pallas_call | solution.py:245
  18.1 1.8 %collective-permute-start.7 = (bf16[512,256]{1,0:T(8,128)(2,1)S(1)}, bf16[512,256]{1,0:T(8,128)(2,1)S(1)}, u32[]{:S(2)}, u32[]{:S(2)}) collective-permute-start(bf16[512,256]{1,0:T(8,128)(2,1)S(1)} %get-tuple-element.46.refs_0_), channel_id=1, source_target_pairs={{0,2},{1,3},{2,0},{3,1},{4,6},{5,7},{6,4},{7,5},{8,10},{9,11},{10,... | collective-permute-start | bytes 786440 | tf_op jit(solution)/shard_map/ppermute | solution.py:274
  19.9 2.2 %collective-permute-start.5 = (bf16[32,384]{1,0:T(8,128)(2,1)S(1)}, bf16[32,384]{1,0:T(8,128)(2,1)S(1)}, u32[]{:S(2)}, u32[]{:S(2)}) collective-permute-start(bf16[32,384]{1,0:T(8,128)(2,1)S(1)} %get-tuple-element.45), channel_id=1, source_target_pairs={{0,4},{4,8},{8,12},{12,16},{16,20},{20,24},{24,28},{1,5},{5,9},{9,... | collective-permute-start | bytes 73736 | tf_op jit(solution)/shard_map/ppermute | solution.py:302
  22.1 1.5 %collective-permute-done.5.prev_ref = bf16[32,384]{1,0:T(8,128)(2,1)S(1)} collective-permute-done((bf16[32,384]{1,0:T(8,128)(2,1)S(1)}, bf16[32,384]{1,0:T(8,128)(2,1)S(1)}, u32[]{:S(2)}, u32[]{:S(2)}) %collective-permute-start.5) | collective-permute-done | bytes 24608 | tf_op jit(solution)/shard_map/ppermute | solution.py:302
  24.4 2.0 %collective-permute-start.9 = (bf16[128,1024]{1,0:T(8,128)(2,1)S(1)}, bf16[128,1024]{1,0:T(8,128)(2,1)S(1)}, u32[]{:S(2)}, u32[]{:S(2)}) collective-permute-start(bf16[128,1024]{1,0:T(8,128)(2,1)S(1)} %collective-permute-done.3.refs_4_), channel_id=1, source_target_pairs={{0,4},{4,0},{8,12},{12,8},{16,20},{20,16},{24,28},{28,24},{1,5},{5... | collective-permute-start | bytes 786440 | tf_op jit(solution)/shard_map/ppermute | solution.py:277
  26.4 1.7 %shard_map.78 = (f32[128,1024]{1,0:T(8,128)S(1)}, bf16[128,1024]{1,0:T(8,128)(2,1)S(1)}, f32[128,1024]{1,0:T(8,128)S(1)}, bf16[128,1024]{1,0:T(8,128)(2,1)S(1)},...) custom-call(bf16[512,256]{1,0:T(8,128)(2,1)S(1)} %get-tuple-element., ...), custom_call_target="tpu_custom_call" | custom-call | tf_op jit(solution)/shard_map/pallas_call | solution.py:245
  29.6 1.6 %collective-permute-start.10 = (bf16[128,1024]{1,0:T(8,128)(2,1)S(1)}, bf16[128,1024]{1,0:T(8,128)(2,1)S(1)}, u32[]{:S(2)}, u32[]{:S(2)}) collective-permute-start(bf16[128,1024]{1,0:T(8,128)(2,1)S(1)} %collective-permute-done.3.refs_4_), channel_id=1, source_target_pairs={{0,8},{4,12},{8,0},{12,4},{16,24},{20,28},{24,16},{28,20},{1,9},{5... | collective-permute-start | bytes 786440 | tf_op jit(solution)/shard_map/ppermute | solution.py:277
  31.2 2.3 %collective-permute-done.9.refs_5_ = bf16[128,1024]{1,0:T(8,128)(2,1)S(1)} collective-permute-done((bf16[128,1024]{1,0:T(8,128)(2,1)S(1)}, bf16[128,1024]{1,0:T(8,128)(2,1)S(1)}, u32[]{:S(2)}, u32[]{:S(2)}) %collective-permute-start.9) | collective-permute-done | bytes 262176 | tf_op jit(solution)/shard_map/ppermute | solution.py:277
  33.5 2.5 %collective-permute-start.11 = (bf16[128,1024]{1,0:T(8,128)(2,1)S(1)}, bf16[128,1024]{1,0:T(8,128)(2,1)S(1)}, u32[]{:S(2)}, u32[]{:S(2)}) collective-permute-start(bf16[128,1024]{1,0:T(8,128)(2,1)S(1)} %collective-permute-done.9.refs_5_), channel_id=1, source_target_pairs={{0,8},{4,12},{8,0},{12,4},{16,24},{20,28},{24,16},{28,20},{1,9},{5... | collective-permute-start | bytes 786440 | tf_op jit(solution)/shard_map/ppermute | solution.py:277
  36.1 2.7 %collective-permute-done.12 = bf16[128,1024]{1,0:T(8,128)(2,1)S(1)} collective-permute-done((bf16[128,1024]{1,0:T(8,128)(2,1)S(1)}, bf16[128,1024]{1,0:T(8,128)(2,1)S(1)}, u32[]{:S(2)}, u32[]{:S(2)}) %collective-permute-start.12) | collective-permute-done | bytes 262176 | tf_op jit(solution)/shard_map/ppermute | solution.py:277
  38.8 2.1 %collective-permute-start.16 = (bf16[128,1024]{1,0:T(8,128)(2,1)S(1)}, bf16[128,1024]{1,0:T(8,128)(2,1)S(1)}, u32[]{:S(2)}, u32[]{:S(2)}) collective-permute-start(bf16[128,1024]{1,0:T(8,128)(2,1)S(1)} %add_convert_fusion.2), channel_id=1, source_target_pairs={{0,8},{4,12},{8,0},{12,4},{16,24},{20,28},{24,16},{28,20},{1,9},{5... | collective-permute-start | bytes 786440 | tf_op jit(solution)/shard_map/ppermute | solution.py:277
  42.1 2.4 %collective-permute-done.11.refs_7_ = bf16[128,1024]{1,0:T(8,128)(2,1)S(1)} collective-permute-done((bf16[128,1024]{1,0:T(8,128)(2,1)S(1)}, bf16[128,1024]{1,0:T(8,128)(2,1)S(1)}, u32[]{:S(2)}, u32[]{:S(2)}) %collective-permute-start.11) | collective-permute-done | bytes 262176 | tf_op jit(solution)/shard_map/ppermute | solution.py:277
  44.4 2.5 %shard_map.79 = (bf16[528,256]{1,0:T(8,128)(2,1)S(1)}, bf16[528,256]{1,0:T(8,128)(2,1)S(1)}, bf16[528,256]{1,0:T(8,128)(2,1)S(1)}, bf16[528,256]{1,0:T(8,128)(2,1)S(1)}, bf16[1024,1024]{1,0:T(8,128)(2,1)}) custom-call(bf16[512,1024]{1,0:T(8,128)(2,1)S(1)} %copy-done, bf16[32,384]{1,0:T(8,128)(2,1)S(1)} %collective-permute-done.5.prev_ref, ...), custom_call_target="tpu_custom_call" | custom-call | tf_op jit(solution)/shard_map/pallas_call | solution.py:245
  47.5 1.7 %shard_map.81 = (bf16[1024,512]{1,0:T(8,128)(2,1)S(1)}, f32[1024,256]{1,0:T(8,128)S(1)}, f32[1024,256]{1,0:T(8,128)S(1)}, f32[1024,256]{1,0:T(8,128)S(1)}) custom-call(bf16[1024,256]{1,0:T(8,128)(2,1)S(1)} %get-tuple-element.37.hidden_ref, bf16[32,384]{1,0:T(8,128)(2,1)S(1)} %collective-permute-done.5.prev_ref, ...), custom_call_target="tpu_custom_call" | custom-call | tf_op jit(solution)/shard_map/pallas_call | solution.py:245
  49.2 1.5 %collective-permute-start.18 = (bf16[128,1024]{1,0:T(8,128)(2,1)S(1)}, bf16[128,1024]{1,0:T(8,128)(2,1)S(1)}, u32[]{:S(2)}, u32[]{:S(2)}) collective-permute-start(bf16[128,1024]{1,0:T(8,128)(2,1)S(1)} %get-tuple-element.64), channel_id=1, source_target_pairs={{0,4},{4,0},{8,12},{12,8},{16,20},{20,16},{24,28},{28,24},{1,5},{5... | collective-permute-start | bytes 786440 | tf_op jit(solution)/shard_map/ppermute | solution.py:277
  51.7 4.2 %collective-permute-start.17 = (bf16[128,1024]{1,0:T(8,128)(2,1)S(1)}, bf16[128,1024]{1,0:T(8,128)(2,1)S(1)}, u32[]{:S(2)}, u32[]{:S(2)}) collective-permute-start(bf16[128,1024]{1,0:T(8,128)(2,1)S(1)} %add_convert_fusion.1), channel_id=1, source_target_pairs={{0,16},{4,20},{8,24},{12,28},{16,0},{20,4},{24,8},{28,12},{1,17},{... | collective-permute-start | bytes 786440 | tf_op jit(solution)/shard_map/ppermute | solution.py:277
  57.9 2.4 %shard_map.80 = bf16[512,1024]{1,0:T(8,128)(2,1)} custom-call(bf16[512,256]{1,0:T(8,128)(2,1)S(1)} %get-tuple-element.46.refs_0_, bf16[512,256]{1,0:T(8,128)(2,1)S(1)} %collective-permute-done.6.refs_1_, bf16[512,256]{1,0:T(8,128)(2,1)S(1)} %collective-permute-done.7.refs_2_, bf16[512,256]{1,0:T(8,128)(2,1)S(1)} %collective-permute-done.8.refs_3_, ...), custom_call_target="tpu_custom_call" | custom-call | tf_op jit(solution)/shard_map/pallas_call | solution.py:245
  60.2 2.2 %shard_map.82 = bf16[1024,256]{1,0:T(8,128)(2,1)} custom-call(bf16[528,256]{1,0:T(8,128)(2,1)S(1)} %get-tuple-element.65.refs_0_, bf16[528,256]{1,0:T(8,128)(2,1)S(1)} %collective-permute-done.20.refs_1_, bf16[528,256]{1,0:T(8,128)(2,1)S(1)} %collective-permute-done.14.refs_2_, bf16[528,256]{1,0:T(8,128)(2,1)S(1)} %collective-permute-done.21.refs_3_, ...), custom_call_target="tpu_custom_call" | custom-call | tf_op jit(solution)/shard_map/pallas_call | solution.py:245
  62.4 5.4 %collective-permute-done.17 = bf16[128,1024]{1,0:T(8,128)(2,1)S(1)} collective-permute-done((bf16[128,1024]{1,0:T(8,128)(2,1)S(1)}, bf16[128,1024]{1,0:T(8,128)(2,1)S(1)}, u32[]{:S(2)}, u32[]{:S(2)}) %collective-permute-start.17) | collective-permute-done | bytes 262176 | tf_op jit(solution)/shard_map/ppermute | solution.py:277
  67.9 1.9 %collective-permute-done.19 = bf16[128,1024]{1,0:T(8,128)(2,1)S(1)} collective-permute-done((bf16[128,1024]{1,0:T(8,128)(2,1)S(1)}, bf16[128,1024]{1,0:T(8,128)(2,1)S(1)}, u32[]{:S(2)}, u32[]{:S(2)}) %collective-permute-start.19) | collective-permute-done | bytes 262176 | tf_op jit(solution)/shard_map/ppermute | solution.py:277
  (43 shorter events, 13.0 us)
Async XLA Ops:
  0.6 25.8 %copy-start = (bf16[512,1024]{1,0:T(8,128)(2,1)S(1)}, bf16[512,1024]{1,0:T(8,128)(2,1)}, u32[]{:S(2)}) copy-start(bf16[512,1024]{1,0:T(8,128)(2,1)} %grad_ref.1) | copy-start | bytes 3145732
  2.5 41.9 %copy-start.2 = (bf16[128,1024]{1,0:T(8,128)(2,1)S(1)}, bf16[128,1024]{1,0:T(8,128)(2,1)}, u32[]{:S(2)}) copy-start(bf16[128,1024]{1,0:T(8,128)(2,1)} %refs_0_) | copy-start | bytes 786436
  2.5 14.1 %collective-permute-start.2 = (bf16[128,1024]{1,0:T(8,128)(2,1)}, bf16[128,1024]{1,0:T(8,128)(2,1)S(1)}, u32[]{:S(2)}, u32[]{:S(2)}) collective-permute-start(bf16[128,1024]{1,0:T(8,128)(2,1)} %refs_0_), channel_id=1, source_target_pairs={{0,8},{4,12},{8,0},{12,4},{16,24},{20,28},{24,16},{28,20},{1,9},{5... | collective-permute-start | bytes 786440 | tf_op jit(solution)/shard_map/ppermute | solution.py:277
  5.6 11.0 %collective-permute-start.1 = (bf16[128,1024]{1,0:T(8,128)(2,1)}, bf16[128,1024]{1,0:T(8,128)(2,1)S(1)}, u32[]{:S(2)}, u32[]{:S(2)}) collective-permute-start(bf16[128,1024]{1,0:T(8,128)(2,1)} %refs_0_), channel_id=1, source_target_pairs={{0,4},{4,0},{8,12},{12,8},{16,20},{20,16},{24,28},{28,24},{1,5},{5... | collective-permute-start | bytes 786440 | tf_op jit(solution)/shard_map/ppermute | solution.py:277
  7.1 6.7 %collective-permute-start = (bf16[16,384]{1,0:T(8,128)(2,1)S(1)}, bf16[16,384]{1,0:T(8,128)(2,1)S(1)}, u32[]{:S(2)}, u32[]{:S(2)}) collective-permute-start(bf16[16,384]{1,0:T(8,128)(2,1)S(1)} %get-tuple-element.38), channel_id=1, source_target_pairs={{4,0},{8,4},{12,8},{16,12},{20,16},{24,20},{28,24},{5,1},{9,5},{13... | collective-permute-start | bytes 36872 | tf_op jit(solution)/shard_map/ppermute | solution.py:301
  8.4 15.2 %collective-permute-start.3 = (bf16[128,1024]{1,0:T(8,128)(2,1)}, bf16[128,1024]{1,0:T(8,128)(2,1)S(1)}, u32[]{:S(2)}, u32[]{:S(2)}) collective-permute-start(bf16[128,1024]{1,0:T(8,128)(2,1)} %refs_0_), channel_id=1, source_target_pairs={{0,16},{4,20},{8,24},{12,28},{16,0},{20,4},{24,8},{28,12},{1,17},{... | collective-permute-start | bytes 786440 | tf_op jit(solution)/shard_map/ppermute | solution.py:277
  16.6 7.0 %collective-permute-start.4 = (bf16[128,1024]{1,0:T(8,128)(2,1)S(1)}, bf16[128,1024]{1,0:T(8,128)(2,1)S(1)}, u32[]{:S(2)}, u32[]{:S(2)}) collective-permute-start(bf16[128,1024]{1,0:T(8,128)(2,1)S(1)} %collective-permute-done.2.refs_2_), channel_id=1, source_target_pairs={{0,4},{4,0},{8,12},{12,8},{16,20},{20,16},{24,28},{28,24},{1,5},{5... | collective-permute-start | bytes 786440 | tf_op jit(solution)/shard_map/ppermute | solution.py:277
  18.1 6.4 %collective-permute-start.7 = (bf16[512,256]{1,0:T(8,128)(2,1)S(1)}, bf16[512,256]{1,0:T(8,128)(2,1)S(1)}, u32[]{:S(2)}, u32[]{:S(2)}) collective-permute-start(bf16[512,256]{1,0:T(8,128)(2,1)S(1)} %get-tuple-element.46.refs_0_), channel_id=1, source_target_pairs={{0,2},{1,3},{2,0},{3,1},{4,6},{5,7},{6,4},{7,5},{8,10},{9,11},{10,... | collective-permute-start | bytes 786440 | tf_op jit(solution)/shard_map/ppermute | solution.py:274
  19.9 3.7 %collective-permute-start.5 = (bf16[32,384]{1,0:T(8,128)(2,1)S(1)}, bf16[32,384]{1,0:T(8,128)(2,1)S(1)}, u32[]{:S(2)}, u32[]{:S(2)}) collective-permute-start(bf16[32,384]{1,0:T(8,128)(2,1)S(1)} %get-tuple-element.45), channel_id=1, source_target_pairs={{0,4},{4,8},{8,12},{12,16},{16,20},{20,24},{24,28},{1,5},{5,9},{9,... | collective-permute-start | bytes 73736 | tf_op jit(solution)/shard_map/ppermute | solution.py:302
  23.6 2.8 %collective-permute-start.6 = (bf16[512,256]{1,0:T(8,128)(2,1)S(1)}, bf16[512,256]{1,0:T(8,128)(2,1)S(1)}, u32[]{:S(2)}, u32[]{:S(2)}) collective-permute-start(bf16[512,256]{1,0:T(8,128)(2,1)S(1)} %get-tuple-element.46.refs_0_), channel_id=1, source_target_pairs={{0,1},{1,0},{2,3},{3,2},{4,5},{5,4},{6,7},{7,6},{8,9},{9,8},{10,11... | collective-permute-start | bytes 786440 | tf_op jit(solution)/shard_map/ppermute | solution.py:274
  24.4 2.0 %collective-permute-start.8 = (bf16[512,256]{1,0:T(8,128)(2,1)S(1)}, bf16[512,256]{1,0:T(8,128)(2,1)S(1)}, u32[]{:S(2)}, u32[]{:S(2)}) collective-permute-start(bf16[512,256]{1,0:T(8,128)(2,1)S(1)} %collective-permute-done.7.refs_2_), channel_id=1, source_target_pairs={{0,1},{1,0},{2,3},{3,2},{4,5},{5,4},{6,7},{7,6},{8,9},{9,8},{10,11... | collective-permute-start | bytes 786440 | tf_op jit(solution)/shard_map/ppermute | solution.py:274
  24.4 9.1 %collective-permute-start.9 = (bf16[128,1024]{1,0:T(8,128)(2,1)S(1)}, bf16[128,1024]{1,0:T(8,128)(2,1)S(1)}, u32[]{:S(2)}, u32[]{:S(2)}) collective-permute-start(bf16[128,1024]{1,0:T(8,128)(2,1)S(1)} %collective-permute-done.3.refs_4_), channel_id=1, source_target_pairs={{0,4},{4,0},{8,12},{12,8},{16,20},{20,16},{24,28},{28,24},{1,5},{5... | collective-permute-start | bytes 786440 | tf_op jit(solution)/shard_map/ppermute | solution.py:277
  28.2 10.6 %collective-permute-start.12 = (bf16[128,1024]{1,0:T(8,128)(2,1)S(1)}, bf16[128,1024]{1,0:T(8,128)(2,1)S(1)}, u32[]{:S(2)}, u32[]{:S(2)}) collective-permute-start(bf16[128,1024]{1,0:T(8,128)(2,1)S(1)} %get-tuple-element.53), channel_id=1, source_target_pairs={{0,4},{4,0},{8,12},{12,8},{16,20},{20,16},{24,28},{28,24},{1,5},{5... | collective-permute-start | bytes 786440 | tf_op jit(solution)/shard_map/ppermute | solution.py:277
  29.6 12.4 %collective-permute-start.10 = (bf16[128,1024]{1,0:T(8,128)(2,1)S(1)}, bf16[128,1024]{1,0:T(8,128)(2,1)S(1)}, u32[]{:S(2)}, u32[]{:S(2)}) collective-permute-start(bf16[128,1024]{1,0:T(8,128)(2,1)S(1)} %collective-permute-done.3.refs_4_), channel_id=1, source_target_pairs={{0,8},{4,12},{8,0},{12,4},{16,24},{20,28},{24,16},{28,20},{1,9},{5... | collective-permute-start | bytes 786440 | tf_op jit(solution)/shard_map/ppermute | solution.py:277
  33.5 10.9 %collective-permute-start.11 = (bf16[128,1024]{1,0:T(8,128)(2,1)S(1)}, bf16[128,1024]{1,0:T(8,128)(2,1)S(1)}, u32[]{:S(2)}, u32[]{:S(2)}) collective-permute-start(bf16[128,1024]{1,0:T(8,128)(2,1)S(1)} %collective-permute-done.9.refs_5_), channel_id=1, source_target_pairs={{0,8},{4,12},{8,0},{12,4},{16,24},{20,28},{24,16},{28,20},{1,9},{5... | collective-permute-start | bytes 786440 | tf_op jit(solution)/shard_map/ppermute | solution.py:277
  38.8 10.4 %collective-permute-start.16 = (bf16[128,1024]{1,0:T(8,128)(2,1)S(1)}, bf16[128,1024]{1,0:T(8,128)(2,1)S(1)}, u32[]{:S(2)}, u32[]{:S(2)}) collective-permute-start(bf16[128,1024]{1,0:T(8,128)(2,1)S(1)} %add_convert_fusion.2), channel_id=1, source_target_pairs={{0,8},{4,12},{8,0},{12,4},{16,24},{20,28},{24,16},{28,20},{1,9},{5... | collective-permute-start | bytes 786440 | tf_op jit(solution)/shard_map/ppermute | solution.py:277
  40.9 10.6 %collective-permute-start.13 = (bf16[128,1024]{1,0:T(8,128)(2,1)S(1)}, bf16[128,1024]{1,0:T(8,128)(2,1)S(1)}, u32[]{:S(2)}, u32[]{:S(2)}) collective-permute-start(bf16[128,1024]{1,0:T(8,128)(2,1)S(1)} %get-tuple-element.54), channel_id=1, source_target_pairs={{0,4},{4,0},{8,12},{12,8},{16,20},{20,16},{24,28},{28,24},{1,5},{5... | collective-permute-start | bytes 786440 | tf_op jit(solution)/shard_map/ppermute | solution.py:277
  46.9 9.0 %collective-permute-start.14 = (bf16[528,256]{1,0:T(8,128)(2,1)S(1)}, bf16[528,256]{1,0:T(8,128)(2,1)S(1)}, u32[]{:S(2)}, u32[]{:S(2)}) collective-permute-start(bf16[528,256]{1,0:T(8,128)(2,1)S(1)} %get-tuple-element.55), channel_id=1, source_target_pairs={{0,2},{1,3},{2,0},{3,1},{4,6},{5,7},{6,4},{7,5},{8,10},{9,11},{10,... | collective-permute-start | bytes 811016 | tf_op jit(solution)/shard_map/ppermute | solution.py:274
  49.2 7.2 %collective-permute-start.18 = (bf16[128,1024]{1,0:T(8,128)(2,1)S(1)}, bf16[128,1024]{1,0:T(8,128)(2,1)S(1)}, u32[]{:S(2)}, u32[]{:S(2)}) collective-permute-start(bf16[128,1024]{1,0:T(8,128)(2,1)S(1)} %get-tuple-element.64), channel_id=1, source_target_pairs={{0,4},{4,0},{8,12},{12,8},{16,20},{20,16},{24,28},{28,24},{1,5},{5... | collective-permute-start | bytes 786440 | tf_op jit(solution)/shard_map/ppermute | solution.py:277
  50.8 9.5 %collective-permute-start.20 = (bf16[528,256]{1,0:T(8,128)(2,1)S(1)}, bf16[528,256]{1,0:T(8,128)(2,1)S(1)}, u32[]{:S(2)}, u32[]{:S(2)}) collective-permute-start(bf16[528,256]{1,0:T(8,128)(2,1)S(1)} %get-tuple-element.66), channel_id=1, source_target_pairs={{0,1},{1,0},{2,3},{3,2},{4,5},{5,4},{6,7},{7,6},{8,9},{9,8},{10,11... | collective-permute-start | bytes 811016 | tf_op jit(solution)/shard_map/ppermute | solution.py:274
  50.8 9.5 %collective-permute-start.21 = (bf16[528,256]{1,0:T(8,128)(2,1)S(1)}, bf16[528,256]{1,0:T(8,128)(2,1)S(1)}, u32[]{:S(2)}, u32[]{:S(2)}) collective-permute-start(bf16[528,256]{1,0:T(8,128)(2,1)S(1)} %get-tuple-element.67), channel_id=1, source_target_pairs={{0,3},{1,2},{2,1},{3,0},{4,7},{5,6},{6,5},{7,4},{8,11},{9,10},{10,... | collective-permute-start | bytes 811016 | tf_op jit(solution)/shard_map/ppermute | solution.py:274
  51.7 16.2 %collective-permute-start.17 = (bf16[128,1024]{1,0:T(8,128)(2,1)S(1)}, bf16[128,1024]{1,0:T(8,128)(2,1)S(1)}, u32[]{:S(2)}, u32[]{:S(2)}) collective-permute-start(bf16[128,1024]{1,0:T(8,128)(2,1)S(1)} %add_convert_fusion.1), channel_id=1, source_target_pairs={{0,16},{4,20},{8,24},{12,28},{16,0},{20,4},{24,8},{28,12},{1,17},{... | collective-permute-start | bytes 786440 | tf_op jit(solution)/shard_map/ppermute | solution.py:277
  55.9 12.0 %collective-permute-start.15 = (bf16[128,1024]{1,0:T(8,128)(2,1)S(1)}, bf16[128,1024]{1,0:T(8,128)(2,1)S(1)}, u32[]{:S(2)}, u32[]{:S(2)}) collective-permute-start(bf16[128,1024]{1,0:T(8,128)(2,1)S(1)} %get-tuple-element.56), channel_id=1, source_target_pairs={{0,4},{4,0},{8,12},{12,8},{16,20},{20,16},{24,28},{28,24},{1,5},{5... | collective-permute-start | bytes 786440 | tf_op jit(solution)/shard_map/ppermute | solution.py:277
  56.5 13.2 %collective-permute-start.19 = (bf16[128,1024]{1,0:T(8,128)(2,1)S(1)}, bf16[128,1024]{1,0:T(8,128)(2,1)S(1)}, u32[]{:S(2)}, u32[]{:S(2)}) collective-permute-start(bf16[128,1024]{1,0:T(8,128)(2,1)S(1)} %add_convert_fusion), channel_id=1, source_target_pairs={{0,8},{4,12},{8,0},{12,4},{16,24},{20,28},{24,16},{28,20},{1,9},{5... | collective-permute-start | bytes 786440 | tf_op jit(solution)/shard_map/ppermute | solution.py:277
  (4 other events, 21.0 us)

commit v12 on v11

--- a/solution.py
+++ b/solution.py
@@ -372,10 +372,10 @@
 
     if staged:
         fetched[6] = trade((terms[6] + fetched[7].astype(F32)).astype(BF16), 2)
-        fetched[3] = trade(after((terms[3], weight_full, share, fetched[6]))[0], 1)
+        fetched[3] = trade(after((terms[3], weight_full, fetched[6]))[0], 1)
         pair = terms[4] + fetched[5].astype(F32) + fetched[6].astype(F32)
         fetched[4] = trade(pair.astype(BF16), 4)
-        fetched[1] = trade(after((terms[1], fetched[5], grads[2]))[0], 1)
+        fetched[1] = trade(after((terms[1], fetched[5], grads[2], share))[0], 1)
         fetched[2] = trade((terms[2] + fetched[3].astype(F32)).astype(BF16), 2)
         grad_weight = terms[0] + fetched[1].astype(F32)
         for step in (4, 2):

time: 70.9 us -> 71.3 us (level)
  waiting for transfers between devices: 19.2 us -> 21 us
  starting transfers between devices: 34.4 us -> 32.9 us
    ppermute x14, starting transfers between devices: 27.8 us -> 25.7 us  [trade(): return lax.ppermute(value, 'seq', [(i, i ^ step) for i in range(n_seq)])]
    ppermute x14, waiting for transfers between devices: 14.7 us -> 16.5 us  [trade(): return lax.ppermute(value, 'seq', [(i, i ^ step) for i in range(n_seq)])]
  transfers between devices with their start and end apart: 22 -> 22, of which waited for: 8 -> 9; matrix products, arithmetic and copies ran while one was open for 0% -> 0% of each run, Pallas kernels for 18% -> 18%
where the time goes in v12:
time: 71.3 us; the launch traced here: 71.1 us
  starting transfers between devices  32.9 us (46%)
  waiting for transfers between devices  21 us (29%)
  Pallas kernels  13.7 us (19%)
  local copies, waits for them, and re-layouts  1.44 us (2%)
  other arithmetic  1.16 us (2%)
  between operations  0.78 us (1%)
    ppermute x14, starting transfers between devices, trade(): return lax.ppermute(value, 'seq', [(i, i ^ step) for i in range(n_seq)])  25.7 us
    ppermute x14, waiting for transfers between devices, trade(): return lax.ppermute(value, 'seq', [(i, i ^ step) for i in range(n_seq)])  16.5 us
    pallas_call x7, Pallas kernels, call(): pl.pallas_call(kernel, out_shape=out_shape, in_specs=in_specs, out_specs=...  13.7 us
    ppermute x6, starting transfers between devices, swap(): return lax.ppermute(value, 'mp', [(i, i ^ step) for i in range(n_mp)])  3.76 us
    ppermute x1, starting transfers between devices, shards(): lax.ppermute(ahead, 'seq', [(i, i + 1) for i in range(n_seq - 1)])  2.21 us
    ppermute x1, waiting for transfers between devices, shards(): following = lax.ppermute(back, 'seq', [(i, i - 1) for i in range(1, n_seq)])  2.15 us
    ppermute x1, waiting for transfers between devices, shards(): lax.ppermute(ahead, 'seq', [(i, i + 1) for i in range(n_seq - 1)])  1.5 us
    unnamed x12, local copies, waits for them, and re-layouts  1.44 us
  transfers between devices with their start and end apart: 22, of which 9 were waited for; matrix products, arithmetic and copies ran while one was open for 0% of the time, Pallas kernels for 18%

profile of v12, /device:TPU:0, one launch (start us, length us, event | category | flops | bytes accessed | tf_op | source)
XLA Modules:
  0.0 71.1 jit_solution(3601590342295395531)
XLA Ops:
  2.5 3.1 %collective-permute-start.2 = (bf16[128,1024]{1,0:T(8,128)(2,1)}, bf16[128,1024]{1,0:T(8,128)(2,1)S(1)}, u32[]{:S(2)}, u32[]{:S(2)}) collective-permute-start(bf16[128,1024]{1,0:T(8,128)(2,1)} %refs_0_), channel_id=1, source_target_pairs={{0,8},{4,12},{8,0},{12,4},{16,24},{20,28},{24,16},{28,20},{1,9},{5... | collective-permute-start | bytes 786440 | tf_op jit(solution)/shard_map/ppermute | solution.py:277
  5.6 1.5 %collective-permute-start.1 = (bf16[128,1024]{1,0:T(8,128)(2,1)}, bf16[128,1024]{1,0:T(8,128)(2,1)S(1)}, u32[]{:S(2)}, u32[]{:S(2)}) collective-permute-start(bf16[128,1024]{1,0:T(8,128)(2,1)} %refs_0_), channel_id=1, source_target_pairs={{0,4},{4,0},{8,12},{12,8},{16,20},{20,16},{24,28},{28,24},{1,5},{5... | collective-permute-start | bytes 786440 | tf_op jit(solution)/shard_map/ppermute | solution.py:277
  8.4 3.3 %collective-permute-start.3 = (bf16[128,1024]{1,0:T(8,128)(2,1)}, bf16[128,1024]{1,0:T(8,128)(2,1)S(1)}, u32[]{:S(2)}, u32[]{:S(2)}) collective-permute-start(bf16[128,1024]{1,0:T(8,128)(2,1)} %refs_0_), channel_id=1, source_target_pairs={{0,16},{4,20},{8,24},{12,28},{16,0},{20,4},{24,8},{28,12},{1,17},{... | collective-permute-start | bytes 786440 | tf_op jit(solution)/shard_map/ppermute | solution.py:277
  11.7 2.1 %collective-permute-done.next_ref = bf16[16,384]{1,0:T(8,128)(2,1)S(1)} collective-permute-done((bf16[16,384]{1,0:T(8,128)(2,1)S(1)}, bf16[16,384]{1,0:T(8,128)(2,1)S(1)}, u32[]{:S(2)}, u32[]{:S(2)}) %collective-permute-start) | collective-permute-done | bytes 12320 | tf_op jit(solution)/shard_map/ppermute | solution.py:301
  14.5 2.1 %shard_map.77 = (bf16[512,256]{1,0:T(8,128)(2,1)S(1)}, f32[512,256]{1,0:T(8,128)S(1)}, f32[512,256]{1,0:T(8,128)S(1)}) custom-call(bf16[1024,256]{1,0:T(8,128)(2,1)S(1)} %get-tuple-element.37.hidden_ref, bf16[16,384]{1,0:T(8,128)(2,1)S(1)} %collective-permute-done.next_ref, s32[8,128]{1,0:T(8,128)S(1)} %get-tuple-element.39.start_ref.refs_4_, ...), custom_call_target="tpu_custom_call" | custom-call | tf_op jit(solution)/shard_map/pallas_call | solution.py:245
  16.6 1.5 %collective-permute-start.4 = (bf16[128,1024]{1,0:T(8,128)(2,1)S(1)}, bf16[128,1024]{1,0:T(8,128)(2,1)S(1)}, u32[]{:S(2)}, u32[]{:S(2)}) collective-permute-start(bf16[128,1024]{1,0:T(8,128)(2,1)S(1)} %collective-permute-done.2.refs_2_), channel_id=1, source_target_pairs={{0,4},{4,0},{8,12},{12,8},{16,20},{20,16},{24,28},{28,24},{1,5},{5... | collective-permute-start | bytes 786440 | tf_op jit(solution)/shard_map/ppermute | solution.py:277
  18.1 1.8 %collective-permute-start.7 = (bf16[512,256]{1,0:T(8,128)(2,1)S(1)}, bf16[512,256]{1,0:T(8,128)(2,1)S(1)}, u32[]{:S(2)}, u32[]{:S(2)}) collective-permute-start(bf16[512,256]{1,0:T(8,128)(2,1)S(1)} %get-tuple-element.46.refs_0_), channel_id=1, source_target_pairs={{0,2},{1,3},{2,0},{3,1},{4,6},{5,7},{6,4},{7,5},{8,10},{9,11},{10,... | collective-permute-start | bytes 786440 | tf_op jit(solution)/shard_map/ppermute | solution.py:274
  19.9 2.2 %collective-permute-start.5 = (bf16[32,384]{1,0:T(8,128)(2,1)S(1)}, bf16[32,384]{1,0:T(8,128)(2,1)S(1)}, u32[]{:S(2)}, u32[]{:S(2)}) collective-permute-start(bf16[32,384]{1,0:T(8,128)(2,1)S(1)} %get-tuple-element.45), channel_id=1, source_target_pairs={{0,4},{4,8},{8,12},{12,16},{16,20},{20,24},{24,28},{1,5},{5,9},{9,... | collective-permute-start | bytes 73736 | tf_op jit(solution)/shard_map/ppermute | solution.py:302
  22.1 1.5 %collective-permute-done.5.prev_ref = bf16[32,384]{1,0:T(8,128)(2,1)S(1)} collective-permute-done((bf16[32,384]{1,0:T(8,128)(2,1)S(1)}, bf16[32,384]{1,0:T(8,128)(2,1)S(1)}, u32[]{:S(2)}, u32[]{:S(2)}) %collective-permute-start.5) | collective-permute-done | bytes 24608 | tf_op jit(solution)/shard_map/ppermute | solution.py:302
  24.4 2.0 %collective-permute-start.9 = (bf16[128,1024]{1,0:T(8,128)(2,1)S(1)}, bf16[128,1024]{1,0:T(8,128)(2,1)S(1)}, u32[]{:S(2)}, u32[]{:S(2)}) collective-permute-start(bf16[128,1024]{1,0:T(8,128)(2,1)S(1)} %collective-permute-done.3.refs_4_), channel_id=1, source_target_pairs={{0,4},{4,0},{8,12},{12,8},{16,20},{20,16},{24,28},{28,24},{1,5},{5... | collective-permute-start | bytes 786440 | tf_op jit(solution)/shard_map/ppermute | solution.py:277
  26.4 1.7 %shard_map.78 = (f32[128,1024]{1,0:T(8,128)S(1)}, bf16[128,1024]{1,0:T(8,128)(2,1)S(1)}, f32[128,1024]{1,0:T(8,128)S(1)}, bf16[128,1024]{1,0:T(8,128)(2,1)S(1)},...) custom-call(bf16[512,256]{1,0:T(8,128)(2,1)S(1)} %get-tuple-element., ...), custom_call_target="tpu_custom_call" | custom-call | tf_op jit(solution)/shard_map/pallas_call | solution.py:245
  29.6 1.6 %collective-permute-start.10 = (bf16[128,1024]{1,0:T(8,128)(2,1)S(1)}, bf16[128,1024]{1,0:T(8,128)(2,1)S(1)}, u32[]{:S(2)}, u32[]{:S(2)}) collective-permute-start(bf16[128,1024]{1,0:T(8,128)(2,1)S(1)} %collective-permute-done.3.refs_4_), channel_id=1, source_target_pairs={{0,8},{4,12},{8,0},{12,4},{16,24},{20,28},{24,16},{28,20},{1,9},{5... | collective-permute-start | bytes 786440 | tf_op jit(solution)/shard_map/ppermute | solution.py:277
  31.2 2.3 %collective-permute-done.9.refs_5_ = bf16[128,1024]{1,0:T(8,128)(2,1)S(1)} collective-permute-done((bf16[128,1024]{1,0:T(8,128)(2,1)S(1)}, bf16[128,1024]{1,0:T(8,128)(2,1)S(1)}, u32[]{:S(2)}, u32[]{:S(2)}) %collective-permute-start.9) | collective-permute-done | bytes 262176 | tf_op jit(solution)/shard_map/ppermute | solution.py:277
  33.5 2.5 %collective-permute-start.11 = (bf16[128,1024]{1,0:T(8,128)(2,1)S(1)}, bf16[128,1024]{1,0:T(8,128)(2,1)S(1)}, u32[]{:S(2)}, u32[]{:S(2)}) collective-permute-start(bf16[128,1024]{1,0:T(8,128)(2,1)S(1)} %collective-permute-done.9.refs_5_), channel_id=1, source_target_pairs={{0,8},{4,12},{8,0},{12,4},{16,24},{20,28},{24,16},{28,20},{1,9},{5... | collective-permute-start | bytes 786440 | tf_op jit(solution)/shard_map/ppermute | solution.py:277
  36.1 2.7 %collective-permute-done.12 = bf16[128,1024]{1,0:T(8,128)(2,1)S(1)} collective-permute-done((bf16[128,1024]{1,0:T(8,128)(2,1)S(1)}, bf16[128,1024]{1,0:T(8,128)(2,1)S(1)}, u32[]{:S(2)}, u32[]{:S(2)}) %collective-permute-start.12) | collective-permute-done | bytes 262176 | tf_op jit(solution)/shard_map/ppermute | solution.py:277
  38.8 2.1 %collective-permute-start.16 = (bf16[128,1024]{1,0:T(8,128)(2,1)S(1)}, bf16[128,1024]{1,0:T(8,128)(2,1)S(1)}, u32[]{:S(2)}, u32[]{:S(2)}) collective-permute-start(bf16[128,1024]{1,0:T(8,128)(2,1)S(1)} %add_convert_fusion.2), channel_id=1, source_target_pairs={{0,8},{4,12},{8,0},{12,4},{16,24},{20,28},{24,16},{28,20},{1,9},{5... | collective-permute-start | bytes 786440 | tf_op jit(solution)/shard_map/ppermute | solution.py:277
  42.1 2.4 %collective-permute-done.11.refs_7_ = bf16[128,1024]{1,0:T(8,128)(2,1)S(1)} collective-permute-done((bf16[128,1024]{1,0:T(8,128)(2,1)S(1)}, bf16[128,1024]{1,0:T(8,128)(2,1)S(1)}, u32[]{:S(2)}, u32[]{:S(2)}) %collective-permute-start.11) | collective-permute-done | bytes 262176 | tf_op jit(solution)/shard_map/ppermute | solution.py:277
  44.4 2.5 %shard_map.79 = (bf16[528,256]{1,0:T(8,128)(2,1)S(1)}, bf16[528,256]{1,0:T(8,128)(2,1)S(1)}, bf16[528,256]{1,0:T(8,128)(2,1)S(1)}, bf16[528,256]{1,0:T(8,128)(2,1)S(1)}, bf16[1024,1024]{1,0:T(8,128)(2,1)}) custom-call(bf16[512,1024]{1,0:T(8,128)(2,1)S(1)} %copy-done, bf16[32,384]{1,0:T(8,128)(2,1)S(1)} %collective-permute-done.5.prev_ref, ...), custom_call_target="tpu_custom_call" | custom-call | tf_op jit(solution)/shard_map/pallas_call | solution.py:245
  49.7 1.7 %shard_map.81 = (bf16[1024,512]{1,0:T(8,128)(2,1)S(1)}, f32[1024,256]{1,0:T(8,128)S(1)}, f32[1024,256]{1,0:T(8,128)S(1)}, f32[1024,256]{1,0:T(8,128)S(1)}) custom-call(bf16[1024,256]{1,0:T(8,128)(2,1)S(1)} %get-tuple-element.37.hidden_ref, bf16[32,384]{1,0:T(8,128)(2,1)S(1)} %collective-permute-done.5.prev_ref, ...), custom_call_target="tpu_custom_call" | custom-call | tf_op jit(solution)/shard_map/pallas_call | solution.py:245
  53.0 3.4 %collective-permute-start.17 = (bf16[128,1024]{1,0:T(8,128)(2,1)S(1)}, bf16[128,1024]{1,0:T(8,128)(2,1)S(1)}, u32[]{:S(2)}, u32[]{:S(2)}) collective-permute-start(bf16[128,1024]{1,0:T(8,128)(2,1)S(1)} %add_convert_fusion.1), channel_id=1, source_target_pairs={{0,16},{4,20},{8,24},{12,28},{16,0},{20,4},{24,8},{28,12},{1,17},{... | collective-permute-start | bytes 786440 | tf_op jit(solution)/shard_map/ppermute | solution.py:277
  57.9 2.4 %shard_map.80 = bf16[512,1024]{1,0:T(8,128)(2,1)} custom-call(bf16[512,256]{1,0:T(8,128)(2,1)S(1)} %get-tuple-element.46.refs_0_, bf16[512,256]{1,0:T(8,128)(2,1)S(1)} %collective-permute-done.6.refs_1_, bf16[512,256]{1,0:T(8,128)(2,1)S(1)} %collective-permute-done.7.refs_2_, bf16[512,256]{1,0:T(8,128)(2,1)S(1)} %collective-permute-done.8.refs_3_, ...), custom_call_target="tpu_custom_call" | custom-call | tf_op jit(solution)/shard_map/pallas_call | solution.py:245
  60.2 2.2 %shard_map.82 = bf16[1024,256]{1,0:T(8,128)(2,1)} custom-call(bf16[528,256]{1,0:T(8,128)(2,1)S(1)} %get-tuple-element.65.refs_0_, bf16[528,256]{1,0:T(8,128)(2,1)S(1)} %collective-permute-done.20.refs_1_, bf16[528,256]{1,0:T(8,128)(2,1)S(1)} %collective-permute-done.14.refs_2_, bf16[528,256]{1,0:T(8,128)(2,1)S(1)} %collective-permute-done.21.refs_3_, ...), custom_call_target="tpu_custom_call" | custom-call | tf_op jit(solution)/shard_map/pallas_call | solution.py:245
  62.5 6.0 %collective-permute-done.17 = bf16[128,1024]{1,0:T(8,128)(2,1)S(1)} collective-permute-done((bf16[128,1024]{1,0:T(8,128)(2,1)S(1)}, bf16[128,1024]{1,0:T(8,128)(2,1)S(1)}, u32[]{:S(2)}, u32[]{:S(2)}) %collective-permute-start.17) | collective-permute-done | bytes 262176 | tf_op jit(solution)/shard_map/ppermute | solution.py:277
  68.5 1.7 %collective-permute-done.19 = bf16[128,1024]{1,0:T(8,128)(2,1)S(1)} collective-permute-done((bf16[128,1024]{1,0:T(8,128)(2,1)S(1)}, bf16[128,1024]{1,0:T(8,128)(2,1)S(1)}, u32[]{:S(2)}, u32[]{:S(2)}) %collective-permute-start.19) | collective-permute-done | bytes 262176 | tf_op jit(solution)/shard_map/ppermute | solution.py:277
  (43 shorter events, 14.0 us)
Async XLA Ops:
  0.6 25.8 %copy-start = (bf16[512,1024]{1,0:T(8,128)(2,1)S(1)}, bf16[512,1024]{1,0:T(8,128)(2,1)}, u32[]{:S(2)}) copy-start(bf16[512,1024]{1,0:T(8,128)(2,1)} %grad_ref.1) | copy-start | bytes 3145732
  2.5 41.9 %copy-start.2 = (bf16[128,1024]{1,0:T(8,128)(2,1)S(1)}, bf16[128,1024]{1,0:T(8,128)(2,1)}, u32[]{:S(2)}) copy-start(bf16[128,1024]{1,0:T(8,128)(2,1)} %refs_0_) | copy-start | bytes 786436
  2.5 14.1 %collective-permute-start.2 = (bf16[128,1024]{1,0:T(8,128)(2,1)}, bf16[128,1024]{1,0:T(8,128)(2,1)S(1)}, u32[]{:S(2)}, u32[]{:S(2)}) collective-permute-start(bf16[128,1024]{1,0:T(8,128)(2,1)} %refs_0_), channel_id=1, source_target_pairs={{0,8},{4,12},{8,0},{12,4},{16,24},{20,28},{24,16},{28,20},{1,9},{5... | collective-permute-start | bytes 786440 | tf_op jit(solution)/shard_map/ppermute | solution.py:277
  5.6 11.0 %collective-permute-start.1 = (bf16[128,1024]{1,0:T(8,128)(2,1)}, bf16[128,1024]{1,0:T(8,128)(2,1)S(1)}, u32[]{:S(2)}, u32[]{:S(2)}) collective-permute-start(bf16[128,1024]{1,0:T(8,128)(2,1)} %refs_0_), channel_id=1, source_target_pairs={{0,4},{4,0},{8,12},{12,8},{16,20},{20,16},{24,28},{28,24},{1,5},{5... | collective-permute-start | bytes 786440 | tf_op jit(solution)/shard_map/ppermute | solution.py:277
  7.1 6.7 %collective-permute-start = (bf16[16,384]{1,0:T(8,128)(2,1)S(1)}, bf16[16,384]{1,0:T(8,128)(2,1)S(1)}, u32[]{:S(2)}, u32[]{:S(2)}) collective-permute-start(bf16[16,384]{1,0:T(8,128)(2,1)S(1)} %get-tuple-element.38), channel_id=1, source_target_pairs={{4,0},{8,4},{12,8},{16,12},{20,16},{24,20},{28,24},{5,1},{9,5},{13... | collective-permute-start | bytes 36872 | tf_op jit(solution)/shard_map/ppermute | solution.py:301
  8.4 15.2 %collective-permute-start.3 = (bf16[128,1024]{1,0:T(8,128)(2,1)}, bf16[128,1024]{1,0:T(8,128)(2,1)S(1)}, u32[]{:S(2)}, u32[]{:S(2)}) collective-permute-start(bf16[128,1024]{1,0:T(8,128)(2,1)} %refs_0_), channel_id=1, source_target_pairs={{0,16},{4,20},{8,24},{12,28},{16,0},{20,4},{24,8},{28,12},{1,17},{... | collective-permute-start | bytes 786440 | tf_op jit(solution)/shard_map/ppermute | solution.py:277
  16.6 7.0 %collective-permute-start.4 = (bf16[128,1024]{1,0:T(8,128)(2,1)S(1)}, bf16[128,1024]{1,0:T(8,128)(2,1)S(1)}, u32[]{:S(2)}, u32[]{:S(2)}) collective-permute-start(bf16[128,1024]{1,0:T(8,128)(2,1)S(1)} %collective-permute-done.2.refs_2_), channel_id=1, source_target_pairs={{0,4},{4,0},{8,12},{12,8},{16,20},{20,16},{24,28},{28,24},{1,5},{5... | collective-permute-start | bytes 786440 | tf_op jit(solution)/shard_map/ppermute | solution.py:277
  18.1 6.4 %collective-permute-start.7 = (bf16[512,256]{1,0:T(8,128)(2,1)S(1)}, bf16[512,256]{1,0:T(8,128)(2,1)S(1)}, u32[]{:S(2)}, u32[]{:S(2)}) collective-permute-start(bf16[512,256]{1,0:T(8,128)(2,1)S(1)} %get-tuple-element.46.refs_0_), channel_id=1, source_target_pairs={{0,2},{1,3},{2,0},{3,1},{4,6},{5,7},{6,4},{7,5},{8,10},{9,11},{10,... | collective-permute-start | bytes 786440 | tf_op jit(solution)/shard_map/ppermute | solution.py:274
  19.9 3.7 %collective-permute-start.5 = (bf16[32,384]{1,0:T(8,128)(2,1)S(1)}, bf16[32,384]{1,0:T(8,128)(2,1)S(1)}, u32[]{:S(2)}, u32[]{:S(2)}) collective-permute-start(bf16[32,384]{1,0:T(8,128)(2,1)S(1)} %get-tuple-element.45), channel_id=1, source_target_pairs={{0,4},{4,8},{8,12},{12,16},{16,20},{20,24},{24,28},{1,5},{5,9},{9,... | collective-permute-start | bytes 73736 | tf_op jit(solution)/shard_map/ppermute | solution.py:302
  23.6 2.8 %collective-permute-start.6 = (bf16[512,256]{1,0:T(8,128)(2,1)S(1)}, bf16[512,256]{1,0:T(8,128)(2,1)S(1)}, u32[]{:S(2)}, u32[]{:S(2)}) collective-permute-start(bf16[512,256]{1,0:T(8,128)(2,1)S(1)} %get-tuple-element.46.refs_0_), channel_id=1, source_target_pairs={{0,1},{1,0},{2,3},{3,2},{4,5},{5,4},{6,7},{7,6},{8,9},{9,8},{10,11... | collective-permute-start | bytes 786440 | tf_op jit(solution)/shard_map/ppermute | solution.py:274
  24.4 2.0 %collective-permute-start.8 = (bf16[512,256]{1,0:T(8,128)(2,1)S(1)}, bf16[512,256]{1,0:T(8,128)(2,1)S(1)}, u32[]{:S(2)}, u32[]{:S(2)}) collective-permute-start(bf16[512,256]{1,0:T(8,128)(2,1)S(1)} %collective-permute-done.7.refs_2_), channel_id=1, source_target_pairs={{0,1},{1,0},{2,3},{3,2},{4,5},{5,4},{6,7},{7,6},{8,9},{9,8},{10,11... | collective-permute-start | bytes 786440 | tf_op jit(solution)/shard_map/ppermute | solution.py:274
  24.4 9.1 %collective-permute-start.9 = (bf16[128,1024]{1,0:T(8,128)(2,1)S(1)}, bf16[128,1024]{1,0:T(8,128)(2,1)S(1)}, u32[]{:S(2)}, u32[]{:S(2)}) collective-permute-start(bf16[128,1024]{1,0:T(8,128)(2,1)S(1)} %collective-permute-done.3.refs_4_), channel_id=1, source_target_pairs={{0,4},{4,0},{8,12},{12,8},{16,20},{20,16},{24,28},{28,24},{1,5},{5... | collective-permute-start | bytes 786440 | tf_op jit(solution)/shard_map/ppermute | solution.py:277
  28.2 10.6 %collective-permute-start.12 = (bf16[128,1024]{1,0:T(8,128)(2,1)S(1)}, bf16[128,1024]{1,0:T(8,128)(2,1)S(1)}, u32[]{:S(2)}, u32[]{:S(2)}) collective-permute-start(bf16[128,1024]{1,0:T(8,128)(2,1)S(1)} %get-tuple-element.53), channel_id=1, source_target_pairs={{0,4},{4,0},{8,12},{12,8},{16,20},{20,16},{24,28},{28,24},{1,5},{5... | collective-permute-start | bytes 786440 | tf_op jit(solution)/shard_map/ppermute | solution.py:277
  29.6 12.4 %collective-permute-start.10 = (bf16[128,1024]{1,0:T(8,128)(2,1)S(1)}, bf16[128,1024]{1,0:T(8,128)(2,1)S(1)}, u32[]{:S(2)}, u32[]{:S(2)}) collective-permute-start(bf16[128,1024]{1,0:T(8,128)(2,1)S(1)} %collective-permute-done.3.refs_4_), channel_id=1, source_target_pairs={{0,8},{4,12},{8,0},{12,4},{16,24},{20,28},{24,16},{28,20},{1,9},{5... | collective-permute-start | bytes 786440 | tf_op jit(solution)/shard_map/ppermute | solution.py:277
  33.5 10.9 %collective-permute-start.11 = (bf16[128,1024]{1,0:T(8,128)(2,1)S(1)}, bf16[128,1024]{1,0:T(8,128)(2,1)S(1)}, u32[]{:S(2)}, u32[]{:S(2)}) collective-permute-start(bf16[128,1024]{1,0:T(8,128)(2,1)S(1)} %collective-permute-done.9.refs_5_), channel_id=1, source_target_pairs={{0,8},{4,12},{8,0},{12,4},{16,24},{20,28},{24,16},{28,20},{1,9},{5... | collective-permute-start | bytes 786440 | tf_op jit(solution)/shard_map/ppermute | solution.py:277
  38.8 10.1 %collective-permute-start.16 = (bf16[128,1024]{1,0:T(8,128)(2,1)S(1)}, bf16[128,1024]{1,0:T(8,128)(2,1)S(1)}, u32[]{:S(2)}, u32[]{:S(2)}) collective-permute-start(bf16[128,1024]{1,0:T(8,128)(2,1)S(1)} %add_convert_fusion.2), channel_id=1, source_target_pairs={{0,8},{4,12},{8,0},{12,4},{16,24},{20,28},{24,16},{28,20},{1,9},{5... | collective-permute-start | bytes 786440 | tf_op jit(solution)/shard_map/ppermute | solution.py:277
  40.9 11.9 %collective-permute-start.13 = (bf16[128,1024]{1,0:T(8,128)(2,1)S(1)}, bf16[128,1024]{1,0:T(8,128)(2,1)S(1)}, u32[]{:S(2)}, u32[]{:S(2)}) collective-permute-start(bf16[128,1024]{1,0:T(8,128)(2,1)S(1)} %get-tuple-element.54), channel_id=1, source_target_pairs={{0,4},{4,0},{8,12},{12,8},{16,20},{20,16},{24,28},{28,24},{1,5},{5... | collective-permute-start | bytes 786440 | tf_op jit(solution)/shard_map/ppermute | solution.py:277
  46.9 9.4 %collective-permute-start.14 = (bf16[528,256]{1,0:T(8,128)(2,1)S(1)}, bf16[528,256]{1,0:T(8,128)(2,1)S(1)}, u32[]{:S(2)}, u32[]{:S(2)}) collective-permute-start(bf16[528,256]{1,0:T(8,128)(2,1)S(1)} %get-tuple-element.55), channel_id=1, source_target_pairs={{0,2},{1,3},{2,0},{3,1},{4,6},{5,7},{6,4},{7,5},{8,10},{9,11},{10,... | collective-permute-start | bytes 811016 | tf_op jit(solution)/shard_map/ppermute | solution.py:274
  48.9 7.8 %collective-permute-start.18 = (bf16[128,1024]{1,0:T(8,128)(2,1)S(1)}, bf16[128,1024]{1,0:T(8,128)(2,1)S(1)}, u32[]{:S(2)}, u32[]{:S(2)}) collective-permute-start(bf16[128,1024]{1,0:T(8,128)(2,1)S(1)} %get-tuple-element.64), channel_id=1, source_target_pairs={{0,4},{4,0},{8,12},{12,8},{16,20},{20,16},{24,28},{28,24},{1,5},{5... | collective-permute-start | bytes 786440 | tf_op jit(solution)/shard_map/ppermute | solution.py:277
  51.4 8.8 %collective-permute-start.20 = (bf16[528,256]{1,0:T(8,128)(2,1)S(1)}, bf16[528,256]{1,0:T(8,128)(2,1)S(1)}, u32[]{:S(2)}, u32[]{:S(2)}) collective-permute-start(bf16[528,256]{1,0:T(8,128)(2,1)S(1)} %get-tuple-element.66), channel_id=1, source_target_pairs={{0,1},{1,0},{2,3},{3,2},{4,5},{5,4},{6,7},{7,6},{8,9},{9,8},{10,11... | collective-permute-start | bytes 811016 | tf_op jit(solution)/shard_map/ppermute | solution.py:274
  51.5 8.7 %collective-permute-start.21 = (bf16[528,256]{1,0:T(8,128)(2,1)S(1)}, bf16[528,256]{1,0:T(8,128)(2,1)S(1)}, u32[]{:S(2)}, u32[]{:S(2)}) collective-permute-start(bf16[528,256]{1,0:T(8,128)(2,1)S(1)} %get-tuple-element.67), channel_id=1, source_target_pairs={{0,3},{1,2},{2,1},{3,0},{4,7},{5,6},{6,5},{7,4},{8,11},{9,10},{10,... | collective-permute-start | bytes 811016 | tf_op jit(solution)/shard_map/ppermute | solution.py:274
  53.0 15.5 %collective-permute-start.17 = (bf16[128,1024]{1,0:T(8,128)(2,1)S(1)}, bf16[128,1024]{1,0:T(8,128)(2,1)S(1)}, u32[]{:S(2)}, u32[]{:S(2)}) collective-permute-start(bf16[128,1024]{1,0:T(8,128)(2,1)S(1)} %add_convert_fusion.1), channel_id=1, source_target_pairs={{0,16},{4,20},{8,24},{12,28},{16,0},{20,4},{24,8},{28,12},{1,17},{... | collective-permute-start | bytes 786440 | tf_op jit(solution)/shard_map/ppermute | solution.py:277
  56.4 12.1 %collective-permute-start.15 = (bf16[128,1024]{1,0:T(8,128)(2,1)S(1)}, bf16[128,1024]{1,0:T(8,128)(2,1)S(1)}, u32[]{:S(2)}, u32[]{:S(2)}) collective-permute-start(bf16[128,1024]{1,0:T(8,128)(2,1)S(1)} %get-tuple-element.59), channel_id=1, source_target_pairs={{0,4},{4,0},{8,12},{12,8},{16,20},{20,16},{24,28},{28,24},{1,5},{5... | collective-permute-start | bytes 786440 | tf_op jit(solution)/shard_map/ppermute | solution.py:277
  56.8 13.3 %collective-permute-start.19 = (bf16[128,1024]{1,0:T(8,128)(2,1)S(1)}, bf16[128,1024]{1,0:T(8,128)(2,1)S(1)}, u32[]{:S(2)}, u32[]{:S(2)}) collective-permute-start(bf16[128,1024]{1,0:T(8,128)(2,1)S(1)} %add_convert_fusion), channel_id=1, source_target_pairs={{0,8},{4,12},{8,0},{12,4},{16,24},{20,28},{24,16},{28,20},{1,9},{5... | collective-permute-start | bytes 786440 | tf_op jit(solution)/shard_map/ppermute | solution.py:277
  (4 other events, 23.3 us)
